TPU v7x, 32 devices: a whole 2x2x4 slice. The times are simulated.
32 devices in a mesh: dom: 2 (over y), atoms: 4 (over z), modes: 2 (over x), sub: 2 (over core).
Axes of the slice: x: 2, y: 2, z: 4, core: 2. Of those that a mesh axis runs over, the one named last changes fastest.
Arguments:
- mode_panel: bfloat16 [3, 6144, 512], P(None, ('dom', 'atoms'), ('modes', 'sub')), parts along dimension 1, may hold values from -6 to 6
- partners: bfloat16 [3, 6144, 2560], P(None, ('dom', 'atoms'), ('modes', 'sub')), parts along dimension 1, may hold values from -6 to 6
- bond_blocks: float32 [9, 6144, 16], P(None, ('dom', 'atoms')), parts along dimension 1, may hold values from -1.5 to 1.5
- neighbors: int32 [6144, 16], P(('dom', 'atoms')), parts along dimension 0, may hold values from 0 to 3071, as said below
- bond_count: int32 [6144], P(('dom', 'atoms')), parts along dimension 0, may hold values from 4 to 16
- panel_freq: float32 [1024], P('dom'), parts along dimension 0, may hold values from 1 to 2
- partner_freq: float32 [5120], P(('dom', 'modes', 'sub')), parts along dimension 0, may hold values from 1 to 2
- win_start: int32 [1024], P('dom'), parts along dimension 0, may hold values from 0 to 1535, as said below
- win_len: int32 [1024], P('dom'), parts along dimension 0, may hold values from 1024 to 2048, as said below
Outputs:
- elements: float32 [1024, 2560], P(('dom', 'atoms'), ('modes', 'sub')), parts along dimension 0
- diffusivity: float32 [1024], P(('dom', 'atoms')), parts along dimension 0
There are 2 independent parts, one for each index of `dom`. A program takes and returns all parts, laid end to end along the dimension named above; each array names one. Nothing has to cross between parts.
Inputs may be any that keep to these rules, and one draw needn't show every extreme that they name: `neighbors`: every neighbor lies within 96 atoms of its own atom in atom order, and some bonds reach exactly 96. Slots k >= bond_count[a] of atom a are padding. Each window lies inside the partner modes: win_start[j] + win_len[j] <= 2560. `win_len`: some panel mode has exactly 2048 partners.
All inputs are finite; a program needn't handle non-finite values.
Results may differ from a plain program's by a relative error of at most 0.003.
Values may be sent and summed in bfloat16 or wider, within the bound.
No kernel may reach another device: no remote copies, remote signals or barrier semaphores. Data moves between devices by JAX's collectives and lax.ppermute only.
A program may use at most 64 MiB of HBM per device.

v0:
```python
import math

import jax
import jax.numpy as jnp
from jax import lax
from jax.sharding import PartitionSpec as P

HALO = 96
BONDS = 16


lorentz_width = 0.05


def padded(cells, sides, width):
    for axis, dim in sides:
        count = lax.axis_size(axis)
        ends = count - 1
        head = lax.slice_in_dim(cells, 0, width, axis=dim)
        tail = lax.slice_in_dim(cells, cells.shape[dim] - width, cells.shape[dim], axis=dim)
        cells = jnp.concatenate(
            [
                lax.ppermute(tail, axis, [(i, (i + 1) % count) for i in range(ends)]),
                cells,
                lax.ppermute(head, axis, [((i + 1) % count, i) for i in range(ends)]),
            ],
            axis=dim,
        )
    return cells


def body(
    mode_panel,
    partners,
    bond_blocks,
    neighbors,
    bond_count,
    panel_freq,
    partner_freq,
    win_start,
    win_len,
):
    atom_rows = mode_panel.shape[1]
    atom_index = lax.axis_index("atoms")
    atom_count = lax.axis_size("atoms")
    column_index = lax.axis_index(("modes", "sub"))
    part_cols = partners.shape[2]
    extended = padded(mode_panel, (("atoms", 1),), HALO)
    local_rows = neighbors - atom_index * atom_rows + HALO
    slot_ids = jnp.arange(BONDS, dtype=jnp.int32)
    live_slot = (slot_ids[None, :] < bond_count[:, None]).astype(jnp.float32)
    coefficient = bond_blocks * live_slot[None]

    def slot_step(slot_index, summed):
        target = lax.dynamic_index_in_dim(local_rows, slot_index, 1, keepdims=False)
        gathered = jnp.take(extended, target, axis=1)
        coef_slot = lax.dynamic_index_in_dim(coefficient, slot_index, 2, keepdims=False).reshape(
            3, 3, atom_rows
        )
        for d in range(3):
            summed = summed + coef_slot[:, d, :, None] * gathered[d][None]
        return summed

    summed = lax.fori_loop(0, BONDS, slot_step, jnp.zeros(mode_panel.shape, jnp.float32))
    images = summed.astype(jnp.bfloat16)
    all_images = lax.all_gather(images, ("modes", "sub"), axis=2, tiled=True)
    panel_total = all_images.shape[2]
    rows_dev = panel_total // atom_count
    first_col = column_index * part_cols
    touched = jnp.any((win_start < first_col + part_cols) & (win_start + win_len > first_col))
    full_sums = lax.psum(
        lax.cond(
            touched,
            lambda: lax.dot_general(
                all_images,
                partners,
                (((0, 1), (0, 1)), ((), ())),
                preferred_element_type=jnp.float32,
            ),
            lambda: jnp.zeros((panel_total, part_cols), jnp.float32),
        ),
        "atoms",
    )
    products = lax.dynamic_slice_in_dim(full_sums, atom_index * rows_dev, rows_dev, 0)
    norm_scale = 1.0 / math.sqrt(3 * atom_rows * atom_count)
    my_start = lax.dynamic_slice_in_dim(win_start, atom_index * rows_dev, rows_dev, 0)
    my_length = lax.dynamic_slice_in_dim(win_len, atom_index * rows_dev, rows_dev, 0)
    my_freq = lax.dynamic_slice_in_dim(panel_freq, atom_index * rows_dev, rows_dev, 0)
    columns = first_col + jnp.arange(part_cols, dtype=jnp.int32)
    inside = (columns[None, :] >= my_start[:, None]) & (
        columns[None, :] < my_start[:, None] + my_length[:, None]
    )
    elements = jnp.where(inside, products * norm_scale, 0.0)
    offset_freq = my_freq[:, None] - partner_freq[None, :]
    lorentz = lorentz_width / (
        math.pi * (offset_freq * offset_freq + lorentz_width * lorentz_width)
    )
    weight = jnp.where(inside, lorentz, 0.0)
    numerator = lax.psum(jnp.sum(weight * elements * elements, axis=1), ("modes", "sub"))
    diffusivity = math.pi / 3.0 * numerator / (my_freq * my_freq)
    return (elements, diffusivity)


def solution(mesh):
    return jax.shard_map(
        body,
        mesh=mesh,
        in_specs=(
            P(None, ("dom", "atoms"), ("modes", "sub")),
            P(None, ("dom", "atoms"), ("modes", "sub")),
            P(None, ("dom", "atoms"), None),
            P(("dom", "atoms"), None),
            P(("dom", "atoms")),
            P("dom"),
            P(("dom", "modes", "sub")),
            P("dom"),
            P("dom"),
        ),
        out_specs=(P(("dom", "atoms"), ("modes", "sub")), P(("dom", "atoms"))),
        check_vma=False,
    )
```

profile of v0, /device:TPU:0, one launch (start us, length us, event | category | flops | bytes accessed | tf_op | source)
XLA Modules:
  0.0 268.6 jit_solution(18099488347501536517)
XLA Ops:
  7.2 1.6 copy.14
  8.9 4.9 %collective-permute-start = (bf16[3,96,128]{2,0,1:T(4,128)(2,1)S(1)}, bf16[3,96,128]{2,0,1:T(4,128)(2,1)S(1)}, u32[]{:S(2)}, u32[]{:S(2)}) collective-permute-start(bf16[3,96,128]{2,0,1:T(4,128)(2,1)S(1)} %get-tuple-element.152), channel_id=1, source_target_pairs={{0,4},{4,8},{8,12},{1,5},{5,9},{9,13},{2,6},{6,10},{10,14},{3,7},{... | collective-permute-start | bytes 221192 | tf_op jit(solution)/shard_map/ppermute | solution.py:23
  13.9 1.3 collective-permute-start.1
  16.4 4.0 %collective-permute-done.1 = bf16[3,96,128]{2,0,1:T(4,128)(2,1)S(1)} collective-permute-done((bf16[3,96,128]{2,0,1:T(4,128)(2,1)S(1)}, bf16[3,96,128]{2,0,1:T(4,128)(2,1)S(1)}, u32[]{:S(2)}, u32[]{:S(2)}) %collective-permute-start.1) | collective-permute-done | bytes 73760 | tf_op jit(solution)/shard_map/ppermute | solution.py:25
  21.1 140.3 %while.14 = (s32[]{:T(128)}, f32[3,768,128]{2,1,0:T(8,128)S(1)}, f32[9,768,16]{1,0,2:T(8,128)}, s32[768,16]{0,1:T(8,128)S(1)}, bf16[3,960,128]{2,0,1:T(4,128)(2,1)S(1)}, /*index=5*/s32[]{:T(128)}, s32[]{:T(128)}) while((s32[]{:T(128)}, f32[3,768,128]{2,1,0:T(8,128)S(1)}, f32[9,768,16]{1,0,2:T(8,128)}, s32[768,16]{0,1:T(8,128)S(1)}, ...), condition=%wide.region_2.3_spmd.clone, body=%wide.region_1.2_spmd.clone.sunk | while | flops 2659843 | bytes 7940707 | solution.py:64
  21.2 2.8 %gather_fusion = bf16[768,3,128]{2,1,0:T(4,128)(2,1)S(1)} fusion(bf16[3,960,128]{2,0,1:T(4,128)(2,1)S(1)} %get-tuple-element.225, s32[1024]{0:T(1024)S(1)} %pad_clamp_fusion.2), kind=kCustom, calls=%fused_computation.clone.clone.1 | custom fusion | bytes 1182720 | tf_op jit(solution)/shard_map/while/body/eval_jaxpr/jit(_take)/gather | solution.py:56
  24.0 2.9 %select_bitcast_fusion.2 = bf16[3,768,128]{2,0,1:T(4,128)(2,1)S(1)} fusion(bf16[768,3,128]{2,1,0:T(4,128)(2,1)S(1)} %gather_fusion, pred[768]{0:T(1024)(128)(4,1)S(1)} %get-tuple-element.198), kind=kLoop, calls=%fused_computation.5.clone.1 | loop fusion | flops 294912 | bytes 1180416 | tf_op jit(solution)/shard_map/while/body/eval_jaxpr/jit(_take)/select_n | solution.py:56
  29.9 2.8 %gather_fusion = bf16[768,3,128]{2,1,0:T(4,128)(2,1)S(1)} fusion(bf16[3,960,128]{2,0,1:T(4,128)(2,1)S(1)} %get-tuple-element.225, s32[1024]{0:T(1024)S(1)} %pad_clamp_fusion.2), kind=kCustom, calls=%fused_computation.clone.clone.1 | custom fusion | bytes 1182720 | tf_op jit(solution)/shard_map/while/body/eval_jaxpr/jit(_take)/gather | solution.py:56
  32.8 2.9 %select_bitcast_fusion.2 = bf16[3,768,128]{2,0,1:T(4,128)(2,1)S(1)} fusion(bf16[768,3,128]{2,1,0:T(4,128)(2,1)S(1)} %gather_fusion, pred[768]{0:T(1024)(128)(4,1)S(1)} %get-tuple-element.198), kind=kLoop, calls=%fused_computation.5.clone.1 | loop fusion | flops 294912 | bytes 1180416 | tf_op jit(solution)/shard_map/while/body/eval_jaxpr/jit(_take)/select_n | solution.py:56
  38.7 2.8 %gather_fusion = bf16[768,3,128]{2,1,0:T(4,128)(2,1)S(1)} fusion(bf16[3,960,128]{2,0,1:T(4,128)(2,1)S(1)} %get-tuple-element.225, s32[1024]{0:T(1024)S(1)} %pad_clamp_fusion.2), kind=kCustom, calls=%fused_computation.clone.clone.1 | custom fusion | bytes 1182720 | tf_op jit(solution)/shard_map/while/body/eval_jaxpr/jit(_take)/gather | solution.py:56
  41.6 2.9 %select_bitcast_fusion.2 = bf16[3,768,128]{2,0,1:T(4,128)(2,1)S(1)} fusion(bf16[768,3,128]{2,1,0:T(4,128)(2,1)S(1)} %gather_fusion, pred[768]{0:T(1024)(128)(4,1)S(1)} %get-tuple-element.198), kind=kLoop, calls=%fused_computation.5.clone.1 | loop fusion | flops 294912 | bytes 1180416 | tf_op jit(solution)/shard_map/while/body/eval_jaxpr/jit(_take)/select_n | solution.py:56
  47.5 2.8 %gather_fusion = bf16[768,3,128]{2,1,0:T(4,128)(2,1)S(1)} fusion(bf16[3,960,128]{2,0,1:T(4,128)(2,1)S(1)} %get-tuple-element.225, s32[1024]{0:T(1024)S(1)} %pad_clamp_fusion.2), kind=kCustom, calls=%fused_computation.clone.clone.1 | custom fusion | bytes 1182720 | tf_op jit(solution)/shard_map/while/body/eval_jaxpr/jit(_take)/gather | solution.py:56
  50.3 2.9 %select_bitcast_fusion.2 = bf16[3,768,128]{2,0,1:T(4,128)(2,1)S(1)} fusion(bf16[768,3,128]{2,1,0:T(4,128)(2,1)S(1)} %gather_fusion, pred[768]{0:T(1024)(128)(4,1)S(1)} %get-tuple-element.198), kind=kLoop, calls=%fused_computation.5.clone.1 | loop fusion | flops 294912 | bytes 1180416 | tf_op jit(solution)/shard_map/while/body/eval_jaxpr/jit(_take)/select_n | solution.py:56
  56.2 2.8 %gather_fusion = bf16[768,3,128]{2,1,0:T(4,128)(2,1)S(1)} fusion(bf16[3,960,128]{2,0,1:T(4,128)(2,1)S(1)} %get-tuple-element.225, s32[1024]{0:T(1024)S(1)} %pad_clamp_fusion.2), kind=kCustom, calls=%fused_computation.clone.clone.1 | custom fusion | bytes 1182720 | tf_op jit(solution)/shard_map/while/body/eval_jaxpr/jit(_take)/gather | solution.py:56
  59.1 2.9 %select_bitcast_fusion.2 = bf16[3,768,128]{2,0,1:T(4,128)(2,1)S(1)} fusion(bf16[768,3,128]{2,1,0:T(4,128)(2,1)S(1)} %gather_fusion, pred[768]{0:T(1024)(128)(4,1)S(1)} %get-tuple-element.198), kind=kLoop, calls=%fused_computation.5.clone.1 | loop fusion | flops 294912 | bytes 1180416 | tf_op jit(solution)/shard_map/while/body/eval_jaxpr/jit(_take)/select_n | solution.py:56
  65.0 2.8 %gather_fusion = bf16[768,3,128]{2,1,0:T(4,128)(2,1)S(1)} fusion(bf16[3,960,128]{2,0,1:T(4,128)(2,1)S(1)} %get-tuple-element.225, s32[1024]{0:T(1024)S(1)} %pad_clamp_fusion.2), kind=kCustom, calls=%fused_computation.clone.clone.1 | custom fusion | bytes 1182720 | tf_op jit(solution)/shard_map/while/body/eval_jaxpr/jit(_take)/gather | solution.py:56
  67.9 2.9 %select_bitcast_fusion.2 = bf16[3,768,128]{2,0,1:T(4,128)(2,1)S(1)} fusion(bf16[768,3,128]{2,1,0:T(4,128)(2,1)S(1)} %gather_fusion, pred[768]{0:T(1024)(128)(4,1)S(1)} %get-tuple-element.198), kind=kLoop, calls=%fused_computation.5.clone.1 | loop fusion | flops 294912 | bytes 1180416 | tf_op jit(solution)/shard_map/while/body/eval_jaxpr/jit(_take)/select_n | solution.py:56
  73.8 2.8 %gather_fusion = bf16[768,3,128]{2,1,0:T(4,128)(2,1)S(1)} fusion(bf16[3,960,128]{2,0,1:T(4,128)(2,1)S(1)} %get-tuple-element.225, s32[1024]{0:T(1024)S(1)} %pad_clamp_fusion.2), kind=kCustom, calls=%fused_computation.clone.clone.1 | custom fusion | bytes 1182720 | tf_op jit(solution)/shard_map/while/body/eval_jaxpr/jit(_take)/gather | solution.py:56
  76.6 2.9 %select_bitcast_fusion.2 = bf16[3,768,128]{2,0,1:T(4,128)(2,1)S(1)} fusion(bf16[768,3,128]{2,1,0:T(4,128)(2,1)S(1)} %gather_fusion, pred[768]{0:T(1024)(128)(4,1)S(1)} %get-tuple-element.198), kind=kLoop, calls=%fused_computation.5.clone.1 | loop fusion | flops 294912 | bytes 1180416 | tf_op jit(solution)/shard_map/while/body/eval_jaxpr/jit(_take)/select_n | solution.py:56
  82.6 2.8 %gather_fusion = bf16[768,3,128]{2,1,0:T(4,128)(2,1)S(1)} fusion(bf16[3,960,128]{2,0,1:T(4,128)(2,1)S(1)} %get-tuple-element.225, s32[1024]{0:T(1024)S(1)} %pad_clamp_fusion.2), kind=kCustom, calls=%fused_computation.clone.clone.1 | custom fusion | bytes 1182720 | tf_op jit(solution)/shard_map/while/body/eval_jaxpr/jit(_take)/gather | solution.py:56
  85.4 2.9 %select_bitcast_fusion.2 = bf16[3,768,128]{2,0,1:T(4,128)(2,1)S(1)} fusion(bf16[768,3,128]{2,1,0:T(4,128)(2,1)S(1)} %gather_fusion, pred[768]{0:T(1024)(128)(4,1)S(1)} %get-tuple-element.198), kind=kLoop, calls=%fused_computation.5.clone.1 | loop fusion | flops 294912 | bytes 1180416 | tf_op jit(solution)/shard_map/while/body/eval_jaxpr/jit(_take)/select_n | solution.py:56
  90.0 1.2 fusion.14
  91.3 2.8 %gather_fusion = bf16[768,3,128]{2,1,0:T(4,128)(2,1)S(1)} fusion(bf16[3,960,128]{2,0,1:T(4,128)(2,1)S(1)} %get-tuple-element.225, s32[1024]{0:T(1024)S(1)} %pad_clamp_fusion.2), kind=kCustom, calls=%fused_computation.clone.clone.1 | custom fusion | bytes 1182720 | tf_op jit(solution)/shard_map/while/body/eval_jaxpr/jit(_take)/gather | solution.py:56
  94.2 2.9 %select_bitcast_fusion.2 = bf16[3,768,128]{2,0,1:T(4,128)(2,1)S(1)} fusion(bf16[768,3,128]{2,1,0:T(4,128)(2,1)S(1)} %gather_fusion, pred[768]{0:T(1024)(128)(4,1)S(1)} %get-tuple-element.198), kind=kLoop, calls=%fused_computation.5.clone.1 | loop fusion | flops 294912 | bytes 1180416 | tf_op jit(solution)/shard_map/while/body/eval_jaxpr/jit(_take)/select_n | solution.py:56
  98.8 1.2 fusion.14
  100.1 2.8 %gather_fusion = bf16[768,3,128]{2,1,0:T(4,128)(2,1)S(1)} fusion(bf16[3,960,128]{2,0,1:T(4,128)(2,1)S(1)} %get-tuple-element.225, s32[1024]{0:T(1024)S(1)} %pad_clamp_fusion.2), kind=kCustom, calls=%fused_computation.clone.clone.1 | custom fusion | bytes 1182720 | tf_op jit(solution)/shard_map/while/body/eval_jaxpr/jit(_take)/gather | solution.py:56
  102.9 2.9 %select_bitcast_fusion.2 = bf16[3,768,128]{2,0,1:T(4,128)(2,1)S(1)} fusion(bf16[768,3,128]{2,1,0:T(4,128)(2,1)S(1)} %gather_fusion, pred[768]{0:T(1024)(128)(4,1)S(1)} %get-tuple-element.198), kind=kLoop, calls=%fused_computation.5.clone.1 | loop fusion | flops 294912 | bytes 1180416 | tf_op jit(solution)/shard_map/while/body/eval_jaxpr/jit(_take)/select_n | solution.py:56
  107.5 1.2 fusion.14
  108.9 2.8 %gather_fusion = bf16[768,3,128]{2,1,0:T(4,128)(2,1)S(1)} fusion(bf16[3,960,128]{2,0,1:T(4,128)(2,1)S(1)} %get-tuple-element.225, s32[1024]{0:T(1024)S(1)} %pad_clamp_fusion.2), kind=kCustom, calls=%fused_computation.clone.clone.1 | custom fusion | bytes 1182720 | tf_op jit(solution)/shard_map/while/body/eval_jaxpr/jit(_take)/gather | solution.py:56
  111.7 2.9 %select_bitcast_fusion.2 = bf16[3,768,128]{2,0,1:T(4,128)(2,1)S(1)} fusion(bf16[768,3,128]{2,1,0:T(4,128)(2,1)S(1)} %gather_fusion, pred[768]{0:T(1024)(128)(4,1)S(1)} %get-tuple-element.198), kind=kLoop, calls=%fused_computation.5.clone.1 | loop fusion | flops 294912 | bytes 1180416 | tf_op jit(solution)/shard_map/while/body/eval_jaxpr/jit(_take)/select_n | solution.py:56
  116.3 1.2 fusion.14
  117.6 2.8 %gather_fusion = bf16[768,3,128]{2,1,0:T(4,128)(2,1)S(1)} fusion(bf16[3,960,128]{2,0,1:T(4,128)(2,1)S(1)} %get-tuple-element.225, s32[1024]{0:T(1024)S(1)} %pad_clamp_fusion.2), kind=kCustom, calls=%fused_computation.clone.clone.1 | custom fusion | bytes 1182720 | tf_op jit(solution)/shard_map/while/body/eval_jaxpr/jit(_take)/gather | solution.py:56
  120.5 2.9 %select_bitcast_fusion.2 = bf16[3,768,128]{2,0,1:T(4,128)(2,1)S(1)} fusion(bf16[768,3,128]{2,1,0:T(4,128)(2,1)S(1)} %gather_fusion, pred[768]{0:T(1024)(128)(4,1)S(1)} %get-tuple-element.198), kind=kLoop, calls=%fused_computation.5.clone.1 | loop fusion | flops 294912 | bytes 1180416 | tf_op jit(solution)/shard_map/while/body/eval_jaxpr/jit(_take)/select_n | solution.py:56
  125.1 1.2 fusion.14
  126.4 2.8 %gather_fusion = bf16[768,3,128]{2,1,0:T(4,128)(2,1)S(1)} fusion(bf16[3,960,128]{2,0,1:T(4,128)(2,1)S(1)} %get-tuple-element.225, s32[1024]{0:T(1024)S(1)} %pad_clamp_fusion.2), kind=kCustom, calls=%fused_computation.clone.clone.1 | custom fusion | bytes 1182720 | tf_op jit(solution)/shard_map/while/body/eval_jaxpr/jit(_take)/gather | solution.py:56
  129.2 2.9 %select_bitcast_fusion.2 = bf16[3,768,128]{2,0,1:T(4,128)(2,1)S(1)} fusion(bf16[768,3,128]{2,1,0:T(4,128)(2,1)S(1)} %gather_fusion, pred[768]{0:T(1024)(128)(4,1)S(1)} %get-tuple-element.198), kind=kLoop, calls=%fused_computation.5.clone.1 | loop fusion | flops 294912 | bytes 1180416 | tf_op jit(solution)/shard_map/while/body/eval_jaxpr/jit(_take)/select_n | solution.py:56
  135.2 2.8 %gather_fusion = bf16[768,3,128]{2,1,0:T(4,128)(2,1)S(1)} fusion(bf16[3,960,128]{2,0,1:T(4,128)(2,1)S(1)} %get-tuple-element.225, s32[1024]{0:T(1024)S(1)} %pad_clamp_fusion.2), kind=kCustom, calls=%fused_computation.clone.clone.1 | custom fusion | bytes 1182720 | tf_op jit(solution)/shard_map/while/body/eval_jaxpr/jit(_take)/gather | solution.py:56
  138.0 2.9 %select_bitcast_fusion.2 = bf16[3,768,128]{2,0,1:T(4,128)(2,1)S(1)} fusion(bf16[768,3,128]{2,1,0:T(4,128)(2,1)S(1)} %gather_fusion, pred[768]{0:T(1024)(128)(4,1)S(1)} %get-tuple-element.198), kind=kLoop, calls=%fused_computation.5.clone.1 | loop fusion | flops 294912 | bytes 1180416 | tf_op jit(solution)/shard_map/while/body/eval_jaxpr/jit(_take)/select_n | solution.py:56
  143.9 2.8 %gather_fusion = bf16[768,3,128]{2,1,0:T(4,128)(2,1)S(1)} fusion(bf16[3,960,128]{2,0,1:T(4,128)(2,1)S(1)} %get-tuple-element.225, s32[1024]{0:T(1024)S(1)} %pad_clamp_fusion.2), kind=kCustom, calls=%fused_computation.clone.clone.1 | custom fusion | bytes 1182720 | tf_op jit(solution)/shard_map/while/body/eval_jaxpr/jit(_take)/gather | solution.py:56
  146.8 2.9 %select_bitcast_fusion.2 = bf16[3,768,128]{2,0,1:T(4,128)(2,1)S(1)} fusion(bf16[768,3,128]{2,1,0:T(4,128)(2,1)S(1)} %gather_fusion, pred[768]{0:T(1024)(128)(4,1)S(1)} %get-tuple-element.198), kind=kLoop, calls=%fused_computation.5.clone.1 | loop fusion | flops 294912 | bytes 1180416 | tf_op jit(solution)/shard_map/while/body/eval_jaxpr/jit(_take)/select_n | solution.py:56
  152.7 2.8 %gather_fusion = bf16[768,3,128]{2,1,0:T(4,128)(2,1)S(1)} fusion(bf16[3,960,128]{2,0,1:T(4,128)(2,1)S(1)} %get-tuple-element.225, s32[1024]{0:T(1024)S(1)} %pad_clamp_fusion.2), kind=kCustom, calls=%fused_computation.clone.clone.1 | custom fusion | bytes 1182720 | tf_op jit(solution)/shard_map/while/body/eval_jaxpr/jit(_take)/gather | solution.py:56
  155.5 2.9 %select_bitcast_fusion.2 = bf16[3,768,128]{2,0,1:T(4,128)(2,1)S(1)} fusion(bf16[768,3,128]{2,1,0:T(4,128)(2,1)S(1)} %gather_fusion, pred[768]{0:T(1024)(128)(4,1)S(1)} %get-tuple-element.198), kind=kLoop, calls=%fused_computation.5.clone.1 | loop fusion | flops 294912 | bytes 1180416 | tf_op jit(solution)/shard_map/while/body/eval_jaxpr/jit(_take)/select_n | solution.py:56
  163.7 23.4 %all-gather.2.cloned.1.call-done = bf16[3,768,512]{2,1,0:T(8,128)(2,1)} async-done(((bf16[3,768,128]{2,1,0:T(8,128)(2,1)}), bf16[3,768,512]{2,1,0:T(8,128)(2,1)}) %all-gather.2.cloned.1.call-update) | async-done | bytes 2359312 | tf_op jit(solution)/shard_map/all_gather | solution.py:66
  187.1 4.6 %conditional.1 = (f32[512,640]{1,0:T(8,128)S(1)}) conditional(s32[]{:T(128)} %convert_element_type.28, () %tuple.28, (bf16[3,768,512]{2,1,0:T(8,128)(2,1)}, bf16[3,768,640]{2,1,0:T(8,128)(2,1)}) %tuple.30), branch_computations={%region_3.4_spmd, %region_4.5_spmd} | conditional | flops 1509949440 | bytes 6619144 | solution.py:72
  187.1 4.6 %convolution_bitcast_fusion = f32[512,640]{1,0:T(8,128)S(1)} fusion(bf16[3,768,512]{2,1,0:T(8,128)(2,1)} %get-tuple-element.128, bf16[3,768,640]{2,1,0:T(8,128)(2,1)} %get-tuple-element.107), kind=kOutput, calls=%fused_computation.1 | convolution fusion | flops 1509949440 | bytes 6619136 | tf_op jit(solution)/shard_map/cond/branch_1_fun/dot_general | solution.py:74
  192.9 60.0 %all-reduce.2.cloned.1.call-done = f32[512,640]{1,0:T(8,128)} async-done(((f32[512,640]{1,0:T(8,128)}), f32[512,640]{1,0:T(8,128)}) %all-reduce.2.cloned.1.call-update) | async-done | bytes 1310736 | tf_op jit(solution)/shard_map/psum | solution.py:71
  252.9 1.9 fusion.2
  254.8 6.4 %psum.15 = f32[128]{0:T(128)S(1)} all-reduce(f32[128]{0:T(128)S(1)} %get-tuple-element.142), channel_id=1, replica_groups=mesh['dom'=2,'atoms'=4,'modes'=2,'sub'=2] {'modes','sub'}, use_global_device_ids=true, to_apply=%region_7.8 | all-reduce | flops 128 | bytes 1024 | tf_op jit(solution)/shard_map/psum | solution.py:99
  (188 shorter events, 46.6 us)
Async XLA Ops:
  7.2 8.0 %copy-start.4 = (s32[768]{0:T(1024)S(1)}, s32[768]{0:T(1024)}, u32[]{:S(2)}) copy-start(s32[768]{0:T(1024)} %param.17) | copy-start | bytes 9220
  7.2 8.0 %copy-start.1 = (f32[9,768,16]{1,2,0:T(8,128)S(1)}, f32[9,768,16]{1,2,0:T(8,128)}, u32[]{:S(2)}) copy-start(f32[9,768,16]{1,2,0:T(8,128)} %param.15) | copy-start | bytes 1327108
  7.2 179.9 %all-gather.2.cloned.1.call-start = ((), (), s32[]{:S(2)}) async-start(), calls=%async_computation | async-start | bytes 2949120 | tf_op jit(solution)/shard_map/all_gather | solution.py:66
  8.8 7.5 %copy-start.2 = (s32[768,16]{0,1:T(8,128)S(1)}, s32[768,16]{0,1:T(8,128)}, u32[]{:S(2)}) copy-start(s32[768,16]{0,1:T(8,128)} %param.16) | copy-start | bytes 147460
  8.9 7.5 %collective-permute-start = (bf16[3,96,128]{2,0,1:T(4,128)(2,1)S(1)}, bf16[3,96,128]{2,0,1:T(4,128)(2,1)S(1)}, u32[]{:S(2)}, u32[]{:S(2)}) collective-permute-start(bf16[3,96,128]{2,0,1:T(4,128)(2,1)S(1)} %get-tuple-element.152), channel_id=1, source_target_pairs={{0,4},{4,8},{8,12},{1,5},{5,9},{9,13},{2,6},{6,10},{10,14},{3,7},{... | collective-permute-start | bytes 221192 | tf_op jit(solution)/shard_map/ppermute | solution.py:23
  13.9 6.5 %collective-permute-start.1 = (bf16[3,96,128]{2,0,1:T(4,128)(2,1)S(1)}, bf16[3,96,128]{2,0,1:T(4,128)(2,1)S(1)}, u32[]{:S(2)}, u32[]{:S(2)}) collective-permute-start(bf16[3,96,128]{2,0,1:T(4,128)(2,1)S(1)} %get-tuple-element.153), channel_id=1, source_target_pairs={{4,0},{8,4},{12,8},{5,1},{9,5},{13,9},{6,2},{10,6},{14,10},{7,3},{... | collective-permute-start | bytes 221192 | tf_op jit(solution)/shard_map/ppermute | solution.py:25
  161.4 1.0 copy-start.5
  161.4 1.0 copy-start.6
  162.3 90.6 %all-reduce.2.cloned.1.call-start = ((), (), s32[]{:S(2)}) async-start(), calls=%async_computation.1 | async-start | bytes 2621440 | tf_op jit(solution)/shard_map/psum | solution.py:71
  191.7 1.1 copy-start
  191.7 1.1 copy-start.7
  191.7 61.2 %copy-start.3 = (f32[640]{0:T(1024)S(1)}, f32[640]{0:T(1024)}, u32[]{:S(2)}) copy-start(f32[640]{0:T(1024)} %param.19) | copy-start | bytes 7684
Sparse Core Ops, SparseCore 0:
  162.5 24.5 all-gather.1
  192.9 59.9 all-reduce.1
where the time goes:
time: 270 us; the launch traced here: 269 us
  waiting for transfers between devices  87.4 us (32%)
  other arithmetic  85.6 us (32%)
  local copies, waits for them, and re-layouts  62.1 us (23%)
  between operations  14.9 us (6%)
  blocking collectives  6.37 us (2%)
  starting transfers between devices  6.3 us (2%)
  matrix products  4.58 us (2%)
    psum x1, waiting for transfers between devices, body(): lax.psum(lax.cond(touched, lambda: lax.dot_general(all_images, partners,...  60 us
    select_n x32, other arithmetic, slot_step(): gathered = jnp.take(extended, target, axis=1)  46.3 us
    gather x16, local copies, waits for them, and re-layouts, slot_step(): gathered = jnp.take(extended, target, axis=1)  45.5 us
    all_gather x1, waiting for transfers between devices, body(): all_images = lax.all_gather(images, ('modes', 'sub'), axis=2, tiled=True)  23.4 us
    add x16, other arithmetic, slot_step(): summed = summed + coef_slot[:, d, :, None] * gathered[d][None]  19.7 us
    mul x16, other arithmetic, slot_step(): summed = summed + coef_slot[:, d, :, None] * gathered[d][None]  13 us
    dynamic_slice x16, local copies, waits for them, and re-layouts, slot_step(): lax.dynamic_index_in_dim(coefficient, slot_index, 2, keepdims=False)  12.9 us
    psum x1, blocking collectives, body(): lax.psum(jnp.sum(weight * elements * elements, axis=1), ('modes', 'sub'))  6.37 us
  transfers between devices with their start and end apart: 4, of which 3 were waited for; matrix products, arithmetic and copies ran while one was open for 1% of the time, Pallas kernels for 0%

commit v1 on v0

v1 whole, which is shorter than its diff:
```python
import math

import jax
import jax.numpy as jnp
from jax import lax
from jax.experimental import pallas as pl
from jax.experimental.pallas import tpu as pltpu
from jax.sharding import PartitionSpec as P

HALO = 96
BONDS = 16
LANES = 128
SPAN = LANES + 2 * HALO
GROUP = 32
VMEM_BYTES = 40 * 1024 * 1024

lorentz_width = 0.05


def build_block(first, base, nbr_ref, coef_ref, count_ref, slot_ref, entry_ref, dense_ref):
    lanes = pl.ds(first, LANES)
    target = nbr_ref[:, lanes] - (base + (first - HALO))
    slot_ids = lax.broadcasted_iota(jnp.int32, (BONDS, LANES), 0)
    live = slot_ids < count_ref[:, lanes]
    coefs = [jnp.where(live, coef_ref[e, :, lanes], 0.0) for e in range(9)]
    merged = [jnp.zeros((BONDS, LANES), jnp.float32) for _ in range(9)]
    for k in range(BONDS):
        same = (target == target[k : k + 1]) & (slot_ids >= k)
        for e in range(9):
            merged[e] = merged[e] + jnp.where(same, coefs[e][k : k + 1], 0.0)
    for k in range(BONDS):
        slot_ref[k] = jnp.broadcast_to(target[k : k + 1], (8, LANES))
        for e in range(9):
            entry_ref[e * BONDS + k] = jnp.broadcast_to(merged[e][k : k + 1], (8, LANES))
    tiles = GROUP // 8
    rows = lax.broadcasted_iota(jnp.int32, (tiles, 8, LANES), 0) * 8 + lax.broadcasted_iota(
        jnp.int32, (tiles, 8, LANES), 1
    )

    def group_step(g, carry):
        here = rows + g * GROUP
        cells = [jnp.zeros((tiles, 8, LANES), jnp.float32) for _ in range(9)]
        for k in range(BONDS):
            hit = slot_ref[k][None] == here
            for e in range(9):
                cells[e] = jnp.where(hit, entry_ref[e * BONDS + k][None], cells[e])
        for r in range(3):
            for c in range(3):
                value = cells[3 * r + c].reshape(GROUP, LANES)
                high = value.astype(jnp.bfloat16)
                low = (value - high.astype(jnp.float32)).astype(jnp.bfloat16)
                at = pl.ds(pl.multiple_of(c * SPAN + g * GROUP, GROUP), GROUP)
                dense_ref[at, 2 * r * LANES : (2 * r + 1) * LANES] = high
                dense_ref[at, (2 * r + 1) * LANES : (2 * r + 2) * LANES] = low
        return carry

    lax.fori_loop(0, SPAN // GROUP, group_step, 0)


def window(first, rows, c, panel_ref, low_ref, high_ref):
    begin, end = first - HALO, first - HALO + SPAN
    if begin < 0:
        return jnp.concatenate([low_ref[c, HALO + begin :], panel_ref[c, :end]], axis=0)
    if end > rows:
        return jnp.concatenate([panel_ref[c, begin:], high_ref[c, : end - rows]], axis=0)
    return panel_ref[c, begin:end]


def image_kernel(blocks, rows, has_halo, *refs):
    if has_halo:
        base_ref, panel_ref, low_ref, high_ref, nbr_ref, coef_ref, count_ref = refs[:7]
    else:
        base_ref, panel_ref, nbr_ref, coef_ref, count_ref = refs[:5]
        low_ref = high_ref = None
    out_ref, slot_ref, entry_ref, dense_ref = refs[-4:]
    width = len(blocks) * LANES
    for place, block in enumerate(blocks):
        first = block * LANES
        build_block(first, base_ref[0], nbr_ref, coef_ref, count_ref, slot_ref, entry_ref, dense_ref)
        cells = jnp.concatenate(
            [window(first, rows, c, panel_ref, low_ref, high_ref) for c in range(3)], axis=0
        )
        both = lax.dot_general(
            cells, dense_ref[...], (((0,), (0,)), ((), ())), preferred_element_type=jnp.float32
        )
        for r in range(3):
            image = both[:, 2 * r * LANES : (2 * r + 1) * LANES] + both[:, (2 * r + 1) * LANES : (2 * r + 2) * LANES]
            at = r * width + place * LANES
            out_ref[:, at : at + LANES] = image.astype(jnp.bfloat16)


def images_of(blocks, base, panel, halos, nbr, coef, count):
    rows, cols = panel.shape[1:]
    vmem = pl.BlockSpec(memory_space=pltpu.VMEM)
    operands = [base, panel, *halos, nbr, coef, count]

    def kernel(*refs):
        image_kernel(blocks, rows, len(halos) > 0, *refs)

    return pl.pallas_call(
        kernel,
        in_specs=[pl.BlockSpec(memory_space=pltpu.SMEM)] + [vmem] * (len(operands) - 1),
        out_specs=vmem,
        out_shape=jax.ShapeDtypeStruct((cols, 3 * LANES * len(blocks)), jnp.bfloat16),
        scratch_shapes=[
            pltpu.VMEM((BONDS, 8, LANES), jnp.int32),
            pltpu.VMEM((9 * BONDS, 8, LANES), jnp.float32),
            pltpu.VMEM((3 * SPAN, 6 * LANES), jnp.bfloat16),
        ],
        compiler_params=pltpu.CompilerParams(vmem_limit_bytes=VMEM_BYTES),
        name="images",
    )(*operands)


def runs_of(blocks):
    runs = []
    for place, block in enumerate(blocks):
        if runs and runs[-1][1] + runs[-1][2] == block:
            runs[-1][2] += 1
        else:
            runs.append([place, block, 1])
    return runs


def product_kernel(chunks, half_ref, partners_ref, *refs):
    out_ref = refs[-1]
    count = len(chunks)
    for who in range(2):
        total = None
        for blocks, image_ref in zip(chunks, refs[who * count : (who + 1) * count]):
            width = len(blocks) * LANES
            for r in range(3):
                for place, block, length in runs_of(blocks):
                    at = r * width + place * LANES
                    part = jnp.dot(
                        image_ref[:, at : at + length * LANES],
                        partners_ref[r, block * LANES : (block + length) * LANES, :],
                        preferred_element_type=jnp.float32,
                    )
                    total = part if total is None else total + part
        half = half_ref[0] if who == 0 else 1 - half_ref[0]
        out_ref[half] = total


def products_of(chunks, half, partners, mine, theirs):
    vmem = pl.BlockSpec(memory_space=pltpu.VMEM)
    modes, cols = mine[0].shape[0], partners.shape[2]

    def kernel(*refs):
        product_kernel(chunks, *refs)

    return pl.pallas_call(
        kernel,
        in_specs=[pl.BlockSpec(memory_space=pltpu.SMEM)] + [vmem] * (1 + 2 * len(chunks)),
        out_specs=vmem,
        out_shape=jax.ShapeDtypeStruct((2, modes, cols), jnp.float32),
        compiler_params=pltpu.CompilerParams(vmem_limit_bytes=VMEM_BYTES),
        name="products",
    )(half, partners, *mine, *theirs)


def reduced(group, shift, rows_dev):
    groups, depth = lax.axis_size("modes"), lax.axis_size("atoms")
    place = lax.axis_index("atoms")
    cells = group.reshape(-1, rows_dev, group.shape[-1])
    bit = 0
    while cells.shape[0] > 1:
        pairs = cells.reshape(cells.shape[0] // 2, 2, rows_dev, -1)
        own = (place >> bit) & 1
        keep = lax.dynamic_index_in_dim(pairs, own, 1, keepdims=False)
        send = lax.dynamic_index_in_dim(pairs, 1 - own, 1, keepdims=False)
        step = 1 << bit
        got = lax.ppermute(send.astype(jnp.bfloat16), "atoms", [(z, z ^ step) for z in range(depth)])
        cells = keep + got.astype(jnp.float32)
        bit += 1
    cells = cells[0]
    low, level = bit, 0
    while (1 << level) < groups:
        moves = []
        for z in range(depth):
            for m in range(groups):
                goal = (m + shift) % groups
                settled = all(((z >> (low + u)) ^ (goal >> u)) & 1 == 0 for u in range(level))
                if settled and ((z >> (low + level)) ^ (goal >> level)) & 1:
                    moves.append((z * groups + m, (z ^ (1 << (low + level))) * groups + m))
        got = lax.ppermute(cells.astype(jnp.bfloat16), ("atoms", "modes"), moves)
        cells = cells + got.astype(jnp.float32)
        level += 1
    return cells


def body(
    mode_panel,
    partners,
    bond_blocks,
    neighbors,
    bond_count,
    panel_freq,
    partner_freq,
    win_start,
    win_len,
):
    atom_rows = mode_panel.shape[1]
    atom_index = lax.axis_index("atoms")
    atom_count = lax.axis_size("atoms")
    groups = lax.axis_size("modes")
    group_index = lax.axis_index("modes")
    half_index = lax.axis_index("sub")
    column_index = lax.axis_index(("modes", "sub"))
    part_cols = partners.shape[2]
    panel_total = win_start.shape[0]
    rows_dev = panel_total // atom_count

    up = [(z, z + 1) for z in range(atom_count - 1)]
    down = [(z + 1, z) for z in range(atom_count - 1)]
    low_halo = lax.ppermute(mode_panel[:, atom_rows - HALO :], "atoms", up)
    high_halo = lax.ppermute(mode_panel[:, :HALO], "atoms", down)

    nbr = neighbors.T
    coef = bond_blocks.transpose(0, 2, 1)
    count = bond_count[None, :]
    base = (atom_index * atom_rows).astype(jnp.int32)[None]
    half = half_index.astype(jnp.int32)[None]

    last = atom_rows // LANES - 1
    middle = list(range(1, last))
    cut = (last + 1) // 2
    chunks = [middle[:cut], middle[cut:] + [last, 0]]
    own = []
    for blocks in chunks:
        edge = 0 in blocks or last in blocks
        own.append(images_of(blocks, base, mode_panel, (low_halo, high_halo) if edge else (), nbr, coef, count))

    swap = [(0, 1), (1, 0)]
    far, sibling, far_sibling = {}, [], {}
    for chunk in own:
        for shift in range(1, groups):
            moves = [((m + shift) % groups, m) for m in range(groups)]
            got = lax.ppermute(chunk, "modes", moves)
            far.setdefault(shift, []).append(got)
        sibling.append(lax.ppermute(chunk, "sub", swap))
    for shift in range(1, groups):
        far_sibling[shift] = [lax.ppermute(got, "sub", swap) for got in far[shift]]

    goal = atom_index * groups // atom_count
    products = None
    for shift in range(groups):
        mine = own if shift == 0 else far[shift]
        theirs = sibling if shift == 0 else far_sibling[shift]
        total = reduced(products_of(chunks, half, partners, mine, theirs), shift, rows_dev)
        if products is None:
            products = total
        else:
            products = jnp.where((group_index + shift) % groups == goal, total, products)

    first_col = column_index * part_cols
    norm_scale = 1.0 / math.sqrt(3 * atom_rows * atom_count)
    my_start = lax.dynamic_slice_in_dim(win_start, atom_index * rows_dev, rows_dev, 0)
    my_length = lax.dynamic_slice_in_dim(win_len, atom_index * rows_dev, rows_dev, 0)
    my_freq = lax.dynamic_slice_in_dim(panel_freq, atom_index * rows_dev, rows_dev, 0)
    columns = first_col + jnp.arange(part_cols, dtype=jnp.int32)
    inside = (columns[None, :] >= my_start[:, None]) & (
        columns[None, :] < my_start[:, None] + my_length[:, None]
    )
    elements = jnp.where(inside, products * norm_scale, 0.0)
    offset_freq = my_freq[:, None] - partner_freq[None, :]
    lorentz = lorentz_width / (
        math.pi * (offset_freq * offset_freq + lorentz_width * lorentz_width)
    )
    weight = jnp.where(inside, lorentz, 0.0)
    numerator = lax.psum(jnp.sum(weight * elements * elements, axis=1), ("modes", "sub"))
    diffusivity = math.pi / 3.0 * numerator / (my_freq * my_freq)
    return (elements, diffusivity)


def solution(mesh):
    return jax.shard_map(
        body,
        mesh=mesh,
        in_specs=(
            P(None, ("dom", "atoms"), ("modes", "sub")),
            P(None, ("dom", "atoms"), ("modes", "sub")),
            P(None, ("dom", "atoms"), None),
            P(("dom", "atoms"), None),
            P(("dom", "atoms")),
            P("dom"),
            P(("dom", "modes", "sub")),
            P("dom"),
            P("dom"),
        ),
        out_specs=(P(("dom", "atoms"), ("modes", "sub")), P(("dom", "atoms"))),
        check_vma=False,
    )
```

time: 270 us -> 73.2 us (0.27)
  other arithmetic: 85.6 us -> 3.53 us
  waiting for transfers between devices: 87.4 us -> 14.9 us
  local copies, waits for them, and re-layouts: 62.1 us -> 10.1 us
  Pallas kernels: 0 us -> 17.1 us
  between operations: 14.9 us -> 0.78 us
  starting transfers between devices: 6.3 us -> 17.2 us
  matrix products: 4.58 us -> 0 us
    psum x1 -> x0, waiting for transfers between devices: 60 us -> none  [body(): lax.psum(lax.cond(touched, lambda: lax.dot_general(all_images, partners,...]
    select_n x32 -> x0, other arithmetic: 46.3 us -> none  [slot_step(): gathered = jnp.take(extended, target, axis=1)]
    gather x16 -> x0, local copies, waits for them, and re-layouts: 45.5 us -> none  [slot_step(): gathered = jnp.take(extended, target, axis=1)]
    all_gather x1 -> x0, waiting for transfers between devices: 23.4 us -> none  [body(): all_images = lax.all_gather(images, ('modes', 'sub'), axis=2, tiled=True)]
    add x17 -> x1, other arithmetic: 19.7 us -> 0.78 us  [body(): my_start[:, None] + my_length[:, None]]
    pallas_call x0 -> x4, Pallas kernels: none -> 17.1 us  [the longest x2 12 us: images_of(): pl.pallas_call(kernel, in_specs=[pl.BlockSpec(memory_space=pltpu.SMEM)] +...]
    mul x17 -> x0, other arithmetic: 14.1 us -> none  [the longest x16 13 us: slot_step(): summed = summed + coef_slot[:, d, :, None] * gathered[d][None]]
    dynamic_slice x16 -> x0, local copies, waits for them, and re-layouts: 12.9 us -> none  [slot_step(): lax.dynamic_index_in_dim(coefficient, slot_index, 2, keepdims=False)]
  transfers between devices with their start and end apart: 4 -> 12, of which waited for: 3 -> 4; matrix products, arithmetic and copies ran while one was open for 1% -> 2% of each run, Pallas kernels for 0% -> 24%
where the time goes in v1:
time: 73.2 us; the launch traced here: 72.6 us
  starting transfers between devices  17.2 us (23%)
  Pallas kernels  17.1 us (23%)
  waiting for transfers between devices  14.9 us (20%)
  local copies, waits for them, and re-layouts  10.1 us (14%)
  blocking collectives  8.95 us (12%)
  other arithmetic  3.53 us (5%)
  between operations  0.78 us (1%)
    pallas_call x2, Pallas kernels, images_of(): pl.pallas_call(kernel, in_specs=[pl.BlockSpec(memory_space=pltpu.SMEM)] +...  12 us
    psum x1, blocking collectives, body(): lax.psum(jnp.sum(weight * elements * elements, axis=1), ('modes', 'sub'))  8.95 us
    unnamed x28, local copies, waits for them, and re-layouts  7.58 us
    ppermute x2, waiting for transfers between devices, body(): got = lax.ppermute(chunk, 'modes', moves)  7.24 us
    ppermute x2, starting transfers between devices, reduced(): got = lax.ppermute(cells.astype(jnp.bfloat16), ('atoms', 'modes'), moves)  5.79 us
    pallas_call x2, Pallas kernels, products_of(): pl.pallas_call(kernel, in_specs=[pl.BlockSpec(memory_space=pltpu.SMEM)] +...  5.14 us
    ppermute x2, waiting for transfers between devices, reduced(): lax.ppermute(send.astype(jnp.bfloat16), 'atoms', [(z, z ^ step) for z in...  4.95 us
    ppermute x1, starting transfers between devices, body(): low_halo = lax.ppermute(mode_panel[:, atom_rows - HALO:], 'atoms', up)  4.92 us
  transfers between devices with their start and end apart: 12, of which 4 were waited for; matrix products, arithmetic and copies ran while one was open for 2% of the time, Pallas kernels for 24%

profile of v1, /device:TPU:0, one launch (start us, length us, event | category | flops | bytes accessed | tf_op | source)
XLA Modules:
  0.0 72.6 jit_solution(3921579547333672445)
XLA Ops:
  0.6 0.0 copy-start
  0.6 1.7 %fusion.5 = (bf16[3,96,128]{2,1,0:T(8,128)(2,1)S(1)}, bf16[3,96,128]{2,1,0:T(8,128)(2,1)}) fusion(bf16[3,768,128]{2,1,0:T(8,128)(2,1)} %refs_1_.5), kind=kLoop, calls=%fused_computation.17 | loop fusion | bytes 294912 | tf_op jit(solution)/shard_map/slice | solution.py:217
  2.4 4.9 %collective-permute-start.1 = (bf16[3,96,128]{2,1,0:T(8,128)(2,1)}, bf16[3,96,128]{2,1,0:T(8,128)(2,1)S(1)}, u32[]{:S(2)}, u32[]{:S(2)}) collective-permute-start(bf16[3,96,128]{2,1,0:T(8,128)(2,1)} %get-tuple-element.7), channel_id=1, source_target_pairs={{0,4},{4,8},{8,12},{1,5},{5,9},{9,13},{2,6},{6,10},{10,14},{3,7},{... | collective-permute-start | bytes 221192 | tf_op jit(solution)/shard_map/ppermute | solution.py:216
  7.3 1.3 %collective-permute-start.2 = (bf16[3,96,128]{2,1,0:T(8,128)(2,1)S(1)}, bf16[3,96,128]{2,1,0:T(8,128)(2,1)S(1)}, u32[]{:S(2)}, u32[]{:S(2)}) collective-permute-start(bf16[3,96,128]{2,1,0:T(8,128)(2,1)S(1)} %get-tuple-element.6), channel_id=1, source_target_pairs={{4,0},{8,4},{12,8},{5,1},{9,5},{13,9},{6,2},{10,6},{14,10},{7,3},{... | collective-permute-start | bytes 221192 | tf_op jit(solution)/shard_map/ppermute | solution.py:217
  8.6 0.7 broadcast_in_dim.23.refs_4_.refs_6_
  9.3 1.1 %copy-done.4 = bf16[3,768,128]{2,1,0:T(8,128)(2,1)S(1)} copy-done((bf16[3,768,128]{2,1,0:T(8,128)(2,1)S(1)}, bf16[3,768,128]{2,1,0:T(8,128)(2,1)}, u32[]{:S(2)}) %copy-start.4) | copy-done | bytes 589848
  10.4 1.0 %copy-done.5 = f32[9,768,16]{1,2,0:T(8,128)S(1)} copy-done((f32[9,768,16]{1,2,0:T(8,128)S(1)}, f32[9,768,16]{1,2,0:T(8,128)}, u32[]{:S(2)}) %copy-start.5) | copy-done | bytes 442392
  11.4 0.8 %copy-done.6 = s32[768,16]{0,1:T(8,128)S(1)} copy-done((s32[768,16]{0,1:T(8,128)S(1)}, s32[768,16]{0,1:T(8,128)}, u32[]{:S(2)}) %copy-start.6) | copy-done | bytes 49176
  12.2 6.0 %images.2.refs_2_ = bf16[128,1152]{1,0:T(8,128)(2,1)S(1)} custom-call(s32[1]{0:T(128)} %bitcast.1.refs_0_, bf16[3,768,128]{2,1,0:T(8,128)(2,1)S(1)} %copy-done.4, s32[16,768]{1,0:T(8,128)S(1)} %bitcast.22, f32[9,16,768]{2,1,0:T(8,128)S(1)} %bitcast.20, s32[1,768]{1,0:T(1,128)S(1)} %broadcast_in_dim.23.refs_4_.refs_6_), custom_call_target="tpu_custom_call" | custom-call | tf_op jit(solution)/shard_map/images/pallas_call | solution.py:100
  18.2 1.6 %collective-permute-start = (bf16[128,1152]{1,0:T(8,128)(2,1)S(1)}, bf16[128,1152]{1,0:T(8,128)(2,1)}, u32[]{:S(2)}, u32[]{:S(2)}) collective-permute-start(bf16[128,1152]{1,0:T(8,128)(2,1)S(1)} %images.2.refs_2_), channel_id=1, source_target_pairs={{2,0},{0,2},{3,1},{1,3},{6,4},{4,6},{7,5},{5,7},{10,8},{8,10},{11,... | collective-permute-start | bytes 884744 | tf_op jit(solution)/shard_map/ppermute | solution.py:239
  19.7 0.0 collective-permute-done.1.refs_2_
  19.7 0.6 copy-done.8
  20.4 0.0 collective-permute-done.2.refs_3_
  20.4 0.6 copy-done.10
  21.0 0.8 %copy-done.7 = s32[768,16]{0,1:T(8,128)S(1)} copy-done((s32[768,16]{0,1:T(8,128)S(1)}, s32[768,16]{0,1:T(8,128)}, u32[]{:S(2)}) %copy-start.7) | copy-done | bytes 49176
  21.8 0.9 %copy-done.9 = bf16[3,96,128]{2,1,0:T(8,128)(2,1)S(1)} copy-done((bf16[3,96,128]{2,1,0:T(8,128)(2,1)S(1)}, bf16[3,96,128]{2,1,0:T(8,128)(2,1)}, u32[]{:S(2)}) %copy-start.9) | copy-done | bytes 73752
  22.7 0.9 %copy-done.11 = bf16[3,96,128]{2,1,0:T(8,128)(2,1)S(1)} copy-done((bf16[3,96,128]{2,1,0:T(8,128)(2,1)S(1)}, bf16[3,96,128]{2,1,0:T(8,128)(2,1)}, u32[]{:S(2)}) %copy-start.11) | copy-done | bytes 73752
  23.6 6.0 %images.3.refs_3_ = bf16[128,1152]{1,0:T(8,128)(2,1)S(1)} custom-call(s32[1]{0:T(128)} %bitcast.1.refs_0_, bf16[3,768,128]{2,1,0:T(8,128)(2,1)S(1)} %copy-done.4, bf16[3,96,128]{2,1,0:T(8,128)(2,1)S(1)} %copy-done.9, bf16[3,96,128]{2,1,0:T(8,128)(2,1)S(1)} %copy-done.11, s32[16,768]{1,0:T(8,128)S(1)} %bitcast.23, f32[9,16,768]{2,1,0:T(8,128)S(1)} %bitcast.21, ...), custom_call_target="tpu_custom_call" | custom-call | tf_op jit(solution)/shard_map/images/pallas_call | solution.py:100
  29.6 0.6 collective-permute-start.3
  30.2 0.0 collective-permute-start.8
  30.2 0.5 collective-permute-start.9
  30.7 0.0 collective-permute-done.refs_2_
  30.7 0.0 collective-permute-start.4
  30.7 7.2 %collective-permute-done.3.refs_3_ = bf16[128,1152]{1,0:T(8,128)(2,1)} collective-permute-done((bf16[128,1152]{1,0:T(8,128)(2,1)S(1)}, bf16[128,1152]{1,0:T(8,128)(2,1)}, u32[]{:S(2)}, u32[]{:S(2)}) %collective-permute-start.3) | collective-permute-done | bytes 294944 | tf_op jit(solution)/shard_map/ppermute | solution.py:239
  37.9 0.0 collective-permute-start.5
  37.9 0.0 collective-permute-done.8.refs_4_
  37.9 0.0 collective-permute-done.9.refs_5_
  37.9 0.0 copy-done
  37.9 2.4 %products.3 = f32[2,128,640]{2,1,0:T(8,128)S(1)} custom-call(s32[1]{0:T(128)} %bitcast.refs_0_, bf16[3,768,640]{2,1,0:T(8,128)(2,1)S(1)} %copy-done, bf16[128,1152]{1,0:T(8,128)(2,1)S(1)} %images.2.refs_2_, bf16[128,1152]{1,0:T(8,128)(2,1)S(1)} %images.3.refs_3_, bf16[128,1152]{1,0:T(8,128)(2,1)} %collective-permute-done.8.refs_4_, ...), custom_call_target="tpu_custom_call" | custom-call | tf_op jit(solution)/shard_map/products/pallas_call | solution.py:152
  40.4 0.0 copy-start.1
  40.4 0.9 %copy-done.1 = f32[2,128,640]{2,1,0:T(8,128)} copy-done((f32[2,128,640]{2,1,0:T(8,128)}, f32[2,128,640]{2,1,0:T(8,128)S(1)}, u32[]{:S(2)}) %copy-start.1) | copy-done | bytes 655384
  41.3 2.4 %collective-permute-start.10 = (bf16[1,128,640]{2,1,0:T(8,128)(2,1)S(1)}, bf16[1,128,640]{2,1,0:T(8,128)(2,1)S(1)}, u32[]{:S(2)}, u32[]{:S(2)}) collective-permute-start(bf16[1,128,640]{2,1,0:T(8,128)(2,1)S(1)} %dynamic-slice_convert_fusion), channel_id=1, source_target_pairs={{0,4},{4,0},{8,12},{12,8},{1,5},{5,1},{9,13},{13,9},{2,6},{6,2},{1... | collective-permute-start | bytes 491528 | tf_op jit(solution)/shard_map/ppermute | solution.py:173
  43.7 0.0 collective-permute-done.4.refs_4_
  43.7 0.0 collective-permute-done.5.refs_5_
  43.7 2.7 %products.2 = f32[2,128,640]{2,1,0:T(8,128)S(1)} custom-call(s32[1]{0:T(128)} %bitcast.refs_0_, bf16[3,768,640]{2,1,0:T(8,128)(2,1)S(1)} %copy-done, bf16[128,1152]{1,0:T(8,128)(2,1)} %collective-permute-done.refs_2_, bf16[128,1152]{1,0:T(8,128)(2,1)} %collective-permute-done.3.refs_3_, bf16[128,1152]{1,0:T(8,128)(2,1)} %collective-permute-done.4.refs_4_, ...), custom_call_target="tpu_custom_call" | custom-call | tf_op jit(solution)/shard_map/products/pallas_call | solution.py:152
  46.5 0.1 collective-permute-start.6
  46.6 2.0 %collective-permute-done.10 = bf16[1,128,640]{2,1,0:T(8,128)(2,1)S(1)} collective-permute-done((bf16[1,128,640]{2,1,0:T(8,128)(2,1)S(1)}, bf16[1,128,640]{2,1,0:T(8,128)(2,1)S(1)}, u32[]{:S(2)}, u32[]{:S(2)}) %collective-permute-start.10) | collective-permute-done | bytes 163872 | tf_op jit(solution)/shard_map/ppermute | solution.py:173
  48.6 1.3 %collective-permute-start.11 = (bf16[128,640]{1,0:T(8,128)(2,1)S(1)}, bf16[128,640]{1,0:T(8,128)(2,1)S(1)}, u32[]{:S(2)}, u32[]{:S(2)}) collective-permute-start(bf16[128,640]{1,0:T(8,128)(2,1)S(1)} %bitcast_convert_fusion), channel_id=1, source_target_pairs={{2,10},{6,14},{8,0},{12,4},{3,11},{7,15},{9,1},{13,5},{18,26},{22,... | collective-permute-start | bytes 491528 | tf_op jit(solution)/shard_map/ppermute | solution.py:186
  49.9 3.0 %collective-permute-done.6 = bf16[1,128,640]{2,1,0:T(8,128)(2,1)S(1)} collective-permute-done((bf16[1,128,640]{2,1,0:T(8,128)(2,1)S(1)}, bf16[1,128,640]{2,1,0:T(8,128)(2,1)S(1)}, u32[]{:S(2)}, u32[]{:S(2)}) %collective-permute-start.6) | collective-permute-done | bytes 163872 | tf_op jit(solution)/shard_map/ppermute | solution.py:173
  52.9 4.5 %collective-permute-start.7 = (bf16[128,640]{1,0:T(8,128)(2,1)S(1)}, bf16[128,640]{1,0:T(8,128)(2,1)S(1)}, u32[]{:S(2)}, u32[]{:S(2)}) collective-permute-start(bf16[128,640]{1,0:T(8,128)(2,1)S(1)} %bitcast_convert_fusion.1), channel_id=1, source_target_pairs={{0,8},{4,12},{10,2},{14,6},{1,9},{5,13},{11,3},{15,7},{16,24},{20,... | collective-permute-start | bytes 491528 | tf_op jit(solution)/shard_map/ppermute | solution.py:186
  57.4 0.8 %dynamic-slice_add_fusion = (s32[128]{0:T(128)S(1)}, s32[128]{0:T(128)S(1)}) fusion(s32[512]{0:T(512)} %param.17, s32[]{:T(128)S(6)} %select_n.40, s32[512]{0:T(512)} %param.16), kind=kLoop, calls=%fused_computation.16 | loop fusion | flops 128 | bytes 2052 | tf_op jit(solution)/shard_map/add | solution.py:263
  58.2 0.1 dynamic_slice.16
  58.3 2.7 %collective-permute-done.11 = bf16[128,640]{1,0:T(8,128)(2,1)S(1)} collective-permute-done((bf16[128,640]{1,0:T(8,128)(2,1)S(1)}, bf16[128,640]{1,0:T(8,128)(2,1)S(1)}, u32[]{:S(2)}, u32[]{:S(2)}) %collective-permute-start.11) | collective-permute-done | bytes 163872 | tf_op jit(solution)/shard_map/ppermute | solution.py:186
  61.0 0.0 collective-permute-done.7
  61.0 0.0 copy-done.12
  61.0 2.1 %fusion = (f32[128]{0:T(128)S(1)}, f32[128,640]{1,0:T(8,128)}) fusion(f32[640]{0:T(1024)S(1)} %copy-done.12, f32[128]{0:T(128)S(1)} %dynamic_slice.16, s32[640]{0:T(1024)S(1)} %iota_add_fusion, s32[128]{0:T(128)S(1)} %get-tuple-element.4, s32[128]{0:T(128)S(1)} %get-tuple-element.5, bf16[128,640]{1,0:T(8,128)(2,1)S(1)} %collective-permute-done.11, ...), kind=kLoop, calls=%fused_computation.1 | loop fusion | flops 1884032 | bytes 1645573 | tf_op jit(solution)/shard_map/reduce_sum | solution.py:271
  63.0 8.9 %psum.7 = f32[128]{0:T(128)S(1)} all-reduce(f32[128]{0:T(128)S(1)} %get-tuple-element.2), channel_id=1, replica_groups=mesh['dom'=2,'atoms'=4,'modes'=2,'sub'=2] {'modes','sub'}, use_global_device_ids=true, to_apply=%region_1.2 | all-reduce | flops 128 | bytes 1024 | tf_op jit(solution)/shard_map/psum | solution.py:271
  72.0 0.6 multiply_divide_fusion
  (20 shorter events, 0.1 us)
Async XLA Ops:
  0.6 37.3 %copy-start = (bf16[3,768,640]{2,1,0:T(8,128)(2,1)S(1)}, bf16[3,768,640]{2,1,0:T(8,128)(2,1)}, u32[]{:S(2)}) copy-start(bf16[3,768,640]{2,1,0:T(8,128)(2,1)} %refs_1_.7) | copy-start | bytes 8847364
  2.4 17.4 %collective-permute-start.1 = (bf16[3,96,128]{2,1,0:T(8,128)(2,1)}, bf16[3,96,128]{2,1,0:T(8,128)(2,1)S(1)}, u32[]{:S(2)}, u32[]{:S(2)}) collective-permute-start(bf16[3,96,128]{2,1,0:T(8,128)(2,1)} %get-tuple-element.7), channel_id=1, source_target_pairs={{0,4},{4,8},{8,12},{1,5},{5,9},{9,13},{2,6},{6,10},{10,14},{3,7},{... | collective-permute-start | bytes 221192 | tf_op jit(solution)/shard_map/ppermute | solution.py:216
  7.3 13.1 %collective-permute-start.2 = (bf16[3,96,128]{2,1,0:T(8,128)(2,1)S(1)}, bf16[3,96,128]{2,1,0:T(8,128)(2,1)S(1)}, u32[]{:S(2)}, u32[]{:S(2)}) collective-permute-start(bf16[3,96,128]{2,1,0:T(8,128)(2,1)S(1)} %get-tuple-element.6), channel_id=1, source_target_pairs={{4,0},{8,4},{12,8},{5,1},{9,5},{13,9},{6,2},{10,6},{14,10},{7,3},{... | collective-permute-start | bytes 221192 | tf_op jit(solution)/shard_map/ppermute | solution.py:217
  9.3 1.1 %copy-start.4 = (bf16[3,768,128]{2,1,0:T(8,128)(2,1)S(1)}, bf16[3,768,128]{2,1,0:T(8,128)(2,1)}, u32[]{:S(2)}) copy-start(bf16[3,768,128]{2,1,0:T(8,128)(2,1)} %refs_1_.5) | copy-start | bytes 1769476
  10.3 1.0 %copy-start.5 = (f32[9,768,16]{1,2,0:T(8,128)S(1)}, f32[9,768,16]{1,2,0:T(8,128)}, u32[]{:S(2)}) copy-start(f32[9,768,16]{1,2,0:T(8,128)} %param.11) | copy-start | bytes 1327108
  11.4 0.8 %copy-start.6 = (s32[768,16]{0,1:T(8,128)S(1)}, s32[768,16]{0,1:T(8,128)}, u32[]{:S(2)}) copy-start(s32[768,16]{0,1:T(8,128)} %param.12) | copy-start | bytes 147460
  18.2 12.5 %collective-permute-start = (bf16[128,1152]{1,0:T(8,128)(2,1)S(1)}, bf16[128,1152]{1,0:T(8,128)(2,1)}, u32[]{:S(2)}, u32[]{:S(2)}) collective-permute-start(bf16[128,1152]{1,0:T(8,128)(2,1)S(1)} %images.2.refs_2_), channel_id=1, source_target_pairs={{2,0},{0,2},{3,1},{1,3},{6,4},{4,6},{7,5},{5,7},{10,8},{8,10},{11,... | collective-permute-start | bytes 884744 | tf_op jit(solution)/shard_map/ppermute | solution.py:239
  19.7 0.6 copy-start.8
  20.4 0.6 copy-start.10
  21.0 0.8 %copy-start.7 = (s32[768,16]{0,1:T(8,128)S(1)}, s32[768,16]{0,1:T(8,128)}, u32[]{:S(2)}) copy-start(s32[768,16]{0,1:T(8,128)} %param.12) | copy-start | bytes 147460
  21.8 0.9 %copy-start.9 = (bf16[3,96,128]{2,1,0:T(8,128)(2,1)S(1)}, bf16[3,96,128]{2,1,0:T(8,128)(2,1)}, u32[]{:S(2)}) copy-start(bf16[3,96,128]{2,1,0:T(8,128)(2,1)} %copy-done.8) | copy-start | bytes 221188
  22.7 0.9 %copy-start.11 = (bf16[3,96,128]{2,1,0:T(8,128)(2,1)S(1)}, bf16[3,96,128]{2,1,0:T(8,128)(2,1)}, u32[]{:S(2)}) copy-start(bf16[3,96,128]{2,1,0:T(8,128)(2,1)} %copy-done.10) | copy-start | bytes 221188
  29.6 8.3 %collective-permute-start.3 = (bf16[128,1152]{1,0:T(8,128)(2,1)S(1)}, bf16[128,1152]{1,0:T(8,128)(2,1)}, u32[]{:S(2)}, u32[]{:S(2)}) collective-permute-start(bf16[128,1152]{1,0:T(8,128)(2,1)S(1)} %images.3.refs_3_), channel_id=1, source_target_pairs={{2,0},{0,2},{3,1},{1,3},{6,4},{4,6},{7,5},{5,7},{10,8},{8,10},{11,... | collective-permute-start | bytes 884744 | tf_op jit(solution)/shard_map/ppermute | solution.py:239
  30.2 7.8 %collective-permute-start.8 = (bf16[128,1152]{1,0:T(8,128)(2,1)S(1)}, bf16[128,1152]{1,0:T(8,128)(2,1)}, u32[]{:S(2)}, u32[]{:S(2)}) collective-permute-start(bf16[128,1152]{1,0:T(8,128)(2,1)S(1)} %images.2.refs_2_), channel_id=1, source_target_pairs={{0,1},{1,0},{2,3},{3,2},{4,5},{5,4},{6,7},{7,6},{8,9},{9,8},{10,11... | collective-permute-start | bytes 884744 | tf_op jit(solution)/shard_map/ppermute | solution.py:241
  30.2 7.8 %collective-permute-start.9 = (bf16[128,1152]{1,0:T(8,128)(2,1)S(1)}, bf16[128,1152]{1,0:T(8,128)(2,1)}, u32[]{:S(2)}, u32[]{:S(2)}) collective-permute-start(bf16[128,1152]{1,0:T(8,128)(2,1)S(1)} %images.3.refs_3_), channel_id=1, source_target_pairs={{0,1},{1,0},{2,3},{3,2},{4,5},{5,4},{6,7},{7,6},{8,9},{9,8},{10,11... | collective-permute-start | bytes 884744 | tf_op jit(solution)/shard_map/ppermute | solution.py:241
  30.7 13.0 %collective-permute-start.4 = (bf16[128,1152]{1,0:T(8,128)(2,1)}, bf16[128,1152]{1,0:T(8,128)(2,1)}, u32[]{:S(2)}, u32[]{:S(2)}) collective-permute-start(bf16[128,1152]{1,0:T(8,128)(2,1)} %collective-permute-done.refs_2_), channel_id=1, source_target_pairs={{0,1},{1,0},{2,3},{3,2},{4,5},{5,4},{6,7},{7,6},{8,9},{9,8},{10,11... | collective-permute-start | bytes 884744 | tf_op jit(solution)/shard_map/ppermute | solution.py:243
  37.9 5.8 %collective-permute-start.5 = (bf16[128,1152]{1,0:T(8,128)(2,1)}, bf16[128,1152]{1,0:T(8,128)(2,1)}, u32[]{:S(2)}, u32[]{:S(2)}) collective-permute-start(bf16[128,1152]{1,0:T(8,128)(2,1)} %collective-permute-done.3.refs_3_), channel_id=1, source_target_pairs={{0,1},{1,0},{2,3},{3,2},{4,5},{5,4},{6,7},{7,6},{8,9},{9,8},{10,11... | collective-permute-start | bytes 884744 | tf_op jit(solution)/shard_map/ppermute | solution.py:243
  40.4 0.9 %copy-start.1 = (f32[2,128,640]{2,1,0:T(8,128)}, f32[2,128,640]{2,1,0:T(8,128)S(1)}, u32[]{:S(2)}) copy-start(f32[2,128,640]{2,1,0:T(8,128)S(1)} %products.3) | copy-start | bytes 1966084
  41.3 7.3 %collective-permute-start.10 = (bf16[1,128,640]{2,1,0:T(8,128)(2,1)S(1)}, bf16[1,128,640]{2,1,0:T(8,128)(2,1)S(1)}, u32[]{:S(2)}, u32[]{:S(2)}) collective-permute-start(bf16[1,128,640]{2,1,0:T(8,128)(2,1)S(1)} %dynamic-slice_convert_fusion), channel_id=1, source_target_pairs={{0,4},{4,0},{8,12},{12,8},{1,5},{5,1},{9,13},{13,9},{2,6},{6,2},{1... | collective-permute-start | bytes 491528 | tf_op jit(solution)/shard_map/ppermute | solution.py:173
  43.7 4.9 %copy-start.2 = (f32[2,128,640]{2,1,0:T(8,128)S(1)}, f32[2,128,640]{2,1,0:T(8,128)}, u32[]{:S(2)}) copy-start(f32[2,128,640]{2,1,0:T(8,128)} %copy-done.1) | copy-start | bytes 1966084
  43.7 14.5 %copy-start.13 = (f32[512]{0:T(512)S(1)}, f32[512]{0:T(512)}, u32[]{:S(2)}) copy-start(f32[512]{0:T(512)} %param.14) | copy-start | bytes 6148
  43.7 17.2 %copy-start.12 = (f32[640]{0:T(1024)S(1)}, f32[640]{0:T(1024)}, u32[]{:S(2)}) copy-start(f32[640]{0:T(1024)} %param.15) | copy-start | bytes 7684
  46.4 6.4 %copy-start.3 = (f32[2,128,640]{2,1,0:T(8,128)}, f32[2,128,640]{2,1,0:T(8,128)S(1)}, u32[]{:S(2)}) copy-start(f32[2,128,640]{2,1,0:T(8,128)S(1)} %products.2) | copy-start | bytes 1966084
  46.5 6.4 %collective-permute-start.6 = (bf16[1,128,640]{2,1,0:T(8,128)(2,1)S(1)}, bf16[1,128,640]{2,1,0:T(8,128)(2,1)S(1)}, u32[]{:S(2)}, u32[]{:S(2)}) collective-permute-start(bf16[1,128,640]{2,1,0:T(8,128)(2,1)S(1)} %dynamic-slice_convert_fusion.1), channel_id=1, source_target_pairs={{0,4},{4,0},{8,12},{12,8},{1,5},{5,1},{9,13},{13,9},{2,6},{6,2},{1... | collective-permute-start | bytes 491528 | tf_op jit(solution)/shard_map/ppermute | solution.py:173
  48.6 12.3 %collective-permute-start.11 = (bf16[128,640]{1,0:T(8,128)(2,1)S(1)}, bf16[128,640]{1,0:T(8,128)(2,1)S(1)}, u32[]{:S(2)}, u32[]{:S(2)}) collective-permute-start(bf16[128,640]{1,0:T(8,128)(2,1)S(1)} %bitcast_convert_fusion), channel_id=1, source_target_pairs={{2,10},{6,14},{8,0},{12,4},{3,11},{7,15},{9,1},{13,5},{18,26},{22,... | collective-permute-start | bytes 491528 | tf_op jit(solution)/shard_map/ppermute | solution.py:186
  52.9 8.0 %collective-permute-start.7 = (bf16[128,640]{1,0:T(8,128)(2,1)S(1)}, bf16[128,640]{1,0:T(8,128)(2,1)S(1)}, u32[]{:S(2)}, u32[]{:S(2)}) collective-permute-start(bf16[128,640]{1,0:T(8,128)(2,1)S(1)} %bitcast_convert_fusion.1), channel_id=1, source_target_pairs={{0,8},{4,12},{10,2},{14,6},{1,9},{5,13},{11,3},{15,7},{16,24},{20,... | collective-permute-start | bytes 491528 | tf_op jit(solution)/shard_map/ppermute | solution.py:186

commit v2 on v0

v2 whole, which is shorter than its diff:
```python
import math

import jax
import jax.numpy as jnp
from jax import lax
from jax.experimental import pallas as pl
from jax.experimental.pallas import tpu as pltpu
from jax.sharding import PartitionSpec as P

HALO = 96
BONDS = 16
LANES = 128
SPAN = LANES + 2 * HALO
GROUP = 16
VMEM_BYTES = 40 * 1024 * 1024

lorentz_width = 0.05

HBM = pl.BlockSpec(memory_space=pl.ANY)
VMEM = pl.BlockSpec(memory_space=pltpu.VMEM)
SMEM = pl.BlockSpec(memory_space=pltpu.SMEM)


def call(kernel, name, in_specs, out_specs, out_shape, operands, busy_us, scratch=()):
    return pl.pallas_call(
        kernel,
        in_specs=in_specs,
        out_specs=out_specs,
        out_shape=out_shape,
        scratch_shapes=list(scratch),
        compiler_params=pltpu.CompilerParams(vmem_limit_bytes=VMEM_BYTES),
        cost_estimate=pl.CostEstimate(
            flops=int(busy_us * 1.1e9), bytes_accessed=int(busy_us * 1e5), transcendentals=0
        ),
        name=name,
    )(*operands)


def runs_of(blocks):
    runs = []
    for place, block in enumerate(blocks):
        if runs and runs[-1][1] + runs[-1][2] == block:
            runs[-1][2] += 1
        else:
            runs.append([place, block, 1])
    return runs


def build_block(first, base, nbr_ref, coef_ref, count_ref, dense_ref):
    lanes = pl.ds(first, LANES)
    target = nbr_ref[:, lanes] - (base + (first - HALO))
    slot_ids = lax.broadcasted_iota(jnp.int32, (BONDS, LANES), 0)
    live = slot_ids < count_ref[lanes].reshape(1, LANES)
    coefs = [jnp.where(live, coef_ref[e, :, lanes], 0.0) for e in range(9)]
    halves = [(target[h : h + 8], slot_ids[h : h + 8]) for h in (0, 8)]
    merged = [[jnp.zeros((8, LANES), jnp.float32) for _ in range(9)] for _ in range(2)]
    named = [jnp.broadcast_to(target[k : k + 1], (8, LANES)) for k in range(BONDS)]
    for k in range(BONDS):
        rows = [jnp.broadcast_to(coefs[e][k : k + 1], (8, LANES)) for e in range(9)]
        for h in range(k // 8, 2):
            same = (halves[h][0] == named[k]) & (halves[h][1] >= k)
            for e in range(9):
                merged[h][e] = merged[h][e] + jnp.where(same, rows[e], 0.0)
    row_ids = lax.broadcasted_iota(jnp.int32, (8, LANES), 0)

    def group_step(g, carry):
        cells = [[] for _ in range(9)]
        for tile in range(GROUP // 8):
            here = row_ids + (g * GROUP + tile * 8)
            slot = jnp.full((8, LANES), -1, jnp.int32)
            for k in range(BONDS):
                slot = jnp.where(named[k] == here, k, slot)
            place = slot & 7
            early, live_cell = slot < 8, slot >= 0
            for e in range(9):
                picks = [
                    jnp.take_along_axis(merged[h][e], place, axis=0, mode="promise_in_bounds")
                    for h in range(2)
                ]
                cells[e].append(jnp.where(live_cell, jnp.where(early, picks[0], picks[1]), 0.0))
        for r in range(3):
            for c in range(3):
                value = jnp.concatenate(cells[3 * r + c], axis=0)
                high = value.astype(jnp.bfloat16)
                low = (value - high.astype(jnp.float32)).astype(jnp.bfloat16)
                at = pl.ds(pl.multiple_of(c * SPAN + g * GROUP, GROUP), GROUP)
                dense_ref[at, 2 * r * LANES : (2 * r + 1) * LANES] = high
                dense_ref[at, (2 * r + 1) * LANES : (2 * r + 2) * LANES] = low
        return carry

    lax.fori_loop(0, SPAN // GROUP, group_step, 0)


def window(first, rows, c, panel_ref, low_ref, high_ref):
    begin, end = first - HALO, first - HALO + SPAN
    if begin < 0:
        return jnp.concatenate([low_ref[c, HALO + begin :], panel_ref[c, :end]], axis=0)
    if end > rows:
        return jnp.concatenate([panel_ref[c, begin:], high_ref[c, : end - rows]], axis=0)
    return panel_ref[c, begin:end]


def images_of(blocks, base, panel, nbr, coef, count, halos=(), before=None, edges=False, parts=0):
    rows, modes = panel.shape[1:]
    before_blocks = before.shape[1] // (3 * LANES) if parts else 0
    width = (len(blocks) + before_blocks) * LANES
    operands = [base, nbr, count, coef, panel, *halos]
    in_specs = [SMEM] + [HBM] * (len(operands) - 1)
    if before is not None:
        operands.append(before)
        in_specs.append(VMEM if parts else HBM)
    out_shape = [jax.ShapeDtypeStruct((modes, 3 * width), jnp.bfloat16)]
    out_specs = [VMEM]
    if edges:
        out_shape += [jax.ShapeDtypeStruct((3, HALO, modes), jnp.bfloat16)] * 2
        out_specs += [HBM] * 2
    out_shape += [jax.ShapeDtypeStruct((modes // parts, 3 * width), jnp.bfloat16)] * parts if parts > 1 else []
    out_specs += [VMEM] * parts if parts > 1 else []
    n_in, n_out = len(operands), len(out_shape)

    def kernel(*refs):
        base_ref, nbr_hbm, count_hbm, coef_hbm, panel_hbm = refs[:5]
        outs = refs[n_in : n_in + n_out]
        nbr_ref, count_ref, coef_ref, panel_ref, low_ref, high_ref, dense_ref, sems = refs[n_in + n_out :]
        copies, panel_copies = [], []

        def start(source, target, kept):
            copy = pltpu.make_async_copy(source, target, sems.at[len(copies) + len(panel_copies)])
            copy.start()
            kept.append(copy)

        start(nbr_hbm, nbr_ref, copies)
        start(count_hbm, count_ref, copies)
        for _, block, length in runs_of(blocks):
            at = pl.ds(block * LANES, length * LANES)
            start(coef_hbm.at[:, :, at], coef_ref.at[:, :, at], copies)
        for _, block, length in runs_of(blocks):
            begin = max(block * LANES - HALO, 0)
            end = min((block + length) * LANES + HALO, rows)
            at = pl.ds(begin, end - begin)
            start(panel_hbm.at[:, at], panel_ref.at[:, at], panel_copies)
        if halos:
            start(refs[5], low_ref, panel_copies)
            start(refs[6], high_ref, panel_copies)
        if edges:
            start(panel_hbm.at[:, pl.ds(0, HALO)], outs[1], panel_copies)
            start(panel_hbm.at[:, pl.ds(rows - HALO, HALO)], outs[2], panel_copies)
        for copy in copies:
            copy.wait()
        for place, block in enumerate(blocks):
            first = block * LANES
            build_block(first, base_ref[0], nbr_ref, coef_ref, count_ref, dense_ref)
            if place == 0:
                for copy in panel_copies:
                    copy.wait()
            cells = jnp.concatenate(
                [window(first, rows, c, panel_ref, low_ref, high_ref) for c in range(3)], axis=0
            )
            both = lax.dot_general(
                cells, dense_ref[...], (((0,), (0,)), ((), ())), preferred_element_type=jnp.float32
            )
            for r in range(3):
                image = both[:, 2 * r * LANES : (2 * r + 1) * LANES]
                image = image + both[:, (2 * r + 1) * LANES : (2 * r + 2) * LANES]
                at = r * width + (before_blocks + place) * LANES
                outs[0][:, at : at + LANES] = image.astype(jnp.bfloat16)
        if parts:
            old = before_blocks * LANES
            for r in range(3):
                outs[0][:, r * width : r * width + old] = refs[n_in - 1][:, r * old : (r + 1) * old]
            for part, out in enumerate(outs[-parts:] if parts > 1 else []):
                span = modes // parts
                out[...] = outs[0][part * span : (part + 1) * span, :]

    copies_most = 2 + 2 * len(runs_of(blocks)) + 4
    scratch = [
        pltpu.VMEM((BONDS, rows), jnp.int32),
        pltpu.VMEM((rows,), jnp.int32),
        pltpu.VMEM((9, BONDS, rows), jnp.float32),
        pltpu.VMEM((3, rows, modes), jnp.bfloat16),
        pltpu.VMEM((3, HALO, modes), jnp.bfloat16),
        pltpu.VMEM((3, HALO, modes), jnp.bfloat16),
        pltpu.VMEM((3 * SPAN, 6 * LANES), jnp.bfloat16),
        pltpu.SemaphoreType.DMA((copies_most,)),
    ]
    return call(kernel, "images", in_specs, out_specs, out_shape, operands, 1.0 + len(blocks), scratch)


def products_of(chunks, place, partners, mine, theirs, rows_from, rows):
    cols = partners.shape[2]
    count = len(chunks)

    def kernel(place_ref, partners_ref, *refs):
        keep_ref, send_ref = refs[-2:]

        def half(who):
            total = None
            for i, blocks in enumerate(chunks):
                image_ref = refs[who * count + i]
                at_rows = slice(rows_from[i], rows_from[i] + rows)
                width = len(blocks) * LANES
                for r in range(3):
                    for spot, block, length in runs_of(blocks):
                        at = r * width + spot * LANES
                        part = jnp.dot(
                            image_ref[at_rows, at : at + length * LANES],
                            partners_ref[r, block * LANES : (block + length) * LANES, :],
                            preferred_element_type=jnp.float32,
                        )
                        total = part if total is None else total + part
            return total

        first, second = half(0), half(1)
        kept = place_ref[0] == place_ref[1]
        keep_ref[...] = jnp.where(kept, first, second)
        send_ref[...] = jnp.where(kept, second, first).astype(jnp.bfloat16)

    return call(
        kernel,
        "products",
        [SMEM] + [VMEM] * (1 + 2 * count),
        [VMEM, VMEM],
        [jax.ShapeDtypeStruct((rows, cols), jnp.float32), jax.ShapeDtypeStruct((rows, cols), jnp.bfloat16)],
        (place, partners, *mine, *theirs),
        2.5,
    )


def all_products(chunks, half, partners, mine, theirs):
    modes, cols = mine[0].shape[0], partners.shape[2]
    place = jnp.stack([half, jnp.zeros((), jnp.int32)])
    low = products_of(chunks, place, partners, mine, theirs, [0] * len(chunks), modes)[0]
    high = products_of(chunks, place + jnp.array([0, 1], jnp.int32), partners, mine, theirs, [0] * len(chunks), modes)[0]
    return jnp.stack([low, high])


def settle(cells, bit, rows_dev):
    depth = lax.axis_size("atoms")
    place = lax.axis_index("atoms")
    while cells.shape[0] > 1:
        pairs = cells.reshape(cells.shape[0] // 2, 2, rows_dev, -1)
        own = (place >> bit) & 1
        keep = lax.dynamic_index_in_dim(pairs, own, 1, keepdims=False)
        send = lax.dynamic_index_in_dim(pairs, 1 - own, 1, keepdims=False)
        step = 1 << bit
        got = lax.ppermute(send.astype(jnp.bfloat16), "atoms", [(z, z ^ step) for z in range(depth)])
        cells = keep + got.astype(jnp.float32)
        bit += 1
    return cells[0], bit


def collected(terms, bit, shift):
    groups, depth = lax.axis_size("modes"), lax.axis_size("atoms")
    level = 0
    while (1 << level) < groups:
        moves = []
        for z in range(depth):
            for m in range(groups):
                goal = m ^ shift
                settled = all(((z >> (bit + u)) ^ (goal >> u)) & 1 == 0 for u in range(level))
                if settled and ((z >> (bit + level)) ^ (goal >> level)) & 1:
                    moves.append((z * groups + m, (z ^ (1 << (bit + level))) * groups + m))
        sent = sum(term.astype(jnp.float32) for term in terms).astype(jnp.bfloat16)
        terms = terms + [lax.ppermute(sent, ("atoms", "modes"), moves)]
        level += 1
    return terms


def finish(flag, early, late, my_start, my_length, my_freq, partner_freq, first_col, norm_scale):
    rows, cols = early[0].shape
    n_early, parts, n_late = len(early), len(late), len(late[0])
    operands = [flag, my_start, my_length, my_freq, partner_freq, *early, *[t for part in late for t in part]]

    def kernel(flag_ref, start_ref, length_ref, freq_ref, partner_ref, *refs):
        out_ref, sum_ref = refs[-2:]
        span = rows // parts

        def sums(some):
            total = some[0][...]
            for ref in some[1:]:
                total = total + ref[...].astype(jnp.float32)
            return total

        @pl.when(flag_ref[0] == 1)
        def _():
            out_ref[...] = sums(refs[:n_early])

        @pl.when(flag_ref[0] == 0)
        def _():
            for part in range(parts):
                at = n_early + part * n_late
                out_ref[part * span : (part + 1) * span, :] = sums(refs[at : at + n_late])

        columns = lax.broadcasted_iota(jnp.int32, (rows, cols), 1) + flag_ref[1]
        start = start_ref[...]
        inside = (columns >= start) & (columns < start + length_ref[...])
        elements = jnp.where(inside, out_ref[...] * norm_scale, 0.0)
        out_ref[...] = elements
        offset = freq_ref[...] - partner_ref[...]
        lorentz = lorentz_width / (math.pi * (offset * offset + lorentz_width * lorentz_width))
        weighted = jnp.where(inside, lorentz, 0.0) * elements * elements
        folded = weighted[:, :LANES]
        for at in range(LANES, cols, LANES):
            folded = folded + weighted[:, at : at + LANES]
        if rows < LANES:
            folded = jnp.concatenate([folded, jnp.zeros((LANES - rows, LANES), jnp.float32)], axis=0)
        sum_ref[...] = jnp.sum(folded.T, axis=0, keepdims=True)

    return call(
        kernel,
        "finish",
        [SMEM] + [VMEM] * (len(operands) - 1),
        [VMEM, VMEM],
        [jax.ShapeDtypeStruct((rows, cols), jnp.float32), jax.ShapeDtypeStruct((1, LANES), jnp.float32)],
        operands,
        2.0,
    )


def body(
    mode_panel,
    partners,
    bond_blocks,
    neighbors,
    bond_count,
    panel_freq,
    partner_freq,
    win_start,
    win_len,
):
    atom_rows, modes = mode_panel.shape[1:]
    atom_index = lax.axis_index("atoms")
    atom_count = lax.axis_size("atoms")
    groups = lax.axis_size("modes")
    group_index = lax.axis_index("modes")
    half_index = lax.axis_index("sub")
    column_index = lax.axis_index(("modes", "sub"))
    part_cols = partners.shape[2]
    panel_total = win_start.shape[0]
    rows_dev = panel_total // atom_count
    whole_halves = rows_dev == modes

    nbr = neighbors.T
    coef = bond_blocks.transpose(0, 2, 1)
    base = (atom_index * atom_rows).astype(jnp.int32)[None]

    last = atom_rows // LANES - 1
    middle = list(range(1, last))
    cut = len(middle) // 2
    shared = (base, mode_panel, nbr, coef, bond_count)
    first_images, head, tail = images_of(middle[:cut], *shared, edges=True)
    low_halo = lax.ppermute(tail, "atoms", [(z, z + 1) for z in range(atom_count - 1)])
    high_halo = lax.ppermute(head, "atoms", [(z + 1, z) for z in range(atom_count - 1)])
    (middle_images,) = images_of(middle[cut:], *shared, before=first_images)
    parts = 2 if whole_halves else 1
    rest, *pieces = images_of(
        [last, 0], *shared, halos=(low_halo, high_halo), before=middle_images, parts=parts
    )
    pieces = pieces or [rest]
    chunks = [middle[:cut], middle[cut:] + [last, 0]]

    swap = [(0, 1), (1, 0)]

    def from_group(cells, shift):
        return lax.ppermute(cells, "modes", [(m ^ shift, m) for m in range(groups)])

    def from_sibling(cells):
        return lax.ppermute(cells, "sub", swap)

    mine = [first_images, rest]
    theirs = [from_sibling(first_images), from_sibling(rest)]
    half = half_index.astype(jnp.int32)
    place = jnp.stack([half, (atom_index & 1).astype(jnp.int32)])
    goal = atom_index * groups // atom_count

    if whole_halves:
        def level_zero(chunk_mine, chunk_theirs, rows_from, rows):
            keep, send = products_of(chunks, place, partners, chunk_mine, chunk_theirs, rows_from, rows)
            got = lax.ppermute(send, "atoms", [(z, z ^ 1) for z in range(atom_count)])
            return [keep, got]

        early = collected(level_zero(mine, theirs, [0, 0], modes), 1, 0)
    else:
        cells, bit = settle(all_products(chunks, half, partners, mine, theirs).reshape(-1, rows_dev, part_cols), 0, rows_dev)
        early = collected([cells], bit, 0)

    late = None
    for shift in range(1, groups):
        far = [from_group(cells, shift) for cells in [first_images] + pieces]
        far_sibling = [from_sibling(cells) for cells in far]
        terms = []
        for part in range(parts):
            pick = [far[0], far[1 + part]]
            pick_sibling = [far_sibling[0], far_sibling[1 + part]]
            if whole_halves:
                span = modes // parts
                found = collected(level_zero(pick, pick_sibling, [part * span, 0], span), 1, shift)
            else:
                cells, bit = settle(
                    all_products(chunks, half, partners, pick, pick_sibling).reshape(-1, rows_dev, part_cols), 0, rows_dev
                )
                found = collected([cells], bit, shift)
            terms.append(found)
        if late is None:
            late = terms
        else:
            here = (group_index ^ shift) == goal
            late = [[jnp.where(here, a, b) for a, b in zip(new, old)] for new, old in zip(terms, late)]

    def my_rows(values):
        return lax.dynamic_slice_in_dim(values, atom_index * rows_dev, rows_dev, 0)

    my_freq = my_rows(panel_freq)
    flag = jnp.stack([(group_index == goal).astype(jnp.int32), (column_index * part_cols).astype(jnp.int32)])
    elements, numerator = finish(
        flag,
        early,
        late,
        my_rows(win_start)[:, None],
        my_rows(win_len)[:, None],
        my_freq[:, None],
        partner_freq[None, :],
        column_index * part_cols,
        1.0 / math.sqrt(3 * atom_rows * atom_count),
    )
    holders = groups * 2
    sums = [numerator] + [
        lax.ppermute(numerator, ("modes", "sub"), [(i, i ^ code) for i in range(holders)])
        for code in range(1, holders)
    ]
    while len(sums) > 1:
        sums = [sums[i] + sums[i + 1] for i in range(0, len(sums), 2)]
    diffusivity = math.pi / 3.0 * sums[0][0, :rows_dev] / (my_freq * my_freq)
    return (elements, diffusivity)


def solution(mesh):
    return jax.shard_map(
        body,
        mesh=mesh,
        in_specs=(
            P(None, ("dom", "atoms"), ("modes", "sub")),
            P(None, ("dom", "atoms"), ("modes", "sub")),
            P(None, ("dom", "atoms"), None),
            P(("dom", "atoms"), None),
            P(("dom", "atoms")),
            P("dom"),
            P(("dom", "modes", "sub")),
            P("dom"),
            P("dom"),
        ),
        out_specs=(P(("dom", "atoms"), ("modes", "sub")), P(("dom", "atoms"))),
        check_vma=False,
    )
```

time: 270 us -> 72.5 us (0.27)
  other arithmetic: 85.6 us -> 0.82 us
  waiting for transfers between devices: 87.4 us -> 19.4 us
  local copies, waits for them, and re-layouts: 62.1 us -> 6.1 us
  starting transfers between devices: 6.3 us -> 27.5 us
  Pallas kernels: 0 us -> 17.3 us
  between operations: 14.9 us -> 0.86 us
  blocking collectives: 6.37 us -> 0 us
  matrix products: 4.58 us -> 0 us
    psum x1 -> x0, waiting for transfers between devices: 60 us -> none  [body(): lax.psum(lax.cond(touched, lambda: lax.dot_general(all_images, partners,...]
    select_n x32 -> x0, other arithmetic: 46.3 us -> none  [slot_step(): gathered = jnp.take(extended, target, axis=1)]
    gather x16 -> x0, local copies, waits for them, and re-layouts: 45.5 us -> none  [slot_step(): gathered = jnp.take(extended, target, axis=1)]
    all_gather x1 -> x0, waiting for transfers between devices: 23.4 us -> none  [body(): all_images = lax.all_gather(images, ('modes', 'sub'), axis=2, tiled=True)]
    ppermute x2 -> x19, starting transfers between devices: 6.23 us -> 27.5 us  [the longest x3 11.3 us: collected(): terms = terms + [lax.ppermute(sent, ('atoms', 'modes'), moves)]]
    add x18 -> x0, other arithmetic: 19.7 us -> none  [the longest x16 19.7 us: slot_step(): summed = summed + coef_slot[:, d, :, None] * gathered[d][None]]
    pallas_call x0 -> x7, Pallas kernels: none -> 17.3 us  [call(): pl.pallas_call(kernel, in_specs=in_specs, out_specs=out_specs, out_shape=...]
    ppermute x2 -> x19, waiting for transfers between devices: 3.97 us -> 19.4 us  [the longest x3 10.7 us: from_group(): return lax.ppermute(cells, 'modes', [(m ^ shift, m) for m in range(groups)])]
  transfers between devices with their start and end apart: 4 -> 19, of which waited for: 3 -> 8; matrix products, arithmetic and copies ran while one was open for 1% -> 2% of each run, Pallas kernels for 0% -> 13%
where the time goes in v2:
time: 72.5 us; the launch traced here: 72 us
  starting transfers between devices  27.5 us (38%)
  waiting for transfers between devices  19.4 us (27%)
  Pallas kernels  17.3 us (24%)
  local copies, waits for them, and re-layouts  6.1 us (8%)
  between operations  0.86 us (1%)
  other arithmetic  0.82 us (1%)
    pallas_call x7, Pallas kernels, call(): pl.pallas_call(kernel, in_specs=in_specs, out_specs=out_specs, out_shape=...  17.3 us
    ppermute x3, starting transfers between devices, collected(): terms = terms + [lax.ppermute(sent, ('atoms', 'modes'), moves)]  11.3 us
    ppermute x3, waiting for transfers between devices, from_group(): return lax.ppermute(cells, 'modes', [(m ^ shift, m) for m in range(groups)])  10.7 us
    ppermute x1, starting transfers between devices, body(): lax.ppermute(tail, 'atoms', [(z, z + 1) for z in range(atom_count - 1)])  4.93 us
    unnamed x20, local copies, waits for them, and re-layouts  4.91 us
    ppermute x3, waiting for transfers between devices, collected(): terms = terms + [lax.ppermute(sent, ('atoms', 'modes'), moves)]  4.69 us
    ppermute x3, starting transfers between devices, level_zero(): got = lax.ppermute(send, 'atoms', [(z, z ^ 1) for z in range(atom_count)])  3.8 us
    ppermute x3, starting transfers between devices, from_group(): return lax.ppermute(cells, 'modes', [(m ^ shift, m) for m in range(groups)])  3.58 us
  transfers between devices with their start and end apart: 19, of which 8 were waited for; matrix products, arithmetic and copies ran while one was open for 2% of the time, Pallas kernels for 13%

profile of v2, /device:TPU:0, one launch (start us, length us, event | category | flops | bytes accessed | tf_op | source)
XLA Modules:
  0.0 72.0 jit_solution(7567132010701776878)
XLA Ops:
  0.6 1.1 %copy-done.1 = bf16[3,768,128]{2,1,0:T(8,128)(2,1)S(1)} copy-done((bf16[3,768,128]{2,1,0:T(8,128)(2,1)S(1)}, bf16[3,768,128]{2,1,0:T(8,128)(2,1)}, u32[]{:S(2)}) %copy-start.1) | copy-done | bytes 589848
  1.7 1.0 %copy-done.2 = f32[9,768,16]{1,2,0:T(8,128)S(1)} copy-done((f32[9,768,16]{1,2,0:T(8,128)S(1)}, f32[9,768,16]{1,2,0:T(8,128)}, u32[]{:S(2)}) %copy-start.2) | copy-done | bytes 442392
  2.7 0.8 %copy-done.5 = s32[768,16]{0,1:T(8,128)S(1)} copy-done((s32[768,16]{0,1:T(8,128)S(1)}, s32[768,16]{0,1:T(8,128)}, u32[]{:S(2)}) %copy-start.5) | copy-done | bytes 49176
  3.5 0.7 copy-done.7
  4.2 3.4 %images.3 = (bf16[128,768]{1,0:T(8,128)(2,1)}, bf16[3,96,128]{2,1,0:T(8,128)(2,1)S(1)}, bf16[3,96,128]{2,1,0:T(8,128)(2,1)S(1)}) custom-call(s32[1]{0:T(128)} %bitcast.7.refs_0_, s32[16,768]{1,0:T(8,128)S(1)} %bitcast.18, s32[768]{0:T(1024)S(1)} %copy-done.7, f32[9,16,768]{2,1,0:T(8,128)S(1)} %bitcast.15, bf16[3,768,128]{2,1,0:T(8,128)(2,1)S(1)} %copy-done.1), custom_call_target="tpu_custom_call" | custom-call | flops 3300000000 | bytes 300000 | tf_op jit(solution)/shard_map/images/pallas_call | solution.py:25
  7.6 4.9 %collective-permute-start = (bf16[3,96,128]{2,1,0:T(8,128)(2,1)S(1)}, bf16[3,96,128]{2,1,0:T(8,128)(2,1)S(1)}, u32[]{:S(2)}, u32[]{:S(2)}) collective-permute-start(bf16[3,96,128]{2,1,0:T(8,128)(2,1)S(1)} %get-tuple-element.17), channel_id=1, source_target_pairs={{0,4},{4,8},{8,12},{1,5},{5,9},{9,13},{2,6},{6,10},{10,14},{3,7},{... | collective-permute-start | bytes 221192 | tf_op jit(solution)/shard_map/ppermute | solution.py:352
  12.6 1.3 %collective-permute-start.1 = (bf16[3,96,128]{2,1,0:T(8,128)(2,1)S(1)}, bf16[3,96,128]{2,1,0:T(8,128)(2,1)S(1)}, u32[]{:S(2)}, u32[]{:S(2)}) collective-permute-start(bf16[3,96,128]{2,1,0:T(8,128)(2,1)S(1)} %get-tuple-element.18), channel_id=1, source_target_pairs={{4,0},{8,4},{12,8},{5,1},{9,5},{13,9},{6,2},{10,6},{14,10},{7,3},{... | collective-permute-start | bytes 221192 | tf_op jit(solution)/shard_map/ppermute | solution.py:353
  13.9 2.7 %images.4.refs_7_ = bf16[128,768]{1,0:T(8,128)(2,1)S(1)} custom-call(s32[1]{0:T(128)} %bitcast.7.refs_0_, s32[16,768]{1,0:T(8,128)S(1)} %bitcast.19, s32[768]{0:T(1024)S(1)} %copy-done.7, f32[9,16,768]{2,1,0:T(8,128)S(1)} %bitcast.16, bf16[3,768,128]{2,1,0:T(8,128)(2,1)S(1)} %copy-done.1, bf16[128,768]{1,0:T(8,128)(2,1)} %get-tuple-element.16.refs_5_.refs_0_), custom_call_target="tpu_custom_call" | custom-call | flops 3300000000 | bytes 300000 | tf_op jit(solution)/shard_map/images/pallas_call | solution.py:25
  16.6 0.0 copy-start.9
  16.6 0.0 copy-start.8
  16.6 0.0 copy-start
  16.6 2.2 %collective-permute-done.1.refs_6_ = bf16[3,96,128]{2,1,0:T(8,128)(2,1)S(1)} collective-permute-done((bf16[3,96,128]{2,1,0:T(8,128)(2,1)S(1)}, bf16[3,96,128]{2,1,0:T(8,128)(2,1)S(1)}, u32[]{:S(2)}, u32[]{:S(2)}) %collective-permute-start.1) | collective-permute-done | bytes 73760 | tf_op jit(solution)/shard_map/ppermute | solution.py:353
  18.8 3.0 %images.5 = (bf16[128,1536]{1,0:T(8,128)(2,1)S(1)}, bf16[64,1536]{1,0:T(8,128)(2,1)S(1)}, bf16[64,1536]{1,0:T(8,128)(2,1)S(1)}) custom-call(s32[1]{0:T(128)} %bitcast.7.refs_0_, s32[16,768]{1,0:T(8,128)S(1)} %bitcast.20, s32[768]{0:T(1024)S(1)} %copy-done.7, f32[9,16,768]{2,1,0:T(8,128)S(1)} %bitcast.17, bf16[3,768,128]{2,1,0:T(8,128)(2,1)S(1)} %copy-done.1, ...), custom_call_target="tpu_custom_call" | custom-call | flops 3300000000 | bytes 300000 | tf_op jit(solution)/shard_map/images/pallas_call | solution.py:25
  21.8 0.7 copy-done.3
  22.5 0.7 copy-done.4
  23.2 0.5 collective-permute-start.2
  23.7 1.5 %collective-permute-start.6 = (bf16[128,768]{1,0:T(8,128)(2,1)}, bf16[128,768]{1,0:T(8,128)(2,1)}, u32[]{:S(2)}, u32[]{:S(2)}) collective-permute-start(bf16[128,768]{1,0:T(8,128)(2,1)} %get-tuple-element.16.refs_5_.refs_0_), channel_id=1, source_target_pairs={{2,0},{0,2},{3,1},{1,3},{6,4},{4,6},{7,5},{5,7},{10,8},{8,10},{11,... | collective-permute-start | bytes 589832 | tf_op jit(solution)/shard_map/ppermute | solution.py:365
  25.2 0.8 %dynamic-slice_bitcast_fusion = (s32[128,1]{0,1:T(1,128)S(1)}, s32[128,1]{0,1:T(1,128)S(1)}) fusion(s32[512]{0:T(512)} %param.17, s32[]{:T(128)S(6)} %select_n.11, s32[512]{0:T(512)} %param.16), kind=kLoop, calls=%fused_computation.6 | loop fusion | bytes 2052 | tf_op jit(solution)/shard_map/broadcast_in_dim | solution.py:420
  25.9 0.1 copy.11.start_ref
  26.1 0.1 copy.12.length_ref
  26.2 0.6 collective-permute-start.7
  26.8 1.5 %collective-permute-start.12 = (bf16[64,1536]{1,0:T(8,128)(2,1)}, bf16[64,1536]{1,0:T(8,128)(2,1)}, u32[]{:S(2)}, u32[]{:S(2)}) collective-permute-start(bf16[64,1536]{1,0:T(8,128)(2,1)} %copy-done.3), channel_id=1, source_target_pairs={{2,0},{0,2},{3,1},{1,3},{6,4},{4,6},{7,5},{5,7},{10,8},{8,10},{11,... | collective-permute-start | bytes 589832 | tf_op jit(solution)/shard_map/ppermute | solution.py:365
  28.3 0.1 dynamic-slice_bitcast_fusion.2
  28.3 0.1 copy.13.freq_ref
  28.5 0.1 pad_add_fusion.1.place_ref
  28.5 3.2 %collective-permute-done.6.refs_0_ = bf16[128,768]{1,0:T(8,128)(2,1)} collective-permute-done((bf16[128,768]{1,0:T(8,128)(2,1)}, bf16[128,768]{1,0:T(8,128)(2,1)}, u32[]{:S(2)}, u32[]{:S(2)}) %collective-permute-start.6) | collective-permute-done | bytes 196640 | tf_op jit(solution)/shard_map/ppermute | solution.py:365
  31.8 0.0 collective-permute-start.8
  31.8 4.2 %collective-permute-done.7.refs_1_ = bf16[64,1536]{1,0:T(8,128)(2,1)} collective-permute-done((bf16[64,1536]{1,0:T(8,128)(2,1)}, bf16[64,1536]{1,0:T(8,128)(2,1)}, u32[]{:S(2)}, u32[]{:S(2)}) %collective-permute-start.7) | collective-permute-done | bytes 196640 | tf_op jit(solution)/shard_map/ppermute | solution.py:365
  36.0 3.2 %collective-permute-done.12.refs_1_ = bf16[64,1536]{1,0:T(8,128)(2,1)} collective-permute-done((bf16[64,1536]{1,0:T(8,128)(2,1)}, bf16[64,1536]{1,0:T(8,128)(2,1)}, u32[]{:S(2)}, u32[]{:S(2)}) %collective-permute-start.12) | collective-permute-done | bytes 196640 | tf_op jit(solution)/shard_map/ppermute | solution.py:365
  39.2 2.5 %products.3 = (f32[128,640]{1,0:T(8,128)S(1)}, bf16[128,640]{1,0:T(8,128)(2,1)S(1)}) custom-call(s32[2]{0:T(128)S(1)} %pad_add_fusion.1.place_ref, bf16[3,768,640]{2,1,0:T(8,128)(2,1)S(1)} %copy-done, bf16[128,768]{1,0:T(8,128)(2,1)} %get-tuple-element.16.refs_5_.refs_0_, bf16[128,1536]{1,0:T(8,128)(2,1)S(1)} %get-tuple-element.19.refs_1_, ...), custom_call_target="tpu_custom_call" | custom-call | flops 2750000128 | bytes 250000 | tf_op jit(solution)/shard_map/products/pallas_call | solution.py:25
  41.8 1.6 %collective-permute-start.4 = (bf16[128,640]{1,0:T(8,128)(2,1)S(1)}, bf16[128,640]{1,0:T(8,128)(2,1)S(1)}, u32[]{:S(2)}, u32[]{:S(2)}) collective-permute-start(bf16[128,640]{1,0:T(8,128)(2,1)S(1)} %get-tuple-element.21), channel_id=1, source_target_pairs={{0,4},{4,0},{8,12},{12,8},{1,5},{5,1},{9,13},{13,9},{2,6},{6,2},{1... | collective-permute-start | bytes 491528 | tf_op jit(solution)/shard_map/ppermute | solution.py:379
  43.4 0.0 collective-permute-done.8.refs_2_
  43.4 2.1 %products.4 = (f32[64,640]{1,0:T(8,128)S(1)}, bf16[64,640]{1,0:T(8,128)(2,1)S(1)}) custom-call(s32[2]{0:T(128)S(1)} %pad_add_fusion.1.place_ref, bf16[3,768,640]{2,1,0:T(8,128)(2,1)S(1)} %copy-done, bf16[128,768]{1,0:T(8,128)(2,1)} %collective-permute-done.6.refs_0_, bf16[64,1536]{1,0:T(8,128)(2,1)} %collective-permute-done.7.refs_1_, ...), custom_call_target="tpu_custom_call" | custom-call | flops 2750000128 | bytes 250000 | tf_op jit(solution)/shard_map/products/pallas_call | solution.py:25
  45.5 0.5 collective-permute-start.10
  46.0 2.1 %products.5 = (f32[64,640]{1,0:T(8,128)S(1)}, bf16[64,640]{1,0:T(8,128)(2,1)S(1)}) custom-call(s32[2]{0:T(128)S(1)} %pad_add_fusion.1.place_ref, bf16[3,768,640]{2,1,0:T(8,128)(2,1)S(1)} %copy-done, bf16[128,768]{1,0:T(8,128)(2,1)} %collective-permute-done.6.refs_0_, bf16[64,1536]{1,0:T(8,128)(2,1)} %collective-permute-done.12.refs_1_, ...), custom_call_target="tpu_custom_call" | custom-call | flops 2750000128 | bytes 250000 | tf_op jit(solution)/shard_map/products/pallas_call | solution.py:25
  48.1 1.6 %collective-permute-start.14 = (bf16[64,640]{1,0:T(8,128)(2,1)S(1)}, bf16[64,640]{1,0:T(8,128)(2,1)S(1)}, u32[]{:S(2)}, u32[]{:S(2)}) collective-permute-start(bf16[64,640]{1,0:T(8,128)(2,1)S(1)} %get-tuple-element.27), channel_id=1, source_target_pairs={{0,4},{4,0},{8,12},{12,8},{1,5},{5,1},{9,13},{13,9},{2,6},{6,2},{1... | collective-permute-start | bytes 245768 | tf_op jit(solution)/shard_map/ppermute | solution.py:379
  49.8 0.4 collective-permute-done.10.refs_4_
  50.2 4.5 %collective-permute-start.11 = (bf16[64,640]{1,0:T(8,128)(2,1)S(1)}, bf16[64,640]{1,0:T(8,128)(2,1)S(1)}, u32[]{:S(2)}, u32[]{:S(2)}) collective-permute-start(bf16[64,640]{1,0:T(8,128)(2,1)S(1)} %add_convert_fusion.2), channel_id=1, source_target_pairs={{0,8},{4,12},{10,2},{14,6},{1,9},{5,13},{11,3},{15,7},{16,24},{20,... | collective-permute-start | bytes 245768 | tf_op jit(solution)/shard_map/ppermute | solution.py:264
  54.8 1.3 %collective-permute-start.5 = (bf16[128,640]{1,0:T(8,128)(2,1)S(1)}, bf16[128,640]{1,0:T(8,128)(2,1)S(1)}, u32[]{:S(2)}, u32[]{:S(2)}) collective-permute-start(bf16[128,640]{1,0:T(8,128)(2,1)S(1)} %add_convert_fusion), channel_id=1, source_target_pairs={{2,10},{6,14},{8,0},{12,4},{3,11},{7,15},{9,1},{13,5},{18,26},{22,... | collective-permute-start | bytes 491528 | tf_op jit(solution)/shard_map/ppermute | solution.py:264
  56.1 5.5 %collective-permute-start.15 = (bf16[64,640]{1,0:T(8,128)(2,1)S(1)}, bf16[64,640]{1,0:T(8,128)(2,1)S(1)}, u32[]{:S(2)}, u32[]{:S(2)}) collective-permute-start(bf16[64,640]{1,0:T(8,128)(2,1)S(1)} %add_convert_fusion.1), channel_id=1, source_target_pairs={{0,8},{4,12},{10,2},{14,6},{1,9},{5,13},{11,3},{15,7},{16,24},{20,... | collective-permute-start | bytes 245768 | tf_op jit(solution)/shard_map/ppermute | solution.py:264
  61.6 0.1 pad_add_fusion.flag_ref
  61.7 2.0 %collective-permute-done.15.refs_8_ = bf16[64,640]{1,0:T(8,128)(2,1)S(1)} collective-permute-done((bf16[64,640]{1,0:T(8,128)(2,1)S(1)}, bf16[64,640]{1,0:T(8,128)(2,1)S(1)}, u32[]{:S(2)}, u32[]{:S(2)}) %collective-permute-start.15) | collective-permute-done | bytes 81952 | tf_op jit(solution)/shard_map/ppermute | solution.py:264
  63.6 2.7 %collective-permute-done.5.refs_2_ = bf16[128,640]{1,0:T(8,128)(2,1)S(1)} collective-permute-done((bf16[128,640]{1,0:T(8,128)(2,1)S(1)}, bf16[128,640]{1,0:T(8,128)(2,1)S(1)}, u32[]{:S(2)}, u32[]{:S(2)}) %collective-permute-start.5) | collective-permute-done | bytes 163872 | tf_op jit(solution)/shard_map/ppermute | solution.py:264
  66.4 1.5 %finish.1 = (f32[128,640]{1,0:T(8,128)}, f32[1,128]{1,0:T(1,128)S(1)}) custom-call(s32[2]{0:T(128)S(1)} %pad_add_fusion.flag_ref, s32[128,1]{1,0:T(8,128)S(1)} %copy.11.start_ref, s32[128,1]{1,0:T(8,128)S(1)} %copy.12.length_ref, f32[128,1]{1,0:T(8,128)S(1)} %copy.13.freq_ref, f32[1,640]{1,0:T(1,128)S(1)} %broadcast_in_dim.18.partner_ref, ...), custom_call_target="tpu_custom_call" | custom-call | flops 2200000000 | bytes 200000 | tf_op jit(solution)/shard_map/finish/pallas_call | solution.py:25
  67.9 1.4 %collective-permute-start.18 = (f32[1,128]{1,0:T(1,128)S(1)}, f32[1,128]{1,0:T(1,128)S(1)}, u32[]{:S(2)}, u32[]{:S(2)}) collective-permute-start(f32[1,128]{1,0:T(1,128)S(1)} %get-tuple-element.29), channel_id=1, source_target_pairs={{0,3},{1,2},{2,1},{3,0},{4,7},{5,6},{6,5},{7,4},{8,11},{9,10},{10,... | collective-permute-start | bytes 1544 | tf_op jit(solution)/shard_map/ppermute | solution.py:428
  69.3 0.8 %collective-permute-start.16 = (f32[1,128]{1,0:T(1,128)S(1)}, f32[1,128]{1,0:T(1,128)S(1)}, u32[]{:S(2)}, u32[]{:S(2)}) collective-permute-start(f32[1,128]{1,0:T(1,128)S(1)} %get-tuple-element.29), channel_id=1, source_target_pairs={{0,1},{1,0},{2,3},{3,2},{4,5},{5,4},{6,7},{7,6},{8,9},{9,8},{10,11... | collective-permute-start | bytes 1544 | tf_op jit(solution)/shard_map/ppermute | solution.py:428
  70.0 1.4 %collective-permute-done.17 = f32[1,128]{1,0:T(1,128)S(1)} collective-permute-done((f32[1,128]{1,0:T(1,128)S(1)}, f32[1,128]{1,0:T(1,128)S(1)}, u32[]{:S(2)}, u32[]{:S(2)}) %collective-permute-start.17) | collective-permute-done | bytes 544 | tf_op jit(solution)/shard_map/ppermute | solution.py:428
  71.4 0.6 bitcast_divide_fusion
  (29 shorter events, 0.1 us)
Async XLA Ops:
  0.6 1.1 %copy-start.1 = (bf16[3,768,128]{2,1,0:T(8,128)(2,1)S(1)}, bf16[3,768,128]{2,1,0:T(8,128)(2,1)}, u32[]{:S(2)}) copy-start(bf16[3,768,128]{2,1,0:T(8,128)(2,1)} %refs_4_.5) | copy-start | bytes 1769476
  1.7 1.0 %copy-start.2 = (f32[9,768,16]{1,2,0:T(8,128)S(1)}, f32[9,768,16]{1,2,0:T(8,128)}, u32[]{:S(2)}) copy-start(f32[9,768,16]{1,2,0:T(8,128)} %param.11) | copy-start | bytes 1327108
  2.7 0.8 %copy-start.5 = (s32[768,16]{0,1:T(8,128)S(1)}, s32[768,16]{0,1:T(8,128)}, u32[]{:S(2)}) copy-start(s32[768,16]{0,1:T(8,128)} %param.12) | copy-start | bytes 147460
  3.5 0.7 copy-start.7
  4.2 9.7 %copy-start.6 = (s32[768,16]{0,1:T(8,128)S(1)}, s32[768,16]{0,1:T(8,128)}, u32[]{:S(2)}) copy-start(s32[768,16]{0,1:T(8,128)} %param.12) | copy-start | bytes 147460
  7.6 9.0 %collective-permute-start = (bf16[3,96,128]{2,1,0:T(8,128)(2,1)S(1)}, bf16[3,96,128]{2,1,0:T(8,128)(2,1)S(1)}, u32[]{:S(2)}, u32[]{:S(2)}) collective-permute-start(bf16[3,96,128]{2,1,0:T(8,128)(2,1)S(1)} %get-tuple-element.17), channel_id=1, source_target_pairs={{0,4},{4,8},{8,12},{1,5},{5,9},{9,13},{2,6},{6,10},{10,14},{3,7},{... | collective-permute-start | bytes 221192 | tf_op jit(solution)/shard_map/ppermute | solution.py:352
  12.6 6.2 %collective-permute-start.1 = (bf16[3,96,128]{2,1,0:T(8,128)(2,1)S(1)}, bf16[3,96,128]{2,1,0:T(8,128)(2,1)S(1)}, u32[]{:S(2)}, u32[]{:S(2)}) collective-permute-start(bf16[3,96,128]{2,1,0:T(8,128)(2,1)S(1)} %get-tuple-element.18), channel_id=1, source_target_pairs={{4,0},{8,4},{12,8},{5,1},{9,5},{13,9},{6,2},{10,6},{14,10},{7,3},{... | collective-permute-start | bytes 221192 | tf_op jit(solution)/shard_map/ppermute | solution.py:353
  16.6 11.7 %copy-start.9 = (f32[512]{0:T(512)S(1)}, f32[512]{0:T(512)}, u32[]{:S(2)}) copy-start(f32[512]{0:T(512)} %param.14) | copy-start | bytes 6148
  16.6 11.9 %copy-start.8 = (f32[640]{0:T(1024)S(1)}, f32[640]{0:T(1024)}, u32[]{:S(2)}) copy-start(f32[640]{0:T(1024)} %param.15) | copy-start | bytes 7684
  16.6 22.6 %copy-start = (bf16[3,768,640]{2,1,0:T(8,128)(2,1)S(1)}, bf16[3,768,640]{2,1,0:T(8,128)(2,1)}, u32[]{:S(2)}) copy-start(bf16[3,768,640]{2,1,0:T(8,128)(2,1)} %partners_ref.5) | copy-start | bytes 8847364
  21.8 0.7 copy-start.3
  22.5 0.7 copy-start.4
  23.2 16.1 %collective-permute-start.3 = (bf16[128,1536]{1,0:T(8,128)(2,1)S(1)}, bf16[128,1536]{1,0:T(8,128)(2,1)}, u32[]{:S(2)}, u32[]{:S(2)}) collective-permute-start(bf16[128,1536]{1,0:T(8,128)(2,1)S(1)} %get-tuple-element.19.refs_1_), channel_id=1, source_target_pairs={{0,1},{1,0},{2,3},{3,2},{4,5},{5,4},{6,7},{7,6},{8,9},{9,8},{10,11... | collective-permute-start | bytes 1179656 | tf_op jit(solution)/shard_map/ppermute | solution.py:368
  23.2 16.1 %collective-permute-start.2 = (bf16[128,768]{1,0:T(8,128)(2,1)}, bf16[128,768]{1,0:T(8,128)(2,1)}, u32[]{:S(2)}, u32[]{:S(2)}) collective-permute-start(bf16[128,768]{1,0:T(8,128)(2,1)} %get-tuple-element.16.refs_5_.refs_0_), channel_id=1, source_target_pairs={{0,1},{1,0},{2,3},{3,2},{4,5},{5,4},{6,7},{7,6},{8,9},{9,8},{10,11... | collective-permute-start | bytes 589832 | tf_op jit(solution)/shard_map/ppermute | solution.py:368
  23.7 8.1 %collective-permute-start.6 = (bf16[128,768]{1,0:T(8,128)(2,1)}, bf16[128,768]{1,0:T(8,128)(2,1)}, u32[]{:S(2)}, u32[]{:S(2)}) collective-permute-start(bf16[128,768]{1,0:T(8,128)(2,1)} %get-tuple-element.16.refs_5_.refs_0_), channel_id=1, source_target_pairs={{2,0},{0,2},{3,1},{1,3},{6,4},{4,6},{7,5},{5,7},{10,8},{8,10},{11,... | collective-permute-start | bytes 589832 | tf_op jit(solution)/shard_map/ppermute | solution.py:365
  26.2 9.8 %collective-permute-start.7 = (bf16[64,1536]{1,0:T(8,128)(2,1)}, bf16[64,1536]{1,0:T(8,128)(2,1)}, u32[]{:S(2)}, u32[]{:S(2)}) collective-permute-start(bf16[64,1536]{1,0:T(8,128)(2,1)} %copy-done.4), channel_id=1, source_target_pairs={{2,0},{0,2},{3,1},{1,3},{6,4},{4,6},{7,5},{5,7},{10,8},{8,10},{11,... | collective-permute-start | bytes 589832 | tf_op jit(solution)/shard_map/ppermute | solution.py:365
  26.8 12.5 %collective-permute-start.12 = (bf16[64,1536]{1,0:T(8,128)(2,1)}, bf16[64,1536]{1,0:T(8,128)(2,1)}, u32[]{:S(2)}, u32[]{:S(2)}) collective-permute-start(bf16[64,1536]{1,0:T(8,128)(2,1)} %copy-done.3), channel_id=1, source_target_pairs={{2,0},{0,2},{3,1},{1,3},{6,4},{4,6},{7,5},{5,7},{10,8},{8,10},{11,... | collective-permute-start | bytes 589832 | tf_op jit(solution)/shard_map/ppermute | solution.py:365
  31.8 11.7 %collective-permute-start.8 = (bf16[128,768]{1,0:T(8,128)(2,1)}, bf16[128,768]{1,0:T(8,128)(2,1)S(1)}, u32[]{:S(2)}, u32[]{:S(2)}) collective-permute-start(bf16[128,768]{1,0:T(8,128)(2,1)} %collective-permute-done.6.refs_0_), channel_id=1, source_target_pairs={{0,1},{1,0},{2,3},{3,2},{4,5},{5,4},{6,7},{7,6},{8,9},{9,8},{10,11... | collective-permute-start | bytes 589832 | tf_op jit(solution)/shard_map/ppermute | solution.py:368
  36.0 7.5 %collective-permute-start.9 = (bf16[64,1536]{1,0:T(8,128)(2,1)}, bf16[64,1536]{1,0:T(8,128)(2,1)S(1)}, u32[]{:S(2)}, u32[]{:S(2)}) collective-permute-start(bf16[64,1536]{1,0:T(8,128)(2,1)} %collective-permute-done.7.refs_1_), channel_id=1, source_target_pairs={{0,1},{1,0},{2,3},{3,2},{4,5},{5,4},{6,7},{7,6},{8,9},{9,8},{10,11... | collective-permute-start | bytes 589832 | tf_op jit(solution)/shard_map/ppermute | solution.py:368
  39.2 6.8 %collective-permute-start.13 = (bf16[64,1536]{1,0:T(8,128)(2,1)}, bf16[64,1536]{1,0:T(8,128)(2,1)S(1)}, u32[]{:S(2)}, u32[]{:S(2)}) collective-permute-start(bf16[64,1536]{1,0:T(8,128)(2,1)} %collective-permute-done.12.refs_1_), channel_id=1, source_target_pairs={{0,1},{1,0},{2,3},{3,2},{4,5},{5,4},{6,7},{7,6},{8,9},{9,8},{10,11... | collective-permute-start | bytes 589832 | tf_op jit(solution)/shard_map/ppermute | solution.py:368
  41.8 13.0 %collective-permute-start.4 = (bf16[128,640]{1,0:T(8,128)(2,1)S(1)}, bf16[128,640]{1,0:T(8,128)(2,1)S(1)}, u32[]{:S(2)}, u32[]{:S(2)}) collective-permute-start(bf16[128,640]{1,0:T(8,128)(2,1)S(1)} %get-tuple-element.21), channel_id=1, source_target_pairs={{0,4},{4,0},{8,12},{12,8},{1,5},{5,1},{9,13},{13,9},{2,6},{6,2},{1... | collective-permute-start | bytes 491528 | tf_op jit(solution)/shard_map/ppermute | solution.py:379
  45.5 4.7 %collective-permute-start.10 = (bf16[64,640]{1,0:T(8,128)(2,1)S(1)}, bf16[64,640]{1,0:T(8,128)(2,1)S(1)}, u32[]{:S(2)}, u32[]{:S(2)}) collective-permute-start(bf16[64,640]{1,0:T(8,128)(2,1)S(1)} %get-tuple-element.24), channel_id=1, source_target_pairs={{0,4},{4,0},{8,12},{12,8},{1,5},{5,1},{9,13},{13,9},{2,6},{6,2},{1... | collective-permute-start | bytes 245768 | tf_op jit(solution)/shard_map/ppermute | solution.py:379
  48.1 8.0 %collective-permute-start.14 = (bf16[64,640]{1,0:T(8,128)(2,1)S(1)}, bf16[64,640]{1,0:T(8,128)(2,1)S(1)}, u32[]{:S(2)}, u32[]{:S(2)}) collective-permute-start(bf16[64,640]{1,0:T(8,128)(2,1)S(1)} %get-tuple-element.27), channel_id=1, source_target_pairs={{0,4},{4,0},{8,12},{12,8},{1,5},{5,1},{9,13},{13,9},{2,6},{6,2},{1... | collective-permute-start | bytes 245768 | tf_op jit(solution)/shard_map/ppermute | solution.py:379
  50.2 11.5 %collective-permute-start.11 = (bf16[64,640]{1,0:T(8,128)(2,1)S(1)}, bf16[64,640]{1,0:T(8,128)(2,1)S(1)}, u32[]{:S(2)}, u32[]{:S(2)}) collective-permute-start(bf16[64,640]{1,0:T(8,128)(2,1)S(1)} %add_convert_fusion.2), channel_id=1, source_target_pairs={{0,8},{4,12},{10,2},{14,6},{1,9},{5,13},{11,3},{15,7},{16,24},{20,... | collective-permute-start | bytes 245768 | tf_op jit(solution)/shard_map/ppermute | solution.py:264
  54.8 11.6 %collective-permute-start.5 = (bf16[128,640]{1,0:T(8,128)(2,1)S(1)}, bf16[128,640]{1,0:T(8,128)(2,1)S(1)}, u32[]{:S(2)}, u32[]{:S(2)}) collective-permute-start(bf16[128,640]{1,0:T(8,128)(2,1)S(1)} %add_convert_fusion), channel_id=1, source_target_pairs={{2,10},{6,14},{8,0},{12,4},{3,11},{7,15},{9,1},{13,5},{18,26},{22,... | collective-permute-start | bytes 491528 | tf_op jit(solution)/shard_map/ppermute | solution.py:264
  56.1 7.5 %collective-permute-start.15 = (bf16[64,640]{1,0:T(8,128)(2,1)S(1)}, bf16[64,640]{1,0:T(8,128)(2,1)S(1)}, u32[]{:S(2)}, u32[]{:S(2)}) collective-permute-start(bf16[64,640]{1,0:T(8,128)(2,1)S(1)} %add_convert_fusion.1), channel_id=1, source_target_pairs={{0,8},{4,12},{10,2},{14,6},{1,9},{5,13},{11,3},{15,7},{16,24},{20,... | collective-permute-start | bytes 245768 | tf_op jit(solution)/shard_map/ppermute | solution.py:264
  67.9 3.5 %collective-permute-start.17 = (f32[1,128]{1,0:T(1,128)S(1)}, f32[1,128]{1,0:T(1,128)S(1)}, u32[]{:S(2)}, u32[]{:S(2)}) collective-permute-start(f32[1,128]{1,0:T(1,128)S(1)} %get-tuple-element.29), channel_id=1, source_target_pairs={{0,2},{1,3},{2,0},{3,1},{4,6},{5,7},{6,4},{7,5},{8,10},{9,11},{10,... | collective-permute-start | bytes 1544 | tf_op jit(solution)/shard_map/ppermute | solution.py:428
  67.9 3.5 %collective-permute-start.18 = (f32[1,128]{1,0:T(1,128)S(1)}, f32[1,128]{1,0:T(1,128)S(1)}, u32[]{:S(2)}, u32[]{:S(2)}) collective-permute-start(f32[1,128]{1,0:T(1,128)S(1)} %get-tuple-element.29), channel_id=1, source_target_pairs={{0,3},{1,2},{2,1},{3,0},{4,7},{5,6},{6,5},{7,4},{8,11},{9,10},{10,... | collective-permute-start | bytes 1544 | tf_op jit(solution)/shard_map/ppermute | solution.py:428
  69.3 2.2 %collective-permute-start.16 = (f32[1,128]{1,0:T(1,128)S(1)}, f32[1,128]{1,0:T(1,128)S(1)}, u32[]{:S(2)}, u32[]{:S(2)}) collective-permute-start(f32[1,128]{1,0:T(1,128)S(1)} %get-tuple-element.29), channel_id=1, source_target_pairs={{0,1},{1,0},{2,3},{3,2},{4,5},{5,4},{6,7},{7,6},{8,9},{9,8},{10,11... | collective-permute-start | bytes 1544 | tf_op jit(solution)/shard_map/ppermute | solution.py:428

commit v3 on v2

--- a/solution.py
+++ b/solution.py
@@ -16,7 +16,8 @@
 
 lorentz_width = 0.05
 
-HBM = pl.BlockSpec(memory_space=pl.ANY)
+HBM = pl.BlockSpec(memory_space=pltpu.HBM)
+ANY = pl.BlockSpec(memory_space=pl.ANY)
 VMEM = pl.BlockSpec(memory_space=pltpu.VMEM)
 SMEM = pl.BlockSpec(memory_space=pltpu.SMEM)
 
@@ -100,22 +101,27 @@
     return panel_ref[c, begin:end]
 
 
-def images_of(blocks, base, panel, nbr, coef, count, halos=(), before=None, edges=False, parts=0):
+def images_of(blocks, base, panel, nbr, coef, count, halos=(), before=None, edges=False, halved=False):
     rows, modes = panel.shape[1:]
-    before_blocks = before.shape[1] // (3 * LANES) if parts else 0
-    width = (len(blocks) + before_blocks) * LANES
-    operands = [base, nbr, count, coef, panel, *halos]
-    in_specs = [SMEM] + [HBM] * (len(operands) - 1)
+    width = len(blocks) * LANES
+    operands = [base, *[pltpu.with_memory_space_constraint(x, pltpu.HBM) for x in (nbr, count, coef, panel)], *halos]
+    in_specs = [SMEM] + [HBM] * 4 + [ANY] * len(halos)
+    old = 0
     if before is not None:
         operands.append(before)
-        in_specs.append(VMEM if parts else HBM)
+        in_specs.append(VMEM)
+        old = before.shape[1] // 3
     out_shape = [jax.ShapeDtypeStruct((modes, 3 * width), jnp.bfloat16)]
     out_specs = [VMEM]
     if edges:
         out_shape += [jax.ShapeDtypeStruct((3, HALO, modes), jnp.bfloat16)] * 2
-        out_specs += [HBM] * 2
-    out_shape += [jax.ShapeDtypeStruct((modes // parts, 3 * width), jnp.bfloat16)] * parts if parts > 1 else []
-    out_specs += [VMEM] * parts if parts > 1 else []
+        out_specs += [ANY] * 2
+    if halved:
+        out_shape.append(jax.ShapeDtypeStruct((modes // 2, 3 * width), jnp.bfloat16))
+        out_specs.append(VMEM)
+        if before is not None:
+            out_shape.append(jax.ShapeDtypeStruct((modes // 2, 3 * (old + width)), jnp.bfloat16))
+            out_specs.append(VMEM)
     n_in, n_out = len(operands), len(out_shape)
 
     def kernel(*refs):
@@ -162,15 +168,17 @@
             for r in range(3):
                 image = both[:, 2 * r * LANES : (2 * r + 1) * LANES]
                 image = image + both[:, (2 * r + 1) * LANES : (2 * r + 2) * LANES]
-                at = r * width + (before_blocks + place) * LANES
+                at = r * width + place * LANES
                 outs[0][:, at : at + LANES] = image.astype(jnp.bfloat16)
-        if parts:
-            old = before_blocks * LANES
-            for r in range(3):
-                outs[0][:, r * width : r * width + old] = refs[n_in - 1][:, r * old : (r + 1) * old]
-            for part, out in enumerate(outs[-parts:] if parts > 1 else []):
-                span = modes // parts
-                out[...] = outs[0][part * span : (part + 1) * span, :]
+        if halved:
+            span = modes // 2
+            half_ref = outs[-1] if before is None else outs[-2]
+            half_ref[...] = outs[0][:span, :]
+            if before is not None:
+                for r in range(3):
+                    at = r * (old + width)
+                    outs[-1][:, at : at + old] = refs[n_in - 1][span:, r * old : (r + 1) * old]
+                    outs[-1][:, at + old : at + old + width] = outs[0][span:, r * width : (r + 1) * width]
 
     copies_most = 2 + 2 * len(runs_of(blocks)) + 4
     scratch = [
@@ -183,10 +191,10 @@
         pltpu.VMEM((3 * SPAN, 6 * LANES), jnp.bfloat16),
         pltpu.SemaphoreType.DMA((copies_most,)),
     ]
-    return call(kernel, "images", in_specs, out_specs, out_shape, operands, 1.0 + len(blocks), scratch)
-
-
-def products_of(chunks, place, partners, mine, theirs, rows_from, rows):
+    return call(kernel, "images", in_specs, out_specs, out_shape, operands, 0.8 + 1.2 * len(blocks), scratch)
+
+
+def products_of(chunks, place, partners, mine, theirs, rows_from, rows, after=()):
     cols = partners.shape[2]
     count = len(chunks)
 
@@ -218,10 +226,10 @@
     return call(
         kernel,
         "products",
-        [SMEM] + [VMEM] * (1 + 2 * count),
+        [SMEM] + [VMEM] * (1 + 2 * count) + [ANY] * len(after),
         [VMEM, VMEM],
         [jax.ShapeDtypeStruct((rows, cols), jnp.float32), jax.ShapeDtypeStruct((rows, cols), jnp.bfloat16)],
-        (place, partners, *mine, *theirs),
+        (place, partners, *mine, *theirs, *after),
         2.5,
     )
 
@@ -346,18 +354,22 @@
 
     last = atom_rows // LANES - 1
     middle = list(range(1, last))
-    cut = len(middle) // 2
+    chunks = [middle, [last, 0]]
     shared = (base, mode_panel, nbr, coef, bond_count)
-    first_images, head, tail = images_of(middle[:cut], *shared, edges=True)
+    first_images, head, tail, *first_half = images_of(middle, *shared, edges=True, halved=whole_halves)
     low_halo = lax.ppermute(tail, "atoms", [(z, z + 1) for z in range(atom_count - 1)])
     high_halo = lax.ppermute(head, "atoms", [(z + 1, z) for z in range(atom_count - 1)])
-    (middle_images,) = images_of(middle[cut:], *shared, before=first_images)
-    parts = 2 if whole_halves else 1
-    rest, *pieces = images_of(
-        [last, 0], *shared, halos=(low_halo, high_halo), before=middle_images, parts=parts
+    edge_images, *rest_half = images_of(
+        [last, 0],
+        *shared,
+        halos=(low_halo, high_halo),
+        before=first_images if whole_halves else None,
+        halved=whole_halves,
     )
-    pieces = pieces or [rest]
-    chunks = [middle[:cut], middle[cut:] + [last, 0]]
+    if whole_halves:
+        pieces = [first_half[0], rest_half[0], rest_half[1]]
+    else:
+        pieces = [first_images, edge_images]
 
     swap = [(0, 1), (1, 0)]
 
@@ -367,40 +379,44 @@
     def from_sibling(cells):
         return lax.ppermute(cells, "sub", swap)
 
-    mine = [first_images, rest]
-    theirs = [from_sibling(first_images), from_sibling(rest)]
+    mine = [first_images, edge_images]
+    theirs = [from_sibling(first_images), from_sibling(edge_images)]
     half = half_index.astype(jnp.int32)
     place = jnp.stack([half, (atom_index & 1).astype(jnp.int32)])
     goal = atom_index * groups // atom_count
 
+    far_all = {shift: [from_group(cells, shift) for cells in pieces] for shift in range(1, groups)}
     if whole_halves:
-        def level_zero(chunk_mine, chunk_theirs, rows_from, rows):
-            keep, send = products_of(chunks, place, partners, chunk_mine, chunk_theirs, rows_from, rows)
+        def level_zero(lists, some_mine, some_theirs, after=()):
+            rows = some_mine[0].shape[0]
+            keep, send = products_of(lists, place, partners, some_mine, some_theirs, [0] * len(lists), rows, after)
             got = lax.ppermute(send, "atoms", [(z, z ^ 1) for z in range(atom_count)])
             return [keep, got]
 
-        early = collected(level_zero(mine, theirs, [0, 0], modes), 1, 0)
+        early_zero = level_zero(chunks, mine, theirs, [far[0] for far in far_all.values()])
+        early = collected(early_zero, 1, 0)
     else:
         cells, bit = settle(all_products(chunks, half, partners, mine, theirs).reshape(-1, rows_dev, part_cols), 0, rows_dev)
         early = collected([cells], bit, 0)
 
     late = None
     for shift in range(1, groups):
-        far = [from_group(cells, shift) for cells in [first_images] + pieces]
-        far_sibling = [from_sibling(cells) for cells in far]
-        terms = []
-        for part in range(parts):
-            pick = [far[0], far[1 + part]]
-            pick_sibling = [far_sibling[0], far_sibling[1 + part]]
-            if whole_halves:
-                span = modes // parts
-                found = collected(level_zero(pick, pick_sibling, [part * span, 0], span), 1, shift)
-            else:
-                cells, bit = settle(
-                    all_products(chunks, half, partners, pick, pick_sibling).reshape(-1, rows_dev, part_cols), 0, rows_dev
-                )
-                found = collected([cells], bit, shift)
-            terms.append(found)
+        far = far_all[shift]
+        if whole_halves:
+            first, early[0] = lax.optimization_barrier((far[1], early[0]))
+            far = [far[0], first, far[2]]
+            near = [from_sibling(far[0]), from_sibling(far[1])]
+            found = level_zero(chunks, far[:2], near)
+            second, found[1] = lax.optimization_barrier((far[2], found[1]))
+            terms = [
+                collected(found, 1, shift),
+                collected(level_zero([middle + [last, 0]], [second], [from_sibling(second)]), 1, shift),
+            ]
+        else:
+            cells, bit = settle(
+                all_products(chunks, half, partners, far, [from_sibling(cells) for cells in far]).reshape(-1, rows_dev, part_cols), 0, rows_dev
+            )
+            terms = [collected([cells], bit, shift)]
         if late is None:
             late = terms
         else:

time: 72.5 us -> 71 us (0.979)
  waiting for transfers between devices: 19.4 us -> 13.7 us
  Pallas kernels: 17.3 us -> 19.7 us
  local copies, waits for them, and re-layouts: 6.1 us -> 8.45 us
    ppermute x3, waiting for transfers between devices: 10.7 us -> 1.42 us  [from_group(): return lax.ppermute(cells, 'modes', [(m ^ shift, m) for m in range(groups)])]
    ppermute x3, waiting for transfers between devices: 0.42 us -> 4.14 us  [level_zero(): got = lax.ppermute(send, 'atoms', [(z, z ^ 1) for z in range(atom_count)])]
    ppermute x3, starting transfers between devices: 2.14 us -> 4.91 us  [body(): lax.ppermute(numerator, ('modes', 'sub'), [(i, i ^ code) for i in range(h...]
    ppermute x3, starting transfers between devices: 11.3 us -> 8.51 us  [collected(): terms = terms + [lax.ppermute(sent, ('atoms', 'modes'), moves)]]
    ppermute x3, waiting for transfers between devices: 4.69 us -> 1.96 us  [collected(): terms = terms + [lax.ppermute(sent, ('atoms', 'modes'), moves)]]
    pallas_call x7 -> x6, Pallas kernels: 17.3 us -> 19.7 us  [call(): pl.pallas_call(kernel, in_specs=in_specs, out_specs=out_specs, out_shape=...]
    unnamed x20, local copies, waits for them, and re-layouts: 4.91 us -> 7.26 us
    ppermute x3, waiting for transfers between devices: 1.4 us -> 2.82 us  [body(): lax.ppermute(numerator, ('modes', 'sub'), [(i, i ^ code) for i in range(h...]
  transfers between devices with their start and end apart: 19 -> 19, of which waited for: 8 -> 7; matrix products, arithmetic and copies ran while one was open for 2% -> 2% of each run, Pallas kernels for 13% -> 16%
where the time goes in v3:
time: 71 us; the launch traced here: 70.6 us
  starting transfers between devices  27.1 us (38%)
  Pallas kernels  19.7 us (28%)
  waiting for transfers between devices  13.7 us (19%)
  local copies, waits for them, and re-layouts  8.45 us (12%)
  between operations  0.82 us (1%)
  other arithmetic  0.81 us (1%)
    pallas_call x6, Pallas kernels, call(): pl.pallas_call(kernel, in_specs=in_specs, out_specs=out_specs, out_shape=...  19.7 us
    ppermute x3, starting transfers between devices, collected(): terms = terms + [lax.ppermute(sent, ('atoms', 'modes'), moves)]  8.51 us
    unnamed x20, local copies, waits for them, and re-layouts  7.26 us
    ppermute x1, starting transfers between devices, body(): lax.ppermute(tail, 'atoms', [(z, z + 1) for z in range(atom_count - 1)])  4.93 us
    ppermute x3, starting transfers between devices, body(): lax.ppermute(numerator, ('modes', 'sub'), [(i, i ^ code) for i in range(h...  4.91 us
    ppermute x3, starting transfers between devices, from_group(): return lax.ppermute(cells, 'modes', [(m ^ shift, m) for m in range(groups)])  4.25 us
    ppermute x3, waiting for transfers between devices, level_zero(): got = lax.ppermute(send, 'atoms', [(z, z ^ 1) for z in range(atom_count)])  4.14 us
    ppermute x1, waiting for transfers between devices, body(): lax.ppermute(head, 'atoms', [(z + 1, z) for z in range(atom_count - 1)])  3.3 us
  transfers between devices with their start and end apart: 19, of which 7 were waited for; matrix products, arithmetic and copies ran while one was open for 2% of the time, Pallas kernels for 16%

profile of v3, /device:TPU:0, one launch (start us, length us, event | category | flops | bytes accessed | tf_op | source)
XLA Modules:
  0.0 70.6 jit_solution(2689434727229068951)
XLA Ops:
  0.6 6.8 %images.2 = (bf16[128,1536]{1,0:T(8,128)(2,1)}, bf16[3,96,128]{2,1,0:T(8,128)(2,1)S(1)}, bf16[3,96,128]{2,1,0:T(8,128)(2,1)S(1)}, bf16[64,1536]{1,0:T(8,128)(2,1)}) custom-call(s32[1]{0:T(128)} %bitcast.5.refs_0_, s32[16,768]{1,0:T(8,128)} %bitcast.17, s32[768]{0:T(1024)} %refs_2_.3, f32[9,16,768]{2,1,0:T(8,128)} %bitcast.15, bf16[3,768,128]{2,1,0:T(8,128)(2,1)} %refs_4_.3), custom_call_target="tpu_custom_call" | custom-call | flops 6160000000 | bytes 560000 | tf_op jit(solution)/shard_map/images/pallas_call | solution.py:26
  7.4 4.9 %collective-permute-start = (bf16[3,96,128]{2,1,0:T(8,128)(2,1)S(1)}, bf16[3,96,128]{2,1,0:T(8,128)(2,1)S(1)}, u32[]{:S(2)}, u32[]{:S(2)}) collective-permute-start(bf16[3,96,128]{2,1,0:T(8,128)(2,1)S(1)} %get-tuple-element.21), channel_id=1, source_target_pairs={{0,4},{4,8},{8,12},{1,5},{5,9},{9,13},{2,6},{6,10},{10,14},{3,7},{... | collective-permute-start | bytes 221192 | tf_op jit(solution)/shard_map/ppermute | solution.py:360
  12.3 1.3 %collective-permute-start.1 = (bf16[3,96,128]{2,1,0:T(8,128)(2,1)S(1)}, bf16[3,96,128]{2,1,0:T(8,128)(2,1)S(1)}, u32[]{:S(2)}, u32[]{:S(2)}) collective-permute-start(bf16[3,96,128]{2,1,0:T(8,128)(2,1)S(1)} %get-tuple-element.22), channel_id=1, source_target_pairs={{4,0},{8,4},{12,8},{5,1},{9,5},{13,9},{6,2},{10,6},{14,10},{7,3},{... | collective-permute-start | bytes 221192 | tf_op jit(solution)/shard_map/ppermute | solution.py:361
  13.6 0.1 collective-permute-start.3
  13.7 0.0 copy-start
  13.7 1.6 %collective-permute-start.5 = (bf16[64,1536]{1,0:T(8,128)(2,1)}, bf16[64,1536]{1,0:T(8,128)(2,1)S(1)}, u32[]{:S(2)}, u32[]{:S(2)}) collective-permute-start(bf16[64,1536]{1,0:T(8,128)(2,1)} %get-tuple-element.26), channel_id=1, source_target_pairs={{2,0},{0,2},{3,1},{1,3},{6,4},{4,6},{7,5},{5,7},{10,8},{8,10},{11,... | collective-permute-start | bytes 589832 | tf_op jit(solution)/shard_map/ppermute | solution.py:377
  15.3 0.0 collective-permute-done.refs_5_
  15.3 3.3 %collective-permute-done.1.refs_6_ = bf16[3,96,128]{2,1,0:T(8,128)(2,1)S(1)} collective-permute-done((bf16[3,96,128]{2,1,0:T(8,128)(2,1)S(1)}, bf16[3,96,128]{2,1,0:T(8,128)(2,1)S(1)}, u32[]{:S(2)}, u32[]{:S(2)}) %collective-permute-start.1) | collective-permute-done | bytes 73760 | tf_op jit(solution)/shard_map/ppermute | solution.py:361
  18.6 5.3 %images.3 = (bf16[128,768]{1,0:T(8,128)(2,1)}, bf16[64,768]{1,0:T(8,128)(2,1)S(1)}, bf16[64,2304]{1,0:T(8,128)(2,1)S(1)}) custom-call(s32[1]{0:T(128)} %bitcast.5.refs_0_, s32[16,768]{1,0:T(8,128)} %bitcast.18, s32[768]{0:T(1024)} %refs_2_.3, f32[9,16,768]{2,1,0:T(8,128)} %bitcast.16, bf16[3,768,128]{2,1,0:T(8,128)(2,1)} %refs_4_.3, ...), custom_call_target="tpu_custom_call" | custom-call | flops 3520000000 | bytes 320000 | tf_op jit(solution)/shard_map/images/pallas_call | solution.py:26
  23.9 0.0 copy-start.3
  23.9 0.7 copy-done.3
  24.6 0.6 copy-done.7
  25.2 0.1 pad_add_fusion.1.place_ref
  25.3 1.5 %collective-permute-start.2 = (bf16[64,768]{1,0:T(8,128)(2,1)}, bf16[64,768]{1,0:T(8,128)(2,1)}, u32[]{:S(2)}, u32[]{:S(2)}) collective-permute-start(bf16[64,768]{1,0:T(8,128)(2,1)} %copy-done.7), channel_id=1, source_target_pairs={{2,0},{0,2},{3,1},{1,3},{6,4},{4,6},{7,5},{5,7},{10,8},{8,10},{11,... | collective-permute-start | bytes 294920 | tf_op jit(solution)/shard_map/ppermute | solution.py:377
  26.8 0.2 collective-permute-start.8
  27.0 0.7 copy-done.4
  27.7 0.9 %copy-done.5 = bf16[128,768]{1,0:T(8,128)(2,1)S(1)} copy-done((bf16[128,768]{1,0:T(8,128)(2,1)S(1)}, bf16[128,768]{1,0:T(8,128)(2,1)}, u32[]{:S(2)}) %copy-start.5) | copy-done | bytes 196632
  28.6 2.5 %products.3 = (f32[128,640]{1,0:T(8,128)S(1)}, bf16[128,640]{1,0:T(8,128)(2,1)S(1)}) custom-call(s32[2]{0:T(128)S(1)} %pad_add_fusion.1.place_ref, bf16[3,768,640]{2,1,0:T(8,128)(2,1)S(1)} %copy-done, bf16[128,1536]{1,0:T(8,128)(2,1)} %get-tuple-element.23.refs_7_.refs_0_, bf16[128,768]{1,0:T(8,128)(2,1)} %get-tuple-element.25.refs_1_, ...), custom_call_target="tpu_custom_call" | custom-call | flops 2750000128 | bytes 250000 | tf_op jit(solution)/shard_map/products/pallas_call | solution.py:26
  31.1 0.6 copy-done.6
  31.8 0.3 collective-permute-start.9
  32.1 1.2 %collective-permute-start.10 = (bf16[64,2304]{1,0:T(8,128)(2,1)}, bf16[64,2304]{1,0:T(8,128)(2,1)S(1)}, u32[]{:S(2)}, u32[]{:S(2)}) collective-permute-start(bf16[64,2304]{1,0:T(8,128)(2,1)} %copy-done.3), channel_id=1, source_target_pairs={{2,0},{0,2},{3,1},{1,3},{6,4},{4,6},{7,5},{5,7},{10,8},{8,10},{11,... | collective-permute-start | bytes 884744 | tf_op jit(solution)/shard_map/ppermute | solution.py:377
  33.3 1.6 %collective-permute-start.6 = (bf16[128,640]{1,0:T(8,128)(2,1)}, bf16[128,640]{1,0:T(8,128)(2,1)S(1)}, u32[]{:S(2)}, u32[]{:S(2)}) collective-permute-start(bf16[128,640]{1,0:T(8,128)(2,1)} %copy-done.6), channel_id=1, source_target_pairs={{0,4},{4,0},{8,12},{12,8},{1,5},{5,1},{9,13},{13,9},{2,6},{6,2},{1... | collective-permute-start | bytes 491528 | tf_op jit(solution)/shard_map/ppermute | solution.py:393
  34.9 1.8 %copy-done.1 = bf16[3,768,640]{2,1,0:T(8,128)(2,1)S(1)} copy-done((bf16[3,768,640]{2,1,0:T(8,128)(2,1)S(1)}, bf16[3,768,640]{2,1,0:T(8,128)(2,1)}, u32[]{:S(2)}) %copy-start.1) | copy-done | bytes 2949144
  36.7 2.0 %products.4 = (f32[64,640]{1,0:T(8,128)S(1)}, bf16[64,640]{1,0:T(8,128)(2,1)S(1)}) custom-call(s32[2]{0:T(128)S(1)} %pad_add_fusion.1.place_ref, bf16[3,768,640]{2,1,0:T(8,128)(2,1)S(1)} %copy-done.1, bf16[64,1536]{1,0:T(8,128)(2,1)S(1)} %collective-permute-done.5.refs_4_.refs_0_, bf16[64,768]{1,0:T(8,128)(2,1)} %collective-permute-done.2.refs_1_, ...), custom_call_target="tpu_custom_call" | custom-call | flops 2750000128 | bytes 250000 | tf_op jit(solution)/shard_map/products/pallas_call | solution.py:26
  38.7 0.5 collective-permute-start.11
  39.2 0.8 %dynamic-slice_bitcast_fusion = (s32[128,1]{0,1:T(1,128)S(1)}, s32[128,1]{0,1:T(1,128)S(1)}) fusion(s32[512]{0:T(512)} %param.17, s32[]{:T(128)S(6)} %select_n.11, s32[512]{0:T(512)} %param.16), kind=kLoop, calls=%fused_computation.6 | loop fusion | bytes 2052 | tf_op jit(solution)/shard_map/broadcast_in_dim | solution.py:436
  40.0 1.4 %collective-permute-done.10.refs_0_ = bf16[64,2304]{1,0:T(8,128)(2,1)S(1)} collective-permute-done((bf16[64,2304]{1,0:T(8,128)(2,1)}, bf16[64,2304]{1,0:T(8,128)(2,1)S(1)}, u32[]{:S(2)}, u32[]{:S(2)}) %collective-permute-start.10) | collective-permute-done | bytes 294944 | tf_op jit(solution)/shard_map/ppermute | solution.py:377
  41.4 1.8 %collective-permute-done.11.refs_4_ = bf16[64,640]{1,0:T(8,128)(2,1)S(1)} collective-permute-done((bf16[64,640]{1,0:T(8,128)(2,1)S(1)}, bf16[64,640]{1,0:T(8,128)(2,1)S(1)}, u32[]{:S(2)}, u32[]{:S(2)}) %collective-permute-start.11) | collective-permute-done | bytes 81952 | tf_op jit(solution)/shard_map/ppermute | solution.py:393
  43.2 0.1 dynamic-slice_bitcast_fusion.2
  43.3 0.1 copy.11.start_ref
  43.4 0.1 copy.12.length_ref
  43.5 0.1 copy.13.freq_ref
  43.7 1.3 %collective-permute-start.7 = (bf16[128,640]{1,0:T(8,128)(2,1)S(1)}, bf16[128,640]{1,0:T(8,128)(2,1)S(1)}, u32[]{:S(2)}, u32[]{:S(2)}) collective-permute-start(bf16[128,640]{1,0:T(8,128)(2,1)S(1)} %add_convert_fusion), channel_id=1, source_target_pairs={{2,10},{6,14},{8,0},{12,4},{3,11},{7,15},{9,1},{13,5},{18,26},{22,... | collective-permute-start | bytes 491528 | tf_op jit(solution)/shard_map/ppermute | solution.py:272
  45.0 0.0 copy-start.2
  45.0 1.8 %copy-done.2 = bf16[3,768,640]{2,1,0:T(8,128)(2,1)S(1)} copy-done((bf16[3,768,640]{2,1,0:T(8,128)(2,1)S(1)}, bf16[3,768,640]{2,1,0:T(8,128)(2,1)}, u32[]{:S(2)}) %copy-start.2) | copy-done | bytes 2949144
  46.9 1.7 %products.5 = (f32[64,640]{1,0:T(8,128)S(1)}, bf16[64,640]{1,0:T(8,128)(2,1)S(1)}) custom-call(s32[2]{0:T(128)S(1)} %pad_add_fusion.1.place_ref, bf16[3,768,640]{2,1,0:T(8,128)(2,1)S(1)} %copy-done.2, bf16[64,2304]{1,0:T(8,128)(2,1)S(1)} %collective-permute-done.10.refs_0_, bf16[64,2304]{1,0:T(8,128)(2,1)S(1)} %collective-permute-done.13.refs_1_), custom_call_target="tpu_custom_call" | custom-call | flops 2750000128 | bytes 250000 | tf_op jit(solution)/shard_map/products/pallas_call | solution.py:26
  48.5 0.5 collective-permute-start.14
  49.1 5.5 %collective-permute-start.12 = (bf16[64,640]{1,0:T(8,128)(2,1)S(1)}, bf16[64,640]{1,0:T(8,128)(2,1)S(1)}, u32[]{:S(2)}, u32[]{:S(2)}) collective-permute-start(bf16[64,640]{1,0:T(8,128)(2,1)S(1)} %add_convert_fusion.2), channel_id=1, source_target_pairs={{0,8},{4,12},{10,2},{14,6},{1,9},{5,13},{11,3},{15,7},{16,24},{20,... | collective-permute-start | bytes 245768 | tf_op jit(solution)/shard_map/ppermute | solution.py:272
  54.5 2.3 %collective-permute-done.14.refs_7_ = bf16[64,640]{1,0:T(8,128)(2,1)S(1)} collective-permute-done((bf16[64,640]{1,0:T(8,128)(2,1)S(1)}, bf16[64,640]{1,0:T(8,128)(2,1)S(1)}, u32[]{:S(2)}, u32[]{:S(2)}) %collective-permute-start.14) | collective-permute-done | bytes 81952 | tf_op jit(solution)/shard_map/ppermute | solution.py:393
  56.9 1.8 %collective-permute-start.15 = (bf16[64,640]{1,0:T(8,128)(2,1)S(1)}, bf16[64,640]{1,0:T(8,128)(2,1)S(1)}, u32[]{:S(2)}, u32[]{:S(2)}) collective-permute-start(bf16[64,640]{1,0:T(8,128)(2,1)S(1)} %add_convert_fusion.1), channel_id=1, source_target_pairs={{0,8},{4,12},{10,2},{14,6},{1,9},{5,13},{11,3},{15,7},{16,24},{20,... | collective-permute-start | bytes 245768 | tf_op jit(solution)/shard_map/ppermute | solution.py:272
  58.7 0.1 pad_add_fusion.flag_ref
  58.7 2.0 %collective-permute-done.15.refs_8_ = bf16[64,640]{1,0:T(8,128)(2,1)S(1)} collective-permute-done((bf16[64,640]{1,0:T(8,128)(2,1)S(1)}, bf16[64,640]{1,0:T(8,128)(2,1)S(1)}, u32[]{:S(2)}, u32[]{:S(2)}) %collective-permute-start.15) | collective-permute-done | bytes 81952 | tf_op jit(solution)/shard_map/ppermute | solution.py:272
  60.7 1.5 %finish.1 = (f32[128,640]{1,0:T(8,128)}, f32[1,128]{1,0:T(1,128)S(1)}) custom-call(s32[2]{0:T(128)S(1)} %pad_add_fusion.flag_ref, s32[128,1]{1,0:T(8,128)S(1)} %copy.11.start_ref, s32[128,1]{1,0:T(8,128)S(1)} %copy.12.length_ref, f32[128,1]{1,0:T(8,128)S(1)} %copy.13.freq_ref, f32[1,640]{1,0:T(1,128)S(1)} %broadcast_in_dim.18.partner_ref, ...), custom_call_target="tpu_custom_call" | custom-call | flops 2200000000 | bytes 200000 | tf_op jit(solution)/shard_map/finish/pallas_call | solution.py:26
  62.2 4.8 %collective-permute-start.17 = (f32[1,128]{1,0:T(1,128)S(1)}, f32[1,128]{1,0:T(1,128)S(1)}, u32[]{:S(2)}, u32[]{:S(2)}) collective-permute-start(f32[1,128]{1,0:T(1,128)S(1)} %get-tuple-element.39), channel_id=1, source_target_pairs={{0,2},{1,3},{2,0},{3,1},{4,6},{5,7},{6,4},{7,5},{8,10},{9,11},{10,... | collective-permute-start | bytes 1544 | tf_op jit(solution)/shard_map/ppermute | solution.py:444
  67.0 0.1 collective-permute-start.18
  67.1 1.4 %collective-permute-done.17 = f32[1,128]{1,0:T(1,128)S(1)} collective-permute-done((f32[1,128]{1,0:T(1,128)S(1)}, f32[1,128]{1,0:T(1,128)S(1)}, u32[]{:S(2)}, u32[]{:S(2)}) %collective-permute-start.17) | collective-permute-done | bytes 544 | tf_op jit(solution)/shard_map/ppermute | solution.py:444
  68.5 1.4 %collective-permute-done.18 = f32[1,128]{1,0:T(1,128)S(1)} collective-permute-done((f32[1,128]{1,0:T(1,128)S(1)}, f32[1,128]{1,0:T(1,128)S(1)}, u32[]{:S(2)}, u32[]{:S(2)}) %collective-permute-start.18) | collective-permute-done | bytes 544 | tf_op jit(solution)/shard_map/ppermute | solution.py:444
  70.0 0.6 bitcast_divide_fusion
  (28 shorter events, 0.1 us)
Async XLA Ops:
  7.4 7.9 %collective-permute-start = (bf16[3,96,128]{2,1,0:T(8,128)(2,1)S(1)}, bf16[3,96,128]{2,1,0:T(8,128)(2,1)S(1)}, u32[]{:S(2)}, u32[]{:S(2)}) collective-permute-start(bf16[3,96,128]{2,1,0:T(8,128)(2,1)S(1)} %get-tuple-element.21), channel_id=1, source_target_pairs={{0,4},{4,8},{8,12},{1,5},{5,9},{9,13},{2,6},{6,10},{10,14},{3,7},{... | collective-permute-start | bytes 221192 | tf_op jit(solution)/shard_map/ppermute | solution.py:360
  12.3 6.2 %collective-permute-start.1 = (bf16[3,96,128]{2,1,0:T(8,128)(2,1)S(1)}, bf16[3,96,128]{2,1,0:T(8,128)(2,1)S(1)}, u32[]{:S(2)}, u32[]{:S(2)}) collective-permute-start(bf16[3,96,128]{2,1,0:T(8,128)(2,1)S(1)} %get-tuple-element.22), channel_id=1, source_target_pairs={{4,0},{8,4},{12,8},{5,1},{9,5},{13,9},{6,2},{10,6},{14,10},{7,3},{... | collective-permute-start | bytes 221192 | tf_op jit(solution)/shard_map/ppermute | solution.py:361
  13.6 14.0 %collective-permute-start.3 = (bf16[128,1536]{1,0:T(8,128)(2,1)}, bf16[128,1536]{1,0:T(8,128)(2,1)}, u32[]{:S(2)}, u32[]{:S(2)}) collective-permute-start(bf16[128,1536]{1,0:T(8,128)(2,1)} %get-tuple-element.23.refs_7_.refs_0_), channel_id=1, source_target_pairs={{0,1},{1,0},{2,3},{3,2},{4,5},{5,4},{6,7},{7,6},{8,9},{9,8},{10,11... | collective-permute-start | bytes 1179656 | tf_op jit(solution)/shard_map/ppermute | solution.py:380
  13.7 14.0 %copy-start = (bf16[3,768,640]{2,1,0:T(8,128)(2,1)S(1)}, bf16[3,768,640]{2,1,0:T(8,128)(2,1)}, u32[]{:S(2)}) copy-start(bf16[3,768,640]{2,1,0:T(8,128)(2,1)} %partners_ref.5) | copy-start | bytes 8847364
  13.7 13.0 %collective-permute-start.5 = (bf16[64,1536]{1,0:T(8,128)(2,1)}, bf16[64,1536]{1,0:T(8,128)(2,1)S(1)}, u32[]{:S(2)}, u32[]{:S(2)}) collective-permute-start(bf16[64,1536]{1,0:T(8,128)(2,1)} %get-tuple-element.26), channel_id=1, source_target_pairs={{2,0},{0,2},{3,1},{1,3},{6,4},{4,6},{7,5},{5,7},{10,8},{8,10},{11,... | collective-permute-start | bytes 589832 | tf_op jit(solution)/shard_map/ppermute | solution.py:377
  23.9 0.7 %copy-start.3 = (bf16[64,2304]{1,0:T(8,128)(2,1)}, bf16[64,2304]{1,0:T(8,128)(2,1)S(1)}, u32[]{:S(2)}) copy-start(bf16[64,2304]{1,0:T(8,128)(2,1)S(1)} %get-tuple-element.32) | copy-start | bytes 884740
  24.6 0.6 copy-start.7
  25.2 1.8 %collective-permute-start.4 = (bf16[128,768]{1,0:T(8,128)(2,1)}, bf16[128,768]{1,0:T(8,128)(2,1)S(1)}, u32[]{:S(2)}, u32[]{:S(2)}) collective-permute-start(bf16[128,768]{1,0:T(8,128)(2,1)} %get-tuple-element.25.refs_1_), channel_id=1, source_target_pairs={{0,1},{1,0},{2,3},{3,2},{4,5},{5,4},{6,7},{7,6},{8,9},{9,8},{10,11... | collective-permute-start | bytes 589832 | tf_op jit(solution)/shard_map/ppermute | solution.py:380
  25.3 6.5 %collective-permute-start.2 = (bf16[64,768]{1,0:T(8,128)(2,1)}, bf16[64,768]{1,0:T(8,128)(2,1)}, u32[]{:S(2)}, u32[]{:S(2)}) collective-permute-start(bf16[64,768]{1,0:T(8,128)(2,1)} %copy-done.7), channel_id=1, source_target_pairs={{2,0},{0,2},{3,1},{1,3},{6,4},{4,6},{7,5},{5,7},{10,8},{8,10},{11,... | collective-permute-start | bytes 294920 | tf_op jit(solution)/shard_map/ppermute | solution.py:377
  26.8 8.1 %collective-permute-start.8 = (bf16[64,1536]{1,0:T(8,128)(2,1)S(1)}, bf16[64,1536]{1,0:T(8,128)(2,1)}, u32[]{:S(2)}, u32[]{:S(2)}) collective-permute-start(bf16[64,1536]{1,0:T(8,128)(2,1)S(1)} %collective-permute-done.5.refs_4_.refs_0_), channel_id=1, source_target_pairs={{0,1},{1,0},{2,3},{3,2},{4,5},{5,4},{6,7},{7,6},{8,9},{9,8},{10,11... | collective-permute-start | bytes 589832 | tf_op jit(solution)/shard_map/ppermute | solution.py:380
  27.0 0.7 copy-start.4
  27.7 0.9 %copy-start.5 = (bf16[128,768]{1,0:T(8,128)(2,1)S(1)}, bf16[128,768]{1,0:T(8,128)(2,1)}, u32[]{:S(2)}) copy-start(bf16[128,768]{1,0:T(8,128)(2,1)} %copy-done.4) | copy-start | bytes 589828
  31.1 0.7 copy-start.6
  31.8 3.1 %collective-permute-start.9 = (bf16[64,768]{1,0:T(8,128)(2,1)}, bf16[64,768]{1,0:T(8,128)(2,1)S(1)}, u32[]{:S(2)}, u32[]{:S(2)}) collective-permute-start(bf16[64,768]{1,0:T(8,128)(2,1)} %collective-permute-done.2.refs_1_), channel_id=1, source_target_pairs={{0,1},{1,0},{2,3},{3,2},{4,5},{5,4},{6,7},{7,6},{8,9},{9,8},{10,11... | collective-permute-start | bytes 294920 | tf_op jit(solution)/shard_map/ppermute | solution.py:380
  32.1 9.4 %collective-permute-start.10 = (bf16[64,2304]{1,0:T(8,128)(2,1)}, bf16[64,2304]{1,0:T(8,128)(2,1)S(1)}, u32[]{:S(2)}, u32[]{:S(2)}) collective-permute-start(bf16[64,2304]{1,0:T(8,128)(2,1)} %copy-done.3), channel_id=1, source_target_pairs={{2,0},{0,2},{3,1},{1,3},{6,4},{4,6},{7,5},{5,7},{10,8},{8,10},{11,... | collective-permute-start | bytes 884744 | tf_op jit(solution)/shard_map/ppermute | solution.py:377
  33.3 10.4 %collective-permute-start.6 = (bf16[128,640]{1,0:T(8,128)(2,1)}, bf16[128,640]{1,0:T(8,128)(2,1)S(1)}, u32[]{:S(2)}, u32[]{:S(2)}) collective-permute-start(bf16[128,640]{1,0:T(8,128)(2,1)} %copy-done.6), channel_id=1, source_target_pairs={{0,4},{4,0},{8,12},{12,8},{1,5},{5,1},{9,13},{13,9},{2,6},{6,2},{1... | collective-permute-start | bytes 491528 | tf_op jit(solution)/shard_map/ppermute | solution.py:393
  34.9 1.8 %copy-start.1 = (bf16[3,768,640]{2,1,0:T(8,128)(2,1)S(1)}, bf16[3,768,640]{2,1,0:T(8,128)(2,1)}, u32[]{:S(2)}) copy-start(bf16[3,768,640]{2,1,0:T(8,128)(2,1)} %partners_ref.5) | copy-start | bytes 8847364
  36.7 6.5 %copy-start.9 = (f32[512]{0:T(512)S(1)}, f32[512]{0:T(512)}, u32[]{:S(2)}) copy-start(f32[512]{0:T(512)} %param.14) | copy-start | bytes 6148
  36.7 6.9 %copy-start.8 = (f32[640]{0:T(1024)S(1)}, f32[640]{0:T(1024)}, u32[]{:S(2)}) copy-start(f32[640]{0:T(1024)} %param.15) | copy-start | bytes 7684
  38.7 4.5 %collective-permute-start.11 = (bf16[64,640]{1,0:T(8,128)(2,1)S(1)}, bf16[64,640]{1,0:T(8,128)(2,1)S(1)}, u32[]{:S(2)}, u32[]{:S(2)}) collective-permute-start(bf16[64,640]{1,0:T(8,128)(2,1)S(1)} %get-tuple-element.33), channel_id=1, source_target_pairs={{0,4},{4,0},{8,12},{12,8},{1,5},{5,1},{9,13},{13,9},{2,6},{6,2},{1... | collective-permute-start | bytes 245768 | tf_op jit(solution)/shard_map/ppermute | solution.py:393
  43.2 1.8 %collective-permute-start.13 = (bf16[64,2304]{1,0:T(8,128)(2,1)S(1)}, bf16[64,2304]{1,0:T(8,128)(2,1)S(1)}, u32[]{:S(2)}, u32[]{:S(2)}) collective-permute-start(bf16[64,2304]{1,0:T(8,128)(2,1)S(1)} %collective-permute-done.10.refs_0_), channel_id=1, source_target_pairs={{0,1},{1,0},{2,3},{3,2},{4,5},{5,4},{6,7},{7,6},{8,9},{9,8},{10,11... | collective-permute-start | bytes 884744 | tf_op jit(solution)/shard_map/ppermute | solution.py:380
  43.7 15.0 %collective-permute-start.7 = (bf16[128,640]{1,0:T(8,128)(2,1)S(1)}, bf16[128,640]{1,0:T(8,128)(2,1)S(1)}, u32[]{:S(2)}, u32[]{:S(2)}) collective-permute-start(bf16[128,640]{1,0:T(8,128)(2,1)S(1)} %add_convert_fusion), channel_id=1, source_target_pairs={{2,10},{6,14},{8,0},{12,4},{3,11},{7,15},{9,1},{13,5},{18,26},{22,... | collective-permute-start | bytes 491528 | tf_op jit(solution)/shard_map/ppermute | solution.py:272
  45.0 1.8 %copy-start.2 = (bf16[3,768,640]{2,1,0:T(8,128)(2,1)S(1)}, bf16[3,768,640]{2,1,0:T(8,128)(2,1)}, u32[]{:S(2)}) copy-start(bf16[3,768,640]{2,1,0:T(8,128)(2,1)} %partners_ref.5) | copy-start | bytes 8847364
  48.5 8.3 %collective-permute-start.14 = (bf16[64,640]{1,0:T(8,128)(2,1)S(1)}, bf16[64,640]{1,0:T(8,128)(2,1)S(1)}, u32[]{:S(2)}, u32[]{:S(2)}) collective-permute-start(bf16[64,640]{1,0:T(8,128)(2,1)S(1)} %get-tuple-element.37), channel_id=1, source_target_pairs={{0,4},{4,0},{8,12},{12,8},{1,5},{5,1},{9,13},{13,9},{2,6},{6,2},{1... | collective-permute-start | bytes 245768 | tf_op jit(solution)/shard_map/ppermute | solution.py:393
  49.1 9.7 %collective-permute-start.12 = (bf16[64,640]{1,0:T(8,128)(2,1)S(1)}, bf16[64,640]{1,0:T(8,128)(2,1)S(1)}, u32[]{:S(2)}, u32[]{:S(2)}) collective-permute-start(bf16[64,640]{1,0:T(8,128)(2,1)S(1)} %add_convert_fusion.2), channel_id=1, source_target_pairs={{0,8},{4,12},{10,2},{14,6},{1,9},{5,13},{11,3},{15,7},{16,24},{20,... | collective-permute-start | bytes 245768 | tf_op jit(solution)/shard_map/ppermute | solution.py:272
  56.9 3.8 %collective-permute-start.15 = (bf16[64,640]{1,0:T(8,128)(2,1)S(1)}, bf16[64,640]{1,0:T(8,128)(2,1)S(1)}, u32[]{:S(2)}, u32[]{:S(2)}) collective-permute-start(bf16[64,640]{1,0:T(8,128)(2,1)S(1)} %add_convert_fusion.1), channel_id=1, source_target_pairs={{0,8},{4,12},{10,2},{14,6},{1,9},{5,13},{11,3},{15,7},{16,24},{20,... | collective-permute-start | bytes 245768 | tf_op jit(solution)/shard_map/ppermute | solution.py:272
  62.2 4.9 %collective-permute-start.16 = (f32[1,128]{1,0:T(1,128)S(1)}, f32[1,128]{1,0:T(1,128)S(1)}, u32[]{:S(2)}, u32[]{:S(2)}) collective-permute-start(f32[1,128]{1,0:T(1,128)S(1)} %get-tuple-element.39), channel_id=1, source_target_pairs={{0,1},{1,0},{2,3},{3,2},{4,5},{5,4},{6,7},{7,6},{8,9},{9,8},{10,11... | collective-permute-start | bytes 1544 | tf_op jit(solution)/shard_map/ppermute | solution.py:444
  62.2 6.3 %collective-permute-start.17 = (f32[1,128]{1,0:T(1,128)S(1)}, f32[1,128]{1,0:T(1,128)S(1)}, u32[]{:S(2)}, u32[]{:S(2)}) collective-permute-start(f32[1,128]{1,0:T(1,128)S(1)} %get-tuple-element.39), channel_id=1, source_target_pairs={{0,2},{1,3},{2,0},{3,1},{4,6},{5,7},{6,4},{7,5},{8,10},{9,11},{10,... | collective-permute-start | bytes 1544 | tf_op jit(solution)/shard_map/ppermute | solution.py:444
  67.0 3.0 %collective-permute-start.18 = (f32[1,128]{1,0:T(1,128)S(1)}, f32[1,128]{1,0:T(1,128)S(1)}, u32[]{:S(2)}, u32[]{:S(2)}) collective-permute-start(f32[1,128]{1,0:T(1,128)S(1)} %get-tuple-element.39), channel_id=1, source_target_pairs={{0,3},{1,2},{2,1},{3,0},{4,7},{5,6},{6,5},{7,4},{8,11},{9,10},{10,... | collective-permute-start | bytes 1544 | tf_op jit(solution)/shard_map/ppermute | solution.py:444

commit v4 on v3

--- a/solution.py
+++ b/solution.py
@@ -12,9 +12,12 @@
 LANES = 128
 SPAN = LANES + 2 * HALO
 GROUP = 16
-VMEM_BYTES = 40 * 1024 * 1024
+VMEM_BYTES = 14 * 1024 * 1024
 
 lorentz_width = 0.05
+
+EARLY_US = 6.0
+LATE_US = 0.1
 
 HBM = pl.BlockSpec(memory_space=pltpu.HBM)
 ANY = pl.BlockSpec(memory_space=pl.ANY)
@@ -101,9 +104,8 @@
     return panel_ref[c, begin:end]
 
 
-def images_of(blocks, base, panel, nbr, coef, count, halos=(), before=None, edges=False, halved=False):
+def images_of(blocks, base, panel, nbr, coef, count, halos=(), before=None, joined=False, edges=False, halved=False):
     rows, modes = panel.shape[1:]
-    width = len(blocks) * LANES
     operands = [base, *[pltpu.with_memory_space_constraint(x, pltpu.HBM) for x in (nbr, count, coef, panel)], *halos]
     in_specs = [SMEM] + [HBM] * 4 + [ANY] * len(halos)
     old = 0
@@ -111,6 +113,9 @@
         operands.append(before)
         in_specs.append(VMEM)
         old = before.shape[1] // 3
+    ahead = old if joined else 0
+    width = ahead + len(blocks) * LANES
+    tail = halved and before is not None and not joined
     out_shape = [jax.ShapeDtypeStruct((modes, 3 * width), jnp.bfloat16)]
     out_specs = [VMEM]
     if edges:
@@ -119,7 +124,7 @@
     if halved:
         out_shape.append(jax.ShapeDtypeStruct((modes // 2, 3 * width), jnp.bfloat16))
         out_specs.append(VMEM)
-        if before is not None:
+        if tail:
             out_shape.append(jax.ShapeDtypeStruct((modes // 2, 3 * (old + width)), jnp.bfloat16))
             out_specs.append(VMEM)
     n_in, n_out = len(operands), len(out_shape)
@@ -168,13 +173,16 @@
             for r in range(3):
                 image = both[:, 2 * r * LANES : (2 * r + 1) * LANES]
                 image = image + both[:, (2 * r + 1) * LANES : (2 * r + 2) * LANES]
-                at = r * width + place * LANES
+                at = r * width + ahead + place * LANES
                 outs[0][:, at : at + LANES] = image.astype(jnp.bfloat16)
+        if joined:
+            for r in range(3):
+                outs[0][:, r * width : r * width + old] = refs[n_in - 1][:, r * old : (r + 1) * old]
         if halved:
             span = modes // 2
-            half_ref = outs[-1] if before is None else outs[-2]
+            half_ref = outs[-2] if tail else outs[-1]
             half_ref[...] = outs[0][:span, :]
-            if before is not None:
+            if tail:
                 for r in range(3):
                     at = r * (old + width)
                     outs[-1][:, at : at + old] = refs[n_in - 1][span:, r * old : (r + 1) * old]
@@ -194,34 +202,28 @@
     return call(kernel, "images", in_specs, out_specs, out_shape, operands, 0.8 + 1.2 * len(blocks), scratch)
 
 
-def products_of(chunks, place, partners, mine, theirs, rows_from, rows, after=()):
-    cols = partners.shape[2]
+def products_of(chunks, place, partners, mine, theirs, after=(), busy_us=2.0):
+    rows, cols = mine[0].shape[0], partners.shape[2]
     count = len(chunks)
+    depth = partners.shape[1]
 
     def kernel(place_ref, partners_ref, *refs):
-        keep_ref, send_ref = refs[-2:]
-
-        def half(who):
-            total = None
+        keep_ref, send_ref, left_ref = refs[-3:]
+        kept = place_ref[0] == place_ref[1]
+        for who in range(2):
+            at_rows = pl.ds(pl.multiple_of(jnp.where(kept == (who == 0), 0, rows), rows), rows)
             for i, blocks in enumerate(chunks):
                 image_ref = refs[who * count + i]
-                at_rows = slice(rows_from[i], rows_from[i] + rows)
                 width = len(blocks) * LANES
                 for r in range(3):
                     for spot, block, length in runs_of(blocks):
-                        at = r * width + spot * LANES
-                        part = jnp.dot(
-                            image_ref[at_rows, at : at + length * LANES],
-                            partners_ref[r, block * LANES : (block + length) * LANES, :],
-                            preferred_element_type=jnp.float32,
-                        )
-                        total = part if total is None else total + part
-            return total
-
-        first, second = half(0), half(1)
-        kept = place_ref[0] == place_ref[1]
-        keep_ref[...] = jnp.where(kept, first, second)
-        send_ref[...] = jnp.where(kept, second, first).astype(jnp.bfloat16)
+                        at, to = r * width + spot * LANES, r * depth + block * LANES
+                        left_ref[at_rows, to : to + length * LANES] = image_ref[:, at : at + length * LANES]
+        total = jnp.dot(
+            left_ref[...], partners_ref[...].reshape(3 * depth, cols), preferred_element_type=jnp.float32
+        )
+        keep_ref[...] = total[:rows]
+        send_ref[...] = total[rows:].astype(jnp.bfloat16)
 
     return call(
         kernel,
@@ -230,15 +232,15 @@
         [VMEM, VMEM],
         [jax.ShapeDtypeStruct((rows, cols), jnp.float32), jax.ShapeDtypeStruct((rows, cols), jnp.bfloat16)],
         (place, partners, *mine, *theirs, *after),
-        2.5,
+        busy_us,
+        [pltpu.VMEM((2 * rows, 3 * depth), jnp.bfloat16)],
     )
 
 
 def all_products(chunks, half, partners, mine, theirs):
-    modes, cols = mine[0].shape[0], partners.shape[2]
     place = jnp.stack([half, jnp.zeros((), jnp.int32)])
-    low = products_of(chunks, place, partners, mine, theirs, [0] * len(chunks), modes)[0]
-    high = products_of(chunks, place + jnp.array([0, 1], jnp.int32), partners, mine, theirs, [0] * len(chunks), modes)[0]
+    low = products_of(chunks, place, partners, mine, theirs)[0]
+    high = products_of(chunks, place + jnp.array([0, 1], jnp.int32), partners, mine, theirs)[0]
     return jnp.stack([low, high])
 
 
@@ -356,9 +358,11 @@
     middle = list(range(1, last))
     chunks = [middle, [last, 0]]
     shared = (base, mode_panel, nbr, coef, bond_count)
-    first_images, head, tail, *first_half = images_of(middle, *shared, edges=True, halved=whole_halves)
+    cut = len(middle) // 2
+    opening, head, tail = images_of(middle[:cut], *shared, edges=True)
     low_halo = lax.ppermute(tail, "atoms", [(z, z + 1) for z in range(atom_count - 1)])
     high_halo = lax.ppermute(head, "atoms", [(z + 1, z) for z in range(atom_count - 1)])
+    first_images, *first_half = images_of(middle[cut:], *shared, before=opening, joined=True, halved=whole_halves)
     edge_images, *rest_half = images_of(
         [last, 0],
         *shared,
@@ -388,8 +392,9 @@
     far_all = {shift: [from_group(cells, shift) for cells in pieces] for shift in range(1, groups)}
     if whole_halves:
         def level_zero(lists, some_mine, some_theirs, after=()):
-            rows = some_mine[0].shape[0]
-            keep, send = products_of(lists, place, partners, some_mine, some_theirs, [0] * len(lists), rows, after)
+            keep, send = products_of(
+                lists, place, partners, some_mine, some_theirs, after, EARLY_US if after else LATE_US
+            )
             got = lax.ppermute(send, "atoms", [(z, z ^ 1) for z in range(atom_count)])
             return [keep, got]
 

time: 71 us -> 67.6 us (0.952)
  waiting for transfers between devices: 13.7 us -> 7.7 us
  starting transfers between devices: 27.1 us -> 31.5 us
  local copies, waits for them, and re-layouts: 8.45 us -> 4.41 us
  Pallas kernels: 19.7 us -> 21 us
  other arithmetic: 0.81 us -> 1.77 us
    unnamed x20 -> x18, local copies, waits for them, and re-layouts: 7.26 us -> 1.35 us
    ppermute x3, starting transfers between devices: 2.61 us -> 5.95 us  [level_zero(): got = lax.ppermute(send, 'atoms', [(z, z ^ 1) for z in range(atom_count)])]
    ppermute x1, waiting for transfers between devices: 3.3 us -> 0.01 us  [body(): lax.ppermute(head, 'atoms', [(z + 1, z) for z in range(atom_count - 1)])]
    ppermute x3, starting transfers between devices: 8.51 us -> 11.3 us  [collected(): terms = terms + [lax.ppermute(sent, ('atoms', 'modes'), moves)]]
    ppermute x3, waiting for transfers between devices: 4.14 us -> 2.17 us  [level_zero(): got = lax.ppermute(send, 'atoms', [(z, z ^ 1) for z in range(atom_count)])]
    pallas_call x6 -> x7, Pallas kernels: 19.7 us -> 21 us  [call(): pl.pallas_call(kernel, in_specs=in_specs, out_specs=out_specs, out_shape=...]
    convert_element_type x3, other arithmetic: 0.07 us -> 1.02 us  [collected(): sum((term.astype(jnp.float32) for term in terms)).astype(jnp.bfloat16)]
  transfers between devices with their start and end apart: 19 -> 19, of which waited for: 7 -> 5; matrix products, arithmetic and copies ran while one was open for 2% -> 6% of each run, Pallas kernels for 16% -> 23%
where the time goes in v4:
time: 67.6 us; the launch traced here: 67.2 us
  starting transfers between devices  31.5 us (47%)
  Pallas kernels  21 us (31%)
  waiting for transfers between devices  7.7 us (11%)
  local copies, waits for them, and re-layouts  4.41 us (7%)
  other arithmetic  1.77 us (3%)
  between operations  0.84 us (1%)
    pallas_call x7, Pallas kernels, call(): pl.pallas_call(kernel, in_specs=in_specs, out_specs=out_specs, out_shape=...  21 us
    ppermute x3, starting transfers between devices, collected(): terms = terms + [lax.ppermute(sent, ('atoms', 'modes'), moves)]  11.3 us
    ppermute x3, starting transfers between devices, level_zero(): got = lax.ppermute(send, 'atoms', [(z, z ^ 1) for z in range(atom_count)])  5.95 us
    ppermute x1, starting transfers between devices, body(): lax.ppermute(tail, 'atoms', [(z, z + 1) for z in range(atom_count - 1)])  4.93 us
    ppermute x3, starting transfers between devices, body(): lax.ppermute(numerator, ('modes', 'sub'), [(i, i ^ code) for i in range(h...  4.21 us
    ppermute x3, starting transfers between devices, from_group(): return lax.ppermute(cells, 'modes', [(m ^ shift, m) for m in range(groups)])  3.6 us
    ppermute x3, waiting for transfers between devices, body(): lax.ppermute(numerator, ('modes', 'sub'), [(i, i ^ code) for i in range(h...  2.82 us
    ppermute x3, waiting for transfers between devices, level_zero(): got = lax.ppermute(send, 'atoms', [(z, z ^ 1) for z in range(atom_count)])  2.17 us
  transfers between devices with their start and end apart: 19, of which 5 were waited for; matrix products, arithmetic and copies ran while one was open for 6% of the time, Pallas kernels for 23%

profile of v4, /device:TPU:0, one launch (start us, length us, event | category | flops | bytes accessed | tf_op | source)
XLA Modules:
  0.0 67.2 jit_solution(11470374361655669016)
XLA Ops:
  0.6 3.5 %images.3 = (bf16[128,768]{1,0:T(8,128)(2,1)S(1)}, bf16[3,96,128]{2,1,0:T(8,128)(2,1)S(1)}, bf16[3,96,128]{2,1,0:T(8,128)(2,1)S(1)}) custom-call(s32[1]{0:T(128)} %bitcast.5.refs_0_, s32[16,768]{1,0:T(8,128)} %bitcast.18, s32[768]{0:T(1024)} %refs_2_.5, f32[9,16,768]{2,1,0:T(8,128)} %bitcast.15, bf16[3,768,128]{2,1,0:T(8,128)(2,1)} %refs_4_.5), custom_call_target="tpu_custom_call" | custom-call | flops 3520000000 | bytes 320000 | tf_op jit(solution)/shard_map/images/pallas_call | solution.py:29
  4.2 4.9 %collective-permute-start = (bf16[3,96,128]{2,1,0:T(8,128)(2,1)S(1)}, bf16[3,96,128]{2,1,0:T(8,128)(2,1)S(1)}, u32[]{:S(2)}, u32[]{:S(2)}) collective-permute-start(bf16[3,96,128]{2,1,0:T(8,128)(2,1)S(1)} %get-tuple-element.22), channel_id=1, source_target_pairs={{0,4},{4,8},{8,12},{1,5},{5,9},{9,13},{2,6},{6,10},{10,14},{3,7},{... | collective-permute-start | bytes 221192 | tf_op jit(solution)/shard_map/ppermute | solution.py:363
  9.1 1.3 %collective-permute-start.1 = (bf16[3,96,128]{2,1,0:T(8,128)(2,1)S(1)}, bf16[3,96,128]{2,1,0:T(8,128)(2,1)S(1)}, u32[]{:S(2)}, u32[]{:S(2)}) collective-permute-start(bf16[3,96,128]{2,1,0:T(8,128)(2,1)S(1)} %get-tuple-element.23), channel_id=1, source_target_pairs={{4,0},{8,4},{12,8},{5,1},{9,5},{13,9},{6,2},{10,6},{14,10},{7,3},{... | collective-permute-start | bytes 221192 | tf_op jit(solution)/shard_map/ppermute | solution.py:364
  10.4 4.3 %images.4 = (bf16[128,1536]{1,0:T(8,128)(2,1)}, bf16[64,1536]{1,0:T(8,128)(2,1)S(1)}) custom-call(s32[1]{0:T(128)} %bitcast.5.refs_0_, s32[16,768]{1,0:T(8,128)} %bitcast.19, s32[768]{0:T(1024)} %refs_2_.5, f32[9,16,768]{2,1,0:T(8,128)} %bitcast.16, bf16[3,768,128]{2,1,0:T(8,128)(2,1)} %refs_4_.5, bf16[128,768]{1,0:T(8,128)(2,1)S(1)} %get-tuple-element.24.refs_5_), custom_call_target="tpu_custom_call" | custom-call | flops 3520000000 | bytes 320000 | tf_op jit(solution)/shard_map/images/pallas_call | solution.py:29
  14.7 0.1 collective-permute-start.3
  14.8 0.0 copy-start
  14.8 1.6 %collective-permute-start.5 = (bf16[64,1536]{1,0:T(8,128)(2,1)S(1)}, bf16[64,1536]{1,0:T(8,128)(2,1)S(1)}, u32[]{:S(2)}, u32[]{:S(2)}) collective-permute-start(bf16[64,1536]{1,0:T(8,128)(2,1)S(1)} %get-tuple-element.28), channel_id=1, source_target_pairs={{2,0},{0,2},{3,1},{1,3},{6,4},{4,6},{7,5},{5,7},{10,8},{8,10},{11,... | collective-permute-start | bytes 589832 | tf_op jit(solution)/shard_map/ppermute | solution.py:381
  16.4 5.4 %images.5 = (bf16[128,768]{1,0:T(8,128)(2,1)}, bf16[64,768]{1,0:T(8,128)(2,1)}, bf16[64,2304]{1,0:T(8,128)(2,1)}) custom-call(s32[1]{0:T(128)} %bitcast.5.refs_0_, s32[16,768]{1,0:T(8,128)} %bitcast.20, s32[768]{0:T(1024)} %refs_2_.5, f32[9,16,768]{2,1,0:T(8,128)} %bitcast.17, bf16[3,768,128]{2,1,0:T(8,128)(2,1)} %refs_4_.5, ...), custom_call_target="tpu_custom_call" | custom-call | flops 3520000000 | bytes 320000 | tf_op jit(solution)/shard_map/images/pallas_call | solution.py:29
  21.8 0.2 collective-permute-start.4
  22.0 0.1 pad_add_fusion.1.place_ref
  22.0 0.7 %collective-permute-start.2 = (bf16[64,768]{1,0:T(8,128)(2,1)}, bf16[64,768]{1,0:T(8,128)(2,1)}, u32[]{:S(2)}, u32[]{:S(2)}) collective-permute-start(bf16[64,768]{1,0:T(8,128)(2,1)} %get-tuple-element.26), channel_id=1, source_target_pairs={{2,0},{0,2},{3,1},{1,3},{6,4},{4,6},{7,5},{5,7},{10,8},{8,10},{11,... | collective-permute-start | bytes 294920 | tf_op jit(solution)/shard_map/ppermute | solution.py:381
  22.7 1.4 %collective-permute-start.10 = (bf16[64,2304]{1,0:T(8,128)(2,1)}, bf16[64,2304]{1,0:T(8,128)(2,1)}, u32[]{:S(2)}, u32[]{:S(2)}) collective-permute-start(bf16[64,2304]{1,0:T(8,128)(2,1)} %get-tuple-element.34), channel_id=1, source_target_pairs={{2,0},{0,2},{3,1},{1,3},{6,4},{4,6},{7,5},{5,7},{10,8},{8,10},{11,... | collective-permute-start | bytes 884744 | tf_op jit(solution)/shard_map/ppermute | solution.py:381
  24.1 0.0 collective-permute-done.5.refs_4_.refs_0_
  24.1 0.0 collective-permute-start.8
  24.1 0.0 collective-permute-done.4.refs_3_
  24.1 2.5 %products.3 = (f32[128,640]{1,0:T(8,128)S(1)}, bf16[128,640]{1,0:T(8,128)(2,1)S(1)}) custom-call(s32[2]{0:T(128)S(1)} %pad_add_fusion.1.place_ref, bf16[3,768,640]{2,1,0:T(8,128)(2,1)S(1)} %copy-done, bf16[128,1536]{1,0:T(8,128)(2,1)} %get-tuple-element.25.refs_7_.refs_0_, bf16[128,768]{1,0:T(8,128)(2,1)} %get-tuple-element.27.refs_1_, ...), custom_call_target="tpu_custom_call" | custom-call | flops 6600000000 | bytes 600000 | tf_op jit(solution)/shard_map/products/pallas_call | solution.py:29
  26.6 0.7 copy-done.6
  27.3 0.7 %collective-permute-done.2.refs_1_ = bf16[64,768]{1,0:T(8,128)(2,1)} collective-permute-done((bf16[64,768]{1,0:T(8,128)(2,1)}, bf16[64,768]{1,0:T(8,128)(2,1)}, u32[]{:S(2)}, u32[]{:S(2)}) %collective-permute-start.2) | collective-permute-done | bytes 98336 | tf_op jit(solution)/shard_map/ppermute | solution.py:381
  28.0 0.0 collective-permute-start.9
  28.0 2.6 %collective-permute-start.6 = (bf16[128,640]{1,0:T(8,128)(2,1)}, bf16[128,640]{1,0:T(8,128)(2,1)}, u32[]{:S(2)}, u32[]{:S(2)}) collective-permute-start(bf16[128,640]{1,0:T(8,128)(2,1)} %copy-done.6), channel_id=1, source_target_pairs={{0,4},{4,0},{8,12},{12,8},{1,5},{5,1},{9,13},{13,9},{2,6},{6,2},{1... | collective-permute-start | bytes 491528 | tf_op jit(solution)/shard_map/ppermute | solution.py:398
  30.6 0.0 collective-permute-done.8.refs_2_
  30.6 0.0 collective-permute-done.9.refs_3_
  30.6 1.7 %products.4 = (f32[64,640]{1,0:T(8,128)S(1)}, bf16[64,640]{1,0:T(8,128)(2,1)S(1)}) custom-call(s32[2]{0:T(128)S(1)} %pad_add_fusion.1.place_ref, bf16[3,768,640]{2,1,0:T(8,128)(2,1)S(1)} %copy-done, bf16[64,1536]{1,0:T(8,128)(2,1)S(1)} %collective-permute-done.5.refs_4_.refs_0_, bf16[64,768]{1,0:T(8,128)(2,1)} %collective-permute-done.2.refs_1_, ...), custom_call_target="tpu_custom_call" | custom-call | flops 110000000 | bytes 10000 | tf_op jit(solution)/shard_map/products/pallas_call | solution.py:29
  32.3 0.7 copy-done.1
  33.0 1.6 %collective-permute-start.11 = (bf16[64,640]{1,0:T(8,128)(2,1)S(1)}, bf16[64,640]{1,0:T(8,128)(2,1)S(1)}, u32[]{:S(2)}, u32[]{:S(2)}) collective-permute-start(bf16[64,640]{1,0:T(8,128)(2,1)S(1)} %get-tuple-element.35), channel_id=1, source_target_pairs={{0,4},{4,0},{8,12},{12,8},{1,5},{5,1},{9,13},{13,9},{2,6},{6,2},{1... | collective-permute-start | bytes 245768 | tf_op jit(solution)/shard_map/ppermute | solution.py:398
  34.6 0.8 %dynamic-slice_bitcast_fusion = (s32[128,1]{0,1:T(1,128)S(1)}, s32[128,1]{0,1:T(1,128)S(1)}) fusion(s32[512]{0:T(512)} %param.17, s32[]{:T(128)S(6)} %select_n.11, s32[512]{0:T(512)} %param.16), kind=kLoop, calls=%fused_computation.6 | loop fusion | bytes 2052 | tf_op jit(solution)/shard_map/broadcast_in_dim | solution.py:441
  35.4 2.2 %collective-permute-done.11.refs_4_ = bf16[64,640]{1,0:T(8,128)(2,1)S(1)} collective-permute-done((bf16[64,640]{1,0:T(8,128)(2,1)S(1)}, bf16[64,640]{1,0:T(8,128)(2,1)S(1)}, u32[]{:S(2)}, u32[]{:S(2)}) %collective-permute-start.11) | collective-permute-done | bytes 81952 | tf_op jit(solution)/shard_map/ppermute | solution.py:398
  37.6 0.1 dynamic-slice_bitcast_fusion.2
  37.6 0.7 %copy.11.start_ref = s32[128,1]{1,0:T(8,128)} copy(s32[128,1]{0,1:T(1,128)S(1)} %get-tuple-element.43) | data formatting | bytes 1024 | tf_op jit(solution)/shard_map/broadcast_in_dim | solution.py:440
  38.4 0.7 %copy.12.length_ref = s32[128,1]{1,0:T(8,128)} copy(s32[128,1]{0,1:T(1,128)S(1)} %get-tuple-element.42) | data formatting | bytes 1024 | tf_op jit(solution)/shard_map/broadcast_in_dim | solution.py:441
  39.1 0.7 %copy.13.freq_ref = f32[128,1]{1,0:T(8,128)} copy(f32[128,1]{0,1:T(1,128)S(1)} %dynamic-slice_bitcast_fusion.2) | data formatting | bytes 1024 | tf_op jit(solution)/shard_map/broadcast_in_dim | solution.py:442
  39.9 0.0 collective-permute-done.6.refs_1_
  39.9 1.0 %add_convert_fusion = bf16[128,640]{1,0:T(8,128)(2,1)S(1)} fusion(f32[128,640]{1,0:T(8,128)S(1)} %get-tuple-element.30.refs_0_, bf16[128,640]{1,0:T(8,128)(2,1)} %collective-permute-done.6.refs_1_), kind=kLoop, calls=%fused_computation | loop fusion | flops 245760 | bytes 655360 | tf_op jit(solution)/shard_map/convert_element_type | solution.py:273
  40.9 1.3 %collective-permute-start.7 = (bf16[128,640]{1,0:T(8,128)(2,1)S(1)}, bf16[128,640]{1,0:T(8,128)(2,1)S(1)}, u32[]{:S(2)}, u32[]{:S(2)}) collective-permute-start(bf16[128,640]{1,0:T(8,128)(2,1)S(1)} %add_convert_fusion), channel_id=1, source_target_pairs={{2,10},{6,14},{8,0},{12,4},{3,11},{7,15},{9,1},{13,5},{18,26},{22,... | collective-permute-start | bytes 491528 | tf_op jit(solution)/shard_map/ppermute | solution.py:274
  42.2 0.0 collective-permute-done.13.refs_1_
  42.2 1.7 %products.5 = (f32[64,640]{1,0:T(8,128)S(1)}, bf16[64,640]{1,0:T(8,128)(2,1)S(1)}) custom-call(s32[2]{0:T(128)S(1)} %pad_add_fusion.1.place_ref, bf16[3,768,640]{2,1,0:T(8,128)(2,1)S(1)} %copy-done, bf16[64,2304]{1,0:T(8,128)(2,1)} %collective-permute-done.10.refs_0_, bf16[64,2304]{1,0:T(8,128)(2,1)} %collective-permute-done.13.refs_1_), custom_call_target="tpu_custom_call" | custom-call | flops 110000000 | bytes 10000 | tf_op jit(solution)/shard_map/products/pallas_call | solution.py:29
  43.9 1.7 %collective-permute-start.14 = (bf16[64,640]{1,0:T(8,128)(2,1)S(1)}, bf16[64,640]{1,0:T(8,128)(2,1)S(1)}, u32[]{:S(2)}, u32[]{:S(2)}) collective-permute-start(bf16[64,640]{1,0:T(8,128)(2,1)S(1)} %get-tuple-element.39), channel_id=1, source_target_pairs={{0,4},{4,0},{8,12},{12,8},{1,5},{5,1},{9,13},{13,9},{2,6},{6,2},{1... | collective-permute-start | bytes 245768 | tf_op jit(solution)/shard_map/ppermute | solution.py:398
  45.6 5.5 %collective-permute-start.12 = (bf16[64,640]{1,0:T(8,128)(2,1)S(1)}, bf16[64,640]{1,0:T(8,128)(2,1)S(1)}, u32[]{:S(2)}, u32[]{:S(2)}) collective-permute-start(bf16[64,640]{1,0:T(8,128)(2,1)S(1)} %add_convert_fusion.2), channel_id=1, source_target_pairs={{0,8},{4,12},{10,2},{14,6},{1,9},{5,13},{11,3},{15,7},{16,24},{20,... | collective-permute-start | bytes 245768 | tf_op jit(solution)/shard_map/ppermute | solution.py:274
  51.1 0.0 collective-permute-done.14.refs_7_
  51.1 4.5 %collective-permute-start.15 = (bf16[64,640]{1,0:T(8,128)(2,1)S(1)}, bf16[64,640]{1,0:T(8,128)(2,1)S(1)}, u32[]{:S(2)}, u32[]{:S(2)}) collective-permute-start(bf16[64,640]{1,0:T(8,128)(2,1)S(1)} %add_convert_fusion.1), channel_id=1, source_target_pairs={{0,8},{4,12},{10,2},{14,6},{1,9},{5,13},{11,3},{15,7},{16,24},{20,... | collective-permute-start | bytes 245768 | tf_op jit(solution)/shard_map/ppermute | solution.py:274
  55.6 0.1 pad_add_fusion.flag_ref
  55.7 2.0 %collective-permute-done.15.refs_8_ = bf16[64,640]{1,0:T(8,128)(2,1)S(1)} collective-permute-done((bf16[64,640]{1,0:T(8,128)(2,1)S(1)}, bf16[64,640]{1,0:T(8,128)(2,1)S(1)}, u32[]{:S(2)}, u32[]{:S(2)}) %collective-permute-start.15) | collective-permute-done | bytes 81952 | tf_op jit(solution)/shard_map/ppermute | solution.py:274
  57.7 1.9 %finish.1 = (f32[128,640]{1,0:T(8,128)}, f32[1,128]{1,0:T(1,128)S(1)}) custom-call(s32[2]{0:T(128)S(1)} %pad_add_fusion.flag_ref, s32[128,1]{1,0:T(8,128)S(1)} %copy-done.3, s32[128,1]{1,0:T(8,128)S(1)} %copy-done.4, f32[128,1]{1,0:T(8,128)S(1)} %copy-done.5, f32[1,640]{1,0:T(1,128)S(1)} %broadcast_in_dim.18.partner_ref, ...), custom_call_target="tpu_custom_call" | custom-call | flops 2200000000 | bytes 200000 | tf_op jit(solution)/shard_map/finish/pallas_call | solution.py:29
  59.6 4.1 %collective-permute-start.17 = (f32[1,128]{1,0:T(1,128)S(1)}, f32[1,128]{1,0:T(1,128)S(1)}, u32[]{:S(2)}, u32[]{:S(2)}) collective-permute-start(f32[1,128]{1,0:T(1,128)S(1)} %get-tuple-element.41), channel_id=1, source_target_pairs={{0,2},{1,3},{2,0},{3,1},{4,6},{5,7},{6,4},{7,5},{8,10},{9,11},{10,... | collective-permute-start | bytes 1544 | tf_op jit(solution)/shard_map/ppermute | solution.py:449
  63.7 0.1 collective-permute-start.18
  63.8 1.4 %collective-permute-done.17 = f32[1,128]{1,0:T(1,128)S(1)} collective-permute-done((f32[1,128]{1,0:T(1,128)S(1)}, f32[1,128]{1,0:T(1,128)S(1)}, u32[]{:S(2)}, u32[]{:S(2)}) %collective-permute-start.17) | collective-permute-done | bytes 544 | tf_op jit(solution)/shard_map/ppermute | solution.py:449
  65.2 1.4 %collective-permute-done.18 = f32[1,128]{1,0:T(1,128)S(1)} collective-permute-done((f32[1,128]{1,0:T(1,128)S(1)}, f32[1,128]{1,0:T(1,128)S(1)}, u32[]{:S(2)}, u32[]{:S(2)}) %collective-permute-start.18) | collective-permute-done | bytes 544 | tf_op jit(solution)/shard_map/ppermute | solution.py:449
  66.6 0.6 bitcast_divide_fusion
  (27 shorter events, 0.1 us)
Async XLA Ops:
  4.2 12.2 %collective-permute-start = (bf16[3,96,128]{2,1,0:T(8,128)(2,1)S(1)}, bf16[3,96,128]{2,1,0:T(8,128)(2,1)S(1)}, u32[]{:S(2)}, u32[]{:S(2)}) collective-permute-start(bf16[3,96,128]{2,1,0:T(8,128)(2,1)S(1)} %get-tuple-element.22), channel_id=1, source_target_pairs={{0,4},{4,8},{8,12},{1,5},{5,9},{9,13},{2,6},{6,10},{10,14},{3,7},{... | collective-permute-start | bytes 221192 | tf_op jit(solution)/shard_map/ppermute | solution.py:363
  9.1 7.3 %collective-permute-start.1 = (bf16[3,96,128]{2,1,0:T(8,128)(2,1)S(1)}, bf16[3,96,128]{2,1,0:T(8,128)(2,1)S(1)}, u32[]{:S(2)}, u32[]{:S(2)}) collective-permute-start(bf16[3,96,128]{2,1,0:T(8,128)(2,1)S(1)} %get-tuple-element.23), channel_id=1, source_target_pairs={{4,0},{8,4},{12,8},{5,1},{9,5},{13,9},{6,2},{10,6},{14,10},{7,3},{... | collective-permute-start | bytes 221192 | tf_op jit(solution)/shard_map/ppermute | solution.py:364
  14.7 9.4 %collective-permute-start.3 = (bf16[128,1536]{1,0:T(8,128)(2,1)}, bf16[128,1536]{1,0:T(8,128)(2,1)}, u32[]{:S(2)}, u32[]{:S(2)}) collective-permute-start(bf16[128,1536]{1,0:T(8,128)(2,1)} %get-tuple-element.25.refs_7_.refs_0_), channel_id=1, source_target_pairs={{0,1},{1,0},{2,3},{3,2},{4,5},{5,4},{6,7},{7,6},{8,9},{9,8},{10,11... | collective-permute-start | bytes 1179656 | tf_op jit(solution)/shard_map/ppermute | solution.py:384
  14.8 9.3 %copy-start = (bf16[3,768,640]{2,1,0:T(8,128)(2,1)S(1)}, bf16[3,768,640]{2,1,0:T(8,128)(2,1)}, u32[]{:S(2)}) copy-start(bf16[3,768,640]{2,1,0:T(8,128)(2,1)} %partners_ref.5) | copy-start | bytes 8847364
  14.8 9.3 %collective-permute-start.5 = (bf16[64,1536]{1,0:T(8,128)(2,1)S(1)}, bf16[64,1536]{1,0:T(8,128)(2,1)S(1)}, u32[]{:S(2)}, u32[]{:S(2)}) collective-permute-start(bf16[64,1536]{1,0:T(8,128)(2,1)S(1)} %get-tuple-element.28), channel_id=1, source_target_pairs={{2,0},{0,2},{3,1},{1,3},{6,4},{4,6},{7,5},{5,7},{10,8},{8,10},{11,... | collective-permute-start | bytes 589832 | tf_op jit(solution)/shard_map/ppermute | solution.py:381
  21.8 2.3 %collective-permute-start.4 = (bf16[128,768]{1,0:T(8,128)(2,1)}, bf16[128,768]{1,0:T(8,128)(2,1)}, u32[]{:S(2)}, u32[]{:S(2)}) collective-permute-start(bf16[128,768]{1,0:T(8,128)(2,1)} %get-tuple-element.27.refs_1_), channel_id=1, source_target_pairs={{0,1},{1,0},{2,3},{3,2},{4,5},{5,4},{6,7},{7,6},{8,9},{9,8},{10,11... | collective-permute-start | bytes 589832 | tf_op jit(solution)/shard_map/ppermute | solution.py:384
  22.0 5.9 %collective-permute-start.2 = (bf16[64,768]{1,0:T(8,128)(2,1)}, bf16[64,768]{1,0:T(8,128)(2,1)}, u32[]{:S(2)}, u32[]{:S(2)}) collective-permute-start(bf16[64,768]{1,0:T(8,128)(2,1)} %get-tuple-element.26), channel_id=1, source_target_pairs={{2,0},{0,2},{3,1},{1,3},{6,4},{4,6},{7,5},{5,7},{10,8},{8,10},{11,... | collective-permute-start | bytes 294920 | tf_op jit(solution)/shard_map/ppermute | solution.py:381
  22.7 12.7 %collective-permute-start.10 = (bf16[64,2304]{1,0:T(8,128)(2,1)}, bf16[64,2304]{1,0:T(8,128)(2,1)}, u32[]{:S(2)}, u32[]{:S(2)}) collective-permute-start(bf16[64,2304]{1,0:T(8,128)(2,1)} %get-tuple-element.34), channel_id=1, source_target_pairs={{2,0},{0,2},{3,1},{1,3},{6,4},{4,6},{7,5},{5,7},{10,8},{8,10},{11,... | collective-permute-start | bytes 884744 | tf_op jit(solution)/shard_map/ppermute | solution.py:381
  24.1 6.5 %collective-permute-start.8 = (bf16[64,1536]{1,0:T(8,128)(2,1)S(1)}, bf16[64,1536]{1,0:T(8,128)(2,1)}, u32[]{:S(2)}, u32[]{:S(2)}) collective-permute-start(bf16[64,1536]{1,0:T(8,128)(2,1)S(1)} %collective-permute-done.5.refs_4_.refs_0_), channel_id=1, source_target_pairs={{0,1},{1,0},{2,3},{3,2},{4,5},{5,4},{6,7},{7,6},{8,9},{9,8},{10,11... | collective-permute-start | bytes 589832 | tf_op jit(solution)/shard_map/ppermute | solution.py:384
  26.6 0.7 %copy-start.6 = (bf16[128,640]{1,0:T(8,128)(2,1)}, bf16[128,640]{1,0:T(8,128)(2,1)S(1)}, u32[]{:S(2)}) copy-start(bf16[128,640]{1,0:T(8,128)(2,1)S(1)} %get-tuple-element.31) | copy-start | bytes 491524
  27.3 10.3 %copy-start.8 = (f32[512]{0:T(512)S(1)}, f32[512]{0:T(512)}, u32[]{:S(2)}) copy-start(f32[512]{0:T(512)} %param.14) | copy-start | bytes 6148
  27.3 12.6 %copy-start.7 = (f32[640]{0:T(1024)S(1)}, f32[640]{0:T(1024)}, u32[]{:S(2)}) copy-start(f32[640]{0:T(1024)} %param.15) | copy-start | bytes 7684
  28.0 2.6 %collective-permute-start.9 = (bf16[64,768]{1,0:T(8,128)(2,1)}, bf16[64,768]{1,0:T(8,128)(2,1)}, u32[]{:S(2)}, u32[]{:S(2)}) collective-permute-start(bf16[64,768]{1,0:T(8,128)(2,1)} %collective-permute-done.2.refs_1_), channel_id=1, source_target_pairs={{0,1},{1,0},{2,3},{3,2},{4,5},{5,4},{6,7},{7,6},{8,9},{9,8},{10,11... | collective-permute-start | bytes 294920 | tf_op jit(solution)/shard_map/ppermute | solution.py:384
  28.0 11.9 %collective-permute-start.6 = (bf16[128,640]{1,0:T(8,128)(2,1)}, bf16[128,640]{1,0:T(8,128)(2,1)}, u32[]{:S(2)}, u32[]{:S(2)}) collective-permute-start(bf16[128,640]{1,0:T(8,128)(2,1)} %copy-done.6), channel_id=1, source_target_pairs={{0,4},{4,0},{8,12},{12,8},{1,5},{5,1},{9,13},{13,9},{2,6},{6,2},{1... | collective-permute-start | bytes 491528 | tf_op jit(solution)/shard_map/ppermute | solution.py:398
  32.3 0.7 copy-start.1
  33.0 12.6 %copy-start.2 = (f32[64,640]{1,0:T(8,128)S(1)}, f32[64,640]{1,0:T(8,128)}, u32[]{:S(2)}) copy-start(f32[64,640]{1,0:T(8,128)} %copy-done.1) | copy-start | bytes 491524
  33.0 4.6 %collective-permute-start.11 = (bf16[64,640]{1,0:T(8,128)(2,1)S(1)}, bf16[64,640]{1,0:T(8,128)(2,1)S(1)}, u32[]{:S(2)}, u32[]{:S(2)}) collective-permute-start(bf16[64,640]{1,0:T(8,128)(2,1)S(1)} %get-tuple-element.35), channel_id=1, source_target_pairs={{0,4},{4,0},{8,12},{12,8},{1,5},{5,1},{9,13},{13,9},{2,6},{6,2},{1... | collective-permute-start | bytes 245768 | tf_op jit(solution)/shard_map/ppermute | solution.py:398
  37.6 4.6 %collective-permute-start.13 = (bf16[64,2304]{1,0:T(8,128)(2,1)}, bf16[64,2304]{1,0:T(8,128)(2,1)}, u32[]{:S(2)}, u32[]{:S(2)}) collective-permute-start(bf16[64,2304]{1,0:T(8,128)(2,1)} %collective-permute-done.10.refs_0_), channel_id=1, source_target_pairs={{0,1},{1,0},{2,3},{3,2},{4,5},{5,4},{6,7},{7,6},{8,9},{9,8},{10,11... | collective-permute-start | bytes 884744 | tf_op jit(solution)/shard_map/ppermute | solution.py:384
  39.8 17.8 %copy-start.3 = (s32[128,1]{1,0:T(8,128)S(1)}, s32[128,1]{1,0:T(8,128)}, u32[]{:S(2)}) copy-start(s32[128,1]{1,0:T(8,128)} %copy.11.start_ref) | copy-start | bytes 1540
  39.9 17.8 %copy-start.4 = (s32[128,1]{1,0:T(8,128)S(1)}, s32[128,1]{1,0:T(8,128)}, u32[]{:S(2)}) copy-start(s32[128,1]{1,0:T(8,128)} %copy.12.length_ref) | copy-start | bytes 1540
  39.9 17.8 %copy-start.5 = (f32[128,1]{1,0:T(8,128)S(1)}, f32[128,1]{1,0:T(8,128)}, u32[]{:S(2)}) copy-start(f32[128,1]{1,0:T(8,128)} %copy.13.freq_ref) | copy-start | bytes 1540
  40.9 14.9 %collective-permute-start.7 = (bf16[128,640]{1,0:T(8,128)(2,1)S(1)}, bf16[128,640]{1,0:T(8,128)(2,1)S(1)}, u32[]{:S(2)}, u32[]{:S(2)}) collective-permute-start(bf16[128,640]{1,0:T(8,128)(2,1)S(1)} %add_convert_fusion), channel_id=1, source_target_pairs={{2,10},{6,14},{8,0},{12,4},{3,11},{7,15},{9,1},{13,5},{18,26},{22,... | collective-permute-start | bytes 491528 | tf_op jit(solution)/shard_map/ppermute | solution.py:274
  43.9 7.2 %collective-permute-start.14 = (bf16[64,640]{1,0:T(8,128)(2,1)S(1)}, bf16[64,640]{1,0:T(8,128)(2,1)S(1)}, u32[]{:S(2)}, u32[]{:S(2)}) collective-permute-start(bf16[64,640]{1,0:T(8,128)(2,1)S(1)} %get-tuple-element.39), channel_id=1, source_target_pairs={{0,4},{4,0},{8,12},{12,8},{1,5},{5,1},{9,13},{13,9},{2,6},{6,2},{1... | collective-permute-start | bytes 245768 | tf_op jit(solution)/shard_map/ppermute | solution.py:398
  45.6 10.1 %collective-permute-start.12 = (bf16[64,640]{1,0:T(8,128)(2,1)S(1)}, bf16[64,640]{1,0:T(8,128)(2,1)S(1)}, u32[]{:S(2)}, u32[]{:S(2)}) collective-permute-start(bf16[64,640]{1,0:T(8,128)(2,1)S(1)} %add_convert_fusion.2), channel_id=1, source_target_pairs={{0,8},{4,12},{10,2},{14,6},{1,9},{5,13},{11,3},{15,7},{16,24},{20,... | collective-permute-start | bytes 245768 | tf_op jit(solution)/shard_map/ppermute | solution.py:274
  51.1 6.6 %collective-permute-start.15 = (bf16[64,640]{1,0:T(8,128)(2,1)S(1)}, bf16[64,640]{1,0:T(8,128)(2,1)S(1)}, u32[]{:S(2)}, u32[]{:S(2)}) collective-permute-start(bf16[64,640]{1,0:T(8,128)(2,1)S(1)} %add_convert_fusion.1), channel_id=1, source_target_pairs={{0,8},{4,12},{10,2},{14,6},{1,9},{5,13},{11,3},{15,7},{16,24},{20,... | collective-permute-start | bytes 245768 | tf_op jit(solution)/shard_map/ppermute | solution.py:274
  59.6 4.2 %collective-permute-start.16 = (f32[1,128]{1,0:T(1,128)S(1)}, f32[1,128]{1,0:T(1,128)S(1)}, u32[]{:S(2)}, u32[]{:S(2)}) collective-permute-start(f32[1,128]{1,0:T(1,128)S(1)} %get-tuple-element.41), channel_id=1, source_target_pairs={{0,1},{1,0},{2,3},{3,2},{4,5},{5,4},{6,7},{7,6},{8,9},{9,8},{10,11... | collective-permute-start | bytes 1544 | tf_op jit(solution)/shard_map/ppermute | solution.py:449
  59.6 5.6 %collective-permute-start.17 = (f32[1,128]{1,0:T(1,128)S(1)}, f32[1,128]{1,0:T(1,128)S(1)}, u32[]{:S(2)}, u32[]{:S(2)}) collective-permute-start(f32[1,128]{1,0:T(1,128)S(1)} %get-tuple-element.41), channel_id=1, source_target_pairs={{0,2},{1,3},{2,0},{3,1},{4,6},{5,7},{6,4},{7,5},{8,10},{9,11},{10,... | collective-permute-start | bytes 1544 | tf_op jit(solution)/shard_map/ppermute | solution.py:449
  63.7 3.0 %collective-permute-start.18 = (f32[1,128]{1,0:T(1,128)S(1)}, f32[1,128]{1,0:T(1,128)S(1)}, u32[]{:S(2)}, u32[]{:S(2)}) collective-permute-start(f32[1,128]{1,0:T(1,128)S(1)} %get-tuple-element.41), channel_id=1, source_target_pairs={{0,3},{1,2},{2,1},{3,0},{4,7},{5,6},{6,5},{7,4},{8,11},{9,10},{10,... | collective-permute-start | bytes 1544 | tf_op jit(solution)/shard_map/ppermute | solution.py:449

commit v5 on v4

--- a/solution.py
+++ b/solution.py
@@ -95,19 +95,14 @@
     lax.fori_loop(0, SPAN // GROUP, group_step, 0)
 
 
-def window(first, rows, c, panel_ref, low_ref, high_ref):
-    begin, end = first - HALO, first - HALO + SPAN
-    if begin < 0:
-        return jnp.concatenate([low_ref[c, HALO + begin :], panel_ref[c, :end]], axis=0)
-    if end > rows:
-        return jnp.concatenate([panel_ref[c, begin:], high_ref[c, : end - rows]], axis=0)
-    return panel_ref[c, begin:end]
-
-
 def images_of(blocks, base, panel, nbr, coef, count, halos=(), before=None, joined=False, edges=False, halved=False):
     rows, modes = panel.shape[1:]
-    operands = [base, *[pltpu.with_memory_space_constraint(x, pltpu.HBM) for x in (nbr, count, coef, panel)], *halos]
-    in_specs = [SMEM] + [HBM] * 4 + [ANY] * len(halos)
+    loads = before is None
+    operands = [nbr, count, coef, panel]
+    if loads:
+        operands = [pltpu.with_memory_space_constraint(x, pltpu.HBM) for x in operands]
+    operands = [base, *operands, *halos]
+    in_specs = [SMEM] + [HBM if loads else VMEM] * 4 + [VMEM] * len(halos)
     old = 0
     if before is not None:
         operands.append(before)
@@ -129,52 +124,77 @@
             out_specs.append(VMEM)
     n_in, n_out = len(operands), len(out_shape)
 
+    def pieces_of(block):
+        begin, end = block * LANES - HALO, (block + 1) * LANES + HALO
+        found = []
+        if begin < 0:
+            found.append((1, HALO + begin, 0, -begin))
+        low, high = max(begin, 0), min(end, rows)
+        found.append((0, low, low - begin, high - low))
+        if end > rows:
+            found.append((2, 0, rows - begin, end - rows))
+        return found
+
     def kernel(*refs):
-        base_ref, nbr_hbm, count_hbm, coef_hbm, panel_hbm = refs[:5]
+        base_ref, nbr_ref, count_ref, coef_ref, panel_ref = refs[:5]
         outs = refs[n_in : n_in + n_out]
-        nbr_ref, count_ref, coef_ref, panel_ref, low_ref, high_ref, dense_ref, sems = refs[n_in + n_out :]
-        copies, panel_copies = [], []
-
-        def start(source, target, kept):
-            copy = pltpu.make_async_copy(source, target, sems.at[len(copies) + len(panel_copies)])
-            copy.start()
-            kept.append(copy)
-
-        start(nbr_hbm, nbr_ref, copies)
-        start(count_hbm, count_ref, copies)
-        for _, block, length in runs_of(blocks):
-            at = pl.ds(block * LANES, length * LANES)
-            start(coef_hbm.at[:, :, at], coef_ref.at[:, :, at], copies)
-        for _, block, length in runs_of(blocks):
-            begin = max(block * LANES - HALO, 0)
-            end = min((block + length) * LANES + HALO, rows)
-            at = pl.ds(begin, end - begin)
-            start(panel_hbm.at[:, at], panel_ref.at[:, at], panel_copies)
-        if halos:
-            start(refs[5], low_ref, panel_copies)
-            start(refs[6], high_ref, panel_copies)
-        if edges:
-            start(panel_hbm.at[:, pl.ds(0, HALO)], outs[1], panel_copies)
-            start(panel_hbm.at[:, pl.ds(rows - HALO, HALO)], outs[2], panel_copies)
-        for copy in copies:
-            copy.wait()
-        for place, block in enumerate(blocks):
-            first = block * LANES
-            build_block(first, base_ref[0], nbr_ref, coef_ref, count_ref, dense_ref)
-            if place == 0:
-                for copy in panel_copies:
-                    copy.wait()
-            cells = jnp.concatenate(
-                [window(first, rows, c, panel_ref, low_ref, high_ref) for c in range(3)], axis=0
-            )
+        window_ref, dense_ref, *scratch_refs = refs[n_in + n_out :]
+        window_copies = []
+        if loads:
+            sources = (nbr_ref, count_ref, coef_ref)
+            nbr_ref, count_ref, coef_ref, sems = scratch_refs
+            copies = []
+
+            def start(source, target, kept):
+                copy = pltpu.make_async_copy(source, target, sems.at[len(copies) + len(window_copies)])
+                copy.start()
+                kept.append(copy)
+
+            start(sources[0], nbr_ref, copies)
+            start(sources[1], count_ref, copies)
+            for _, block, length in runs_of(blocks):
+                at = pl.ds(block * LANES, length * LANES)
+                start(sources[2].at[:, :, at], coef_ref.at[:, :, at], copies)
+            for place, block in enumerate(blocks):
+                for _, source, at, length in pieces_of(block):
+                    start(
+                        panel_ref.at[:, pl.ds(source, length)], window_ref.at[place, :, pl.ds(at, length)], window_copies
+                    )
+            if edges:
+                start(panel_ref.at[:, pl.ds(0, HALO)], outs[1], window_copies)
+                start(panel_ref.at[:, pl.ds(rows - HALO, HALO)], outs[2], window_copies)
+            for copy in copies:
+                copy.wait()
+        else:
+            for place, block in enumerate(blocks):
+                for which, source, at, length in pieces_of(block):
+                    source_ref = (panel_ref, *refs[5:])[which]
+                    window_ref[place, :, at : at + length, :] = source_ref[:, source : source + length, :]
+
+        def block_step(place, carry):
+            first = (blocks[0] + place * (blocks[1] - blocks[0])) * LANES
+            build_block(pl.multiple_of(first, LANES), base_ref[0], nbr_ref, coef_ref, count_ref, dense_ref)
+            if loads:
+
+                @pl.when(place == 0)
+                def _():
+                    for copy in window_copies:
+                        copy.wait()
+
             both = lax.dot_general(
-                cells, dense_ref[...], (((0,), (0,)), ((), ())), preferred_element_type=jnp.float32
+                window_ref[place].reshape(3 * SPAN, modes),
+                dense_ref[...],
+                (((0,), (0,)), ((), ())),
+                preferred_element_type=jnp.float32,
             )
             for r in range(3):
                 image = both[:, 2 * r * LANES : (2 * r + 1) * LANES]
                 image = image + both[:, (2 * r + 1) * LANES : (2 * r + 2) * LANES]
-                at = r * width + ahead + place * LANES
-                outs[0][:, at : at + LANES] = image.astype(jnp.bfloat16)
+                at = pl.multiple_of(r * width + ahead + place * LANES, LANES)
+                outs[0][:, pl.ds(at, LANES)] = image.astype(jnp.bfloat16)
+            return carry
+
+        lax.fori_loop(0, len(blocks), block_step, 0)
         if joined:
             for r in range(3):
                 outs[0][:, r * width : r * width + old] = refs[n_in - 1][:, r * old : (r + 1) * old]
@@ -188,17 +208,17 @@
                     outs[-1][:, at : at + old] = refs[n_in - 1][span:, r * old : (r + 1) * old]
                     outs[-1][:, at + old : at + old + width] = outs[0][span:, r * width : (r + 1) * width]
 
-    copies_most = 2 + 2 * len(runs_of(blocks)) + 4
     scratch = [
-        pltpu.VMEM((BONDS, rows), jnp.int32),
-        pltpu.VMEM((rows,), jnp.int32),
-        pltpu.VMEM((9, BONDS, rows), jnp.float32),
-        pltpu.VMEM((3, rows, modes), jnp.bfloat16),
-        pltpu.VMEM((3, HALO, modes), jnp.bfloat16),
-        pltpu.VMEM((3, HALO, modes), jnp.bfloat16),
+        pltpu.VMEM((len(blocks), 3, SPAN, modes), jnp.bfloat16),
         pltpu.VMEM((3 * SPAN, 6 * LANES), jnp.bfloat16),
-        pltpu.SemaphoreType.DMA((copies_most,)),
     ]
+    if loads:
+        scratch += [
+            pltpu.VMEM((BONDS, rows), jnp.int32),
+            pltpu.VMEM((rows,), jnp.int32),
+            pltpu.VMEM((9, BONDS, rows), jnp.float32),
+            pltpu.SemaphoreType.DMA((4 + 3 * len(blocks) + 2,)),
+        ]
     return call(kernel, "images", in_specs, out_specs, out_shape, operands, 0.8 + 1.2 * len(blocks), scratch)
 
 
@@ -208,7 +228,7 @@
     depth = partners.shape[1]
 
     def kernel(place_ref, partners_ref, *refs):
-        keep_ref, send_ref, left_ref = refs[-3:]
+        keep_ref, send_ref, left_ref, total_ref = refs[-4:]
         kept = place_ref[0] == place_ref[1]
         for who in range(2):
             at_rows = pl.ds(pl.multiple_of(jnp.where(kept == (who == 0), 0, rows), rows), rows)
@@ -217,13 +237,19 @@
                 width = len(blocks) * LANES
                 for r in range(3):
                     for spot, block, length in runs_of(blocks):
-                        at, to = r * width + spot * LANES, r * depth + block * LANES
-                        left_ref[at_rows, to : to + length * LANES] = image_ref[:, at : at + length * LANES]
-        total = jnp.dot(
-            left_ref[...], partners_ref[...].reshape(3 * depth, cols), preferred_element_type=jnp.float32
-        )
-        keep_ref[...] = total[:rows]
-        send_ref[...] = total[rows:].astype(jnp.bfloat16)
+                        at, to = r * width + spot * LANES, block * LANES
+                        left_ref[r, at_rows, to : to + length * LANES] = image_ref[:, at : at + length * LANES]
+
+        def component(r, carry):
+            total_ref[...] = total_ref[...] + jnp.dot(
+                left_ref[r], partners_ref[r], preferred_element_type=jnp.float32
+            )
+            return carry
+
+        total_ref[...] = jnp.zeros_like(total_ref)
+        lax.fori_loop(0, 3, component, 0)
+        keep_ref[...] = total_ref[:rows]
+        send_ref[...] = total_ref[rows:].astype(jnp.bfloat16)
 
     return call(
         kernel,
@@ -233,7 +259,7 @@
         [jax.ShapeDtypeStruct((rows, cols), jnp.float32), jax.ShapeDtypeStruct((rows, cols), jnp.bfloat16)],
         (place, partners, *mine, *theirs, *after),
         busy_us,
-        [pltpu.VMEM((2 * rows, 3 * depth), jnp.bfloat16)],
+        [pltpu.VMEM((3, 2 * rows, depth), jnp.bfloat16), pltpu.VMEM((2 * rows, cols), jnp.float32)],
     )
 
 
@@ -276,13 +302,14 @@
     return terms
 
 
-def finish(flag, early, late, my_start, my_length, my_freq, partner_freq, first_col, norm_scale):
+def finish(flag, early, late, starts, lengths, freqs, partner_freq, norm_scale):
     rows, cols = early[0].shape
     n_early, parts, n_late = len(early), len(late), len(late[0])
-    operands = [flag, my_start, my_length, my_freq, partner_freq, *early, *[t for part in late for t in part]]
-
-    def kernel(flag_ref, start_ref, length_ref, freq_ref, partner_ref, *refs):
-        out_ref, sum_ref = refs[-2:]
+    operands = [flag, starts, lengths, freqs, partner_freq, *early, *[t for part in late for t in part]]
+    step = 16
+
+    def kernel(flag_ref, starts_ref, lengths_ref, freqs_ref, partner_ref, *refs):
+        out_ref, sum_ref, start_ref, end_ref, freq_ref, folded_ref = refs[-6:]
         span = rows // parts
 
         def sums(some):
@@ -301,29 +328,43 @@
                 at = n_early + part * n_late
                 out_ref[part * span : (part + 1) * span, :] = sums(refs[at : at + n_late])
 
-        columns = lax.broadcasted_iota(jnp.int32, (rows, cols), 1) + flag_ref[1]
-        start = start_ref[...]
-        inside = (columns >= start) & (columns < start + length_ref[...])
-        elements = jnp.where(inside, out_ref[...] * norm_scale, 0.0)
-        out_ref[...] = elements
-        offset = freq_ref[...] - partner_ref[...]
-        lorentz = lorentz_width / (math.pi * (offset * offset + lorentz_width * lorentz_width))
-        weighted = jnp.where(inside, lorentz, 0.0) * elements * elements
-        folded = weighted[:, :LANES]
-        for at in range(LANES, cols, LANES):
-            folded = folded + weighted[:, at : at + LANES]
-        if rows < LANES:
-            folded = jnp.concatenate([folded, jnp.zeros((LANES - rows, LANES), jnp.float32)], axis=0)
-        sum_ref[...] = jnp.sum(folded.T, axis=0, keepdims=True)
+        def turned(row):
+            return jnp.broadcast_to(row, (LANES, rows)).T
+
+        mine = pl.ds(flag_ref[2], 1)
+        start_row = starts_ref[mine, :].astype(jnp.float32)
+        start_ref[...] = turned(start_row)
+        end_ref[...] = turned(start_row + lengths_ref[mine, :].astype(jnp.float32))
+        freq_ref[...] = turned(freqs_ref[mine, :])
+        lane_ids = lax.broadcasted_iota(jnp.int32, (step, LANES), 1)
+
+        def row_step(i, carry):
+            at_rows = pl.ds(pl.multiple_of(i * step, step), step)
+            start, end, freq = start_ref[at_rows, :], end_ref[at_rows, :], freq_ref[at_rows, :]
+            folded = jnp.zeros((step, LANES), jnp.float32)
+            for at in range(0, cols, LANES):
+                columns = (lane_ids + (flag_ref[1] + at)).astype(jnp.float32)
+                inside = (columns >= start) & (columns < end)
+                elements = jnp.where(inside, out_ref[at_rows, at : at + LANES] * norm_scale, 0.0)
+                out_ref[at_rows, at : at + LANES] = elements
+                offset = freq - partner_ref[:, at : at + LANES]
+                lorentz = lorentz_width / (math.pi * (offset * offset + lorentz_width * lorentz_width))
+                folded = folded + jnp.where(inside, lorentz, 0.0) * elements * elements
+            folded_ref[at_rows, :] = folded
+            return carry
+
+        lax.fori_loop(0, rows // step, row_step, 0)
+        sum_ref[...] = jnp.sum(folded_ref[...].T, axis=0, keepdims=True)
 
     return call(
         kernel,
         "finish",
         [SMEM] + [VMEM] * (len(operands) - 1),
         [VMEM, VMEM],
-        [jax.ShapeDtypeStruct((rows, cols), jnp.float32), jax.ShapeDtypeStruct((1, LANES), jnp.float32)],
+        [jax.ShapeDtypeStruct((rows, cols), jnp.float32), jax.ShapeDtypeStruct((1, rows), jnp.float32)],
         operands,
         2.0,
+        [pltpu.VMEM((rows, LANES), jnp.float32)] * 4,
     )
 
 
@@ -432,16 +473,21 @@
         return lax.dynamic_slice_in_dim(values, atom_index * rows_dev, rows_dev, 0)
 
     my_freq = my_rows(panel_freq)
-    flag = jnp.stack([(group_index == goal).astype(jnp.int32), (column_index * part_cols).astype(jnp.int32)])
+    flag = jnp.stack(
+        [
+            (group_index == goal).astype(jnp.int32),
+            (column_index * part_cols).astype(jnp.int32),
+            atom_index.astype(jnp.int32),
+        ]
+    )
     elements, numerator = finish(
         flag,
         early,
         late,
-        my_rows(win_start)[:, None],
-        my_rows(win_len)[:, None],
-        my_freq[:, None],
+        win_start.reshape(atom_count, rows_dev),
+        win_len.reshape(atom_count, rows_dev),
+        panel_freq.reshape(atom_count, rows_dev),
         partner_freq[None, :],
-        column_index * part_cols,
         1.0 / math.sqrt(3 * atom_rows * atom_count),
     )
     holders = groups * 2
@@ -451,7 +497,7 @@
     ]
     while len(sums) > 1:
         sums = [sums[i] + sums[i + 1] for i in range(0, len(sums), 2)]
-    diffusivity = math.pi / 3.0 * sums[0][0, :rows_dev] / (my_freq * my_freq)
+    diffusivity = math.pi / 3.0 * sums[0][0] / (my_freq * my_freq)
     return (elements, diffusivity)
 
 

time: 67.6 us -> 63.7 us (0.942)
  local copies, waits for them, and re-layouts: 4.41 us -> 0.7 us
  waiting for transfers between devices: 7.7 us -> 8.57 us
    broadcast_in_dim x5 -> x0, local copies, waits for them, and re-layouts: 3.05 us -> none  [the longest x2 1.5 us: body(): my_rows(win_len)[:, None]]
    ppermute x3, waiting for transfers between devices: 2.17 us -> 3.45 us  [level_zero(): got = lax.ppermute(send, 'atoms', [(z, z ^ 1) for z in range(atom_count)])]
    ppermute x3, starting transfers between devices: 5.95 us -> 5.24 us  [level_zero(): got = lax.ppermute(send, 'atoms', [(z, z ^ 1) for z in range(atom_count)])]
  transfers between devices with their start and end apart: 19 -> 19, of which waited for: 5 -> 6; matrix products, arithmetic and copies ran while one was open for 6% -> 2% of each run, Pallas kernels for 23% -> 23%
where the time goes in v5:
time: 63.7 us; the launch traced here: 63.4 us
  starting transfers between devices  31 us (49%)
  Pallas kernels  20.5 us (32%)
  waiting for transfers between devices  8.57 us (13%)
  other arithmetic  1.73 us (3%)
  between operations  0.86 us (1%)
  local copies, waits for them, and re-layouts  0.7 us (1%)
    pallas_call x7, Pallas kernels, call(): pl.pallas_call(kernel, in_specs=in_specs, out_specs=out_specs, out_shape=...  20.5 us
    ppermute x3, starting transfers between devices, collected(): terms = terms + [lax.ppermute(sent, ('atoms', 'modes'), moves)]  10.8 us
    ppermute x3, starting transfers between devices, level_zero(): got = lax.ppermute(send, 'atoms', [(z, z ^ 1) for z in range(atom_count)])  5.24 us
    ppermute x1, starting transfers between devices, body(): lax.ppermute(tail, 'atoms', [(z, z + 1) for z in range(atom_count - 1)])  4.93 us
    ppermute x3, starting transfers between devices, body(): lax.ppermute(numerator, ('modes', 'sub'), [(i, i ^ code) for i in range(h...  4.73 us
    ppermute x3, starting transfers between devices, from_group(): return lax.ppermute(cells, 'modes', [(m ^ shift, m) for m in range(groups)])  3.52 us
    ppermute x3, waiting for transfers between devices, level_zero(): got = lax.ppermute(send, 'atoms', [(z, z ^ 1) for z in range(atom_count)])  3.45 us
    ppermute x3, waiting for transfers between devices, body(): lax.ppermute(numerator, ('modes', 'sub'), [(i, i ^ code) for i in range(h...  2.82 us
  transfers between devices with their start and end apart: 19, of which 6 were waited for; matrix products, arithmetic and copies ran while one was open for 2% of the time, Pallas kernels for 23%

profile of v5, /device:TPU:0, one launch (start us, length us, event | category | flops | bytes accessed | tf_op | source)
XLA Modules:
  0.0 63.4 jit_solution(4130114943012788203)
XLA Ops:
  0.7 3.6 %images.3 = (bf16[128,768]{1,0:T(8,128)(2,1)S(1)}, bf16[3,96,128]{2,1,0:T(8,128)(2,1)S(1)}, bf16[3,96,128]{2,1,0:T(8,128)(2,1)S(1)}) custom-call(s32[1]{0:T(128)} %bitcast.6.refs_0_, s32[16,768]{1,0:T(8,128)} %bitcast.17, s32[768]{0:T(1024)} %refs_2_.5, f32[9,16,768]{2,1,0:T(8,128)} %bitcast.14, bf16[3,768,128]{2,1,0:T(8,128)(2,1)} %refs_4_.5), custom_call_target="tpu_custom_call" | custom-call | flops 3520000000 | bytes 320000 | tf_op jit(solution)/shard_map/images/pallas_call | solution.py:29
  4.3 4.9 %collective-permute-start = (bf16[3,96,128]{2,1,0:T(8,128)(2,1)S(1)}, bf16[3,96,128]{2,1,0:T(8,128)(2,1)S(1)}, u32[]{:S(2)}, u32[]{:S(2)}) collective-permute-start(bf16[3,96,128]{2,1,0:T(8,128)(2,1)S(1)} %get-tuple-element.22), channel_id=1, source_target_pairs={{0,4},{4,8},{8,12},{1,5},{5,9},{9,13},{2,6},{6,10},{10,14},{3,7},{... | collective-permute-start | bytes 221192 | tf_op jit(solution)/shard_map/ppermute | solution.py:404
  9.2 1.3 %collective-permute-start.1 = (bf16[3,96,128]{2,1,0:T(8,128)(2,1)S(1)}, bf16[3,96,128]{2,1,0:T(8,128)(2,1)S(1)}, u32[]{:S(2)}, u32[]{:S(2)}) collective-permute-start(bf16[3,96,128]{2,1,0:T(8,128)(2,1)S(1)} %get-tuple-element.23), channel_id=1, source_target_pairs={{4,0},{8,4},{12,8},{5,1},{9,5},{13,9},{6,2},{10,6},{14,10},{7,3},{... | collective-permute-start | bytes 221192 | tf_op jit(solution)/shard_map/ppermute | solution.py:405
  10.6 3.3 %images.4 = (bf16[128,1536]{1,0:T(8,128)(2,1)}, bf16[64,1536]{1,0:T(8,128)(2,1)S(1)}) custom-call(s32[1]{0:T(128)} %bitcast.6.refs_0_, s32[16,768]{1,0:T(8,128)S(1)} %bitcast.18, s32[768]{0:T(1024)S(1)} %copy-done.7, f32[9,16,768]{2,1,0:T(8,128)S(1)} %bitcast.15, bf16[3,768,128]{2,1,0:T(8,128)(2,1)S(1)} %copy-done.4, ...), custom_call_target="tpu_custom_call" | custom-call | flops 3520000000 | bytes 320000 | tf_op jit(solution)/shard_map/images/pallas_call | solution.py:29
  13.8 0.0 collective-permute-start.3
  13.8 1.5 %collective-permute-start.5 = (bf16[64,1536]{1,0:T(8,128)(2,1)S(1)}, bf16[64,1536]{1,0:T(8,128)(2,1)S(1)}, u32[]{:S(2)}, u32[]{:S(2)}) collective-permute-start(bf16[64,1536]{1,0:T(8,128)(2,1)S(1)} %get-tuple-element.28), channel_id=1, source_target_pairs={{2,0},{0,2},{3,1},{1,3},{6,4},{4,6},{7,5},{5,7},{10,8},{8,10},{11,... | collective-permute-start | bytes 589832 | tf_op jit(solution)/shard_map/ppermute | solution.py:422
  15.3 0.0 collective-permute-done.refs_5_
  15.3 0.1 collective-permute-done.1.refs_6_
  15.5 4.3 %images.5 = (bf16[128,768]{1,0:T(8,128)(2,1)}, bf16[64,768]{1,0:T(8,128)(2,1)}, bf16[64,2304]{1,0:T(8,128)(2,1)}) custom-call(s32[1]{0:T(128)} %bitcast.6.refs_0_, s32[16,768]{1,0:T(8,128)S(1)} %bitcast.19, s32[768]{0:T(1024)S(1)} %copy-done.7, f32[9,16,768]{2,1,0:T(8,128)S(1)} %bitcast.16, bf16[3,768,128]{2,1,0:T(8,128)(2,1)S(1)} %copy-done.4, ...), custom_call_target="tpu_custom_call" | custom-call | flops 3520000000 | bytes 320000 | tf_op jit(solution)/shard_map/images/pallas_call | solution.py:29
  19.8 0.1 collective-permute-start.4
  19.9 0.1 pad_add_fusion.1.place_ref
  19.9 1.4 %collective-permute-start.2 = (bf16[64,768]{1,0:T(8,128)(2,1)}, bf16[64,768]{1,0:T(8,128)(2,1)S(1)}, u32[]{:S(2)}, u32[]{:S(2)}) collective-permute-start(bf16[64,768]{1,0:T(8,128)(2,1)} %get-tuple-element.26), channel_id=1, source_target_pairs={{2,0},{0,2},{3,1},{1,3},{6,4},{4,6},{7,5},{5,7},{10,8},{8,10},{11,... | collective-permute-start | bytes 294920 | tf_op jit(solution)/shard_map/ppermute | solution.py:422
  21.3 0.6 collective-permute-start.10
  22.0 0.0 collective-permute-done.5.refs_4_.refs_0_
  22.0 0.0 collective-permute-start.8
  22.0 0.0 collective-permute-done.4.refs_3_
  22.0 0.0 collective-permute-done.3.refs_2_
  22.0 3.6 %products.3 = (f32[128,640]{1,0:T(8,128)S(1)}, bf16[128,640]{1,0:T(8,128)(2,1)}) custom-call(s32[2]{0:T(128)S(1)} %pad_add_fusion.1.place_ref, bf16[3,768,640]{2,1,0:T(8,128)(2,1)S(1)} %copy-done, bf16[128,1536]{1,0:T(8,128)(2,1)} %get-tuple-element.25.refs_7_.refs_0_, bf16[128,768]{1,0:T(8,128)(2,1)} %get-tuple-element.27.refs_1_, ...), custom_call_target="tpu_custom_call" | custom-call | flops 6600000000 | bytes 600000 | tf_op jit(solution)/shard_map/products/pallas_call | solution.py:29
  25.6 0.2 collective-permute-done.2.refs_1_
  25.7 0.3 collective-permute-start.9
  26.1 2.6 %collective-permute-start.6 = (bf16[128,640]{1,0:T(8,128)(2,1)}, bf16[128,640]{1,0:T(8,128)(2,1)}, u32[]{:S(2)}, u32[]{:S(2)}) collective-permute-start(bf16[128,640]{1,0:T(8,128)(2,1)} %get-tuple-element.31), channel_id=1, source_target_pairs={{0,4},{4,0},{8,12},{12,8},{1,5},{5,1},{9,13},{13,9},{2,6},{6,2},{1... | collective-permute-start | bytes 491528 | tf_op jit(solution)/shard_map/ppermute | solution.py:439
  28.7 0.0 collective-permute-done.8.refs_2_
  28.7 0.0 collective-permute-done.9.refs_3_
  28.7 1.6 %products.4 = (f32[64,640]{1,0:T(8,128)S(1)}, bf16[64,640]{1,0:T(8,128)(2,1)S(1)}) custom-call(s32[2]{0:T(128)S(1)} %pad_add_fusion.1.place_ref, bf16[3,768,640]{2,1,0:T(8,128)(2,1)S(1)} %copy-done, bf16[64,1536]{1,0:T(8,128)(2,1)S(1)} %collective-permute-done.5.refs_4_.refs_0_, bf16[64,768]{1,0:T(8,128)(2,1)S(1)} %collective-permute-done.2.refs_1_, ...), custom_call_target="tpu_custom_call" | custom-call | flops 110000000 | bytes 10000 | tf_op jit(solution)/shard_map/products/pallas_call | solution.py:29
  30.3 0.7 %copy-done.1 = f32[64,640]{1,0:T(8,128)} copy-done((f32[64,640]{1,0:T(8,128)}, f32[64,640]{1,0:T(8,128)S(1)}, u32[]{:S(2)}) %copy-start.1) | copy-done | bytes 163864
  31.0 1.1 %collective-permute-start.11 = (bf16[64,640]{1,0:T(8,128)(2,1)S(1)}, bf16[64,640]{1,0:T(8,128)(2,1)S(1)}, u32[]{:S(2)}, u32[]{:S(2)}) collective-permute-start(bf16[64,640]{1,0:T(8,128)(2,1)S(1)} %get-tuple-element.35), channel_id=1, source_target_pairs={{0,4},{4,0},{8,12},{12,8},{1,5},{5,1},{9,13},{13,9},{2,6},{6,2},{1... | collective-permute-start | bytes 245768 | tf_op jit(solution)/shard_map/ppermute | solution.py:439
  32.1 0.0 collective-permute-done.10.refs_0_
  32.1 3.4 %collective-permute-done.11.refs_4_ = bf16[64,640]{1,0:T(8,128)(2,1)S(1)} collective-permute-done((bf16[64,640]{1,0:T(8,128)(2,1)S(1)}, bf16[64,640]{1,0:T(8,128)(2,1)S(1)}, u32[]{:S(2)}, u32[]{:S(2)}) %collective-permute-start.11) | collective-permute-done | bytes 81952 | tf_op jit(solution)/shard_map/ppermute | solution.py:439
  35.5 0.0 collective-permute-start.13
  35.5 0.0 collective-permute-done.6.refs_1_
  35.5 0.9 %add_convert_fusion = bf16[128,640]{1,0:T(8,128)(2,1)S(1)} fusion(f32[128,640]{1,0:T(8,128)S(1)} %get-tuple-element.30.refs_0_, bf16[128,640]{1,0:T(8,128)(2,1)} %collective-permute-done.6.refs_1_), kind=kLoop, calls=%fused_computation | loop fusion | flops 245760 | bytes 655360 | tf_op jit(solution)/shard_map/convert_element_type | solution.py:299
  36.5 1.3 %collective-permute-start.7 = (bf16[128,640]{1,0:T(8,128)(2,1)S(1)}, bf16[128,640]{1,0:T(8,128)(2,1)S(1)}, u32[]{:S(2)}, u32[]{:S(2)}) collective-permute-start(bf16[128,640]{1,0:T(8,128)(2,1)S(1)} %add_convert_fusion), channel_id=1, source_target_pairs={{2,10},{6,14},{8,0},{12,4},{3,11},{7,15},{9,1},{13,5},{18,26},{22,... | collective-permute-start | bytes 491528 | tf_op jit(solution)/shard_map/ppermute | solution.py:300
  37.8 0.0 collective-permute-done.13.refs_1_
  37.8 2.1 %products.5 = (f32[64,640]{1,0:T(8,128)S(1)}, bf16[64,640]{1,0:T(8,128)(2,1)S(1)}) custom-call(s32[2]{0:T(128)S(1)} %pad_add_fusion.1.place_ref, bf16[3,768,640]{2,1,0:T(8,128)(2,1)S(1)} %copy-done, bf16[64,2304]{1,0:T(8,128)(2,1)} %collective-permute-done.10.refs_0_, bf16[64,2304]{1,0:T(8,128)(2,1)} %collective-permute-done.13.refs_1_), custom_call_target="tpu_custom_call" | custom-call | flops 110000000 | bytes 10000 | tf_op jit(solution)/shard_map/products/pallas_call | solution.py:29
  39.9 1.5 %collective-permute-start.14 = (bf16[64,640]{1,0:T(8,128)(2,1)S(1)}, bf16[64,640]{1,0:T(8,128)(2,1)S(1)}, u32[]{:S(2)}, u32[]{:S(2)}) collective-permute-start(bf16[64,640]{1,0:T(8,128)(2,1)S(1)} %get-tuple-element.39), channel_id=1, source_target_pairs={{0,4},{4,0},{8,12},{12,8},{1,5},{5,1},{9,13},{13,9},{2,6},{6,2},{1... | collective-permute-start | bytes 245768 | tf_op jit(solution)/shard_map/ppermute | solution.py:439
  41.5 5.4 %collective-permute-start.12 = (bf16[64,640]{1,0:T(8,128)(2,1)S(1)}, bf16[64,640]{1,0:T(8,128)(2,1)S(1)}, u32[]{:S(2)}, u32[]{:S(2)}) collective-permute-start(bf16[64,640]{1,0:T(8,128)(2,1)S(1)} %add_convert_fusion.2), channel_id=1, source_target_pairs={{0,8},{4,12},{10,2},{14,6},{1,9},{5,13},{11,3},{15,7},{16,24},{20,... | collective-permute-start | bytes 245768 | tf_op jit(solution)/shard_map/ppermute | solution.py:300
  46.9 0.0 collective-permute-done.14.refs_7_
  47.0 4.1 %collective-permute-start.15 = (bf16[64,640]{1,0:T(8,128)(2,1)S(1)}, bf16[64,640]{1,0:T(8,128)(2,1)S(1)}, u32[]{:S(2)}, u32[]{:S(2)}) collective-permute-start(bf16[64,640]{1,0:T(8,128)(2,1)S(1)} %add_convert_fusion.1), channel_id=1, source_target_pairs={{0,8},{4,12},{10,2},{14,6},{1,9},{5,13},{11,3},{15,7},{16,24},{20,... | collective-permute-start | bytes 245768 | tf_op jit(solution)/shard_map/ppermute | solution.py:300
  51.1 0.1 pad_add_fusion.flag_ref
  51.2 0.0 collective-permute-done.12.refs_5_
  51.2 2.0 %collective-permute-done.15.refs_8_ = bf16[64,640]{1,0:T(8,128)(2,1)S(1)} collective-permute-done((bf16[64,640]{1,0:T(8,128)(2,1)S(1)}, bf16[64,640]{1,0:T(8,128)(2,1)S(1)}, u32[]{:S(2)}, u32[]{:S(2)}) %collective-permute-start.15) | collective-permute-done | bytes 81952 | tf_op jit(solution)/shard_map/ppermute | solution.py:300
  53.1 2.1 %finish.1 = (f32[128,640]{1,0:T(8,128)}, f32[1,128]{1,0:T(1,128)S(1)}) custom-call(s32[3]{0:T(128)S(1)} %pad_add_fusion.flag_ref, s32[4,128]{1,0:T(4,128)S(1)} %bitcast.20, s32[4,128]{1,0:T(4,128)S(1)} %bitcast.21, f32[4,128]{1,0:T(4,128)S(1)} %bitcast.13, f32[1,640]{1,0:T(1,128)S(1)} %broadcast_in_dim.6.partner_ref, ...), custom_call_target="tpu_custom_call" | custom-call | flops 2200000000 | bytes 200000 | tf_op jit(solution)/shard_map/finish/pallas_call | solution.py:29
  55.2 4.6 %collective-permute-start.17 = (f32[1,128]{1,0:T(1,128)S(1)}, f32[1,128]{1,0:T(1,128)S(1)}, u32[]{:S(2)}, u32[]{:S(2)}) collective-permute-start(f32[1,128]{1,0:T(1,128)S(1)} %get-tuple-element.41), channel_id=1, source_target_pairs={{0,2},{1,3},{2,0},{3,1},{4,6},{5,7},{6,4},{7,5},{8,10},{9,11},{10,... | collective-permute-start | bytes 1544 | tf_op jit(solution)/shard_map/ppermute | solution.py:495
  59.8 0.1 collective-permute-start.18
  60.0 0.0 collective-permute-done.16
  60.0 1.4 %collective-permute-done.17 = f32[1,128]{1,0:T(1,128)S(1)} collective-permute-done((f32[1,128]{1,0:T(1,128)S(1)}, f32[1,128]{1,0:T(1,128)S(1)}, u32[]{:S(2)}, u32[]{:S(2)}) %collective-permute-start.17) | collective-permute-done | bytes 544 | tf_op jit(solution)/shard_map/ppermute | solution.py:495
  61.3 1.4 %collective-permute-done.18 = f32[1,128]{1,0:T(1,128)S(1)} collective-permute-done((f32[1,128]{1,0:T(1,128)S(1)}, f32[1,128]{1,0:T(1,128)S(1)}, u32[]{:S(2)}, u32[]{:S(2)}) %collective-permute-start.18) | collective-permute-done | bytes 544 | tf_op jit(solution)/shard_map/ppermute | solution.py:495
  62.8 0.6 bitcast_divide_fusion
  (26 shorter events, 0.1 us)
Async XLA Ops:
  0.6 9.9 %copy-start.4 = (bf16[3,768,128]{2,1,0:T(8,128)(2,1)S(1)}, bf16[3,768,128]{2,1,0:T(8,128)(2,1)}, u32[]{:S(2)}) copy-start(bf16[3,768,128]{2,1,0:T(8,128)(2,1)} %refs_4_.5) | copy-start | bytes 1769476
  0.6 9.9 %copy-start.5 = (f32[9,768,16]{1,2,0:T(8,128)S(1)}, f32[9,768,16]{1,2,0:T(8,128)}, u32[]{:S(2)}) copy-start(f32[9,768,16]{1,2,0:T(8,128)} %param.11) | copy-start | bytes 1327108
  0.7 9.9 %copy-start.6 = (s32[768,16]{0,1:T(8,128)S(1)}, s32[768,16]{0,1:T(8,128)}, u32[]{:S(2)}) copy-start(s32[768,16]{0,1:T(8,128)} %param.12) | copy-start | bytes 147460
  0.7 9.9 %copy-start.7 = (s32[768]{0:T(1024)S(1)}, s32[768]{0:T(1024)}, u32[]{:S(2)}) copy-start(s32[768]{0:T(1024)} %refs_2_.5) | copy-start | bytes 9220
  4.3 11.0 %collective-permute-start = (bf16[3,96,128]{2,1,0:T(8,128)(2,1)S(1)}, bf16[3,96,128]{2,1,0:T(8,128)(2,1)S(1)}, u32[]{:S(2)}, u32[]{:S(2)}) collective-permute-start(bf16[3,96,128]{2,1,0:T(8,128)(2,1)S(1)} %get-tuple-element.22), channel_id=1, source_target_pairs={{0,4},{4,8},{8,12},{1,5},{5,9},{9,13},{2,6},{6,10},{10,14},{3,7},{... | collective-permute-start | bytes 221192 | tf_op jit(solution)/shard_map/ppermute | solution.py:404
  9.2 6.2 %collective-permute-start.1 = (bf16[3,96,128]{2,1,0:T(8,128)(2,1)S(1)}, bf16[3,96,128]{2,1,0:T(8,128)(2,1)S(1)}, u32[]{:S(2)}, u32[]{:S(2)}) collective-permute-start(bf16[3,96,128]{2,1,0:T(8,128)(2,1)S(1)} %get-tuple-element.23), channel_id=1, source_target_pairs={{4,0},{8,4},{12,8},{5,1},{9,5},{13,9},{6,2},{10,6},{14,10},{7,3},{... | collective-permute-start | bytes 221192 | tf_op jit(solution)/shard_map/ppermute | solution.py:405
  13.8 8.1 %collective-permute-start.3 = (bf16[128,1536]{1,0:T(8,128)(2,1)}, bf16[128,1536]{1,0:T(8,128)(2,1)}, u32[]{:S(2)}, u32[]{:S(2)}) collective-permute-start(bf16[128,1536]{1,0:T(8,128)(2,1)} %get-tuple-element.25.refs_7_.refs_0_), channel_id=1, source_target_pairs={{0,1},{1,0},{2,3},{3,2},{4,5},{5,4},{6,7},{7,6},{8,9},{9,8},{10,11... | collective-permute-start | bytes 1179656 | tf_op jit(solution)/shard_map/ppermute | solution.py:425
  13.8 8.1 %copy-start = (bf16[3,768,640]{2,1,0:T(8,128)(2,1)S(1)}, bf16[3,768,640]{2,1,0:T(8,128)(2,1)}, u32[]{:S(2)}) copy-start(bf16[3,768,640]{2,1,0:T(8,128)(2,1)} %partners_ref.5) | copy-start | bytes 8847364
  13.8 8.1 %collective-permute-start.5 = (bf16[64,1536]{1,0:T(8,128)(2,1)S(1)}, bf16[64,1536]{1,0:T(8,128)(2,1)S(1)}, u32[]{:S(2)}, u32[]{:S(2)}) collective-permute-start(bf16[64,1536]{1,0:T(8,128)(2,1)S(1)} %get-tuple-element.28), channel_id=1, source_target_pairs={{2,0},{0,2},{3,1},{1,3},{6,4},{4,6},{7,5},{5,7},{10,8},{8,10},{11,... | collective-permute-start | bytes 589832 | tf_op jit(solution)/shard_map/ppermute | solution.py:422
  19.8 2.2 %collective-permute-start.4 = (bf16[128,768]{1,0:T(8,128)(2,1)}, bf16[128,768]{1,0:T(8,128)(2,1)}, u32[]{:S(2)}, u32[]{:S(2)}) collective-permute-start(bf16[128,768]{1,0:T(8,128)(2,1)} %get-tuple-element.27.refs_1_), channel_id=1, source_target_pairs={{0,1},{1,0},{2,3},{3,2},{4,5},{5,4},{6,7},{7,6},{8,9},{9,8},{10,11... | collective-permute-start | bytes 589832 | tf_op jit(solution)/shard_map/ppermute | solution.py:425
  19.9 5.8 %collective-permute-start.2 = (bf16[64,768]{1,0:T(8,128)(2,1)}, bf16[64,768]{1,0:T(8,128)(2,1)S(1)}, u32[]{:S(2)}, u32[]{:S(2)}) collective-permute-start(bf16[64,768]{1,0:T(8,128)(2,1)} %get-tuple-element.26), channel_id=1, source_target_pairs={{2,0},{0,2},{3,1},{1,3},{6,4},{4,6},{7,5},{5,7},{10,8},{8,10},{11,... | collective-permute-start | bytes 294920 | tf_op jit(solution)/shard_map/ppermute | solution.py:422
  21.3 10.7 %collective-permute-start.10 = (bf16[64,2304]{1,0:T(8,128)(2,1)}, bf16[64,2304]{1,0:T(8,128)(2,1)}, u32[]{:S(2)}, u32[]{:S(2)}) collective-permute-start(bf16[64,2304]{1,0:T(8,128)(2,1)} %get-tuple-element.34), channel_id=1, source_target_pairs={{2,0},{0,2},{3,1},{1,3},{6,4},{4,6},{7,5},{5,7},{10,8},{8,10},{11,... | collective-permute-start | bytes 884744 | tf_op jit(solution)/shard_map/ppermute | solution.py:422
  22.0 6.7 %collective-permute-start.8 = (bf16[64,1536]{1,0:T(8,128)(2,1)S(1)}, bf16[64,1536]{1,0:T(8,128)(2,1)S(1)}, u32[]{:S(2)}, u32[]{:S(2)}) collective-permute-start(bf16[64,1536]{1,0:T(8,128)(2,1)S(1)} %collective-permute-done.5.refs_4_.refs_0_), channel_id=1, source_target_pairs={{0,1},{1,0},{2,3},{3,2},{4,5},{5,4},{6,7},{7,6},{8,9},{9,8},{10,11... | collective-permute-start | bytes 589832 | tf_op jit(solution)/shard_map/ppermute | solution.py:425
  25.6 10.0 %copy-start.10 = (f32[640]{0:T(1024)S(1)}, f32[640]{0:T(1024)}, u32[]{:S(2)}) copy-start(f32[640]{0:T(1024)} %param.15) | copy-start | bytes 7684
  25.7 3.0 %collective-permute-start.9 = (bf16[64,768]{1,0:T(8,128)(2,1)S(1)}, bf16[64,768]{1,0:T(8,128)(2,1)S(1)}, u32[]{:S(2)}, u32[]{:S(2)}) collective-permute-start(bf16[64,768]{1,0:T(8,128)(2,1)S(1)} %collective-permute-done.2.refs_1_), channel_id=1, source_target_pairs={{0,1},{1,0},{2,3},{3,2},{4,5},{5,4},{6,7},{7,6},{8,9},{9,8},{10,11... | collective-permute-start | bytes 294920 | tf_op jit(solution)/shard_map/ppermute | solution.py:425
  26.1 9.5 %collective-permute-start.6 = (bf16[128,640]{1,0:T(8,128)(2,1)}, bf16[128,640]{1,0:T(8,128)(2,1)}, u32[]{:S(2)}, u32[]{:S(2)}) collective-permute-start(bf16[128,640]{1,0:T(8,128)(2,1)} %get-tuple-element.31), channel_id=1, source_target_pairs={{0,4},{4,0},{8,12},{12,8},{1,5},{5,1},{9,13},{13,9},{2,6},{6,2},{1... | collective-permute-start | bytes 491528 | tf_op jit(solution)/shard_map/ppermute | solution.py:439
  30.3 0.7 %copy-start.1 = (f32[64,640]{1,0:T(8,128)}, f32[64,640]{1,0:T(8,128)S(1)}, u32[]{:S(2)}) copy-start(f32[64,640]{1,0:T(8,128)S(1)} %get-tuple-element.33.refs_3_) | copy-start | bytes 491524
  31.0 22.1 %copy-start.3 = (f32[512]{0:T(512)S(1)}, f32[512]{0:T(512)}, u32[]{:S(2)}) copy-start(f32[512]{0:T(512)} %param.14) | copy-start | bytes 6148
  31.0 22.1 %copy-start.8 = (s32[512]{0:T(512)S(1)}, s32[512]{0:T(512)}, u32[]{:S(2)}) copy-start(s32[512]{0:T(512)} %param.16) | copy-start | bytes 6148
  31.0 22.1 %copy-start.9 = (s32[512]{0:T(512)S(1)}, s32[512]{0:T(512)}, u32[]{:S(2)}) copy-start(s32[512]{0:T(512)} %param.17) | copy-start | bytes 6148
  31.0 10.5 %copy-start.2 = (f32[64,640]{1,0:T(8,128)S(1)}, f32[64,640]{1,0:T(8,128)}, u32[]{:S(2)}) copy-start(f32[64,640]{1,0:T(8,128)} %copy-done.1) | copy-start | bytes 491524
  31.0 4.5 %collective-permute-start.11 = (bf16[64,640]{1,0:T(8,128)(2,1)S(1)}, bf16[64,640]{1,0:T(8,128)(2,1)S(1)}, u32[]{:S(2)}, u32[]{:S(2)}) collective-permute-start(bf16[64,640]{1,0:T(8,128)(2,1)S(1)} %get-tuple-element.35), channel_id=1, source_target_pairs={{0,4},{4,0},{8,12},{12,8},{1,5},{5,1},{9,13},{13,9},{2,6},{6,2},{1... | collective-permute-start | bytes 245768 | tf_op jit(solution)/shard_map/ppermute | solution.py:439
  35.5 2.3 %collective-permute-start.13 = (bf16[64,2304]{1,0:T(8,128)(2,1)}, bf16[64,2304]{1,0:T(8,128)(2,1)}, u32[]{:S(2)}, u32[]{:S(2)}) collective-permute-start(bf16[64,2304]{1,0:T(8,128)(2,1)} %collective-permute-done.10.refs_0_), channel_id=1, source_target_pairs={{0,1},{1,0},{2,3},{3,2},{4,5},{5,4},{6,7},{7,6},{8,9},{9,8},{10,11... | collective-permute-start | bytes 884744 | tf_op jit(solution)/shard_map/ppermute | solution.py:425
  36.5 14.7 %collective-permute-start.7 = (bf16[128,640]{1,0:T(8,128)(2,1)S(1)}, bf16[128,640]{1,0:T(8,128)(2,1)S(1)}, u32[]{:S(2)}, u32[]{:S(2)}) collective-permute-start(bf16[128,640]{1,0:T(8,128)(2,1)S(1)} %add_convert_fusion), channel_id=1, source_target_pairs={{2,10},{6,14},{8,0},{12,4},{3,11},{7,15},{9,1},{13,5},{18,26},{22,... | collective-permute-start | bytes 491528 | tf_op jit(solution)/shard_map/ppermute | solution.py:300
  39.9 7.0 %collective-permute-start.14 = (bf16[64,640]{1,0:T(8,128)(2,1)S(1)}, bf16[64,640]{1,0:T(8,128)(2,1)S(1)}, u32[]{:S(2)}, u32[]{:S(2)}) collective-permute-start(bf16[64,640]{1,0:T(8,128)(2,1)S(1)} %get-tuple-element.39), channel_id=1, source_target_pairs={{0,4},{4,0},{8,12},{12,8},{1,5},{5,1},{9,13},{13,9},{2,6},{6,2},{1... | collective-permute-start | bytes 245768 | tf_op jit(solution)/shard_map/ppermute | solution.py:439
  41.5 9.7 %collective-permute-start.12 = (bf16[64,640]{1,0:T(8,128)(2,1)S(1)}, bf16[64,640]{1,0:T(8,128)(2,1)S(1)}, u32[]{:S(2)}, u32[]{:S(2)}) collective-permute-start(bf16[64,640]{1,0:T(8,128)(2,1)S(1)} %add_convert_fusion.2), channel_id=1, source_target_pairs={{0,8},{4,12},{10,2},{14,6},{1,9},{5,13},{11,3},{15,7},{16,24},{20,... | collective-permute-start | bytes 245768 | tf_op jit(solution)/shard_map/ppermute | solution.py:300
  47.0 6.1 %collective-permute-start.15 = (bf16[64,640]{1,0:T(8,128)(2,1)S(1)}, bf16[64,640]{1,0:T(8,128)(2,1)S(1)}, u32[]{:S(2)}, u32[]{:S(2)}) collective-permute-start(bf16[64,640]{1,0:T(8,128)(2,1)S(1)} %add_convert_fusion.1), channel_id=1, source_target_pairs={{0,8},{4,12},{10,2},{14,6},{1,9},{5,13},{11,3},{15,7},{16,24},{20,... | collective-permute-start | bytes 245768 | tf_op jit(solution)/shard_map/ppermute | solution.py:300
  55.2 4.7 %collective-permute-start.16 = (f32[1,128]{1,0:T(1,128)S(1)}, f32[1,128]{1,0:T(1,128)S(1)}, u32[]{:S(2)}, u32[]{:S(2)}) collective-permute-start(f32[1,128]{1,0:T(1,128)S(1)} %get-tuple-element.41), channel_id=1, source_target_pairs={{0,1},{1,0},{2,3},{3,2},{4,5},{5,4},{6,7},{7,6},{8,9},{9,8},{10,11... | collective-permute-start | bytes 1544 | tf_op jit(solution)/shard_map/ppermute | solution.py:495
  55.2 6.1 %collective-permute-start.17 = (f32[1,128]{1,0:T(1,128)S(1)}, f32[1,128]{1,0:T(1,128)S(1)}, u32[]{:S(2)}, u32[]{:S(2)}) collective-permute-start(f32[1,128]{1,0:T(1,128)S(1)} %get-tuple-element.41), channel_id=1, source_target_pairs={{0,2},{1,3},{2,0},{3,1},{4,6},{5,7},{6,4},{7,5},{8,10},{9,11},{10,... | collective-permute-start | bytes 1544 | tf_op jit(solution)/shard_map/ppermute | solution.py:495
  59.8 3.0 %collective-permute-start.18 = (f32[1,128]{1,0:T(1,128)S(1)}, f32[1,128]{1,0:T(1,128)S(1)}, u32[]{:S(2)}, u32[]{:S(2)}) collective-permute-start(f32[1,128]{1,0:T(1,128)S(1)} %get-tuple-element.41), channel_id=1, source_target_pairs={{0,3},{1,2},{2,1},{3,0},{4,7},{5,6},{6,5},{7,4},{8,11},{9,10},{10,... | collective-permute-start | bytes 1544 | tf_op jit(solution)/shard_map/ppermute | solution.py:495

commit v6 on v5

--- a/solution.py
+++ b/solution.py
@@ -95,33 +95,23 @@
     lax.fori_loop(0, SPAN // GROUP, group_step, 0)
 
 
-def images_of(blocks, base, panel, nbr, coef, count, halos=(), before=None, joined=False, edges=False, halved=False):
+def images_of(blocks, spot, panel, nbr, coef, count, halos=(), before=None, edges=False):
     rows, modes = panel.shape[1:]
     loads = before is None
     operands = [nbr, count, coef, panel]
     if loads:
         operands = [pltpu.with_memory_space_constraint(x, pltpu.HBM) for x in operands]
-    operands = [base, *operands, *halos]
+    operands = [spot, *operands, *halos]
     in_specs = [SMEM] + [HBM if loads else VMEM] * 4 + [VMEM] * len(halos)
-    old = 0
     if before is not None:
         operands.append(before)
-        in_specs.append(VMEM)
-        old = before.shape[1] // 3
-    ahead = old if joined else 0
-    width = ahead + len(blocks) * LANES
-    tail = halved and before is not None and not joined
+        in_specs.append(ANY)
+    width = len(blocks) * LANES
     out_shape = [jax.ShapeDtypeStruct((modes, 3 * width), jnp.bfloat16)]
     out_specs = [VMEM]
     if edges:
         out_shape += [jax.ShapeDtypeStruct((3, HALO, modes), jnp.bfloat16)] * 2
         out_specs += [ANY] * 2
-    if halved:
-        out_shape.append(jax.ShapeDtypeStruct((modes // 2, 3 * width), jnp.bfloat16))
-        out_specs.append(VMEM)
-        if tail:
-            out_shape.append(jax.ShapeDtypeStruct((modes // 2, 3 * (old + width)), jnp.bfloat16))
-            out_specs.append(VMEM)
     n_in, n_out = len(operands), len(out_shape)
 
     def pieces_of(block):
@@ -136,7 +126,8 @@
         return found
 
     def kernel(*refs):
-        base_ref, nbr_ref, count_ref, coef_ref, panel_ref = refs[:5]
+        spot_ref, nbr_ref, count_ref, coef_ref, panel_ref = refs[:5]
+        odd = spot_ref[1]
         outs = refs[n_in : n_in + n_out]
         window_ref, dense_ref, *scratch_refs = refs[n_in + n_out :]
         window_copies = []
@@ -161,19 +152,24 @@
                         panel_ref.at[:, pl.ds(source, length)], window_ref.at[place, :, pl.ds(at, length)], window_copies
                     )
             if edges:
-                start(panel_ref.at[:, pl.ds(0, HALO)], outs[1], window_copies)
-                start(panel_ref.at[:, pl.ds(rows - HALO, HALO)], outs[2], window_copies)
+                for turn, out in enumerate(outs[1:3]):
+                    at = pl.multiple_of(jnp.where(odd == turn, rows - HALO, 0), 32)
+                    start(panel_ref.at[:, pl.ds(at, HALO)], out, window_copies)
             for copy in copies:
                 copy.wait()
         else:
             for place, block in enumerate(blocks):
                 for which, source, at, length in pieces_of(block):
-                    source_ref = (panel_ref, *refs[5:])[which]
-                    window_ref[place, :, at : at + length, :] = source_ref[:, source : source + length, :]
+                    there = slice(source, source + length)
+                    if which == 0:
+                        found = panel_ref[:, there, :]
+                    else:
+                        found = jnp.where((odd == 1) == (which == 1), refs[5][:, there, :], refs[6][:, there, :])
+                    window_ref[place, :, at : at + length, :] = found
 
         def block_step(place, carry):
             first = (blocks[0] + place * (blocks[1] - blocks[0])) * LANES
-            build_block(pl.multiple_of(first, LANES), base_ref[0], nbr_ref, coef_ref, count_ref, dense_ref)
+            build_block(pl.multiple_of(first, LANES), spot_ref[0], nbr_ref, coef_ref, count_ref, dense_ref)
             if loads:
 
                 @pl.when(place == 0)
@@ -190,23 +186,11 @@
             for r in range(3):
                 image = both[:, 2 * r * LANES : (2 * r + 1) * LANES]
                 image = image + both[:, (2 * r + 1) * LANES : (2 * r + 2) * LANES]
-                at = pl.multiple_of(r * width + ahead + place * LANES, LANES)
+                at = pl.multiple_of(r * width + place * LANES, LANES)
                 outs[0][:, pl.ds(at, LANES)] = image.astype(jnp.bfloat16)
             return carry
 
         lax.fori_loop(0, len(blocks), block_step, 0)
-        if joined:
-            for r in range(3):
-                outs[0][:, r * width : r * width + old] = refs[n_in - 1][:, r * old : (r + 1) * old]
-        if halved:
-            span = modes // 2
-            half_ref = outs[-2] if tail else outs[-1]
-            half_ref[...] = outs[0][:span, :]
-            if tail:
-                for r in range(3):
-                    at = r * (old + width)
-                    outs[-1][:, at : at + old] = refs[n_in - 1][span:, r * old : (r + 1) * old]
-                    outs[-1][:, at + old : at + old + width] = outs[0][span:, r * width : (r + 1) * width]
 
     scratch = [
         pltpu.VMEM((len(blocks), 3, SPAN, modes), jnp.bfloat16),
@@ -228,7 +212,7 @@
     depth = partners.shape[1]
 
     def kernel(place_ref, partners_ref, *refs):
-        keep_ref, send_ref, left_ref, total_ref = refs[-4:]
+        keep_ref, send_ref, left_ref = refs[-3:]
         kept = place_ref[0] == place_ref[1]
         for who in range(2):
             at_rows = pl.ds(pl.multiple_of(jnp.where(kept == (who == 0), 0, rows), rows), rows)
@@ -237,19 +221,13 @@
                 width = len(blocks) * LANES
                 for r in range(3):
                     for spot, block, length in runs_of(blocks):
-                        at, to = r * width + spot * LANES, block * LANES
-                        left_ref[r, at_rows, to : to + length * LANES] = image_ref[:, at : at + length * LANES]
-
-        def component(r, carry):
-            total_ref[...] = total_ref[...] + jnp.dot(
-                left_ref[r], partners_ref[r], preferred_element_type=jnp.float32
-            )
-            return carry
-
-        total_ref[...] = jnp.zeros_like(total_ref)
-        lax.fori_loop(0, 3, component, 0)
-        keep_ref[...] = total_ref[:rows]
-        send_ref[...] = total_ref[rows:].astype(jnp.bfloat16)
+                        at, to = r * width + spot * LANES, r * depth + block * LANES
+                        left_ref[at_rows, to : to + length * LANES] = image_ref[:, at : at + length * LANES]
+        total = jnp.dot(
+            left_ref[...], partners_ref[...].reshape(3 * depth, cols), preferred_element_type=jnp.float32
+        )
+        keep_ref[...] = total[:rows]
+        send_ref[...] = total[rows:].astype(jnp.bfloat16)
 
     return call(
         kernel,
@@ -259,7 +237,7 @@
         [jax.ShapeDtypeStruct((rows, cols), jnp.float32), jax.ShapeDtypeStruct((rows, cols), jnp.bfloat16)],
         (place, partners, *mine, *theirs, *after),
         busy_us,
-        [pltpu.VMEM((3, 2 * rows, depth), jnp.bfloat16), pltpu.VMEM((2 * rows, cols), jnp.float32)],
+        [pltpu.VMEM((2 * rows, 3 * depth), jnp.bfloat16)],
     )
 
 
@@ -304,14 +282,12 @@
 
 def finish(flag, early, late, starts, lengths, freqs, partner_freq, norm_scale):
     rows, cols = early[0].shape
-    n_early, parts, n_late = len(early), len(late), len(late[0])
-    operands = [flag, starts, lengths, freqs, partner_freq, *early, *[t for part in late for t in part]]
+    n_early = len(early)
+    operands = [flag, starts, lengths, freqs, partner_freq, *early, *late]
     step = 16
 
     def kernel(flag_ref, starts_ref, lengths_ref, freqs_ref, partner_ref, *refs):
         out_ref, sum_ref, start_ref, end_ref, freq_ref, folded_ref = refs[-6:]
-        span = rows // parts
-
         def sums(some):
             total = some[0][...]
             for ref in some[1:]:
@@ -324,9 +300,7 @@
 
         @pl.when(flag_ref[0] == 0)
         def _():
-            for part in range(parts):
-                at = n_early + part * n_late
-                out_ref[part * span : (part + 1) * span, :] = sums(refs[at : at + n_late])
+            out_ref[...] = sums(refs[n_early:-6])
 
         def turned(row):
             return jnp.broadcast_to(row, (LANES, rows)).T
@@ -389,90 +363,74 @@
     part_cols = partners.shape[2]
     panel_total = win_start.shape[0]
     rows_dev = panel_total // atom_count
-    whole_halves = rows_dev == modes
 
     nbr = neighbors.T
     coef = bond_blocks.transpose(0, 2, 1)
-    base = (atom_index * atom_rows).astype(jnp.int32)[None]
+    spot = jnp.stack([(atom_index * atom_rows).astype(jnp.int32), (atom_index & 1).astype(jnp.int32)])
 
     last = atom_rows // LANES - 1
     middle = list(range(1, last))
-    chunks = [middle, [last, 0]]
-    shared = (base, mode_panel, nbr, coef, bond_count)
     cut = len(middle) // 2
-    opening, head, tail = images_of(middle[:cut], *shared, edges=True)
-    low_halo = lax.ppermute(tail, "atoms", [(z, z + 1) for z in range(atom_count - 1)])
-    high_halo = lax.ppermute(head, "atoms", [(z + 1, z) for z in range(atom_count - 1)])
-    first_images, *first_half = images_of(middle[cut:], *shared, before=opening, joined=True, halved=whole_halves)
-    edge_images, *rest_half = images_of(
-        [last, 0],
-        *shared,
-        halos=(low_halo, high_halo),
-        before=first_images if whole_halves else None,
-        halved=whole_halves,
-    )
-    if whole_halves:
-        pieces = [first_half[0], rest_half[0], rest_half[1]]
-    else:
-        pieces = [first_images, edge_images]
-
-    swap = [(0, 1), (1, 0)]
+    chunks = [middle[:cut], middle[cut:], [last, 0]]
+    shared = (spot, mode_panel, nbr, coef, bond_count)
+    near, edge_one, edge_two = images_of(chunks[0], *shared, edges=True)
+    pairs = [(z, z ^ 1) for z in range(atom_count)]
+    others = [(z, ((z + 1) ^ 1) - 1) for z in range(1, atom_count - 1)]
+    halos = (lax.ppermute(edge_one, "atoms", pairs), lax.ppermute(edge_two, "atoms", others))
+    middle_images = images_of(chunks[1], *shared, before=near)[0]
+    mine = [near, middle_images, images_of(chunks[2], *shared, halos=halos, before=middle_images)[0]]
 
     def from_group(cells, shift):
         return lax.ppermute(cells, "modes", [(m ^ shift, m) for m in range(groups)])
 
     def from_sibling(cells):
-        return lax.ppermute(cells, "sub", swap)
-
-    mine = [first_images, edge_images]
-    theirs = [from_sibling(first_images), from_sibling(edge_images)]
+        return lax.ppermute(cells, "sub", [(0, 1), (1, 0)])
+
+    theirs = [from_sibling(cells) for cells in mine]
+    far_all = {shift: [from_group(cells, shift) for cells in mine] for shift in range(1, groups)}
     half = half_index.astype(jnp.int32)
-    place = jnp.stack([half, (atom_index & 1).astype(jnp.int32)])
     goal = atom_index * groups // atom_count
 
-    far_all = {shift: [from_group(cells, shift) for cells in pieces] for shift in range(1, groups)}
-    if whole_halves:
-        def level_zero(lists, some_mine, some_theirs, after=()):
+    if rows_dev == modes and groups == 2:
+        place = jnp.stack([half, (atom_index & 1).astype(jnp.int32)])
+
+        def next_door(some_mine, some_theirs, after=()):
             keep, send = products_of(
-                lists, place, partners, some_mine, some_theirs, after, EARLY_US if after else LATE_US
+                chunks, place, partners, some_mine, some_theirs, after, EARLY_US if after else LATE_US
             )
-            got = lax.ppermute(send, "atoms", [(z, z ^ 1) for z in range(atom_count)])
-            return [keep, got]
-
-        early_zero = level_zero(chunks, mine, theirs, [far[0] for far in far_all.values()])
-        early = collected(early_zero, 1, 0)
+            return keep, lax.ppermute(send, "atoms", pairs)
+
+        far = far_all[1]
+        early = next_door(mine, theirs, far[:1])
+        second, kept = lax.optimization_barrier((far[1], early[0]))
+        third, kept = lax.optimization_barrier((far[2], kept))
+        early = (kept, early[1])
+        far = [far[0], second, third]
+        late = next_door(far, [from_sibling(cells) for cells in far])
+        sent = jnp.where(
+            group_index == goal,
+            late[0] + late[1].astype(jnp.float32),
+            early[0] + early[1].astype(jnp.float32),
+        ).astype(jnp.bfloat16)
+        swapped = lax.ppermute(sent, "atoms", [(z, z ^ 2) for z in range(atom_count)])
+        early, late = [*early, swapped], [*late, swapped]
     else:
-        cells, bit = settle(all_products(chunks, half, partners, mine, theirs).reshape(-1, rows_dev, part_cols), 0, rows_dev)
-        early = collected([cells], bit, 0)
-
-    late = None
-    for shift in range(1, groups):
-        far = far_all[shift]
-        if whole_halves:
-            first, early[0] = lax.optimization_barrier((far[1], early[0]))
-            far = [far[0], first, far[2]]
-            near = [from_sibling(far[0]), from_sibling(far[1])]
-            found = level_zero(chunks, far[:2], near)
-            second, found[1] = lax.optimization_barrier((far[2], found[1]))
-            terms = [
-                collected(found, 1, shift),
-                collected(level_zero([middle + [last, 0]], [second], [from_sibling(second)]), 1, shift),
-            ]
-        else:
-            cells, bit = settle(
-                all_products(chunks, half, partners, far, [from_sibling(cells) for cells in far]).reshape(-1, rows_dev, part_cols), 0, rows_dev
-            )
-            terms = [collected([cells], bit, shift)]
-        if late is None:
-            late = terms
-        else:
-            here = (group_index ^ shift) == goal
-            late = [[jnp.where(here, a, b) for a, b in zip(new, old)] for new, old in zip(terms, late)]
-
-    def my_rows(values):
-        return lax.dynamic_slice_in_dim(values, atom_index * rows_dev, rows_dev, 0)
-
-    my_freq = my_rows(panel_freq)
+
+        def settled(some_mine, some_theirs, shift):
+            cells = all_products(chunks, half, partners, some_mine, some_theirs)
+            cells, bit = settle(cells.reshape(-1, rows_dev, part_cols), 0, rows_dev)
+            return collected([cells], bit, shift)
+
+        early, late = settled(mine, theirs, 0), None
+        for shift, far in far_all.items():
+            terms = settled(far, [from_sibling(cells) for cells in far], shift)
+            if late is None:
+                late = terms
+            else:
+                here = (group_index ^ shift) == goal
+                late = [jnp.where(here, new, old) for new, old in zip(terms, late)]
+
+    my_freq = lax.dynamic_slice_in_dim(panel_freq, atom_index * rows_dev, rows_dev, 0)
     flag = jnp.stack(
         [
             (group_index == goal).astype(jnp.int32),

time: 63.7 us -> 62.2 us (0.976)
  starting transfers between devices: 31 us -> 17.6 us
  waiting for transfers between devices: 8.57 us -> 19.4 us
  local copies, waits for them, and re-layouts: 0.7 us -> 2.66 us
  Pallas kernels: 20.5 us -> 19.5 us
    ppermute x13 -> x11, starting transfers between devices: 22.7 us -> 10.7 us  [the longest x2 5.6 us: next_door(): return (keep, lax.ppermute(send, 'atoms', pairs))]
    ppermute x13 -> x11, waiting for transfers between devices: 5.57 us -> 12.5 us  [the longest x1 7.68 us: body(): lax.ppermute(sent, 'atoms', [(z, z ^ 2) for z in range(atom_count)])]
    ppermute x3, waiting for transfers between devices: 0.18 us -> 5.22 us  [from_group(): return lax.ppermute(cells, 'modes', [(m ^ shift, m) for m in range(groups)])]
    ppermute x3, starting transfers between devices: 4.73 us -> 1.86 us  [body(): lax.ppermute(numerator, ('modes', 'sub'), [(i, i ^ code) for i in range(h...]
    unnamed x22 -> x26, local copies, waits for them, and re-layouts: 0.7 us -> 2.66 us
    ppermute x3, starting transfers between devices: 3.52 us -> 5.03 us  [from_group(): return lax.ppermute(cells, 'modes', [(m ^ shift, m) for m in range(groups)])]
    ppermute x3, waiting for transfers between devices: 2.82 us -> 1.68 us  [body(): lax.ppermute(numerator, ('modes', 'sub'), [(i, i ^ code) for i in range(h...]
    pallas_call x7 -> x6, Pallas kernels: 20.5 us -> 19.5 us  [call(): pl.pallas_call(kernel, in_specs=in_specs, out_specs=out_specs, out_shape=...]
  transfers between devices with their start and end apart: 19 -> 17, of which waited for: 6 -> 5; matrix products, arithmetic and copies ran while one was open for 2% -> 0% of each run, Pallas kernels for 23% -> 22%
where the time goes in v6:
time: 62.2 us; the launch traced here: 61.9 us
  Pallas kernels  19.5 us (31%)
  waiting for transfers between devices  19.4 us (31%)
  starting transfers between devices  17.6 us (28%)
  local copies, waits for them, and re-layouts  2.66 us (4%)
  other arithmetic  1.94 us (3%)
  between operations  0.78 us (1%)
    pallas_call x6, Pallas kernels, call(): pl.pallas_call(kernel, in_specs=in_specs, out_specs=out_specs, out_shape=...  19.5 us
    ppermute x1, waiting for transfers between devices, body(): lax.ppermute(sent, 'atoms', [(z, z ^ 2) for z in range(atom_count)])  7.68 us
    ppermute x2, starting transfers between devices, next_door(): return (keep, lax.ppermute(send, 'atoms', pairs))  5.6 us
    ppermute x3, waiting for transfers between devices, from_group(): return lax.ppermute(cells, 'modes', [(m ^ shift, m) for m in range(groups)])  5.22 us
    ppermute x3, starting transfers between devices, from_group(): return lax.ppermute(cells, 'modes', [(m ^ shift, m) for m in range(groups)])  5.03 us
    ppermute x2, waiting for transfers between devices, next_door(): return (keep, lax.ppermute(send, 'atoms', pairs))  4.8 us
    unnamed x26, local copies, waits for them, and re-layouts  2.66 us
    ppermute x3, starting transfers between devices, body(): lax.ppermute(numerator, ('modes', 'sub'), [(i, i ^ code) for i in range(h...  1.86 us
  transfers between devices with their start and end apart: 17, of which 5 were waited for; matrix products, arithmetic and copies ran while one was open for 0% of the time, Pallas kernels for 22%

profile of v6, /device:TPU:0, one launch (start us, length us, event | category | flops | bytes accessed | tf_op | source)
XLA Modules:
  0.0 61.9 jit_solution(7949794394358388379)
XLA Ops:
  0.6 0.1 pad_add_fusion.1.refs_0_
  0.7 4.1 %images.3 = (bf16[128,768]{1,0:T(8,128)(2,1)S(1)}, bf16[3,96,128]{2,1,0:T(8,128)(2,1)S(1)}, bf16[3,96,128]{2,1,0:T(8,128)(2,1)S(1)}) custom-call(s32[2]{0:T(128)S(1)} %pad_add_fusion.1.refs_0_, s32[16,768]{1,0:T(8,128)} %bitcast.17, s32[768]{0:T(1024)} %refs_2_.5, f32[9,16,768]{2,1,0:T(8,128)} %bitcast.14, bf16[3,768,128]{2,1,0:T(8,128)(2,1)} %refs_4_.5), custom_call_target="tpu_custom_call" | custom-call | flops 3520000000 | bytes 320000 | tf_op jit(solution)/shard_map/images/pallas_call | solution.py:29
  4.8 0.0 copy-start.6
  4.8 3.0 %collective-permute-start.7 = (bf16[128,768]{1,0:T(8,128)(2,1)S(1)}, bf16[128,768]{1,0:T(8,128)(2,1)S(1)}, u32[]{:S(2)}, u32[]{:S(2)}) collective-permute-start(bf16[128,768]{1,0:T(8,128)(2,1)S(1)} %get-tuple-element.17.refs_5_.refs_0_), channel_id=1, source_target_pairs={{2,0},{0,2},{3,1},{1,3},{6,4},{4,6},{7,5},{5,7},{10,8},{8,10},{11,... | collective-permute-start | bytes 589832 | tf_op jit(solution)/shard_map/ppermute | solution.py:384
  7.8 0.0 collective-permute-start.4
  7.8 1.6 %collective-permute-start = (bf16[3,96,128]{2,1,0:T(8,128)(2,1)S(1)}, bf16[3,96,128]{2,1,0:T(8,128)(2,1)S(1)}, u32[]{:S(2)}, u32[]{:S(2)}) collective-permute-start(bf16[3,96,128]{2,1,0:T(8,128)(2,1)S(1)} %get-tuple-element.15), channel_id=1, source_target_pairs={{0,4},{4,0},{8,12},{12,8},{1,5},{5,1},{9,13},{13,9},{2,6},{6,2},{1... | collective-permute-start | bytes 221192 | tf_op jit(solution)/shard_map/ppermute | solution.py:379
  9.4 0.7 %collective-permute-start.1 = (bf16[3,96,128]{2,1,0:T(8,128)(2,1)S(1)}, bf16[3,96,128]{2,1,0:T(8,128)(2,1)S(1)}, u32[]{:S(2)}, u32[]{:S(2)}) collective-permute-start(bf16[3,96,128]{2,1,0:T(8,128)(2,1)S(1)} %get-tuple-element.16), channel_id=1, source_target_pairs={{4,8},{8,4},{5,9},{9,5},{6,10},{10,6},{7,11},{11,7},{20,24},{24,20... | collective-permute-start | bytes 221192 | tf_op jit(solution)/shard_map/ppermute | solution.py:379
  10.1 3.7 %images.4.refs_7_.refs_1_ = bf16[128,768]{1,0:T(8,128)(2,1)} custom-call(s32[2]{0:T(128)S(1)} %pad_add_fusion.1.refs_0_, s32[16,768]{1,0:T(8,128)S(1)} %bitcast.18, s32[768]{0:T(1024)S(1)} %copy-done.9, f32[9,16,768]{2,1,0:T(8,128)S(1)} %bitcast.15, bf16[3,768,128]{2,1,0:T(8,128)(2,1)S(1)} %copy-done.4, bf16[128,768]{1,0:T(8,128)(2,1)S(1)} %get-tuple-element.17.refs_5_.refs_0_), custom_call_target="tpu_custom_call" | custom-call | flops 3520000000 | bytes 320000 | tf_op jit(solution)/shard_map/images/pallas_call | solution.py:29
  13.8 0.2 collective-permute-start.5
  14.0 0.0 collective-permute-done.refs_5_
  14.0 0.0 collective-permute-done.1.refs_6_
  14.0 3.7 %images.5.refs_2_ = bf16[128,768]{1,0:T(8,128)(2,1)} custom-call(s32[2]{0:T(128)S(1)} %pad_add_fusion.1.refs_0_, s32[16,768]{1,0:T(8,128)S(1)} %bitcast.19, s32[768]{0:T(1024)S(1)} %copy-done.9, f32[9,16,768]{2,1,0:T(8,128)S(1)} %bitcast.16, bf16[3,768,128]{2,1,0:T(8,128)(2,1)S(1)} %copy-done.4, bf16[3,96,128]{2,1,0:T(8,128)(2,1)S(1)} %collective-permute-done.refs_5_, ...), custom_call_target="tpu_custom_call" | custom-call | flops 3520000000 | bytes 320000 | tf_op jit(solution)/shard_map/images/pallas_call | solution.py:29
  17.8 0.3 collective-permute-start.6
  18.1 0.5 collective-permute-start.3
  18.6 0.1 pad_add_fusion.2.place_ref
  18.7 0.0 collective-permute-done.5.refs_4_
  18.7 1.5 %collective-permute-start.2 = (bf16[128,768]{1,0:T(8,128)(2,1)}, bf16[128,768]{1,0:T(8,128)(2,1)S(1)}, u32[]{:S(2)}, u32[]{:S(2)}) collective-permute-start(bf16[128,768]{1,0:T(8,128)(2,1)} %images.5.refs_2_), channel_id=1, source_target_pairs={{2,0},{0,2},{3,1},{1,3},{6,4},{4,6},{7,5},{5,7},{10,8},{8,10},{11,... | collective-permute-start | bytes 589832 | tf_op jit(solution)/shard_map/ppermute | solution.py:384
  20.2 0.0 collective-permute-done.7.refs_6_.refs_0_
  20.2 0.0 collective-permute-start.9
  20.2 0.0 collective-permute-done.4.refs_3_
  20.2 0.0 collective-permute-done.6.refs_5_
  20.2 0.0 copy-start.7
  20.2 0.9 %copy-done.7 = bf16[128,768]{1,0:T(8,128)(2,1)S(1)} copy-done((bf16[128,768]{1,0:T(8,128)(2,1)S(1)}, bf16[128,768]{1,0:T(8,128)(2,1)}, u32[]{:S(2)}) %copy-start.7) | copy-done | bytes 196632
  21.1 3.1 %products.2 = (f32[128,640]{1,0:T(8,128)S(1)}, bf16[128,640]{1,0:T(8,128)(2,1)}) custom-call(s32[2]{0:T(128)S(1)} %pad_add_fusion.2.place_ref, bf16[3,768,640]{2,1,0:T(8,128)(2,1)S(1)} %copy-done, bf16[128,768]{1,0:T(8,128)(2,1)S(1)} %copy-done.7, bf16[128,768]{1,0:T(8,128)(2,1)} %images.4.refs_7_.refs_1_, bf16[128,768]{1,0:T(8,128)(2,1)} %images.5.refs_2_, ...), custom_call_target="tpu_custom_call" | custom-call | flops 6600000000 | bytes 600000 | tf_op jit(solution)/shard_map/products/pallas_call | solution.py:29
  24.3 0.0 copy-start.11
  24.3 1.8 %collective-permute-done.3.refs_1_ = bf16[128,768]{1,0:T(8,128)(2,1)} collective-permute-done((bf16[128,768]{1,0:T(8,128)(2,1)}, bf16[128,768]{1,0:T(8,128)(2,1)}, u32[]{:S(2)}, u32[]{:S(2)}) %collective-permute-start.3) | collective-permute-done | bytes 196640 | tf_op jit(solution)/shard_map/ppermute | solution.py:384
  26.1 3.4 %collective-permute-done.2.refs_2_ = bf16[128,768]{1,0:T(8,128)(2,1)S(1)} collective-permute-done((bf16[128,768]{1,0:T(8,128)(2,1)}, bf16[128,768]{1,0:T(8,128)(2,1)S(1)}, u32[]{:S(2)}, u32[]{:S(2)}) %collective-permute-start.2) | collective-permute-done | bytes 196640 | tf_op jit(solution)/shard_map/ppermute | solution.py:384
  29.5 0.0 collective-permute-start.11
  29.5 0.5 collective-permute-start.10
  30.0 4.2 %collective-permute-start.8 = (bf16[128,640]{1,0:T(8,128)(2,1)}, bf16[128,640]{1,0:T(8,128)(2,1)}, u32[]{:S(2)}, u32[]{:S(2)}) collective-permute-start(bf16[128,640]{1,0:T(8,128)(2,1)} %get-tuple-element.21), channel_id=1, source_target_pairs={{0,4},{4,0},{8,12},{12,8},{1,5},{5,1},{9,13},{13,9},{2,6},{6,2},{1... | collective-permute-start | bytes 491528 | tf_op jit(solution)/shard_map/ppermute | solution.py:401
  34.2 0.0 collective-permute-done.9.refs_3_
  34.2 2.8 %products.3 = (f32[128,640]{1,0:T(8,128)S(1)}, bf16[128,640]{1,0:T(8,128)(2,1)}) custom-call(s32[2]{0:T(128)S(1)} %pad_add_fusion.2.place_ref, bf16[3,768,640]{2,1,0:T(8,128)(2,1)S(1)} %copy-done, bf16[128,768]{1,0:T(8,128)(2,1)S(1)} %collective-permute-done.7.refs_6_.refs_0_, bf16[128,768]{1,0:T(8,128)(2,1)} %collective-permute-done.3.refs_1_, ...), custom_call_target="tpu_custom_call" | custom-call | flops 110000000 | bytes 10000 | tf_op jit(solution)/shard_map/products/pallas_call | solution.py:29
  37.0 0.7 %copy-done.1 = f32[128,640]{1,0:T(8,128)} copy-done((f32[128,640]{1,0:T(8,128)}, f32[128,640]{1,0:T(8,128)S(1)}, u32[]{:S(2)}) %copy-start.1) | copy-done | bytes 327704
  37.8 1.4 %collective-permute-start.12 = (bf16[128,640]{1,0:T(8,128)(2,1)}, bf16[128,640]{1,0:T(8,128)(2,1)S(1)}, u32[]{:S(2)}, u32[]{:S(2)}) collective-permute-start(bf16[128,640]{1,0:T(8,128)(2,1)} %get-tuple-element.25), channel_id=1, source_target_pairs={{0,4},{4,0},{8,12},{12,8},{1,5},{5,1},{9,13},{13,9},{2,6},{6,2},{1... | collective-permute-start | bytes 491528 | tf_op jit(solution)/shard_map/ppermute | solution.py:401
  39.2 4.8 %collective-permute-done.12.refs_4_ = bf16[128,640]{1,0:T(8,128)(2,1)S(1)} collective-permute-done((bf16[128,640]{1,0:T(8,128)(2,1)}, bf16[128,640]{1,0:T(8,128)(2,1)S(1)}, u32[]{:S(2)}, u32[]{:S(2)}) %collective-permute-start.12) | collective-permute-done | bytes 163872 | tf_op jit(solution)/shard_map/ppermute | solution.py:401
  44.0 1.1 %select_convert_fusion = bf16[128,640]{1,0:T(8,128)(2,1)S(1)} fusion(f32[128,640]{1,0:T(8,128)S(1)} %get-tuple-element.20.refs_0_, bf16[128,640]{1,0:T(8,128)(2,1)} %collective-permute-done.8.refs_1_, f32[128,640]{1,0:T(8,128)} %copy-done.1, bf16[128,640]{1,0:T(8,128)(2,1)S(1)} %collective-permute-done.12.refs_4_, pred[]{:T(512)S(6)} %eq.4), kind=kLoop, calls=%fused_computation | loop fusion | flops 491520 | bytes 1146881 | tf_op jit(solution)/shard_map/convert_element_type | solution.py:414
  45.1 1.8 %collective-permute-start.13 = (bf16[128,640]{1,0:T(8,128)(2,1)S(1)}, bf16[128,640]{1,0:T(8,128)(2,1)S(1)}, u32[]{:S(2)}, u32[]{:S(2)}) collective-permute-start(bf16[128,640]{1,0:T(8,128)(2,1)S(1)} %select_convert_fusion), channel_id=1, source_target_pairs={{0,8},{4,12},{8,0},{12,4},{1,9},{5,13},{9,1},{13,5},{2,10},{6,14},... | collective-permute-start | bytes 491528 | tf_op jit(solution)/shard_map/ppermute | solution.py:415
  46.9 0.1 pad_add_fusion.flag_ref
  47.0 7.7 %collective-permute-done.13.refs_2_.refs_5_ = bf16[128,640]{1,0:T(8,128)(2,1)S(1)} collective-permute-done((bf16[128,640]{1,0:T(8,128)(2,1)S(1)}, bf16[128,640]{1,0:T(8,128)(2,1)S(1)}, u32[]{:S(2)}, u32[]{:S(2)}) %collective-permute-start.13) | collective-permute-done | bytes 163872 | tf_op jit(solution)/shard_map/ppermute | solution.py:415
  54.7 0.0 copy-start.2
  54.7 1.0 %copy-done.2 = f32[128,640]{1,0:T(8,128)S(1)} copy-done((f32[128,640]{1,0:T(8,128)S(1)}, f32[128,640]{1,0:T(8,128)}, u32[]{:S(2)}) %copy-start.2) | copy-done | bytes 327704
  55.7 2.1 %finish.1 = (f32[128,640]{1,0:T(8,128)}, f32[1,128]{1,0:T(1,128)S(1)}) custom-call(s32[3]{0:T(128)S(1)} %pad_add_fusion.flag_ref, s32[4,128]{1,0:T(4,128)S(1)} %bitcast.20, s32[4,128]{1,0:T(4,128)S(1)} %bitcast.21, f32[4,128]{1,0:T(4,128)S(1)} %bitcast.13, f32[1,640]{1,0:T(1,128)S(1)} %broadcast_in_dim.3.partner_ref, ...), custom_call_target="tpu_custom_call" | custom-call | flops 2200000000 | bytes 200000 | tf_op jit(solution)/shard_map/finish/pallas_call | solution.py:29
  57.8 0.0 collective-permute-start.14
  57.8 0.5 collective-permute-start.15
  58.3 1.3 %collective-permute-start.16 = (f32[1,128]{1,0:T(1,128)S(1)}, f32[1,128]{1,0:T(1,128)S(1)}, u32[]{:S(2)}, u32[]{:S(2)}) collective-permute-start(f32[1,128]{1,0:T(1,128)S(1)} %get-tuple-element.27), channel_id=1, source_target_pairs={{0,3},{1,2},{2,1},{3,0},{4,7},{5,6},{6,5},{7,4},{8,11},{9,10},{10,... | collective-permute-start | bytes 1544 | tf_op jit(solution)/shard_map/ppermute | solution.py:453
  59.6 1.7 %collective-permute-done.15 = f32[1,128]{1,0:T(1,128)S(1)} collective-permute-done((f32[1,128]{1,0:T(1,128)S(1)}, f32[1,128]{1,0:T(1,128)S(1)}, u32[]{:S(2)}, u32[]{:S(2)}) %collective-permute-start.15) | collective-permute-done | bytes 544 | tf_op jit(solution)/shard_map/ppermute | solution.py:453
  61.3 0.0 collective-permute-done.16
  61.3 0.6 bitcast_divide_fusion
  (24 shorter events, 0.0 us)
Async XLA Ops:
  0.7 9.3 %copy-start.4 = (bf16[3,768,128]{2,1,0:T(8,128)(2,1)S(1)}, bf16[3,768,128]{2,1,0:T(8,128)(2,1)}, u32[]{:S(2)}) copy-start(bf16[3,768,128]{2,1,0:T(8,128)(2,1)} %refs_4_.5) | copy-start | bytes 1769476
  0.7 9.4 %copy-start.5 = (f32[9,768,16]{1,2,0:T(8,128)S(1)}, f32[9,768,16]{1,2,0:T(8,128)}, u32[]{:S(2)}) copy-start(f32[9,768,16]{1,2,0:T(8,128)} %param.11) | copy-start | bytes 1327108
  0.7 9.4 %copy-start.8 = (s32[768,16]{0,1:T(8,128)S(1)}, s32[768,16]{0,1:T(8,128)}, u32[]{:S(2)}) copy-start(s32[768,16]{0,1:T(8,128)} %param.12) | copy-start | bytes 147460
  0.7 9.4 %copy-start.9 = (s32[768]{0:T(1024)S(1)}, s32[768]{0:T(1024)}, u32[]{:S(2)}) copy-start(s32[768]{0:T(1024)} %refs_2_.5) | copy-start | bytes 9220
  4.8 9.0 %copy-start.6 = (bf16[128,768]{1,0:T(8,128)(2,1)}, bf16[128,768]{1,0:T(8,128)(2,1)S(1)}, u32[]{:S(2)}) copy-start(bf16[128,768]{1,0:T(8,128)(2,1)S(1)} %get-tuple-element.17.refs_5_.refs_0_) | copy-start | bytes 589828
  4.8 15.3 %collective-permute-start.7 = (bf16[128,768]{1,0:T(8,128)(2,1)S(1)}, bf16[128,768]{1,0:T(8,128)(2,1)S(1)}, u32[]{:S(2)}, u32[]{:S(2)}) collective-permute-start(bf16[128,768]{1,0:T(8,128)(2,1)S(1)} %get-tuple-element.17.refs_5_.refs_0_), channel_id=1, source_target_pairs={{2,0},{0,2},{3,1},{1,3},{6,4},{4,6},{7,5},{5,7},{10,8},{8,10},{11,... | collective-permute-start | bytes 589832 | tf_op jit(solution)/shard_map/ppermute | solution.py:384
  7.8 12.4 %collective-permute-start.4 = (bf16[128,768]{1,0:T(8,128)(2,1)S(1)}, bf16[128,768]{1,0:T(8,128)(2,1)}, u32[]{:S(2)}, u32[]{:S(2)}) collective-permute-start(bf16[128,768]{1,0:T(8,128)(2,1)S(1)} %get-tuple-element.17.refs_5_.refs_0_), channel_id=1, source_target_pairs={{0,1},{1,0},{2,3},{3,2},{4,5},{5,4},{6,7},{7,6},{8,9},{9,8},{10,11... | collective-permute-start | bytes 589832 | tf_op jit(solution)/shard_map/ppermute | solution.py:387
  7.8 6.2 %collective-permute-start = (bf16[3,96,128]{2,1,0:T(8,128)(2,1)S(1)}, bf16[3,96,128]{2,1,0:T(8,128)(2,1)S(1)}, u32[]{:S(2)}, u32[]{:S(2)}) collective-permute-start(bf16[3,96,128]{2,1,0:T(8,128)(2,1)S(1)} %get-tuple-element.15), channel_id=1, source_target_pairs={{0,4},{4,0},{8,12},{12,8},{1,5},{5,1},{9,13},{13,9},{2,6},{6,2},{1... | collective-permute-start | bytes 221192 | tf_op jit(solution)/shard_map/ppermute | solution.py:379
  9.4 4.7 %collective-permute-start.1 = (bf16[3,96,128]{2,1,0:T(8,128)(2,1)S(1)}, bf16[3,96,128]{2,1,0:T(8,128)(2,1)S(1)}, u32[]{:S(2)}, u32[]{:S(2)}) collective-permute-start(bf16[3,96,128]{2,1,0:T(8,128)(2,1)S(1)} %get-tuple-element.16), channel_id=1, source_target_pairs={{4,8},{8,4},{5,9},{9,5},{6,10},{10,6},{7,11},{11,7},{20,24},{24,20... | collective-permute-start | bytes 221192 | tf_op jit(solution)/shard_map/ppermute | solution.py:379
  13.8 6.4 %copy-start = (bf16[3,768,640]{2,1,0:T(8,128)(2,1)S(1)}, bf16[3,768,640]{2,1,0:T(8,128)(2,1)}, u32[]{:S(2)}) copy-start(bf16[3,768,640]{2,1,0:T(8,128)(2,1)} %partners_ref.3) | copy-start | bytes 8847364
  13.8 4.9 %collective-permute-start.5 = (bf16[128,768]{1,0:T(8,128)(2,1)}, bf16[128,768]{1,0:T(8,128)(2,1)}, u32[]{:S(2)}, u32[]{:S(2)}) collective-permute-start(bf16[128,768]{1,0:T(8,128)(2,1)} %images.4.refs_7_.refs_1_), channel_id=1, source_target_pairs={{0,1},{1,0},{2,3},{3,2},{4,5},{5,4},{6,7},{7,6},{8,9},{9,8},{10,11... | collective-permute-start | bytes 589832 | tf_op jit(solution)/shard_map/ppermute | solution.py:387
  17.8 2.4 %collective-permute-start.6 = (bf16[128,768]{1,0:T(8,128)(2,1)}, bf16[128,768]{1,0:T(8,128)(2,1)}, u32[]{:S(2)}, u32[]{:S(2)}) collective-permute-start(bf16[128,768]{1,0:T(8,128)(2,1)} %images.5.refs_2_), channel_id=1, source_target_pairs={{0,1},{1,0},{2,3},{3,2},{4,5},{5,4},{6,7},{7,6},{8,9},{9,8},{10,11... | collective-permute-start | bytes 589832 | tf_op jit(solution)/shard_map/ppermute | solution.py:387
  18.1 8.1 %collective-permute-start.3 = (bf16[128,768]{1,0:T(8,128)(2,1)}, bf16[128,768]{1,0:T(8,128)(2,1)}, u32[]{:S(2)}, u32[]{:S(2)}) collective-permute-start(bf16[128,768]{1,0:T(8,128)(2,1)} %images.4.refs_7_.refs_1_), channel_id=1, source_target_pairs={{2,0},{0,2},{3,1},{1,3},{6,4},{4,6},{7,5},{5,7},{10,8},{8,10},{11,... | collective-permute-start | bytes 589832 | tf_op jit(solution)/shard_map/ppermute | solution.py:384
  18.7 10.8 %collective-permute-start.2 = (bf16[128,768]{1,0:T(8,128)(2,1)}, bf16[128,768]{1,0:T(8,128)(2,1)S(1)}, u32[]{:S(2)}, u32[]{:S(2)}) collective-permute-start(bf16[128,768]{1,0:T(8,128)(2,1)} %images.5.refs_2_), channel_id=1, source_target_pairs={{2,0},{0,2},{3,1},{1,3},{6,4},{4,6},{7,5},{5,7},{10,8},{8,10},{11,... | collective-permute-start | bytes 589832 | tf_op jit(solution)/shard_map/ppermute | solution.py:384
  20.2 14.1 %collective-permute-start.9 = (bf16[128,768]{1,0:T(8,128)(2,1)S(1)}, bf16[128,768]{1,0:T(8,128)(2,1)S(1)}, u32[]{:S(2)}, u32[]{:S(2)}) collective-permute-start(bf16[128,768]{1,0:T(8,128)(2,1)S(1)} %collective-permute-done.7.refs_6_.refs_0_), channel_id=1, source_target_pairs={{0,1},{1,0},{2,3},{3,2},{4,5},{5,4},{6,7},{7,6},{8,9},{9,8},{10,11... | collective-permute-start | bytes 589832 | tf_op jit(solution)/shard_map/ppermute | solution.py:387
  20.2 0.9 %copy-start.7 = (bf16[128,768]{1,0:T(8,128)(2,1)S(1)}, bf16[128,768]{1,0:T(8,128)(2,1)}, u32[]{:S(2)}) copy-start(bf16[128,768]{1,0:T(8,128)(2,1)} %copy-done.6) | copy-start | bytes 589828
  24.3 22.7 %copy-start.12 = (f32[640]{0:T(1024)S(1)}, f32[640]{0:T(1024)}, u32[]{:S(2)}) copy-start(f32[640]{0:T(1024)} %param.15) | copy-start | bytes 7684
  24.3 30.4 %copy-start.3 = (f32[512]{0:T(512)S(1)}, f32[512]{0:T(512)}, u32[]{:S(2)}) copy-start(f32[512]{0:T(512)} %param.14) | copy-start | bytes 6148
  24.3 30.4 %copy-start.10 = (s32[512]{0:T(512)S(1)}, s32[512]{0:T(512)}, u32[]{:S(2)}) copy-start(s32[512]{0:T(512)} %param.16) | copy-start | bytes 6148
  24.3 30.4 %copy-start.11 = (s32[512]{0:T(512)S(1)}, s32[512]{0:T(512)}, u32[]{:S(2)}) copy-start(s32[512]{0:T(512)} %param.17) | copy-start | bytes 6148
  29.5 4.7 %collective-permute-start.11 = (bf16[128,768]{1,0:T(8,128)(2,1)S(1)}, bf16[128,768]{1,0:T(8,128)(2,1)S(1)}, u32[]{:S(2)}, u32[]{:S(2)}) collective-permute-start(bf16[128,768]{1,0:T(8,128)(2,1)S(1)} %collective-permute-done.2.refs_2_), channel_id=1, source_target_pairs={{0,1},{1,0},{2,3},{3,2},{4,5},{5,4},{6,7},{7,6},{8,9},{9,8},{10,11... | collective-permute-start | bytes 589832 | tf_op jit(solution)/shard_map/ppermute | solution.py:387
  29.5 4.7 %collective-permute-start.10 = (bf16[128,768]{1,0:T(8,128)(2,1)}, bf16[128,768]{1,0:T(8,128)(2,1)S(1)}, u32[]{:S(2)}, u32[]{:S(2)}) collective-permute-start(bf16[128,768]{1,0:T(8,128)(2,1)} %collective-permute-done.3.refs_1_), channel_id=1, source_target_pairs={{0,1},{1,0},{2,3},{3,2},{4,5},{5,4},{6,7},{7,6},{8,9},{9,8},{10,11... | collective-permute-start | bytes 589832 | tf_op jit(solution)/shard_map/ppermute | solution.py:387
  30.0 9.2 %collective-permute-start.8 = (bf16[128,640]{1,0:T(8,128)(2,1)}, bf16[128,640]{1,0:T(8,128)(2,1)}, u32[]{:S(2)}, u32[]{:S(2)}) collective-permute-start(bf16[128,640]{1,0:T(8,128)(2,1)} %get-tuple-element.21), channel_id=1, source_target_pairs={{0,4},{4,0},{8,12},{12,8},{1,5},{5,1},{9,13},{13,9},{2,6},{6,2},{1... | collective-permute-start | bytes 491528 | tf_op jit(solution)/shard_map/ppermute | solution.py:401
  37.0 0.7 %copy-start.1 = (f32[128,640]{1,0:T(8,128)}, f32[128,640]{1,0:T(8,128)S(1)}, u32[]{:S(2)}) copy-start(f32[128,640]{1,0:T(8,128)S(1)} %get-tuple-element.24.refs_3_) | copy-start | bytes 983044
  37.8 6.2 %collective-permute-start.12 = (bf16[128,640]{1,0:T(8,128)(2,1)}, bf16[128,640]{1,0:T(8,128)(2,1)S(1)}, u32[]{:S(2)}, u32[]{:S(2)}) collective-permute-start(bf16[128,640]{1,0:T(8,128)(2,1)} %get-tuple-element.25), channel_id=1, source_target_pairs={{0,4},{4,0},{8,12},{12,8},{1,5},{5,1},{9,13},{13,9},{2,6},{6,2},{1... | collective-permute-start | bytes 491528 | tf_op jit(solution)/shard_map/ppermute | solution.py:401
  45.1 9.6 %collective-permute-start.13 = (bf16[128,640]{1,0:T(8,128)(2,1)S(1)}, bf16[128,640]{1,0:T(8,128)(2,1)S(1)}, u32[]{:S(2)}, u32[]{:S(2)}) collective-permute-start(bf16[128,640]{1,0:T(8,128)(2,1)S(1)} %select_convert_fusion), channel_id=1, source_target_pairs={{0,8},{4,12},{8,0},{12,4},{1,9},{5,13},{9,1},{13,5},{2,10},{6,14},... | collective-permute-start | bytes 491528 | tf_op jit(solution)/shard_map/ppermute | solution.py:415
  54.7 1.0 %copy-start.2 = (f32[128,640]{1,0:T(8,128)S(1)}, f32[128,640]{1,0:T(8,128)}, u32[]{:S(2)}) copy-start(f32[128,640]{1,0:T(8,128)} %copy-done.1) | copy-start | bytes 983044
  57.8 1.9 %collective-permute-start.14 = (f32[1,128]{1,0:T(1,128)S(1)}, f32[1,128]{1,0:T(1,128)S(1)}, u32[]{:S(2)}, u32[]{:S(2)}) collective-permute-start(f32[1,128]{1,0:T(1,128)S(1)} %get-tuple-element.27), channel_id=1, source_target_pairs={{0,1},{1,0},{2,3},{3,2},{4,5},{5,4},{6,7},{7,6},{8,9},{9,8},{10,11... | collective-permute-start | bytes 1544 | tf_op jit(solution)/shard_map/ppermute | solution.py:453
  57.8 3.5 %collective-permute-start.15 = (f32[1,128]{1,0:T(1,128)S(1)}, f32[1,128]{1,0:T(1,128)S(1)}, u32[]{:S(2)}, u32[]{:S(2)}) collective-permute-start(f32[1,128]{1,0:T(1,128)S(1)} %get-tuple-element.27), channel_id=1, source_target_pairs={{0,2},{1,3},{2,0},{3,1},{4,6},{5,7},{6,4},{7,5},{8,10},{9,11},{10,... | collective-permute-start | bytes 1544 | tf_op jit(solution)/shard_map/ppermute | solution.py:453
  58.3 3.0 %collective-permute-start.16 = (f32[1,128]{1,0:T(1,128)S(1)}, f32[1,128]{1,0:T(1,128)S(1)}, u32[]{:S(2)}, u32[]{:S(2)}) collective-permute-start(f32[1,128]{1,0:T(1,128)S(1)} %get-tuple-element.27), channel_id=1, source_target_pairs={{0,3},{1,2},{2,1},{3,0},{4,7},{5,6},{6,5},{7,4},{8,11},{9,10},{10,... | collective-permute-start | bytes 1544 | tf_op jit(solution)/shard_map/ppermute | solution.py:453

commit v7 on v6

--- a/solution.py
+++ b/solution.py
@@ -11,7 +11,7 @@
 BONDS = 16
 LANES = 128
 SPAN = LANES + 2 * HALO
-GROUP = 16
+GROUP = 32
 VMEM_BYTES = 14 * 1024 * 1024
 
 lorentz_width = 0.05
@@ -95,19 +95,16 @@
     lax.fori_loop(0, SPAN // GROUP, group_step, 0)
 
 
-def images_of(blocks, spot, panel, nbr, coef, count, halos=(), before=None, edges=False):
+def images_of(blocks, spot, panel, nbr, coef, count, halos=(), before=(), edges=False):
     rows, modes = panel.shape[1:]
-    loads = before is None
+    loads = len(before) == 0
     operands = [nbr, count, coef, panel]
     if loads:
         operands = [pltpu.with_memory_space_constraint(x, pltpu.HBM) for x in operands]
-    operands = [spot, *operands, *halos]
-    in_specs = [SMEM] + [HBM if loads else VMEM] * 4 + [VMEM] * len(halos)
-    if before is not None:
-        operands.append(before)
-        in_specs.append(ANY)
+    operands = [spot, *operands, *halos, *before]
+    in_specs = [SMEM] + [HBM if loads else VMEM] * 4 + [VMEM] * len(halos) + [ANY] * len(before)
     width = len(blocks) * LANES
-    out_shape = [jax.ShapeDtypeStruct((modes, 3 * width), jnp.bfloat16)]
+    out_shape = [pltpu.VMEM((modes, 3 * width), jnp.bfloat16)]
     out_specs = [VMEM]
     if edges:
         out_shape += [jax.ShapeDtypeStruct((3, HALO, modes), jnp.bfloat16)] * 2
@@ -167,16 +164,11 @@
                         found = jnp.where((odd == 1) == (which == 1), refs[5][:, there, :], refs[6][:, there, :])
                     window_ref[place, :, at : at + length, :] = found
 
-        def block_step(place, carry):
-            first = (blocks[0] + place * (blocks[1] - blocks[0])) * LANES
-            build_block(pl.multiple_of(first, LANES), spot_ref[0], nbr_ref, coef_ref, count_ref, dense_ref)
-            if loads:
-
-                @pl.when(place == 0)
-                def _():
-                    for copy in window_copies:
-                        copy.wait()
-
+        for place, block in enumerate(blocks):
+            build_block(block * LANES, spot_ref[0], nbr_ref, coef_ref, count_ref, dense_ref)
+            if loads and place == 0:
+                for copy in window_copies:
+                    copy.wait()
             both = lax.dot_general(
                 window_ref[place].reshape(3 * SPAN, modes),
                 dense_ref[...],
@@ -186,11 +178,8 @@
             for r in range(3):
                 image = both[:, 2 * r * LANES : (2 * r + 1) * LANES]
                 image = image + both[:, (2 * r + 1) * LANES : (2 * r + 2) * LANES]
-                at = pl.multiple_of(r * width + place * LANES, LANES)
-                outs[0][:, pl.ds(at, LANES)] = image.astype(jnp.bfloat16)
-            return carry
-
-        lax.fori_loop(0, len(blocks), block_step, 0)
+                at = r * width + place * LANES
+                outs[0][:, at : at + LANES] = image.astype(jnp.bfloat16)
 
     scratch = [
         pltpu.VMEM((len(blocks), 3, SPAN, modes), jnp.bfloat16),
@@ -234,7 +223,7 @@
         "products",
         [SMEM] + [VMEM] * (1 + 2 * count) + [ANY] * len(after),
         [VMEM, VMEM],
-        [jax.ShapeDtypeStruct((rows, cols), jnp.float32), jax.ShapeDtypeStruct((rows, cols), jnp.bfloat16)],
+        [pltpu.VMEM((rows, cols), jnp.float32), pltpu.VMEM((rows, cols), jnp.bfloat16)],
         (place, partners, *mine, *theirs, *after),
         busy_us,
         [pltpu.VMEM((2 * rows, 3 * depth), jnp.bfloat16)],
@@ -377,8 +366,6 @@
     pairs = [(z, z ^ 1) for z in range(atom_count)]
     others = [(z, ((z + 1) ^ 1) - 1) for z in range(1, atom_count - 1)]
     halos = (lax.ppermute(edge_one, "atoms", pairs), lax.ppermute(edge_two, "atoms", others))
-    middle_images = images_of(chunks[1], *shared, before=near)[0]
-    mine = [near, middle_images, images_of(chunks[2], *shared, halos=halos, before=middle_images)[0]]
 
     def from_group(cells, shift):
         return lax.ppermute(cells, "modes", [(m ^ shift, m) for m in range(groups)])
@@ -386,8 +373,13 @@
     def from_sibling(cells):
         return lax.ppermute(cells, "sub", [(0, 1), (1, 0)])
 
+    far_all = {shift: [from_group(near, shift)] for shift in range(1, groups)}
+    middle_images = images_of(chunks[1], *shared, before=[near])[0]
+    before = [middle_images, *[far[0] for far in far_all.values()]]
+    mine = [near, middle_images, images_of(chunks[2], *shared, halos=halos, before=before)[0]]
+    for shift, far in far_all.items():
+        far += [from_group(cells, shift) for cells in mine[1:]]
     theirs = [from_sibling(cells) for cells in mine]
-    far_all = {shift: [from_group(cells, shift) for cells in mine] for shift in range(1, groups)}
     half = half_index.astype(jnp.int32)
     goal = atom_index * groups // atom_count
 
@@ -401,11 +393,10 @@
             return keep, lax.ppermute(send, "atoms", pairs)
 
         far = far_all[1]
-        early = next_door(mine, theirs, far[:1])
-        second, kept = lax.optimization_barrier((far[1], early[0]))
-        third, kept = lax.optimization_barrier((far[2], kept))
+        early = next_door(mine, theirs, far[:2])
+        third, kept = lax.optimization_barrier((far[2], early[0]))
         early = (kept, early[1])
-        far = [far[0], second, third]
+        far = [far[0], far[1], third]
         late = next_door(far, [from_sibling(cells) for cells in far])
         sent = jnp.where(
             group_index == goal,

time: 62.2 us -> 60.9 us (0.979)
  waiting for transfers between devices: 19.4 us -> 18.2 us
  starting transfers between devices: 17.6 us -> 16.9 us
  Pallas kernels: 19.5 us -> 20.2 us
    ppermute x3, waiting for transfers between devices: 5.22 us -> 1.36 us  [from_group(): return lax.ppermute(cells, 'modes', [(m ^ shift, m) for m in range(groups)])]
    ppermute x1, waiting for transfers between devices: 7.68 us -> 9.06 us  [body(): lax.ppermute(sent, 'atoms', [(z, z ^ 2) for z in range(atom_count)])]
    ppermute x1, starting transfers between devices: 1.84 us -> 0.85 us  [body(): lax.ppermute(sent, 'atoms', [(z, z ^ 2) for z in range(atom_count)])]
    ppermute x3, waiting for transfers between devices: 1.68 us -> 2.6 us  [body(): lax.ppermute(numerator, ('modes', 'sub'), [(i, i ^ code) for i in range(h...]
    pallas_call x6, Pallas kernels: 19.5 us -> 20.2 us  [call(): pl.pallas_call(kernel, in_specs=in_specs, out_specs=out_specs, out_shape=...]
  transfers between devices with their start and end apart: 17 -> 17, of which waited for: 5 -> 6; matrix products, arithmetic and copies ran while one was open for 0% -> 0% of each run, Pallas kernels for 22% -> 23%
where the time goes in v7:
time: 60.9 us; the launch traced here: 60.6 us
  Pallas kernels  20.2 us (33%)
  waiting for transfers between devices  18.2 us (30%)
  starting transfers between devices  16.9 us (28%)
  local copies, waits for them, and re-layouts  2.66 us (4%)
  other arithmetic  1.94 us (3%)
  between operations  0.77 us (1%)
    pallas_call x6, Pallas kernels, call(): pl.pallas_call(kernel, in_specs=in_specs, out_specs=out_specs, out_shape=...  20.2 us
    ppermute x1, waiting for transfers between devices, body(): lax.ppermute(sent, 'atoms', [(z, z ^ 2) for z in range(atom_count)])  9.06 us
    ppermute x2, starting transfers between devices, next_door(): return (keep, lax.ppermute(send, 'atoms', pairs))  5.81 us
    ppermute x2, waiting for transfers between devices, next_door(): return (keep, lax.ppermute(send, 'atoms', pairs))  5.12 us
    ppermute x3, starting transfers between devices, from_group(): return lax.ppermute(cells, 'modes', [(m ^ shift, m) for m in range(groups)])  5.03 us
    unnamed x26, local copies, waits for them, and re-layouts  2.66 us
    ppermute x3, waiting for transfers between devices, body(): lax.ppermute(numerator, ('modes', 'sub'), [(i, i ^ code) for i in range(h...  2.6 us
    ppermute x3, starting transfers between devices, body(): lax.ppermute(numerator, ('modes', 'sub'), [(i, i ^ code) for i in range(h...  1.86 us
  transfers between devices with their start and end apart: 17, of which 6 were waited for; matrix products, arithmetic and copies ran while one was open for 0% of the time, Pallas kernels for 23%

profile of v7, /device:TPU:0, one launch (start us, length us, event | category | flops | bytes accessed | tf_op | source)
XLA Modules:
  0.0 60.6 jit_solution(2713718498720688133)
XLA Ops:
  0.6 0.1 pad_add_fusion.1.refs_0_
  0.7 4.3 %images.3 = (bf16[128,768]{1,0:T(8,128)(2,1)S(1)}, bf16[3,96,128]{2,1,0:T(8,128)(2,1)S(1)}, bf16[3,96,128]{2,1,0:T(8,128)(2,1)S(1)}) custom-call(s32[2]{0:T(128)S(1)} %pad_add_fusion.1.refs_0_, s32[16,768]{1,0:T(8,128)} %bitcast.17, s32[768]{0:T(1024)} %refs_2_.5, f32[9,16,768]{2,1,0:T(8,128)} %bitcast.14, bf16[3,768,128]{2,1,0:T(8,128)(2,1)} %refs_4_.5), custom_call_target="tpu_custom_call" | custom-call | flops 3520000000 | bytes 320000 | tf_op jit(solution)/shard_map/images/pallas_call | solution.py:29
  5.0 0.0 copy-start.6
  5.0 3.0 %collective-permute-start.2 = (bf16[128,768]{1,0:T(8,128)(2,1)S(1)}, bf16[128,768]{1,0:T(8,128)(2,1)S(1)}, u32[]{:S(2)}, u32[]{:S(2)}) collective-permute-start(bf16[128,768]{1,0:T(8,128)(2,1)S(1)} %get-tuple-element.15.refs_5_.refs_0_), channel_id=1, source_target_pairs={{2,0},{0,2},{3,1},{1,3},{6,4},{4,6},{7,5},{5,7},{10,8},{8,10},{11,... | collective-permute-start | bytes 589832 | tf_op jit(solution)/shard_map/ppermute | solution.py:371
  8.0 1.6 %collective-permute-start = (bf16[3,96,128]{2,1,0:T(8,128)(2,1)S(1)}, bf16[3,96,128]{2,1,0:T(8,128)(2,1)S(1)}, u32[]{:S(2)}, u32[]{:S(2)}) collective-permute-start(bf16[3,96,128]{2,1,0:T(8,128)(2,1)S(1)} %get-tuple-element.13), channel_id=1, source_target_pairs={{0,4},{4,0},{8,12},{12,8},{1,5},{5,1},{9,13},{13,9},{2,6},{6,2},{1... | collective-permute-start | bytes 221192 | tf_op jit(solution)/shard_map/ppermute | solution.py:368
  9.6 0.7 %collective-permute-start.1 = (bf16[3,96,128]{2,1,0:T(8,128)(2,1)S(1)}, bf16[3,96,128]{2,1,0:T(8,128)(2,1)S(1)}, u32[]{:S(2)}, u32[]{:S(2)}) collective-permute-start(bf16[3,96,128]{2,1,0:T(8,128)(2,1)S(1)} %get-tuple-element.14), channel_id=1, source_target_pairs={{4,8},{8,4},{5,9},{9,5},{6,10},{10,6},{7,11},{11,7},{20,24},{24,20... | collective-permute-start | bytes 221192 | tf_op jit(solution)/shard_map/ppermute | solution.py:368
  10.3 3.9 %images.4.refs_7_.refs_1_ = bf16[128,768]{1,0:T(8,128)(2,1)} custom-call(s32[2]{0:T(128)S(1)} %pad_add_fusion.1.refs_0_, s32[16,768]{1,0:T(8,128)S(1)} %bitcast.18, s32[768]{0:T(1024)S(1)} %copy-done.9, f32[9,16,768]{2,1,0:T(8,128)S(1)} %bitcast.15, bf16[3,768,128]{2,1,0:T(8,128)(2,1)S(1)} %copy-done.4, bf16[128,768]{1,0:T(8,128)(2,1)S(1)} %get-tuple-element.15.refs_5_.refs_0_), custom_call_target="tpu_custom_call" | custom-call | flops 3520000000 | bytes 320000 | tf_op jit(solution)/shard_map/images/pallas_call | solution.py:29
  14.2 0.6 collective-permute-start.7
  14.8 0.0 collective-permute-start.5
  14.8 0.0 collective-permute-done.refs_5_
  14.8 0.5 collective-permute-start.4
  15.3 0.0 collective-permute-done.1.refs_6_
  15.3 0.0 collective-permute-done.2.refs_8_.refs_6_.refs_0_
  15.3 3.9 %images.5.refs_2_ = bf16[128,768]{1,0:T(8,128)(2,1)} custom-call(s32[2]{0:T(128)S(1)} %pad_add_fusion.1.refs_0_, s32[16,768]{1,0:T(8,128)S(1)} %bitcast.19, s32[768]{0:T(1024)S(1)} %copy-done.9, f32[9,16,768]{2,1,0:T(8,128)S(1)} %bitcast.16, bf16[3,768,128]{2,1,0:T(8,128)(2,1)S(1)} %copy-done.4, bf16[3,96,128]{2,1,0:T(8,128)(2,1)S(1)} %collective-permute-done.refs_5_, ...), custom_call_target="tpu_custom_call" | custom-call | flops 3520000000 | bytes 320000 | tf_op jit(solution)/shard_map/images/pallas_call | solution.py:29
  19.3 0.1 collective-permute-start.6
  19.3 0.1 pad_add_fusion.2.place_ref
  19.4 1.5 %collective-permute-start.3 = (bf16[128,768]{1,0:T(8,128)(2,1)}, bf16[128,768]{1,0:T(8,128)(2,1)S(1)}, u32[]{:S(2)}, u32[]{:S(2)}) collective-permute-start(bf16[128,768]{1,0:T(8,128)(2,1)} %images.5.refs_2_), channel_id=1, source_target_pairs={{2,0},{0,2},{3,1},{1,3},{6,4},{4,6},{7,5},{5,7},{10,8},{8,10},{11,... | collective-permute-start | bytes 589832 | tf_op jit(solution)/shard_map/ppermute | solution.py:371
  20.9 0.0 collective-permute-done.7.refs_7_.refs_1_
  20.9 0.2 collective-permute-start.9
  21.1 0.3 collective-permute-start.10
  21.4 0.0 collective-permute-done.4.refs_3_
  21.4 0.0 collective-permute-done.6.refs_5_
  21.4 0.0 copy-start.7
  21.4 0.9 %copy-done.7 = bf16[128,768]{1,0:T(8,128)(2,1)S(1)} copy-done((bf16[128,768]{1,0:T(8,128)(2,1)S(1)}, bf16[128,768]{1,0:T(8,128)(2,1)}, u32[]{:S(2)}) %copy-start.7) | copy-done | bytes 196632
  22.3 3.1 %products.2 = (f32[128,640]{1,0:T(8,128)S(1)}, bf16[128,640]{1,0:T(8,128)(2,1)}) custom-call(s32[2]{0:T(128)S(1)} %pad_add_fusion.2.place_ref, bf16[3,768,640]{2,1,0:T(8,128)(2,1)S(1)} %copy-done, bf16[128,768]{1,0:T(8,128)(2,1)S(1)} %copy-done.7, bf16[128,768]{1,0:T(8,128)(2,1)} %images.4.refs_7_.refs_1_, bf16[128,768]{1,0:T(8,128)(2,1)} %images.5.refs_2_, ...), custom_call_target="tpu_custom_call" | custom-call | flops 6600000000 | bytes 600000 | tf_op jit(solution)/shard_map/products/pallas_call | solution.py:29
  25.5 0.0 copy-start.11
  25.5 1.4 %collective-permute-done.3.refs_2_ = bf16[128,768]{1,0:T(8,128)(2,1)S(1)} collective-permute-done((bf16[128,768]{1,0:T(8,128)(2,1)}, bf16[128,768]{1,0:T(8,128)(2,1)S(1)}, u32[]{:S(2)}, u32[]{:S(2)}) %collective-permute-start.3) | collective-permute-done | bytes 196640 | tf_op jit(solution)/shard_map/ppermute | solution.py:371
  26.9 0.0 collective-permute-start.11
  26.9 4.4 %collective-permute-start.8 = (bf16[128,640]{1,0:T(8,128)(2,1)}, bf16[128,640]{1,0:T(8,128)(2,1)}, u32[]{:S(2)}, u32[]{:S(2)}) collective-permute-start(bf16[128,640]{1,0:T(8,128)(2,1)} %get-tuple-element.18), channel_id=1, source_target_pairs={{0,4},{4,0},{8,12},{12,8},{1,5},{5,1},{9,13},{13,9},{2,6},{6,2},{1... | collective-permute-start | bytes 491528 | tf_op jit(solution)/shard_map/ppermute | solution.py:393
  31.3 0.0 collective-permute-done.9.refs_3_
  31.3 0.0 collective-permute-done.11.refs_5_
  31.3 2.8 %products.3 = (f32[128,640]{1,0:T(8,128)S(1)}, bf16[128,640]{1,0:T(8,128)(2,1)}) custom-call(s32[2]{0:T(128)S(1)} %pad_add_fusion.2.place_ref, bf16[3,768,640]{2,1,0:T(8,128)(2,1)S(1)} %copy-done, bf16[128,768]{1,0:T(8,128)(2,1)S(1)} %collective-permute-done.2.refs_8_.refs_6_.refs_0_, bf16[128,768]{1,0:T(8,128)(2,1)} %collective-permute-done.7.refs_7_.refs_1_, ...), custom_call_target="tpu_custom_call" | custom-call | flops 110000000 | bytes 10000 | tf_op jit(solution)/shard_map/products/pallas_call | solution.py:29
  34.1 0.7 %copy-done.1 = f32[128,640]{1,0:T(8,128)} copy-done((f32[128,640]{1,0:T(8,128)}, f32[128,640]{1,0:T(8,128)S(1)}, u32[]{:S(2)}) %copy-start.1) | copy-done | bytes 327704
  34.8 1.4 %collective-permute-start.12 = (bf16[128,640]{1,0:T(8,128)(2,1)}, bf16[128,640]{1,0:T(8,128)(2,1)S(1)}, u32[]{:S(2)}, u32[]{:S(2)}) collective-permute-start(bf16[128,640]{1,0:T(8,128)(2,1)} %get-tuple-element.21), channel_id=1, source_target_pairs={{0,4},{4,0},{8,12},{12,8},{1,5},{5,1},{9,13},{13,9},{2,6},{6,2},{1... | collective-permute-start | bytes 491528 | tf_op jit(solution)/shard_map/ppermute | solution.py:393
  36.2 0.2 collective-permute-done.8.refs_1_
  36.4 4.9 %collective-permute-done.12.refs_4_ = bf16[128,640]{1,0:T(8,128)(2,1)S(1)} collective-permute-done((bf16[128,640]{1,0:T(8,128)(2,1)}, bf16[128,640]{1,0:T(8,128)(2,1)S(1)}, u32[]{:S(2)}, u32[]{:S(2)}) %collective-permute-start.12) | collective-permute-done | bytes 163872 | tf_op jit(solution)/shard_map/ppermute | solution.py:393
  41.3 1.1 %select_convert_fusion = bf16[128,640]{1,0:T(8,128)(2,1)S(1)} fusion(f32[128,640]{1,0:T(8,128)S(1)} %get-tuple-element.17.refs_0_, bf16[128,640]{1,0:T(8,128)(2,1)} %collective-permute-done.8.refs_1_, f32[128,640]{1,0:T(8,128)} %copy-done.1, bf16[128,640]{1,0:T(8,128)(2,1)S(1)} %collective-permute-done.12.refs_4_, pred[]{:T(512)S(6)} %eq.4), kind=kLoop, calls=%fused_computation | loop fusion | flops 491520 | bytes 1146881 | tf_op jit(solution)/shard_map/convert_element_type | solution.py:405
  42.5 0.8 %collective-permute-start.13 = (bf16[128,640]{1,0:T(8,128)(2,1)S(1)}, bf16[128,640]{1,0:T(8,128)(2,1)S(1)}, u32[]{:S(2)}, u32[]{:S(2)}) collective-permute-start(bf16[128,640]{1,0:T(8,128)(2,1)S(1)} %select_convert_fusion), channel_id=1, source_target_pairs={{0,8},{4,12},{8,0},{12,4},{1,9},{5,13},{9,1},{13,5},{2,10},{6,14},... | collective-permute-start | bytes 491528 | tf_op jit(solution)/shard_map/ppermute | solution.py:406
  43.3 0.1 pad_add_fusion.flag_ref
  43.4 9.1 %collective-permute-done.13.refs_2_.refs_5_ = bf16[128,640]{1,0:T(8,128)(2,1)S(1)} collective-permute-done((bf16[128,640]{1,0:T(8,128)(2,1)S(1)}, bf16[128,640]{1,0:T(8,128)(2,1)S(1)}, u32[]{:S(2)}, u32[]{:S(2)}) %collective-permute-start.13) | collective-permute-done | bytes 163872 | tf_op jit(solution)/shard_map/ppermute | solution.py:406
  52.5 0.0 copy-start.2
  52.5 1.0 %copy-done.2 = f32[128,640]{1,0:T(8,128)S(1)} copy-done((f32[128,640]{1,0:T(8,128)S(1)}, f32[128,640]{1,0:T(8,128)}, u32[]{:S(2)}) %copy-start.2) | copy-done | bytes 327704
  53.4 2.1 %finish.1 = (f32[128,640]{1,0:T(8,128)}, f32[1,128]{1,0:T(1,128)S(1)}) custom-call(s32[3]{0:T(128)S(1)} %pad_add_fusion.flag_ref, s32[4,128]{1,0:T(4,128)S(1)} %bitcast.20, s32[4,128]{1,0:T(4,128)S(1)} %bitcast.21, f32[4,128]{1,0:T(4,128)S(1)} %bitcast.13, f32[1,640]{1,0:T(1,128)S(1)} %broadcast_in_dim.3.partner_ref, ...), custom_call_target="tpu_custom_call" | custom-call | flops 2200000000 | bytes 200000 | tf_op jit(solution)/shard_map/finish/pallas_call | solution.py:29
  55.5 1.5 %collective-permute-start.15 = (f32[1,128]{1,0:T(1,128)S(1)}, f32[1,128]{1,0:T(1,128)S(1)}, u32[]{:S(2)}, u32[]{:S(2)}) collective-permute-start(f32[1,128]{1,0:T(1,128)S(1)} %get-tuple-element.23), channel_id=1, source_target_pairs={{0,2},{1,3},{2,0},{3,1},{4,6},{5,7},{6,4},{7,5},{8,10},{9,11},{10,... | collective-permute-start | bytes 1544 | tf_op jit(solution)/shard_map/ppermute | solution.py:444
  57.0 0.4 collective-permute-start.16
  57.4 1.7 %collective-permute-done.15 = f32[1,128]{1,0:T(1,128)S(1)} collective-permute-done((f32[1,128]{1,0:T(1,128)S(1)}, f32[1,128]{1,0:T(1,128)S(1)}, u32[]{:S(2)}, u32[]{:S(2)}) %collective-permute-start.15) | collective-permute-done | bytes 544 | tf_op jit(solution)/shard_map/ppermute | solution.py:444
  59.1 0.9 %collective-permute-done.16 = f32[1,128]{1,0:T(1,128)S(1)} collective-permute-done((f32[1,128]{1,0:T(1,128)S(1)}, f32[1,128]{1,0:T(1,128)S(1)}, u32[]{:S(2)}, u32[]{:S(2)}) %collective-permute-start.16) | collective-permute-done | bytes 544 | tf_op jit(solution)/shard_map/ppermute | solution.py:444
  60.0 0.6 bitcast_divide_fusion
  (24 shorter events, 0.0 us)
Async XLA Ops:
  0.7 9.6 %copy-start.4 = (bf16[3,768,128]{2,1,0:T(8,128)(2,1)S(1)}, bf16[3,768,128]{2,1,0:T(8,128)(2,1)}, u32[]{:S(2)}) copy-start(bf16[3,768,128]{2,1,0:T(8,128)(2,1)} %refs_4_.5) | copy-start | bytes 1769476
  0.7 9.6 %copy-start.5 = (f32[9,768,16]{1,2,0:T(8,128)S(1)}, f32[9,768,16]{1,2,0:T(8,128)}, u32[]{:S(2)}) copy-start(f32[9,768,16]{1,2,0:T(8,128)} %param.11) | copy-start | bytes 1327108
  0.7 9.6 %copy-start.8 = (s32[768,16]{0,1:T(8,128)S(1)}, s32[768,16]{0,1:T(8,128)}, u32[]{:S(2)}) copy-start(s32[768,16]{0,1:T(8,128)} %param.12) | copy-start | bytes 147460
  0.7 9.6 %copy-start.9 = (s32[768]{0:T(1024)S(1)}, s32[768]{0:T(1024)}, u32[]{:S(2)}) copy-start(s32[768]{0:T(1024)} %refs_2_.5) | copy-start | bytes 9220
  5.0 9.8 %copy-start.6 = (bf16[128,768]{1,0:T(8,128)(2,1)}, bf16[128,768]{1,0:T(8,128)(2,1)S(1)}, u32[]{:S(2)}) copy-start(bf16[128,768]{1,0:T(8,128)(2,1)S(1)} %get-tuple-element.15.refs_5_.refs_0_) | copy-start | bytes 589828
  5.0 10.3 %collective-permute-start.2 = (bf16[128,768]{1,0:T(8,128)(2,1)S(1)}, bf16[128,768]{1,0:T(8,128)(2,1)S(1)}, u32[]{:S(2)}, u32[]{:S(2)}) collective-permute-start(bf16[128,768]{1,0:T(8,128)(2,1)S(1)} %get-tuple-element.15.refs_5_.refs_0_), channel_id=1, source_target_pairs={{2,0},{0,2},{3,1},{1,3},{6,4},{4,6},{7,5},{5,7},{10,8},{8,10},{11,... | collective-permute-start | bytes 589832 | tf_op jit(solution)/shard_map/ppermute | solution.py:371
  8.0 6.8 %collective-permute-start = (bf16[3,96,128]{2,1,0:T(8,128)(2,1)S(1)}, bf16[3,96,128]{2,1,0:T(8,128)(2,1)S(1)}, u32[]{:S(2)}, u32[]{:S(2)}) collective-permute-start(bf16[3,96,128]{2,1,0:T(8,128)(2,1)S(1)} %get-tuple-element.13), channel_id=1, source_target_pairs={{0,4},{4,0},{8,12},{12,8},{1,5},{5,1},{9,13},{13,9},{2,6},{6,2},{1... | collective-permute-start | bytes 221192 | tf_op jit(solution)/shard_map/ppermute | solution.py:368
  9.6 5.7 %collective-permute-start.1 = (bf16[3,96,128]{2,1,0:T(8,128)(2,1)S(1)}, bf16[3,96,128]{2,1,0:T(8,128)(2,1)S(1)}, u32[]{:S(2)}, u32[]{:S(2)}) collective-permute-start(bf16[3,96,128]{2,1,0:T(8,128)(2,1)S(1)} %get-tuple-element.14), channel_id=1, source_target_pairs={{4,8},{8,4},{5,9},{9,5},{6,10},{10,6},{7,11},{11,7},{20,24},{24,20... | collective-permute-start | bytes 221192 | tf_op jit(solution)/shard_map/ppermute | solution.py:368
  14.2 7.2 %copy-start = (bf16[3,768,640]{2,1,0:T(8,128)(2,1)S(1)}, bf16[3,768,640]{2,1,0:T(8,128)(2,1)}, u32[]{:S(2)}) copy-start(bf16[3,768,640]{2,1,0:T(8,128)(2,1)} %partners_ref.3) | copy-start | bytes 8847364
  14.2 6.6 %collective-permute-start.7 = (bf16[128,768]{1,0:T(8,128)(2,1)}, bf16[128,768]{1,0:T(8,128)(2,1)}, u32[]{:S(2)}, u32[]{:S(2)}) collective-permute-start(bf16[128,768]{1,0:T(8,128)(2,1)} %images.4.refs_7_.refs_1_), channel_id=1, source_target_pairs={{2,0},{0,2},{3,1},{1,3},{6,4},{4,6},{7,5},{5,7},{10,8},{8,10},{11,... | collective-permute-start | bytes 589832 | tf_op jit(solution)/shard_map/ppermute | solution.py:371
  14.8 6.3 %collective-permute-start.5 = (bf16[128,768]{1,0:T(8,128)(2,1)}, bf16[128,768]{1,0:T(8,128)(2,1)}, u32[]{:S(2)}, u32[]{:S(2)}) collective-permute-start(bf16[128,768]{1,0:T(8,128)(2,1)} %images.4.refs_7_.refs_1_), channel_id=1, source_target_pairs={{0,1},{1,0},{2,3},{3,2},{4,5},{5,4},{6,7},{7,6},{8,9},{9,8},{10,11... | collective-permute-start | bytes 589832 | tf_op jit(solution)/shard_map/ppermute | solution.py:374
  14.8 6.6 %collective-permute-start.4 = (bf16[128,768]{1,0:T(8,128)(2,1)S(1)}, bf16[128,768]{1,0:T(8,128)(2,1)}, u32[]{:S(2)}, u32[]{:S(2)}) collective-permute-start(bf16[128,768]{1,0:T(8,128)(2,1)S(1)} %get-tuple-element.15.refs_5_.refs_0_), channel_id=1, source_target_pairs={{0,1},{1,0},{2,3},{3,2},{4,5},{5,4},{6,7},{7,6},{8,9},{9,8},{10,11... | collective-permute-start | bytes 589832 | tf_op jit(solution)/shard_map/ppermute | solution.py:374
  19.3 2.1 %collective-permute-start.6 = (bf16[128,768]{1,0:T(8,128)(2,1)}, bf16[128,768]{1,0:T(8,128)(2,1)}, u32[]{:S(2)}, u32[]{:S(2)}) collective-permute-start(bf16[128,768]{1,0:T(8,128)(2,1)} %images.5.refs_2_), channel_id=1, source_target_pairs={{0,1},{1,0},{2,3},{3,2},{4,5},{5,4},{6,7},{7,6},{8,9},{9,8},{10,11... | collective-permute-start | bytes 589832 | tf_op jit(solution)/shard_map/ppermute | solution.py:374
  19.4 7.5 %collective-permute-start.3 = (bf16[128,768]{1,0:T(8,128)(2,1)}, bf16[128,768]{1,0:T(8,128)(2,1)S(1)}, u32[]{:S(2)}, u32[]{:S(2)}) collective-permute-start(bf16[128,768]{1,0:T(8,128)(2,1)} %images.5.refs_2_), channel_id=1, source_target_pairs={{2,0},{0,2},{3,1},{1,3},{6,4},{4,6},{7,5},{5,7},{10,8},{8,10},{11,... | collective-permute-start | bytes 589832 | tf_op jit(solution)/shard_map/ppermute | solution.py:371
  20.9 10.4 %collective-permute-start.9 = (bf16[128,768]{1,0:T(8,128)(2,1)S(1)}, bf16[128,768]{1,0:T(8,128)(2,1)S(1)}, u32[]{:S(2)}, u32[]{:S(2)}) collective-permute-start(bf16[128,768]{1,0:T(8,128)(2,1)S(1)} %collective-permute-done.2.refs_8_.refs_6_.refs_0_), channel_id=1, source_target_pairs={{0,1},{1,0},{2,3},{3,2},{4,5},{5,4},{6,7},{7,6},{8,9},{9,8},{10,11... | collective-permute-start | bytes 589832 | tf_op jit(solution)/shard_map/ppermute | solution.py:374
  21.1 10.2 %collective-permute-start.10 = (bf16[128,768]{1,0:T(8,128)(2,1)}, bf16[128,768]{1,0:T(8,128)(2,1)S(1)}, u32[]{:S(2)}, u32[]{:S(2)}) collective-permute-start(bf16[128,768]{1,0:T(8,128)(2,1)} %collective-permute-done.7.refs_7_.refs_1_), channel_id=1, source_target_pairs={{0,1},{1,0},{2,3},{3,2},{4,5},{5,4},{6,7},{7,6},{8,9},{9,8},{10,11... | collective-permute-start | bytes 589832 | tf_op jit(solution)/shard_map/ppermute | solution.py:374
  21.4 0.9 %copy-start.7 = (bf16[128,768]{1,0:T(8,128)(2,1)S(1)}, bf16[128,768]{1,0:T(8,128)(2,1)}, u32[]{:S(2)}) copy-start(bf16[128,768]{1,0:T(8,128)(2,1)} %copy-done.6) | copy-start | bytes 589828
  25.5 17.8 %copy-start.12 = (f32[640]{0:T(1024)S(1)}, f32[640]{0:T(1024)}, u32[]{:S(2)}) copy-start(f32[640]{0:T(1024)} %param.15) | copy-start | bytes 7684
  25.5 27.0 %copy-start.3 = (f32[512]{0:T(512)S(1)}, f32[512]{0:T(512)}, u32[]{:S(2)}) copy-start(f32[512]{0:T(512)} %param.14) | copy-start | bytes 6148
  25.5 27.0 %copy-start.10 = (s32[512]{0:T(512)S(1)}, s32[512]{0:T(512)}, u32[]{:S(2)}) copy-start(s32[512]{0:T(512)} %param.16) | copy-start | bytes 6148
  25.5 27.0 %copy-start.11 = (s32[512]{0:T(512)S(1)}, s32[512]{0:T(512)}, u32[]{:S(2)}) copy-start(s32[512]{0:T(512)} %param.17) | copy-start | bytes 6148
  26.9 4.4 %collective-permute-start.11 = (bf16[128,768]{1,0:T(8,128)(2,1)S(1)}, bf16[128,768]{1,0:T(8,128)(2,1)S(1)}, u32[]{:S(2)}, u32[]{:S(2)}) collective-permute-start(bf16[128,768]{1,0:T(8,128)(2,1)S(1)} %collective-permute-done.3.refs_2_), channel_id=1, source_target_pairs={{0,1},{1,0},{2,3},{3,2},{4,5},{5,4},{6,7},{7,6},{8,9},{9,8},{10,11... | collective-permute-start | bytes 589832 | tf_op jit(solution)/shard_map/ppermute | solution.py:374
  26.9 9.6 %collective-permute-start.8 = (bf16[128,640]{1,0:T(8,128)(2,1)}, bf16[128,640]{1,0:T(8,128)(2,1)}, u32[]{:S(2)}, u32[]{:S(2)}) collective-permute-start(bf16[128,640]{1,0:T(8,128)(2,1)} %get-tuple-element.18), channel_id=1, source_target_pairs={{0,4},{4,0},{8,12},{12,8},{1,5},{5,1},{9,13},{13,9},{2,6},{6,2},{1... | collective-permute-start | bytes 491528 | tf_op jit(solution)/shard_map/ppermute | solution.py:393
  34.1 0.7 %copy-start.1 = (f32[128,640]{1,0:T(8,128)}, f32[128,640]{1,0:T(8,128)S(1)}, u32[]{:S(2)}) copy-start(f32[128,640]{1,0:T(8,128)S(1)} %get-tuple-element.20.refs_3_) | copy-start | bytes 983044
  34.8 6.5 %collective-permute-start.12 = (bf16[128,640]{1,0:T(8,128)(2,1)}, bf16[128,640]{1,0:T(8,128)(2,1)S(1)}, u32[]{:S(2)}, u32[]{:S(2)}) collective-permute-start(bf16[128,640]{1,0:T(8,128)(2,1)} %get-tuple-element.21), channel_id=1, source_target_pairs={{0,4},{4,0},{8,12},{12,8},{1,5},{5,1},{9,13},{13,9},{2,6},{6,2},{1... | collective-permute-start | bytes 491528 | tf_op jit(solution)/shard_map/ppermute | solution.py:393
  42.5 10.0 %collective-permute-start.13 = (bf16[128,640]{1,0:T(8,128)(2,1)S(1)}, bf16[128,640]{1,0:T(8,128)(2,1)S(1)}, u32[]{:S(2)}, u32[]{:S(2)}) collective-permute-start(bf16[128,640]{1,0:T(8,128)(2,1)S(1)} %select_convert_fusion), channel_id=1, source_target_pairs={{0,8},{4,12},{8,0},{12,4},{1,9},{5,13},{9,1},{13,5},{2,10},{6,14},... | collective-permute-start | bytes 491528 | tf_op jit(solution)/shard_map/ppermute | solution.py:406
  52.5 1.0 %copy-start.2 = (f32[128,640]{1,0:T(8,128)S(1)}, f32[128,640]{1,0:T(8,128)}, u32[]{:S(2)}) copy-start(f32[128,640]{1,0:T(8,128)} %copy-done.1) | copy-start | bytes 983044
  55.5 1.9 %collective-permute-start.14 = (f32[1,128]{1,0:T(1,128)S(1)}, f32[1,128]{1,0:T(1,128)S(1)}, u32[]{:S(2)}, u32[]{:S(2)}) collective-permute-start(f32[1,128]{1,0:T(1,128)S(1)} %get-tuple-element.23), channel_id=1, source_target_pairs={{0,1},{1,0},{2,3},{3,2},{4,5},{5,4},{6,7},{7,6},{8,9},{9,8},{10,11... | collective-permute-start | bytes 1544 | tf_op jit(solution)/shard_map/ppermute | solution.py:444
  55.5 3.5 %collective-permute-start.15 = (f32[1,128]{1,0:T(1,128)S(1)}, f32[1,128]{1,0:T(1,128)S(1)}, u32[]{:S(2)}, u32[]{:S(2)}) collective-permute-start(f32[1,128]{1,0:T(1,128)S(1)} %get-tuple-element.23), channel_id=1, source_target_pairs={{0,2},{1,3},{2,0},{3,1},{4,6},{5,7},{6,4},{7,5},{8,10},{9,11},{10,... | collective-permute-start | bytes 1544 | tf_op jit(solution)/shard_map/ppermute | solution.py:444
  57.0 3.0 %collective-permute-start.16 = (f32[1,128]{1,0:T(1,128)S(1)}, f32[1,128]{1,0:T(1,128)S(1)}, u32[]{:S(2)}, u32[]{:S(2)}) collective-permute-start(f32[1,128]{1,0:T(1,128)S(1)} %get-tuple-element.23), channel_id=1, source_target_pairs={{0,3},{1,2},{2,1},{3,0},{4,7},{5,6},{6,5},{7,4},{8,11},{9,10},{10,... | collective-permute-start | bytes 1544 | tf_op jit(solution)/shard_map/ppermute | solution.py:444

commit v8 on v7

--- a/solution.py
+++ b/solution.py
@@ -11,7 +11,7 @@
 BONDS = 16
 LANES = 128
 SPAN = LANES + 2 * HALO
-GROUP = 32
+GROUP = 16
 VMEM_BYTES = 14 * 1024 * 1024
 
 lorentz_width = 0.05
@@ -26,6 +26,10 @@
 
 
 def call(kernel, name, in_specs, out_specs, out_shape, operands, busy_us, scratch=()):
+    operands = [
+        pltpu.with_memory_space_constraint(x, spec.memory_space) if spec is VMEM or spec is HBM else x
+        for spec, x in zip(in_specs, operands)
+    ]
     return pl.pallas_call(
         kernel,
         in_specs=in_specs,
@@ -98,10 +102,7 @@
 def images_of(blocks, spot, panel, nbr, coef, count, halos=(), before=(), edges=False):
     rows, modes = panel.shape[1:]
     loads = len(before) == 0
-    operands = [nbr, count, coef, panel]
-    if loads:
-        operands = [pltpu.with_memory_space_constraint(x, pltpu.HBM) for x in operands]
-    operands = [spot, *operands, *halos, *before]
+    operands = [spot, nbr, count, coef, panel, *halos, *before]
     in_specs = [SMEM] + [HBM if loads else VMEM] * 4 + [VMEM] * len(halos) + [ANY] * len(before)
     width = len(blocks) * LANES
     out_shape = [pltpu.VMEM((modes, 3 * width), jnp.bfloat16)]

time: 60.9 us -> 60.3 us (level)
  transfers between devices with their start and end apart: 17 -> 17, of which waited for: 6 -> 6; matrix products, arithmetic and copies ran while one was open for 0% -> 0% of each run, Pallas kernels for 23% -> 22%
where the time goes in v8:
time: 60.3 us; the launch traced here: 60 us
  Pallas kernels  19.6 us (33%)
  waiting for transfers between devices  18.2 us (30%)
  starting transfers between devices  16.8 us (28%)
  local copies, waits for them, and re-layouts  2.66 us (4%)
  other arithmetic  1.94 us (3%)
  between operations  0.77 us (1%)
    pallas_call x6, Pallas kernels, call(): pl.pallas_call(kernel, in_specs=in_specs, out_specs=out_specs, out_shape=...  19.6 us
    ppermute x1, waiting for transfers between devices, body(): lax.ppermute(sent, 'atoms', [(z, z ^ 2) for z in range(atom_count)])  9.05 us
    ppermute x2, starting transfers between devices, next_door(): return (keep, lax.ppermute(send, 'atoms', pairs))  5.8 us
    ppermute x2, waiting for transfers between devices, next_door(): return (keep, lax.ppermute(send, 'atoms', pairs))  5.12 us
    ppermute x3, starting transfers between devices, from_group(): return lax.ppermute(cells, 'modes', [(m ^ shift, m) for m in range(groups)])  5.02 us
    unnamed x26, local copies, waits for them, and re-layouts  2.66 us
    ppermute x3, waiting for transfers between devices, body(): lax.ppermute(numerator, ('modes', 'sub'), [(i, i ^ code) for i in range(h...  2.62 us
    ppermute x3, starting transfers between devices, body(): lax.ppermute(numerator, ('modes', 'sub'), [(i, i ^ code) for i in range(h...  1.86 us
  transfers between devices with their start and end apart: 17, of which 6 were waited for; matrix products, arithmetic and copies ran while one was open for 0% of the time, Pallas kernels for 22%

profile of v8, /device:TPU:0, one launch (start us, length us, event | category | flops | bytes accessed | tf_op | source)
XLA Modules:
  0.0 60.0 jit_solution(18281834530769400617)
XLA Ops:
  0.6 0.1 pad_add_fusion.1.refs_0_
  0.7 4.1 %images.3 = (bf16[128,768]{1,0:T(8,128)(2,1)S(1)}, bf16[3,96,128]{2,1,0:T(8,128)(2,1)S(1)}, bf16[3,96,128]{2,1,0:T(8,128)(2,1)S(1)}) custom-call(s32[2]{0:T(128)S(1)} %pad_add_fusion.1.refs_0_, s32[16,768]{1,0:T(8,128)} %bitcast.17, s32[768]{0:T(1024)} %refs_2_.5, f32[9,16,768]{2,1,0:T(8,128)} %bitcast.14, bf16[3,768,128]{2,1,0:T(8,128)(2,1)} %refs_4_.5), custom_call_target="tpu_custom_call" | custom-call | flops 3520000000 | bytes 320000 | tf_op jit(solution)/shard_map/images/pallas_call | solution.py:33
  4.8 0.0 copy-start.6
  4.8 3.0 %collective-permute-start.2 = (bf16[128,768]{1,0:T(8,128)(2,1)S(1)}, bf16[128,768]{1,0:T(8,128)(2,1)S(1)}, u32[]{:S(2)}, u32[]{:S(2)}) collective-permute-start(bf16[128,768]{1,0:T(8,128)(2,1)S(1)} %get-tuple-element.15.refs_5_.refs_0_), channel_id=1, source_target_pairs={{2,0},{0,2},{3,1},{1,3},{6,4},{4,6},{7,5},{5,7},{10,8},{8,10},{11,... | collective-permute-start | bytes 589832 | tf_op jit(solution)/shard_map/ppermute | solution.py:372
  7.8 1.6 %collective-permute-start = (bf16[3,96,128]{2,1,0:T(8,128)(2,1)S(1)}, bf16[3,96,128]{2,1,0:T(8,128)(2,1)S(1)}, u32[]{:S(2)}, u32[]{:S(2)}) collective-permute-start(bf16[3,96,128]{2,1,0:T(8,128)(2,1)S(1)} %get-tuple-element.13), channel_id=1, source_target_pairs={{0,4},{4,0},{8,12},{12,8},{1,5},{5,1},{9,13},{13,9},{2,6},{6,2},{1... | collective-permute-start | bytes 221192 | tf_op jit(solution)/shard_map/ppermute | solution.py:369
  9.4 0.7 %collective-permute-start.1 = (bf16[3,96,128]{2,1,0:T(8,128)(2,1)S(1)}, bf16[3,96,128]{2,1,0:T(8,128)(2,1)S(1)}, u32[]{:S(2)}, u32[]{:S(2)}) collective-permute-start(bf16[3,96,128]{2,1,0:T(8,128)(2,1)S(1)} %get-tuple-element.14), channel_id=1, source_target_pairs={{4,8},{8,4},{5,9},{9,5},{6,10},{10,6},{7,11},{11,7},{20,24},{24,20... | collective-permute-start | bytes 221192 | tf_op jit(solution)/shard_map/ppermute | solution.py:369
  10.1 3.8 %images.4.refs_7_.refs_1_ = bf16[128,768]{1,0:T(8,128)(2,1)} custom-call(s32[2]{0:T(128)S(1)} %pad_add_fusion.1.refs_0_, s32[16,768]{1,0:T(8,128)S(1)} %bitcast.18, s32[768]{0:T(1024)S(1)} %copy-done.9, f32[9,16,768]{2,1,0:T(8,128)S(1)} %bitcast.15, bf16[3,768,128]{2,1,0:T(8,128)(2,1)S(1)} %copy-done.4, bf16[128,768]{1,0:T(8,128)(2,1)S(1)} %get-tuple-element.15.refs_5_.refs_0_), custom_call_target="tpu_custom_call" | custom-call | flops 3520000000 | bytes 320000 | tf_op jit(solution)/shard_map/images/pallas_call | solution.py:33
  13.9 0.5 collective-permute-start.7
  14.4 0.0 collective-permute-start.5
  14.4 0.0 collective-permute-done.refs_5_
  14.4 0.5 collective-permute-start.4
  14.9 0.0 collective-permute-done.1.refs_6_
  14.9 0.0 collective-permute-done.2.refs_8_.refs_6_.refs_0_
  14.9 3.8 %images.5.refs_2_ = bf16[128,768]{1,0:T(8,128)(2,1)} custom-call(s32[2]{0:T(128)S(1)} %pad_add_fusion.1.refs_0_, s32[16,768]{1,0:T(8,128)S(1)} %bitcast.19, s32[768]{0:T(1024)S(1)} %copy-done.9, f32[9,16,768]{2,1,0:T(8,128)S(1)} %bitcast.16, bf16[3,768,128]{2,1,0:T(8,128)(2,1)S(1)} %copy-done.4, bf16[3,96,128]{2,1,0:T(8,128)(2,1)S(1)} %collective-permute-done.refs_5_, ...), custom_call_target="tpu_custom_call" | custom-call | flops 3520000000 | bytes 320000 | tf_op jit(solution)/shard_map/images/pallas_call | solution.py:33
  18.7 0.1 collective-permute-start.6
  18.8 0.1 pad_add_fusion.2.place_ref
  18.8 1.5 %collective-permute-start.3 = (bf16[128,768]{1,0:T(8,128)(2,1)}, bf16[128,768]{1,0:T(8,128)(2,1)S(1)}, u32[]{:S(2)}, u32[]{:S(2)}) collective-permute-start(bf16[128,768]{1,0:T(8,128)(2,1)} %images.5.refs_2_), channel_id=1, source_target_pairs={{2,0},{0,2},{3,1},{1,3},{6,4},{4,6},{7,5},{5,7},{10,8},{8,10},{11,... | collective-permute-start | bytes 589832 | tf_op jit(solution)/shard_map/ppermute | solution.py:372
  20.3 0.0 collective-permute-done.7.refs_7_.refs_1_
  20.3 0.2 collective-permute-start.9
  20.5 0.3 collective-permute-start.10
  20.8 0.0 copy-start.7
  20.9 0.9 %copy-done.7 = bf16[128,768]{1,0:T(8,128)(2,1)S(1)} copy-done((bf16[128,768]{1,0:T(8,128)(2,1)S(1)}, bf16[128,768]{1,0:T(8,128)(2,1)}, u32[]{:S(2)}) %copy-start.7) | copy-done | bytes 196632
  21.8 3.1 %products.2 = (f32[128,640]{1,0:T(8,128)S(1)}, bf16[128,640]{1,0:T(8,128)(2,1)}) custom-call(s32[2]{0:T(128)S(1)} %pad_add_fusion.2.place_ref, bf16[3,768,640]{2,1,0:T(8,128)(2,1)S(1)} %copy-done, bf16[128,768]{1,0:T(8,128)(2,1)S(1)} %copy-done.7, bf16[128,768]{1,0:T(8,128)(2,1)} %images.4.refs_7_.refs_1_, bf16[128,768]{1,0:T(8,128)(2,1)} %images.5.refs_2_, ...), custom_call_target="tpu_custom_call" | custom-call | flops 6600000000 | bytes 600000 | tf_op jit(solution)/shard_map/products/pallas_call | solution.py:33
  24.9 0.0 copy-start.11
  24.9 1.4 %collective-permute-done.3.refs_2_ = bf16[128,768]{1,0:T(8,128)(2,1)S(1)} collective-permute-done((bf16[128,768]{1,0:T(8,128)(2,1)}, bf16[128,768]{1,0:T(8,128)(2,1)S(1)}, u32[]{:S(2)}, u32[]{:S(2)}) %collective-permute-start.3) | collective-permute-done | bytes 196640 | tf_op jit(solution)/shard_map/ppermute | solution.py:372
  26.3 0.0 collective-permute-start.11
  26.3 4.4 %collective-permute-start.8 = (bf16[128,640]{1,0:T(8,128)(2,1)}, bf16[128,640]{1,0:T(8,128)(2,1)}, u32[]{:S(2)}, u32[]{:S(2)}) collective-permute-start(bf16[128,640]{1,0:T(8,128)(2,1)} %get-tuple-element.18), channel_id=1, source_target_pairs={{0,4},{4,0},{8,12},{12,8},{1,5},{5,1},{9,13},{13,9},{2,6},{6,2},{1... | collective-permute-start | bytes 491528 | tf_op jit(solution)/shard_map/ppermute | solution.py:394
  30.7 0.0 collective-permute-done.10.refs_4_
  30.7 0.0 collective-permute-done.9.refs_3_
  30.7 2.8 %products.3 = (f32[128,640]{1,0:T(8,128)S(1)}, bf16[128,640]{1,0:T(8,128)(2,1)}) custom-call(s32[2]{0:T(128)S(1)} %pad_add_fusion.2.place_ref, bf16[3,768,640]{2,1,0:T(8,128)(2,1)S(1)} %copy-done, bf16[128,768]{1,0:T(8,128)(2,1)S(1)} %collective-permute-done.2.refs_8_.refs_6_.refs_0_, bf16[128,768]{1,0:T(8,128)(2,1)} %collective-permute-done.7.refs_7_.refs_1_, ...), custom_call_target="tpu_custom_call" | custom-call | flops 110000000 | bytes 10000 | tf_op jit(solution)/shard_map/products/pallas_call | solution.py:33
  33.5 0.7 %copy-done.1 = f32[128,640]{1,0:T(8,128)} copy-done((f32[128,640]{1,0:T(8,128)}, f32[128,640]{1,0:T(8,128)S(1)}, u32[]{:S(2)}) %copy-start.1) | copy-done | bytes 327704
  34.2 1.4 %collective-permute-start.12 = (bf16[128,640]{1,0:T(8,128)(2,1)}, bf16[128,640]{1,0:T(8,128)(2,1)S(1)}, u32[]{:S(2)}, u32[]{:S(2)}) collective-permute-start(bf16[128,640]{1,0:T(8,128)(2,1)} %get-tuple-element.21), channel_id=1, source_target_pairs={{0,4},{4,0},{8,12},{12,8},{1,5},{5,1},{9,13},{13,9},{2,6},{6,2},{1... | collective-permute-start | bytes 491528 | tf_op jit(solution)/shard_map/ppermute | solution.py:394
  35.6 0.2 collective-permute-done.8.refs_1_
  35.9 4.9 %collective-permute-done.12.refs_4_ = bf16[128,640]{1,0:T(8,128)(2,1)S(1)} collective-permute-done((bf16[128,640]{1,0:T(8,128)(2,1)}, bf16[128,640]{1,0:T(8,128)(2,1)S(1)}, u32[]{:S(2)}, u32[]{:S(2)}) %collective-permute-start.12) | collective-permute-done | bytes 163872 | tf_op jit(solution)/shard_map/ppermute | solution.py:394
  40.8 1.1 %select_convert_fusion = bf16[128,640]{1,0:T(8,128)(2,1)S(1)} fusion(f32[128,640]{1,0:T(8,128)S(1)} %get-tuple-element.17.refs_0_, bf16[128,640]{1,0:T(8,128)(2,1)} %collective-permute-done.8.refs_1_, f32[128,640]{1,0:T(8,128)} %copy-done.1, bf16[128,640]{1,0:T(8,128)(2,1)S(1)} %collective-permute-done.12.refs_4_, pred[]{:T(512)S(6)} %eq.4), kind=kLoop, calls=%fused_computation | loop fusion | flops 491520 | bytes 1146881 | tf_op jit(solution)/shard_map/convert_element_type | solution.py:406
  41.9 0.9 %collective-permute-start.13 = (bf16[128,640]{1,0:T(8,128)(2,1)S(1)}, bf16[128,640]{1,0:T(8,128)(2,1)S(1)}, u32[]{:S(2)}, u32[]{:S(2)}) collective-permute-start(bf16[128,640]{1,0:T(8,128)(2,1)S(1)} %select_convert_fusion), channel_id=1, source_target_pairs={{0,8},{4,12},{8,0},{12,4},{1,9},{5,13},{9,1},{13,5},{2,10},{6,14},... | collective-permute-start | bytes 491528 | tf_op jit(solution)/shard_map/ppermute | solution.py:407
  42.7 0.1 pad_add_fusion.flag_ref
  42.8 9.1 %collective-permute-done.13.refs_2_.refs_5_ = bf16[128,640]{1,0:T(8,128)(2,1)S(1)} collective-permute-done((bf16[128,640]{1,0:T(8,128)(2,1)S(1)}, bf16[128,640]{1,0:T(8,128)(2,1)S(1)}, u32[]{:S(2)}, u32[]{:S(2)}) %collective-permute-start.13) | collective-permute-done | bytes 163872 | tf_op jit(solution)/shard_map/ppermute | solution.py:407
  51.9 0.0 copy-start.2
  51.9 1.0 %copy-done.2 = f32[128,640]{1,0:T(8,128)S(1)} copy-done((f32[128,640]{1,0:T(8,128)S(1)}, f32[128,640]{1,0:T(8,128)}, u32[]{:S(2)}) %copy-start.2) | copy-done | bytes 327704
  52.9 2.1 %finish.1 = (f32[128,640]{1,0:T(8,128)}, f32[1,128]{1,0:T(1,128)S(1)}) custom-call(s32[3]{0:T(128)S(1)} %pad_add_fusion.flag_ref, s32[4,128]{1,0:T(4,128)S(1)} %bitcast.20, s32[4,128]{1,0:T(4,128)S(1)} %bitcast.21, f32[4,128]{1,0:T(4,128)S(1)} %bitcast.13, f32[1,640]{1,0:T(1,128)S(1)} %broadcast_in_dim.3.partner_ref, ...), custom_call_target="tpu_custom_call" | custom-call | flops 2200000000 | bytes 200000 | tf_op jit(solution)/shard_map/finish/pallas_call | solution.py:33
  54.9 0.0 collective-permute-start.14
  54.9 1.5 %collective-permute-start.15 = (f32[1,128]{1,0:T(1,128)S(1)}, f32[1,128]{1,0:T(1,128)S(1)}, u32[]{:S(2)}, u32[]{:S(2)}) collective-permute-start(f32[1,128]{1,0:T(1,128)S(1)} %get-tuple-element.23), channel_id=1, source_target_pairs={{0,2},{1,3},{2,0},{3,1},{4,6},{5,7},{6,4},{7,5},{8,10},{9,11},{10,... | collective-permute-start | bytes 1544 | tf_op jit(solution)/shard_map/ppermute | solution.py:445
  56.5 0.3 collective-permute-start.16
  56.8 0.0 collective-permute-done.14
  56.8 1.7 %collective-permute-done.15 = f32[1,128]{1,0:T(1,128)S(1)} collective-permute-done((f32[1,128]{1,0:T(1,128)S(1)}, f32[1,128]{1,0:T(1,128)S(1)}, u32[]{:S(2)}, u32[]{:S(2)}) %collective-permute-start.15) | collective-permute-done | bytes 544 | tf_op jit(solution)/shard_map/ppermute | solution.py:445
  58.5 0.9 %collective-permute-done.16 = f32[1,128]{1,0:T(1,128)S(1)} collective-permute-done((f32[1,128]{1,0:T(1,128)S(1)}, f32[1,128]{1,0:T(1,128)S(1)}, u32[]{:S(2)}, u32[]{:S(2)}) %collective-permute-start.16) | collective-permute-done | bytes 544 | tf_op jit(solution)/shard_map/ppermute | solution.py:445
  59.4 0.6 bitcast_divide_fusion
  (24 shorter events, 0.0 us)
Async XLA Ops:
  0.7 9.4 %copy-start.4 = (bf16[3,768,128]{2,1,0:T(8,128)(2,1)S(1)}, bf16[3,768,128]{2,1,0:T(8,128)(2,1)}, u32[]{:S(2)}) copy-start(bf16[3,768,128]{2,1,0:T(8,128)(2,1)} %refs_4_.5) | copy-start | bytes 1769476
  0.7 9.4 %copy-start.5 = (f32[9,768,16]{1,2,0:T(8,128)S(1)}, f32[9,768,16]{1,2,0:T(8,128)}, u32[]{:S(2)}) copy-start(f32[9,768,16]{1,2,0:T(8,128)} %param.11) | copy-start | bytes 1327108
  0.7 9.4 %copy-start.8 = (s32[768,16]{0,1:T(8,128)S(1)}, s32[768,16]{0,1:T(8,128)}, u32[]{:S(2)}) copy-start(s32[768,16]{0,1:T(8,128)} %param.12) | copy-start | bytes 147460
  0.7 9.4 %copy-start.9 = (s32[768]{0:T(1024)S(1)}, s32[768]{0:T(1024)}, u32[]{:S(2)}) copy-start(s32[768]{0:T(1024)} %refs_2_.5) | copy-start | bytes 9220
  4.8 9.6 %copy-start.6 = (bf16[128,768]{1,0:T(8,128)(2,1)}, bf16[128,768]{1,0:T(8,128)(2,1)S(1)}, u32[]{:S(2)}) copy-start(bf16[128,768]{1,0:T(8,128)(2,1)S(1)} %get-tuple-element.15.refs_5_.refs_0_) | copy-start | bytes 589828
  4.8 10.1 %collective-permute-start.2 = (bf16[128,768]{1,0:T(8,128)(2,1)S(1)}, bf16[128,768]{1,0:T(8,128)(2,1)S(1)}, u32[]{:S(2)}, u32[]{:S(2)}) collective-permute-start(bf16[128,768]{1,0:T(8,128)(2,1)S(1)} %get-tuple-element.15.refs_5_.refs_0_), channel_id=1, source_target_pairs={{2,0},{0,2},{3,1},{1,3},{6,4},{4,6},{7,5},{5,7},{10,8},{8,10},{11,... | collective-permute-start | bytes 589832 | tf_op jit(solution)/shard_map/ppermute | solution.py:372
  7.8 6.6 %collective-permute-start = (bf16[3,96,128]{2,1,0:T(8,128)(2,1)S(1)}, bf16[3,96,128]{2,1,0:T(8,128)(2,1)S(1)}, u32[]{:S(2)}, u32[]{:S(2)}) collective-permute-start(bf16[3,96,128]{2,1,0:T(8,128)(2,1)S(1)} %get-tuple-element.13), channel_id=1, source_target_pairs={{0,4},{4,0},{8,12},{12,8},{1,5},{5,1},{9,13},{13,9},{2,6},{6,2},{1... | collective-permute-start | bytes 221192 | tf_op jit(solution)/shard_map/ppermute | solution.py:369
  9.4 5.5 %collective-permute-start.1 = (bf16[3,96,128]{2,1,0:T(8,128)(2,1)S(1)}, bf16[3,96,128]{2,1,0:T(8,128)(2,1)S(1)}, u32[]{:S(2)}, u32[]{:S(2)}) collective-permute-start(bf16[3,96,128]{2,1,0:T(8,128)(2,1)S(1)} %get-tuple-element.14), channel_id=1, source_target_pairs={{4,8},{8,4},{5,9},{9,5},{6,10},{10,6},{7,11},{11,7},{20,24},{24,20... | collective-permute-start | bytes 221192 | tf_op jit(solution)/shard_map/ppermute | solution.py:369
  13.9 7.0 %copy-start = (bf16[3,768,640]{2,1,0:T(8,128)(2,1)S(1)}, bf16[3,768,640]{2,1,0:T(8,128)(2,1)}, u32[]{:S(2)}) copy-start(bf16[3,768,640]{2,1,0:T(8,128)(2,1)} %partners_ref.3) | copy-start | bytes 8847364
  13.9 6.4 %collective-permute-start.7 = (bf16[128,768]{1,0:T(8,128)(2,1)}, bf16[128,768]{1,0:T(8,128)(2,1)}, u32[]{:S(2)}, u32[]{:S(2)}) collective-permute-start(bf16[128,768]{1,0:T(8,128)(2,1)} %images.4.refs_7_.refs_1_), channel_id=1, source_target_pairs={{2,0},{0,2},{3,1},{1,3},{6,4},{4,6},{7,5},{5,7},{10,8},{8,10},{11,... | collective-permute-start | bytes 589832 | tf_op jit(solution)/shard_map/ppermute | solution.py:372
  14.4 6.1 %collective-permute-start.5 = (bf16[128,768]{1,0:T(8,128)(2,1)}, bf16[128,768]{1,0:T(8,128)(2,1)}, u32[]{:S(2)}, u32[]{:S(2)}) collective-permute-start(bf16[128,768]{1,0:T(8,128)(2,1)} %images.4.refs_7_.refs_1_), channel_id=1, source_target_pairs={{0,1},{1,0},{2,3},{3,2},{4,5},{5,4},{6,7},{7,6},{8,9},{9,8},{10,11... | collective-permute-start | bytes 589832 | tf_op jit(solution)/shard_map/ppermute | solution.py:375
  14.4 6.4 %collective-permute-start.4 = (bf16[128,768]{1,0:T(8,128)(2,1)S(1)}, bf16[128,768]{1,0:T(8,128)(2,1)}, u32[]{:S(2)}, u32[]{:S(2)}) collective-permute-start(bf16[128,768]{1,0:T(8,128)(2,1)S(1)} %get-tuple-element.15.refs_5_.refs_0_), channel_id=1, source_target_pairs={{0,1},{1,0},{2,3},{3,2},{4,5},{5,4},{6,7},{7,6},{8,9},{9,8},{10,11... | collective-permute-start | bytes 589832 | tf_op jit(solution)/shard_map/ppermute | solution.py:375
  18.7 2.1 %collective-permute-start.6 = (bf16[128,768]{1,0:T(8,128)(2,1)}, bf16[128,768]{1,0:T(8,128)(2,1)}, u32[]{:S(2)}, u32[]{:S(2)}) collective-permute-start(bf16[128,768]{1,0:T(8,128)(2,1)} %images.5.refs_2_), channel_id=1, source_target_pairs={{0,1},{1,0},{2,3},{3,2},{4,5},{5,4},{6,7},{7,6},{8,9},{9,8},{10,11... | collective-permute-start | bytes 589832 | tf_op jit(solution)/shard_map/ppermute | solution.py:375
  18.8 7.5 %collective-permute-start.3 = (bf16[128,768]{1,0:T(8,128)(2,1)}, bf16[128,768]{1,0:T(8,128)(2,1)S(1)}, u32[]{:S(2)}, u32[]{:S(2)}) collective-permute-start(bf16[128,768]{1,0:T(8,128)(2,1)} %images.5.refs_2_), channel_id=1, source_target_pairs={{2,0},{0,2},{3,1},{1,3},{6,4},{4,6},{7,5},{5,7},{10,8},{8,10},{11,... | collective-permute-start | bytes 589832 | tf_op jit(solution)/shard_map/ppermute | solution.py:372
  20.3 10.4 %collective-permute-start.9 = (bf16[128,768]{1,0:T(8,128)(2,1)S(1)}, bf16[128,768]{1,0:T(8,128)(2,1)S(1)}, u32[]{:S(2)}, u32[]{:S(2)}) collective-permute-start(bf16[128,768]{1,0:T(8,128)(2,1)S(1)} %collective-permute-done.2.refs_8_.refs_6_.refs_0_), channel_id=1, source_target_pairs={{0,1},{1,0},{2,3},{3,2},{4,5},{5,4},{6,7},{7,6},{8,9},{9,8},{10,11... | collective-permute-start | bytes 589832 | tf_op jit(solution)/shard_map/ppermute | solution.py:375
  20.5 10.2 %collective-permute-start.10 = (bf16[128,768]{1,0:T(8,128)(2,1)}, bf16[128,768]{1,0:T(8,128)(2,1)S(1)}, u32[]{:S(2)}, u32[]{:S(2)}) collective-permute-start(bf16[128,768]{1,0:T(8,128)(2,1)} %collective-permute-done.7.refs_7_.refs_1_), channel_id=1, source_target_pairs={{0,1},{1,0},{2,3},{3,2},{4,5},{5,4},{6,7},{7,6},{8,9},{9,8},{10,11... | collective-permute-start | bytes 589832 | tf_op jit(solution)/shard_map/ppermute | solution.py:375
  20.8 0.9 %copy-start.7 = (bf16[128,768]{1,0:T(8,128)(2,1)S(1)}, bf16[128,768]{1,0:T(8,128)(2,1)}, u32[]{:S(2)}) copy-start(bf16[128,768]{1,0:T(8,128)(2,1)} %copy-done.6) | copy-start | bytes 589828
  24.9 17.8 %copy-start.12 = (f32[640]{0:T(1024)S(1)}, f32[640]{0:T(1024)}, u32[]{:S(2)}) copy-start(f32[640]{0:T(1024)} %param.15) | copy-start | bytes 7684
  24.9 27.0 %copy-start.3 = (f32[512]{0:T(512)S(1)}, f32[512]{0:T(512)}, u32[]{:S(2)}) copy-start(f32[512]{0:T(512)} %param.14) | copy-start | bytes 6148
  24.9 27.0 %copy-start.10 = (s32[512]{0:T(512)S(1)}, s32[512]{0:T(512)}, u32[]{:S(2)}) copy-start(s32[512]{0:T(512)} %param.16) | copy-start | bytes 6148
  24.9 27.0 %copy-start.11 = (s32[512]{0:T(512)S(1)}, s32[512]{0:T(512)}, u32[]{:S(2)}) copy-start(s32[512]{0:T(512)} %param.17) | copy-start | bytes 6148
  26.3 4.4 %collective-permute-start.11 = (bf16[128,768]{1,0:T(8,128)(2,1)S(1)}, bf16[128,768]{1,0:T(8,128)(2,1)S(1)}, u32[]{:S(2)}, u32[]{:S(2)}) collective-permute-start(bf16[128,768]{1,0:T(8,128)(2,1)S(1)} %collective-permute-done.3.refs_2_), channel_id=1, source_target_pairs={{0,1},{1,0},{2,3},{3,2},{4,5},{5,4},{6,7},{7,6},{8,9},{9,8},{10,11... | collective-permute-start | bytes 589832 | tf_op jit(solution)/shard_map/ppermute | solution.py:375
  26.3 9.6 %collective-permute-start.8 = (bf16[128,640]{1,0:T(8,128)(2,1)}, bf16[128,640]{1,0:T(8,128)(2,1)}, u32[]{:S(2)}, u32[]{:S(2)}) collective-permute-start(bf16[128,640]{1,0:T(8,128)(2,1)} %get-tuple-element.18), channel_id=1, source_target_pairs={{0,4},{4,0},{8,12},{12,8},{1,5},{5,1},{9,13},{13,9},{2,6},{6,2},{1... | collective-permute-start | bytes 491528 | tf_op jit(solution)/shard_map/ppermute | solution.py:394
  33.5 0.7 %copy-start.1 = (f32[128,640]{1,0:T(8,128)}, f32[128,640]{1,0:T(8,128)S(1)}, u32[]{:S(2)}) copy-start(f32[128,640]{1,0:T(8,128)S(1)} %get-tuple-element.20.refs_3_) | copy-start | bytes 983044
  34.2 6.5 %collective-permute-start.12 = (bf16[128,640]{1,0:T(8,128)(2,1)}, bf16[128,640]{1,0:T(8,128)(2,1)S(1)}, u32[]{:S(2)}, u32[]{:S(2)}) collective-permute-start(bf16[128,640]{1,0:T(8,128)(2,1)} %get-tuple-element.21), channel_id=1, source_target_pairs={{0,4},{4,0},{8,12},{12,8},{1,5},{5,1},{9,13},{13,9},{2,6},{6,2},{1... | collective-permute-start | bytes 491528 | tf_op jit(solution)/shard_map/ppermute | solution.py:394
  41.9 10.0 %collective-permute-start.13 = (bf16[128,640]{1,0:T(8,128)(2,1)S(1)}, bf16[128,640]{1,0:T(8,128)(2,1)S(1)}, u32[]{:S(2)}, u32[]{:S(2)}) collective-permute-start(bf16[128,640]{1,0:T(8,128)(2,1)S(1)} %select_convert_fusion), channel_id=1, source_target_pairs={{0,8},{4,12},{8,0},{12,4},{1,9},{5,13},{9,1},{13,5},{2,10},{6,14},... | collective-permute-start | bytes 491528 | tf_op jit(solution)/shard_map/ppermute | solution.py:407
  51.9 1.0 %copy-start.2 = (f32[128,640]{1,0:T(8,128)S(1)}, f32[128,640]{1,0:T(8,128)}, u32[]{:S(2)}) copy-start(f32[128,640]{1,0:T(8,128)} %copy-done.1) | copy-start | bytes 983044
  54.9 1.9 %collective-permute-start.14 = (f32[1,128]{1,0:T(1,128)S(1)}, f32[1,128]{1,0:T(1,128)S(1)}, u32[]{:S(2)}, u32[]{:S(2)}) collective-permute-start(f32[1,128]{1,0:T(1,128)S(1)} %get-tuple-element.23), channel_id=1, source_target_pairs={{0,1},{1,0},{2,3},{3,2},{4,5},{5,4},{6,7},{7,6},{8,9},{9,8},{10,11... | collective-permute-start | bytes 1544 | tf_op jit(solution)/shard_map/ppermute | solution.py:445
  54.9 3.5 %collective-permute-start.15 = (f32[1,128]{1,0:T(1,128)S(1)}, f32[1,128]{1,0:T(1,128)S(1)}, u32[]{:S(2)}, u32[]{:S(2)}) collective-permute-start(f32[1,128]{1,0:T(1,128)S(1)} %get-tuple-element.23), channel_id=1, source_target_pairs={{0,2},{1,3},{2,0},{3,1},{4,6},{5,7},{6,4},{7,5},{8,10},{9,11},{10,... | collective-permute-start | bytes 1544 | tf_op jit(solution)/shard_map/ppermute | solution.py:445
  56.5 3.0 %collective-permute-start.16 = (f32[1,128]{1,0:T(1,128)S(1)}, f32[1,128]{1,0:T(1,128)S(1)}, u32[]{:S(2)}, u32[]{:S(2)}) collective-permute-start(f32[1,128]{1,0:T(1,128)S(1)} %get-tuple-element.23), channel_id=1, source_target_pairs={{0,3},{1,2},{2,1},{3,0},{4,7},{5,6},{6,5},{7,4},{8,11},{9,10},{10,... | collective-permute-start | bytes 1544 | tf_op jit(solution)/shard_map/ppermute | solution.py:445

commit v9 on v8

--- a/solution.py
+++ b/solution.py
@@ -201,8 +201,13 @@
     count = len(chunks)
     depth = partners.shape[1]
 
-    def kernel(place_ref, partners_ref, *refs):
-        keep_ref, send_ref, left_ref = refs[-3:]
+    def kernel(place_ref, partners_hbm, *refs):
+        keep_ref, send_ref, left_ref, partners_ref, sems = refs[-5:]
+        copies = [
+            pltpu.make_async_copy(partners_hbm.at[r], partners_ref.at[r], sems.at[r]) for r in range(3)
+        ]
+        for copy in copies:
+            copy.start()
         kept = place_ref[0] == place_ref[1]
         for who in range(2):
             at_rows = pl.ds(pl.multiple_of(jnp.where(kept == (who == 0), 0, rows), rows), rows)
@@ -213,21 +218,29 @@
                     for spot, block, length in runs_of(blocks):
                         at, to = r * width + spot * LANES, r * depth + block * LANES
                         left_ref[at_rows, to : to + length * LANES] = image_ref[:, at : at + length * LANES]
-        total = jnp.dot(
-            left_ref[...], partners_ref[...].reshape(3 * depth, cols), preferred_element_type=jnp.float32
-        )
+        total = None
+        for r, copy in enumerate(copies):
+            copy.wait()
+            part = jnp.dot(
+                left_ref[:, r * depth : (r + 1) * depth], partners_ref[r], preferred_element_type=jnp.float32
+            )
+            total = part if total is None else total + part
         keep_ref[...] = total[:rows]
         send_ref[...] = total[rows:].astype(jnp.bfloat16)
 
     return call(
         kernel,
         "products",
-        [SMEM] + [VMEM] * (1 + 2 * count) + [ANY] * len(after),
+        [SMEM, HBM] + [VMEM] * (2 * count) + [ANY] * len(after),
         [VMEM, VMEM],
         [pltpu.VMEM((rows, cols), jnp.float32), pltpu.VMEM((rows, cols), jnp.bfloat16)],
         (place, partners, *mine, *theirs, *after),
         busy_us,
-        [pltpu.VMEM((2 * rows, 3 * depth), jnp.bfloat16)],
+        [
+            pltpu.VMEM((2 * rows, 3 * depth), jnp.bfloat16),
+            pltpu.VMEM((3, depth, cols), jnp.bfloat16),
+            pltpu.SemaphoreType.DMA((3,)),
+        ],
     )
 
 

time: 60.3 us -> 56.1 us (0.930)
  local copies, waits for them, and re-layouts: 2.66 us -> 0.04 us
  other arithmetic: 1.94 us -> 0.88 us
  Pallas kernels: 19.6 us -> 18.7 us
    unnamed x26 -> x16, local copies, waits for them, and re-layouts: 2.66 us -> 0.04 us
    convert_element_type x1, other arithmetic: 1.12 us -> 0.06 us  [body(): sent = jnp.where(group_index == goal, late[0] + late[1].astype(jnp.float3...]
    pallas_call x6, Pallas kernels: 19.6 us -> 18.7 us  [call(): pl.pallas_call(kernel, in_specs=in_specs, out_specs=out_specs, out_shape=...]
  transfers between devices with their start and end apart: 17 -> 17, of which waited for: 6 -> 6; matrix products, arithmetic and copies ran while one was open for 0% -> 0% of each run, Pallas kernels for 22% -> 23%
where the time goes in v9:
time: 56.1 us; the launch traced here: 55.9 us
  Pallas kernels  18.7 us (33%)
  waiting for transfers between devices  18.3 us (33%)
  starting transfers between devices  17.1 us (30%)
  other arithmetic  0.88 us (2%)
  between operations  0.78 us (1%)
    pallas_call x6, Pallas kernels, call(): pl.pallas_call(kernel, in_specs=in_specs, out_specs=out_specs, out_shape=...  18.7 us
    ppermute x1, waiting for transfers between devices, body(): lax.ppermute(sent, 'atoms', [(z, z ^ 2) for z in range(atom_count)])  8.95 us
    ppermute x2, starting transfers between devices, next_door(): return (keep, lax.ppermute(send, 'atoms', pairs))  5.88 us
    ppermute x3, starting transfers between devices, from_group(): return lax.ppermute(cells, 'modes', [(m ^ shift, m) for m in range(groups)])  5.1 us
    ppermute x2, waiting for transfers between devices, next_door(): return (keep, lax.ppermute(send, 'atoms', pairs))  4.91 us
    ppermute x3, waiting for transfers between devices, body(): lax.ppermute(numerator, ('modes', 'sub'), [(i, i ^ code) for i in range(h...  2.6 us
    ppermute x3, starting transfers between devices, body(): lax.ppermute(numerator, ('modes', 'sub'), [(i, i ^ code) for i in range(h...  1.86 us
    ppermute x3, waiting for transfers between devices, from_group(): return lax.ppermute(cells, 'modes', [(m ^ shift, m) for m in range(groups)])  1.83 us
  transfers between devices with their start and end apart: 17, of which 6 were waited for; matrix products, arithmetic and copies ran while one was open for 0% of the time, Pallas kernels for 23%

profile of v9, /device:TPU:0, one launch (start us, length us, event | category | flops | bytes accessed | tf_op | source)
XLA Modules:
  0.0 55.9 jit_solution(5571850924127772674)
XLA Ops:
  0.6 0.1 pad_add_fusion.1.refs_0_
  0.7 4.1 %images.3 = (bf16[128,768]{1,0:T(8,128)(2,1)S(1)}, bf16[3,96,128]{2,1,0:T(8,128)(2,1)S(1)}, bf16[3,96,128]{2,1,0:T(8,128)(2,1)S(1)}) custom-call(s32[2]{0:T(128)S(1)} %pad_add_fusion.1.refs_0_, s32[16,768]{1,0:T(8,128)} %bitcast.17, s32[768]{0:T(1024)} %refs_2_.5, f32[9,16,768]{2,1,0:T(8,128)} %bitcast.14, bf16[3,768,128]{2,1,0:T(8,128)(2,1)} %refs_4_.5), custom_call_target="tpu_custom_call" | custom-call | flops 3520000000 | bytes 320000 | tf_op jit(solution)/shard_map/images/pallas_call | solution.py:33
  4.8 3.0 %collective-permute-start.2 = (bf16[128,768]{1,0:T(8,128)(2,1)S(1)}, bf16[128,768]{1,0:T(8,128)(2,1)S(1)}, u32[]{:S(2)}, u32[]{:S(2)}) collective-permute-start(bf16[128,768]{1,0:T(8,128)(2,1)S(1)} %get-tuple-element.15.refs_5_.refs_0_), channel_id=1, source_target_pairs={{2,0},{0,2},{3,1},{1,3},{6,4},{4,6},{7,5},{5,7},{10,8},{8,10},{11,... | collective-permute-start | bytes 589832 | tf_op jit(solution)/shard_map/ppermute | solution.py:385
  7.8 1.6 %collective-permute-start = (bf16[3,96,128]{2,1,0:T(8,128)(2,1)S(1)}, bf16[3,96,128]{2,1,0:T(8,128)(2,1)S(1)}, u32[]{:S(2)}, u32[]{:S(2)}) collective-permute-start(bf16[3,96,128]{2,1,0:T(8,128)(2,1)S(1)} %get-tuple-element.13), channel_id=1, source_target_pairs={{0,4},{4,0},{8,12},{12,8},{1,5},{5,1},{9,13},{13,9},{2,6},{6,2},{1... | collective-permute-start | bytes 221192 | tf_op jit(solution)/shard_map/ppermute | solution.py:382
  9.4 0.7 %collective-permute-start.1 = (bf16[3,96,128]{2,1,0:T(8,128)(2,1)S(1)}, bf16[3,96,128]{2,1,0:T(8,128)(2,1)S(1)}, u32[]{:S(2)}, u32[]{:S(2)}) collective-permute-start(bf16[3,96,128]{2,1,0:T(8,128)(2,1)S(1)} %get-tuple-element.14), channel_id=1, source_target_pairs={{4,8},{8,4},{5,9},{9,5},{6,10},{10,6},{7,11},{11,7},{20,24},{24,20... | collective-permute-start | bytes 221192 | tf_op jit(solution)/shard_map/ppermute | solution.py:382
  10.1 3.1 %images.4.refs_7_.refs_1_ = bf16[128,768]{1,0:T(8,128)(2,1)S(1)} custom-call(s32[2]{0:T(128)S(1)} %pad_add_fusion.1.refs_0_, s32[16,768]{1,0:T(8,128)S(1)} %bitcast.18, s32[768]{0:T(1024)S(1)} %copy-done.4, f32[9,16,768]{2,1,0:T(8,128)S(1)} %bitcast.15, bf16[3,768,128]{2,1,0:T(8,128)(2,1)S(1)} %copy-done.1, ...), custom_call_target="tpu_custom_call" | custom-call | flops 3520000000 | bytes 320000 | tf_op jit(solution)/shard_map/images/pallas_call | solution.py:33
  13.2 0.6 %collective-permute-start.7 = (bf16[128,768]{1,0:T(8,128)(2,1)S(1)}, bf16[128,768]{1,0:T(8,128)(2,1)S(1)}, u32[]{:S(2)}, u32[]{:S(2)}) collective-permute-start(bf16[128,768]{1,0:T(8,128)(2,1)S(1)} %images.4.refs_7_.refs_1_), channel_id=1, source_target_pairs={{2,0},{0,2},{3,1},{1,3},{6,4},{4,6},{7,5},{5,7},{10,8},{8,10},{11,... | collective-permute-start | bytes 589832 | tf_op jit(solution)/shard_map/ppermute | solution.py:385
  13.8 0.0 collective-permute-start.5
  13.8 0.0 collective-permute-done.refs_5_
  13.8 0.5 collective-permute-start.4
  14.3 0.0 collective-permute-done.1.refs_6_
  14.3 0.0 collective-permute-done.2.refs_8_.refs_6_.refs_0_
  14.3 3.0 %images.5.refs_2_ = bf16[128,768]{1,0:T(8,128)(2,1)S(1)} custom-call(s32[2]{0:T(128)S(1)} %pad_add_fusion.1.refs_0_, s32[16,768]{1,0:T(8,128)S(1)} %bitcast.19, s32[768]{0:T(1024)S(1)} %copy-done.4, f32[9,16,768]{2,1,0:T(8,128)S(1)} %bitcast.16, bf16[3,768,128]{2,1,0:T(8,128)(2,1)S(1)} %copy-done.1, bf16[3,96,128]{2,1,0:T(8,128)(2,1)S(1)} %collective-permute-done.refs_5_, ...), custom_call_target="tpu_custom_call" | custom-call | flops 3520000000 | bytes 320000 | tf_op jit(solution)/shard_map/images/pallas_call | solution.py:33
  17.4 0.1 collective-permute-start.6
  17.5 0.1 pad_add_fusion.2.place_ref
  17.5 1.5 %collective-permute-start.3 = (bf16[128,768]{1,0:T(8,128)(2,1)S(1)}, bf16[128,768]{1,0:T(8,128)(2,1)S(1)}, u32[]{:S(2)}, u32[]{:S(2)}) collective-permute-start(bf16[128,768]{1,0:T(8,128)(2,1)S(1)} %images.5.refs_2_), channel_id=1, source_target_pairs={{2,0},{0,2},{3,1},{1,3},{6,4},{4,6},{7,5},{5,7},{10,8},{8,10},{11,... | collective-permute-start | bytes 589832 | tf_op jit(solution)/shard_map/ppermute | solution.py:385
  19.0 0.3 collective-permute-done.7.refs_7_.refs_1_
  19.3 0.0 collective-permute-start.9
  19.3 0.0 collective-permute-done.5.refs_4_
  19.3 0.5 collective-permute-start.10
  19.8 0.0 collective-permute-done.4.refs_3_
  19.8 0.0 collective-permute-done.6.refs_5_
  19.8 3.4 %products.2 = (f32[128,640]{1,0:T(8,128)S(1)}, bf16[128,640]{1,0:T(8,128)(2,1)S(1)}) custom-call(s32[2]{0:T(128)S(1)} %pad_add_fusion.2.place_ref, bf16[3,768,640]{2,1,0:T(8,128)(2,1)} %partners_hbm.3, bf16[128,768]{1,0:T(8,128)(2,1)S(1)} %get-tuple-element.15.refs_5_.refs_0_, bf16[128,768]{1,0:T(8,128)(2,1)S(1)} %images.4.refs_7_.refs_1_, ...), custom_call_target="tpu_custom_call" | custom-call | flops 6600000000 | bytes 600000 | tf_op jit(solution)/shard_map/products/pallas_call | solution.py:33
  23.3 0.0 copy-start.7
  23.3 0.0 copy-start
  23.3 0.0 copy-start.5
  23.3 0.0 copy-start.6
  23.3 1.5 %collective-permute-done.3.refs_2_ = bf16[128,768]{1,0:T(8,128)(2,1)S(1)} collective-permute-done((bf16[128,768]{1,0:T(8,128)(2,1)S(1)}, bf16[128,768]{1,0:T(8,128)(2,1)S(1)}, u32[]{:S(2)}, u32[]{:S(2)}) %collective-permute-start.3) | collective-permute-done | bytes 196640 | tf_op jit(solution)/shard_map/ppermute | solution.py:385
  24.8 0.0 collective-permute-start.11
  24.8 4.4 %collective-permute-start.8 = (bf16[128,640]{1,0:T(8,128)(2,1)S(1)}, bf16[128,640]{1,0:T(8,128)(2,1)S(1)}, u32[]{:S(2)}, u32[]{:S(2)}) collective-permute-start(bf16[128,640]{1,0:T(8,128)(2,1)S(1)} %get-tuple-element.18), channel_id=1, source_target_pairs={{0,4},{4,0},{8,12},{12,8},{1,5},{5,1},{9,13},{13,9},{2,6},{6,2},{1... | collective-permute-start | bytes 491528 | tf_op jit(solution)/shard_map/ppermute | solution.py:407
  29.2 0.0 collective-permute-done.10.refs_4_
  29.2 0.0 collective-permute-done.9.refs_3_
  29.2 0.0 collective-permute-done.11.refs_5_
  29.2 3.4 %products.3 = (f32[128,640]{1,0:T(8,128)S(1)}, bf16[128,640]{1,0:T(8,128)(2,1)S(1)}) custom-call(s32[2]{0:T(128)S(1)} %pad_add_fusion.2.place_ref, bf16[3,768,640]{2,1,0:T(8,128)(2,1)} %partners_hbm.3, bf16[128,768]{1,0:T(8,128)(2,1)S(1)} %collective-permute-done.2.refs_8_.refs_6_.refs_0_, bf16[128,768]{1,0:T(8,128)(2,1)S(1)} %collective-permute-done.7.refs_7_.refs_1_, ...), custom_call_target="tpu_custom_call" | custom-call | flops 110000000 | bytes 10000 | tf_op jit(solution)/shard_map/products/pallas_call | solution.py:33
  32.6 1.5 %collective-permute-start.12 = (bf16[128,640]{1,0:T(8,128)(2,1)S(1)}, bf16[128,640]{1,0:T(8,128)(2,1)S(1)}, u32[]{:S(2)}, u32[]{:S(2)}) collective-permute-start(bf16[128,640]{1,0:T(8,128)(2,1)S(1)} %get-tuple-element.21), channel_id=1, source_target_pairs={{0,4},{4,0},{8,12},{12,8},{1,5},{5,1},{9,13},{13,9},{2,6},{6,2},{1... | collective-permute-start | bytes 491528 | tf_op jit(solution)/shard_map/ppermute | solution.py:407
  34.1 0.0 collective-permute-done.8.refs_1_
  34.1 4.9 %collective-permute-done.12.refs_4_ = bf16[128,640]{1,0:T(8,128)(2,1)S(1)} collective-permute-done((bf16[128,640]{1,0:T(8,128)(2,1)S(1)}, bf16[128,640]{1,0:T(8,128)(2,1)S(1)}, u32[]{:S(2)}, u32[]{:S(2)}) %collective-permute-start.12) | collective-permute-done | bytes 163872 | tf_op jit(solution)/shard_map/ppermute | solution.py:407
  39.0 0.1 select_convert_fusion
  39.1 1.0 %collective-permute-start.13 = (bf16[128,640]{1,0:T(8,128)(2,1)S(1)}, bf16[128,640]{1,0:T(8,128)(2,1)S(1)}, u32[]{:S(2)}, u32[]{:S(2)}) collective-permute-start(bf16[128,640]{1,0:T(8,128)(2,1)S(1)} %select_convert_fusion), channel_id=1, source_target_pairs={{0,8},{4,12},{8,0},{12,4},{1,9},{5,13},{9,1},{13,5},{2,10},{6,14},... | collective-permute-start | bytes 491528 | tf_op jit(solution)/shard_map/ppermute | solution.py:420
  40.1 0.1 pad_add_fusion.flag_ref
  40.1 8.9 %collective-permute-done.13.refs_2_.refs_5_ = bf16[128,640]{1,0:T(8,128)(2,1)S(1)} collective-permute-done((bf16[128,640]{1,0:T(8,128)(2,1)S(1)}, bf16[128,640]{1,0:T(8,128)(2,1)S(1)}, u32[]{:S(2)}, u32[]{:S(2)}) %collective-permute-start.13) | collective-permute-done | bytes 163872 | tf_op jit(solution)/shard_map/ppermute | solution.py:420
  49.1 1.7 %finish.1 = (f32[128,640]{1,0:T(8,128)}, f32[1,128]{1,0:T(1,128)S(1)}) custom-call(s32[3]{0:T(128)S(1)} %pad_add_fusion.flag_ref, s32[4,128]{1,0:T(4,128)S(1)} %bitcast.20, s32[4,128]{1,0:T(4,128)S(1)} %bitcast.21, f32[4,128]{1,0:T(4,128)S(1)} %bitcast.13, f32[1,640]{1,0:T(1,128)S(1)} %broadcast_in_dim.3.partner_ref, ...), custom_call_target="tpu_custom_call" | custom-call | flops 2200000000 | bytes 200000 | tf_op jit(solution)/shard_map/finish/pallas_call | solution.py:33
  50.8 1.5 %collective-permute-start.15 = (f32[1,128]{1,0:T(1,128)S(1)}, f32[1,128]{1,0:T(1,128)S(1)}, u32[]{:S(2)}, u32[]{:S(2)}) collective-permute-start(f32[1,128]{1,0:T(1,128)S(1)} %get-tuple-element.23), channel_id=1, source_target_pairs={{0,2},{1,3},{2,0},{3,1},{4,6},{5,7},{6,4},{7,5},{8,10},{9,11},{10,... | collective-permute-start | bytes 1544 | tf_op jit(solution)/shard_map/ppermute | solution.py:458
  52.3 0.4 collective-permute-start.16
  52.7 0.0 collective-permute-done.14
  52.7 1.7 %collective-permute-done.15 = f32[1,128]{1,0:T(1,128)S(1)} collective-permute-done((f32[1,128]{1,0:T(1,128)S(1)}, f32[1,128]{1,0:T(1,128)S(1)}, u32[]{:S(2)}, u32[]{:S(2)}) %collective-permute-start.15) | collective-permute-done | bytes 544 | tf_op jit(solution)/shard_map/ppermute | solution.py:458
  54.3 0.9 %collective-permute-done.16 = f32[1,128]{1,0:T(1,128)S(1)} collective-permute-done((f32[1,128]{1,0:T(1,128)S(1)}, f32[1,128]{1,0:T(1,128)S(1)}, u32[]{:S(2)}, u32[]{:S(2)}) %collective-permute-start.16) | collective-permute-done | bytes 544 | tf_op jit(solution)/shard_map/ppermute | solution.py:458
  55.3 0.6 %bitcast_divide_fusion = f32[128]{0:T(128)} fusion(f32[512]{0:T(512)S(1)} %copy-done, s32[]{:T(128)S(6)} %select_n.19, f32[1,128]{1,0:T(1,128)S(1)} %collective-permute-done.15, f32[1,128]{1,0:T(1,128)S(1)} %collective-permute-done.16, f32[1,128]{1,0:T(1,128)S(1)} %get-tuple-element.23, f32[1,128]{1,0:T(1,128)S(1)} %collective-permute-done.14), kind=kLoop, calls=%fused_computation.4 | loop fusion | flops 768 | bytes 3076 | tf_op jit(solution)/shard_map/div | solution.py:463
  (14 shorter events, 0.0 us)
Async XLA Ops:
  0.7 9.4 %copy-start.1 = (bf16[3,768,128]{2,1,0:T(8,128)(2,1)S(1)}, bf16[3,768,128]{2,1,0:T(8,128)(2,1)}, u32[]{:S(2)}) copy-start(bf16[3,768,128]{2,1,0:T(8,128)(2,1)} %refs_4_.5) | copy-start | bytes 1769476
  0.7 9.4 %copy-start.2 = (f32[9,768,16]{1,2,0:T(8,128)S(1)}, f32[9,768,16]{1,2,0:T(8,128)}, u32[]{:S(2)}) copy-start(f32[9,768,16]{1,2,0:T(8,128)} %param.11) | copy-start | bytes 1327108
  0.7 9.4 %copy-start.3 = (s32[768,16]{0,1:T(8,128)S(1)}, s32[768,16]{0,1:T(8,128)}, u32[]{:S(2)}) copy-start(s32[768,16]{0,1:T(8,128)} %param.12) | copy-start | bytes 147460
  0.7 9.4 %copy-start.4 = (s32[768]{0:T(1024)S(1)}, s32[768]{0:T(1024)}, u32[]{:S(2)}) copy-start(s32[768]{0:T(1024)} %refs_2_.5) | copy-start | bytes 9220
  4.8 9.5 %collective-permute-start.2 = (bf16[128,768]{1,0:T(8,128)(2,1)S(1)}, bf16[128,768]{1,0:T(8,128)(2,1)S(1)}, u32[]{:S(2)}, u32[]{:S(2)}) collective-permute-start(bf16[128,768]{1,0:T(8,128)(2,1)S(1)} %get-tuple-element.15.refs_5_.refs_0_), channel_id=1, source_target_pairs={{2,0},{0,2},{3,1},{1,3},{6,4},{4,6},{7,5},{5,7},{10,8},{8,10},{11,... | collective-permute-start | bytes 589832 | tf_op jit(solution)/shard_map/ppermute | solution.py:385
  7.8 6.0 %collective-permute-start = (bf16[3,96,128]{2,1,0:T(8,128)(2,1)S(1)}, bf16[3,96,128]{2,1,0:T(8,128)(2,1)S(1)}, u32[]{:S(2)}, u32[]{:S(2)}) collective-permute-start(bf16[3,96,128]{2,1,0:T(8,128)(2,1)S(1)} %get-tuple-element.13), channel_id=1, source_target_pairs={{0,4},{4,0},{8,12},{12,8},{1,5},{5,1},{9,13},{13,9},{2,6},{6,2},{1... | collective-permute-start | bytes 221192 | tf_op jit(solution)/shard_map/ppermute | solution.py:382
  9.4 4.9 %collective-permute-start.1 = (bf16[3,96,128]{2,1,0:T(8,128)(2,1)S(1)}, bf16[3,96,128]{2,1,0:T(8,128)(2,1)S(1)}, u32[]{:S(2)}, u32[]{:S(2)}) collective-permute-start(bf16[3,96,128]{2,1,0:T(8,128)(2,1)S(1)} %get-tuple-element.14), channel_id=1, source_target_pairs={{4,8},{8,4},{5,9},{9,5},{6,10},{10,6},{7,11},{11,7},{20,24},{24,20... | collective-permute-start | bytes 221192 | tf_op jit(solution)/shard_map/ppermute | solution.py:382
  13.2 6.2 %collective-permute-start.7 = (bf16[128,768]{1,0:T(8,128)(2,1)S(1)}, bf16[128,768]{1,0:T(8,128)(2,1)S(1)}, u32[]{:S(2)}, u32[]{:S(2)}) collective-permute-start(bf16[128,768]{1,0:T(8,128)(2,1)S(1)} %images.4.refs_7_.refs_1_), channel_id=1, source_target_pairs={{2,0},{0,2},{3,1},{1,3},{6,4},{4,6},{7,5},{5,7},{10,8},{8,10},{11,... | collective-permute-start | bytes 589832 | tf_op jit(solution)/shard_map/ppermute | solution.py:385
  13.8 5.5 %collective-permute-start.5 = (bf16[128,768]{1,0:T(8,128)(2,1)S(1)}, bf16[128,768]{1,0:T(8,128)(2,1)S(1)}, u32[]{:S(2)}, u32[]{:S(2)}) collective-permute-start(bf16[128,768]{1,0:T(8,128)(2,1)S(1)} %images.4.refs_7_.refs_1_), channel_id=1, source_target_pairs={{0,1},{1,0},{2,3},{3,2},{4,5},{5,4},{6,7},{7,6},{8,9},{9,8},{10,11... | collective-permute-start | bytes 589832 | tf_op jit(solution)/shard_map/ppermute | solution.py:388
  13.8 6.1 %collective-permute-start.4 = (bf16[128,768]{1,0:T(8,128)(2,1)S(1)}, bf16[128,768]{1,0:T(8,128)(2,1)S(1)}, u32[]{:S(2)}, u32[]{:S(2)}) collective-permute-start(bf16[128,768]{1,0:T(8,128)(2,1)S(1)} %get-tuple-element.15.refs_5_.refs_0_), channel_id=1, source_target_pairs={{0,1},{1,0},{2,3},{3,2},{4,5},{5,4},{6,7},{7,6},{8,9},{9,8},{10,11... | collective-permute-start | bytes 589832 | tf_op jit(solution)/shard_map/ppermute | solution.py:388
  17.4 2.5 %collective-permute-start.6 = (bf16[128,768]{1,0:T(8,128)(2,1)S(1)}, bf16[128,768]{1,0:T(8,128)(2,1)S(1)}, u32[]{:S(2)}, u32[]{:S(2)}) collective-permute-start(bf16[128,768]{1,0:T(8,128)(2,1)S(1)} %images.5.refs_2_), channel_id=1, source_target_pairs={{0,1},{1,0},{2,3},{3,2},{4,5},{5,4},{6,7},{7,6},{8,9},{9,8},{10,11... | collective-permute-start | bytes 589832 | tf_op jit(solution)/shard_map/ppermute | solution.py:388
  17.5 7.3 %collective-permute-start.3 = (bf16[128,768]{1,0:T(8,128)(2,1)S(1)}, bf16[128,768]{1,0:T(8,128)(2,1)S(1)}, u32[]{:S(2)}, u32[]{:S(2)}) collective-permute-start(bf16[128,768]{1,0:T(8,128)(2,1)S(1)} %images.5.refs_2_), channel_id=1, source_target_pairs={{2,0},{0,2},{3,1},{1,3},{6,4},{4,6},{7,5},{5,7},{10,8},{8,10},{11,... | collective-permute-start | bytes 589832 | tf_op jit(solution)/shard_map/ppermute | solution.py:385
  19.3 9.9 %collective-permute-start.9 = (bf16[128,768]{1,0:T(8,128)(2,1)S(1)}, bf16[128,768]{1,0:T(8,128)(2,1)S(1)}, u32[]{:S(2)}, u32[]{:S(2)}) collective-permute-start(bf16[128,768]{1,0:T(8,128)(2,1)S(1)} %collective-permute-done.2.refs_8_.refs_6_.refs_0_), channel_id=1, source_target_pairs={{0,1},{1,0},{2,3},{3,2},{4,5},{5,4},{6,7},{7,6},{8,9},{9,8},{10,11... | collective-permute-start | bytes 589832 | tf_op jit(solution)/shard_map/ppermute | solution.py:388
  19.3 9.9 %collective-permute-start.10 = (bf16[128,768]{1,0:T(8,128)(2,1)S(1)}, bf16[128,768]{1,0:T(8,128)(2,1)S(1)}, u32[]{:S(2)}, u32[]{:S(2)}) collective-permute-start(bf16[128,768]{1,0:T(8,128)(2,1)S(1)} %collective-permute-done.7.refs_7_.refs_1_), channel_id=1, source_target_pairs={{0,1},{1,0},{2,3},{3,2},{4,5},{5,4},{6,7},{7,6},{8,9},{9,8},{10,11... | collective-permute-start | bytes 589832 | tf_op jit(solution)/shard_map/ppermute | solution.py:388
  23.3 16.8 %copy-start.7 = (f32[640]{0:T(1024)S(1)}, f32[640]{0:T(1024)}, u32[]{:S(2)}) copy-start(f32[640]{0:T(1024)} %param.15) | copy-start | bytes 7684
  23.3 25.8 %copy-start = (f32[512]{0:T(512)S(1)}, f32[512]{0:T(512)}, u32[]{:S(2)}) copy-start(f32[512]{0:T(512)} %param.14) | copy-start | bytes 6148
  23.3 25.8 %copy-start.5 = (s32[512]{0:T(512)S(1)}, s32[512]{0:T(512)}, u32[]{:S(2)}) copy-start(s32[512]{0:T(512)} %param.16) | copy-start | bytes 6148
  23.3 25.8 %copy-start.6 = (s32[512]{0:T(512)S(1)}, s32[512]{0:T(512)}, u32[]{:S(2)}) copy-start(s32[512]{0:T(512)} %param.17) | copy-start | bytes 6148
  24.8 4.4 %collective-permute-start.11 = (bf16[128,768]{1,0:T(8,128)(2,1)S(1)}, bf16[128,768]{1,0:T(8,128)(2,1)S(1)}, u32[]{:S(2)}, u32[]{:S(2)}) collective-permute-start(bf16[128,768]{1,0:T(8,128)(2,1)S(1)} %collective-permute-done.3.refs_2_), channel_id=1, source_target_pairs={{0,1},{1,0},{2,3},{3,2},{4,5},{5,4},{6,7},{7,6},{8,9},{9,8},{10,11... | collective-permute-start | bytes 589832 | tf_op jit(solution)/shard_map/ppermute | solution.py:388
  24.8 9.3 %collective-permute-start.8 = (bf16[128,640]{1,0:T(8,128)(2,1)S(1)}, bf16[128,640]{1,0:T(8,128)(2,1)S(1)}, u32[]{:S(2)}, u32[]{:S(2)}) collective-permute-start(bf16[128,640]{1,0:T(8,128)(2,1)S(1)} %get-tuple-element.18), channel_id=1, source_target_pairs={{0,4},{4,0},{8,12},{12,8},{1,5},{5,1},{9,13},{13,9},{2,6},{6,2},{1... | collective-permute-start | bytes 491528 | tf_op jit(solution)/shard_map/ppermute | solution.py:407
  32.6 6.4 %collective-permute-start.12 = (bf16[128,640]{1,0:T(8,128)(2,1)S(1)}, bf16[128,640]{1,0:T(8,128)(2,1)S(1)}, u32[]{:S(2)}, u32[]{:S(2)}) collective-permute-start(bf16[128,640]{1,0:T(8,128)(2,1)S(1)} %get-tuple-element.21), channel_id=1, source_target_pairs={{0,4},{4,0},{8,12},{12,8},{1,5},{5,1},{9,13},{13,9},{2,6},{6,2},{1... | collective-permute-start | bytes 491528 | tf_op jit(solution)/shard_map/ppermute | solution.py:407
  39.1 10.0 %collective-permute-start.13 = (bf16[128,640]{1,0:T(8,128)(2,1)S(1)}, bf16[128,640]{1,0:T(8,128)(2,1)S(1)}, u32[]{:S(2)}, u32[]{:S(2)}) collective-permute-start(bf16[128,640]{1,0:T(8,128)(2,1)S(1)} %select_convert_fusion), channel_id=1, source_target_pairs={{0,8},{4,12},{8,0},{12,4},{1,9},{5,13},{9,1},{13,5},{2,10},{6,14},... | collective-permute-start | bytes 491528 | tf_op jit(solution)/shard_map/ppermute | solution.py:420
  50.8 1.9 %collective-permute-start.14 = (f32[1,128]{1,0:T(1,128)S(1)}, f32[1,128]{1,0:T(1,128)S(1)}, u32[]{:S(2)}, u32[]{:S(2)}) collective-permute-start(f32[1,128]{1,0:T(1,128)S(1)} %get-tuple-element.23), channel_id=1, source_target_pairs={{0,1},{1,0},{2,3},{3,2},{4,5},{5,4},{6,7},{7,6},{8,9},{9,8},{10,11... | collective-permute-start | bytes 1544 | tf_op jit(solution)/shard_map/ppermute | solution.py:458
  50.8 3.5 %collective-permute-start.15 = (f32[1,128]{1,0:T(1,128)S(1)}, f32[1,128]{1,0:T(1,128)S(1)}, u32[]{:S(2)}, u32[]{:S(2)}) collective-permute-start(f32[1,128]{1,0:T(1,128)S(1)} %get-tuple-element.23), channel_id=1, source_target_pairs={{0,2},{1,3},{2,0},{3,1},{4,6},{5,7},{6,4},{7,5},{8,10},{9,11},{10,... | collective-permute-start | bytes 1544 | tf_op jit(solution)/shard_map/ppermute | solution.py:458
  52.3 3.0 %collective-permute-start.16 = (f32[1,128]{1,0:T(1,128)S(1)}, f32[1,128]{1,0:T(1,128)S(1)}, u32[]{:S(2)}, u32[]{:S(2)}) collective-permute-start(f32[1,128]{1,0:T(1,128)S(1)} %get-tuple-element.23), channel_id=1, source_target_pairs={{0,3},{1,2},{2,1},{3,0},{4,7},{5,6},{6,5},{7,4},{8,11},{9,10},{10,... | collective-permute-start | bytes 1544 | tf_op jit(solution)/shard_map/ppermute | solution.py:458

commit v10 on v9

--- a/solution.py
+++ b/solution.py
@@ -99,7 +99,32 @@
     lax.fori_loop(0, SPAN // GROUP, group_step, 0)
 
 
-def images_of(blocks, spot, panel, nbr, coef, count, halos=(), before=(), edges=False):
+def edges_of(spot, panel):
+    rows, modes = panel.shape[1:]
+
+    def kernel(spot_ref, panel_hbm, one_ref, two_ref, sems):
+        copies = []
+        for turn, out in enumerate((one_ref, two_ref)):
+            at = pl.multiple_of(jnp.where(spot_ref[1] == turn, rows - HALO, 0), 32)
+            copies.append(pltpu.make_async_copy(panel_hbm.at[:, pl.ds(at, HALO)], out, sems.at[turn]))
+        for copy in copies:
+            copy.start()
+        for copy in copies:
+            copy.wait()
+
+    return call(
+        kernel,
+        "edges",
+        [SMEM, HBM],
+        [VMEM] * 2,
+        [pltpu.VMEM((3, HALO, modes), jnp.bfloat16)] * 2,
+        (spot, panel),
+        1.0,
+        [pltpu.SemaphoreType.DMA((2,))],
+    )
+
+
+def images_of(blocks, spot, panel, nbr, coef, count, halos=(), before=()):
     rows, modes = panel.shape[1:]
     loads = len(before) == 0
     operands = [spot, nbr, count, coef, panel, *halos, *before]
@@ -107,9 +132,6 @@
     width = len(blocks) * LANES
     out_shape = [pltpu.VMEM((modes, 3 * width), jnp.bfloat16)]
     out_specs = [VMEM]
-    if edges:
-        out_shape += [jax.ShapeDtypeStruct((3, HALO, modes), jnp.bfloat16)] * 2
-        out_specs += [ANY] * 2
     n_in, n_out = len(operands), len(out_shape)
 
     def pieces_of(block):
@@ -149,10 +171,6 @@
                     start(
                         panel_ref.at[:, pl.ds(source, length)], window_ref.at[place, :, pl.ds(at, length)], window_copies
                     )
-            if edges:
-                for turn, out in enumerate(outs[1:3]):
-                    at = pl.multiple_of(jnp.where(odd == turn, rows - HALO, 0), 32)
-                    start(panel_ref.at[:, pl.ds(at, HALO)], out, window_copies)
             for copy in copies:
                 copy.wait()
         else:
@@ -191,7 +209,7 @@
             pltpu.VMEM((BONDS, rows), jnp.int32),
             pltpu.VMEM((rows,), jnp.int32),
             pltpu.VMEM((9, BONDS, rows), jnp.float32),
-            pltpu.SemaphoreType.DMA((4 + 3 * len(blocks) + 2,)),
+            pltpu.SemaphoreType.DMA((4 + 3 * len(blocks),)),
         ]
     return call(kernel, "images", in_specs, out_specs, out_shape, operands, 0.8 + 1.2 * len(blocks), scratch)
 
@@ -376,10 +394,11 @@
     cut = len(middle) // 2
     chunks = [middle[:cut], middle[cut:], [last, 0]]
     shared = (spot, mode_panel, nbr, coef, bond_count)
-    near, edge_one, edge_two = images_of(chunks[0], *shared, edges=True)
+    edge_one, edge_two = edges_of(spot, mode_panel)
     pairs = [(z, z ^ 1) for z in range(atom_count)]
     others = [(z, ((z + 1) ^ 1) - 1) for z in range(1, atom_count - 1)]
     halos = (lax.ppermute(edge_one, "atoms", pairs), lax.ppermute(edge_two, "atoms", others))
+    near = images_of(chunks[0], *shared)[0]
 
     def from_group(cells, shift):
         return lax.ppermute(cells, "modes", [(m ^ shift, m) for m in range(groups)])
@@ -388,7 +407,7 @@
         return lax.ppermute(cells, "sub", [(0, 1), (1, 0)])
 
     far_all = {shift: [from_group(near, shift)] for shift in range(1, groups)}
-    middle_images = images_of(chunks[1], *shared, before=[near])[0]
+    middle_images = images_of(chunks[1], *shared, before=[near, *halos])[0]
     before = [middle_images, *[far[0] for far in far_all.values()]]
     mine = [near, middle_images, images_of(chunks[2], *shared, halos=halos, before=before)[0]]
     for shift, far in far_all.items():

time: 56.1 us -> 58.1 us (1.036)
  Pallas kernels: 18.7 us -> 20.2 us
  waiting for transfers between devices: 18.3 us -> 19.4 us
  starting transfers between devices: 17.1 us -> 16.5 us
    ppermute x1, starting transfers between devices: 1.58 us -> 3.09 us  [body(): lax.ppermute(edge_one, 'atoms', pairs)]
    pallas_call x6 -> x7, Pallas kernels: 18.7 us -> 20.2 us  [call(): pl.pallas_call(kernel, in_specs=in_specs, out_specs=out_specs, out_shape=...]
    ppermute x3, starting transfers between devices: 5.1 us -> 3.68 us  [from_group(): return lax.ppermute(cells, 'modes', [(m ^ shift, m) for m in range(groups)])]
    ppermute x3, waiting for transfers between devices: 1.83 us -> 3.05 us  [from_group(): return lax.ppermute(cells, 'modes', [(m ^ shift, m) for m in range(groups)])]
    ppermute x6, starting transfers between devices: 1.11 us -> 0.5 us  [from_sibling(): return lax.ppermute(cells, 'sub', [(0, 1), (1, 0)])]
  transfers between devices with their start and end apart: 17 -> 17, of which waited for: 6 -> 7; matrix products, arithmetic and copies ran while one was open for 0% -> 0% of each run, Pallas kernels for 23% -> 29%
where the time goes in v10:
time: 58.1 us; the launch traced here: 57.8 us
  Pallas kernels  20.2 us (35%)
  waiting for transfers between devices  19.4 us (33%)
  starting transfers between devices  16.5 us (28%)
  other arithmetic  0.88 us (2%)
  between operations  0.83 us (1%)
    pallas_call x7, Pallas kernels, call(): pl.pallas_call(kernel, in_specs=in_specs, out_specs=out_specs, out_shape=...  20.2 us
    ppermute x1, waiting for transfers between devices, body(): lax.ppermute(sent, 'atoms', [(z, z ^ 2) for z in range(atom_count)])  8.77 us
    ppermute x2, starting transfers between devices, next_door(): return (keep, lax.ppermute(send, 'atoms', pairs))  5.6 us
    ppermute x2, waiting for transfers between devices, next_door(): return (keep, lax.ppermute(send, 'atoms', pairs))  4.91 us
    ppermute x3, starting transfers between devices, from_group(): return lax.ppermute(cells, 'modes', [(m ^ shift, m) for m in range(groups)])  3.68 us
    ppermute x1, starting transfers between devices, body(): lax.ppermute(edge_one, 'atoms', pairs)  3.09 us
    ppermute x3, waiting for transfers between devices, from_group(): return lax.ppermute(cells, 'modes', [(m ^ shift, m) for m in range(groups)])  3.05 us
    ppermute x3, waiting for transfers between devices, body(): lax.ppermute(numerator, ('modes', 'sub'), [(i, i ^ code) for i in range(h...  2.63 us
  transfers between devices with their start and end apart: 17, of which 7 were waited for; matrix products, arithmetic and copies ran while one was open for 0% of the time, Pallas kernels for 29%

profile of v10, /device:TPU:0, one launch (start us, length us, event | category | flops | bytes accessed | tf_op | source)
XLA Modules:
  0.0 57.8 jit_solution(10695771620339387916)
XLA Ops:
  0.6 0.1 pad_add_fusion.1.spot_ref.refs_0_
  0.7 1.5 %edges.1 = (bf16[3,96,128]{2,1,0:T(8,128)(2,1)S(1)}, bf16[3,96,128]{2,1,0:T(8,128)(2,1)S(1)}) custom-call(s32[2]{0:T(128)S(1)} %pad_add_fusion.1.spot_ref.refs_0_, bf16[3,768,128]{2,1,0:T(8,128)(2,1)} %refs_4_.5), custom_call_target="tpu_custom_call" | custom-call | flops 1100000000 | bytes 100000 | tf_op jit(solution)/shard_map/edges/pallas_call | solution.py:33
  2.2 3.1 %collective-permute-start = (bf16[3,96,128]{2,1,0:T(8,128)(2,1)S(1)}, bf16[3,96,128]{2,1,0:T(8,128)(2,1)S(1)}, u32[]{:S(2)}, u32[]{:S(2)}) collective-permute-start(bf16[3,96,128]{2,1,0:T(8,128)(2,1)S(1)} %get-tuple-element.12), channel_id=1, source_target_pairs={{0,4},{4,0},{8,12},{12,8},{1,5},{5,1},{9,13},{13,9},{2,6},{6,2},{1... | collective-permute-start | bytes 221192 | tf_op jit(solution)/shard_map/ppermute | solution.py:400
  5.3 0.7 %collective-permute-start.1 = (bf16[3,96,128]{2,1,0:T(8,128)(2,1)S(1)}, bf16[3,96,128]{2,1,0:T(8,128)(2,1)S(1)}, u32[]{:S(2)}, u32[]{:S(2)}) collective-permute-start(bf16[3,96,128]{2,1,0:T(8,128)(2,1)S(1)} %get-tuple-element.13), channel_id=1, source_target_pairs={{4,8},{8,4},{5,9},{9,5},{6,10},{10,6},{7,11},{11,7},{20,24},{24,20... | collective-permute-start | bytes 221192 | tf_op jit(solution)/shard_map/ppermute | solution.py:400
  6.0 0.0 copy-start.1
  6.0 0.0 copy-start.2
  6.0 0.0 copy-start.3
  6.0 0.0 copy-start.4
  6.0 4.1 %images.3.refs_5_.refs_0_ = bf16[128,768]{1,0:T(8,128)(2,1)S(1)} custom-call(s32[2]{0:T(128)S(1)} %pad_add_fusion.1.spot_ref.refs_0_, s32[16,768]{1,0:T(8,128)} %bitcast.17, s32[768]{0:T(1024)} %refs_2_.5, f32[9,16,768]{2,1,0:T(8,128)} %bitcast.14, bf16[3,768,128]{2,1,0:T(8,128)(2,1)} %refs_4_.5), custom_call_target="tpu_custom_call" | custom-call | flops 3520000000 | bytes 320000 | tf_op jit(solution)/shard_map/images/pallas_call | solution.py:33
  10.1 1.6 %collective-permute-start.2 = (bf16[128,768]{1,0:T(8,128)(2,1)S(1)}, bf16[128,768]{1,0:T(8,128)(2,1)S(1)}, u32[]{:S(2)}, u32[]{:S(2)}) collective-permute-start(bf16[128,768]{1,0:T(8,128)(2,1)S(1)} %images.3.refs_5_.refs_0_), channel_id=1, source_target_pairs={{2,0},{0,2},{3,1},{1,3},{6,4},{4,6},{7,5},{5,7},{10,8},{8,10},{11,... | collective-permute-start | bytes 589832 | tf_op jit(solution)/shard_map/ppermute | solution.py:404
  11.7 0.0 collective-permute-done.refs_6_.refs_5_
  11.7 0.0 collective-permute-done.1.refs_7_.refs_6_
  11.7 3.1 %images.4.refs_7_.refs_1_ = bf16[128,768]{1,0:T(8,128)(2,1)S(1)} custom-call(s32[2]{0:T(128)S(1)} %pad_add_fusion.1.spot_ref.refs_0_, s32[16,768]{1,0:T(8,128)S(1)} %bitcast.18, s32[768]{0:T(1024)S(1)} %copy-done.4, f32[9,16,768]{2,1,0:T(8,128)S(1)} %bitcast.15, bf16[3,768,128]{2,1,0:T(8,128)(2,1)S(1)} %copy-done.1, ...), custom_call_target="tpu_custom_call" | custom-call | flops 3520000000 | bytes 320000 | tf_op jit(solution)/shard_map/images/pallas_call | solution.py:33
  14.8 0.6 %collective-permute-start.7 = (bf16[128,768]{1,0:T(8,128)(2,1)S(1)}, bf16[128,768]{1,0:T(8,128)(2,1)S(1)}, u32[]{:S(2)}, u32[]{:S(2)}) collective-permute-start(bf16[128,768]{1,0:T(8,128)(2,1)S(1)} %images.4.refs_7_.refs_1_), channel_id=1, source_target_pairs={{2,0},{0,2},{3,1},{1,3},{6,4},{4,6},{7,5},{5,7},{10,8},{8,10},{11,... | collective-permute-start | bytes 589832 | tf_op jit(solution)/shard_map/ppermute | solution.py:404
  15.4 0.2 collective-permute-start.5
  15.6 0.9 %collective-permute-done.2.refs_8_.refs_6_.refs_0_ = bf16[128,768]{1,0:T(8,128)(2,1)S(1)} collective-permute-done((bf16[128,768]{1,0:T(8,128)(2,1)S(1)}, bf16[128,768]{1,0:T(8,128)(2,1)S(1)}, u32[]{:S(2)}, u32[]{:S(2)}) %collective-permute-start.2) | collective-permute-done | bytes 196640 | tf_op jit(solution)/shard_map/ppermute | solution.py:404
  16.5 3.0 %images.5.refs_2_ = bf16[128,768]{1,0:T(8,128)(2,1)S(1)} custom-call(s32[2]{0:T(128)S(1)} %pad_add_fusion.1.spot_ref.refs_0_, s32[16,768]{1,0:T(8,128)S(1)} %bitcast.19, s32[768]{0:T(1024)S(1)} %copy-done.4, f32[9,16,768]{2,1,0:T(8,128)S(1)} %bitcast.16, bf16[3,768,128]{2,1,0:T(8,128)(2,1)S(1)} %copy-done.1, ...), custom_call_target="tpu_custom_call" | custom-call | flops 3520000000 | bytes 320000 | tf_op jit(solution)/shard_map/images/pallas_call | solution.py:33
  19.6 0.1 collective-permute-start.6
  19.6 0.1 pad_add_fusion.2.place_ref
  19.7 1.5 %collective-permute-start.3 = (bf16[128,768]{1,0:T(8,128)(2,1)S(1)}, bf16[128,768]{1,0:T(8,128)(2,1)S(1)}, u32[]{:S(2)}, u32[]{:S(2)}) collective-permute-start(bf16[128,768]{1,0:T(8,128)(2,1)S(1)} %images.5.refs_2_), channel_id=1, source_target_pairs={{2,0},{0,2},{3,1},{1,3},{6,4},{4,6},{7,5},{5,7},{10,8},{8,10},{11,... | collective-permute-start | bytes 589832 | tf_op jit(solution)/shard_map/ppermute | solution.py:404
  21.2 0.0 collective-permute-done.4.refs_3_
  21.2 0.2 collective-permute-start.9
  21.4 0.7 %collective-permute-done.7.refs_7_.refs_1_ = bf16[128,768]{1,0:T(8,128)(2,1)S(1)} collective-permute-done((bf16[128,768]{1,0:T(8,128)(2,1)S(1)}, bf16[128,768]{1,0:T(8,128)(2,1)S(1)}, u32[]{:S(2)}, u32[]{:S(2)}) %collective-permute-start.7) | collective-permute-done | bytes 196640 | tf_op jit(solution)/shard_map/ppermute | solution.py:404
  22.1 0.0 collective-permute-start.10
  22.1 0.0 collective-permute-done.5.refs_4_
  22.1 3.4 %products.2 = (f32[128,640]{1,0:T(8,128)S(1)}, bf16[128,640]{1,0:T(8,128)(2,1)S(1)}) custom-call(s32[2]{0:T(128)S(1)} %pad_add_fusion.2.place_ref, bf16[3,768,640]{2,1,0:T(8,128)(2,1)} %partners_hbm.3, bf16[128,768]{1,0:T(8,128)(2,1)S(1)} %images.3.refs_5_.refs_0_, bf16[128,768]{1,0:T(8,128)(2,1)S(1)} %images.4.refs_7_.refs_1_, ...), custom_call_target="tpu_custom_call" | custom-call | flops 6600000000 | bytes 600000 | tf_op jit(solution)/shard_map/products/pallas_call | solution.py:33
  25.6 0.0 copy-start.7
  25.6 0.0 copy-start
  25.6 0.0 copy-start.5
  25.6 0.0 copy-start.6
  25.6 1.4 %collective-permute-done.3.refs_2_ = bf16[128,768]{1,0:T(8,128)(2,1)S(1)} collective-permute-done((bf16[128,768]{1,0:T(8,128)(2,1)S(1)}, bf16[128,768]{1,0:T(8,128)(2,1)S(1)}, u32[]{:S(2)}, u32[]{:S(2)}) %collective-permute-start.3) | collective-permute-done | bytes 196640 | tf_op jit(solution)/shard_map/ppermute | solution.py:404
  27.0 4.1 %collective-permute-start.8 = (bf16[128,640]{1,0:T(8,128)(2,1)S(1)}, bf16[128,640]{1,0:T(8,128)(2,1)S(1)}, u32[]{:S(2)}, u32[]{:S(2)}) collective-permute-start(bf16[128,640]{1,0:T(8,128)(2,1)S(1)} %get-tuple-element.16), channel_id=1, source_target_pairs={{0,4},{4,0},{8,12},{12,8},{1,5},{5,1},{9,13},{13,9},{2,6},{6,2},{1... | collective-permute-start | bytes 491528 | tf_op jit(solution)/shard_map/ppermute | solution.py:426
  31.1 0.0 collective-permute-done.9.refs_3_
  31.1 0.0 collective-permute-done.10.refs_4_
  31.1 0.0 collective-permute-done.11.refs_5_
  31.2 3.4 %products.3 = (f32[128,640]{1,0:T(8,128)S(1)}, bf16[128,640]{1,0:T(8,128)(2,1)S(1)}) custom-call(s32[2]{0:T(128)S(1)} %pad_add_fusion.2.place_ref, bf16[3,768,640]{2,1,0:T(8,128)(2,1)} %partners_hbm.3, bf16[128,768]{1,0:T(8,128)(2,1)S(1)} %collective-permute-done.2.refs_8_.refs_6_.refs_0_, bf16[128,768]{1,0:T(8,128)(2,1)S(1)} %collective-permute-done.7.refs_7_.refs_1_, ...), custom_call_target="tpu_custom_call" | custom-call | flops 110000000 | bytes 10000 | tf_op jit(solution)/shard_map/products/pallas_call | solution.py:33
  34.6 1.5 %collective-permute-start.12 = (bf16[128,640]{1,0:T(8,128)(2,1)S(1)}, bf16[128,640]{1,0:T(8,128)(2,1)S(1)}, u32[]{:S(2)}, u32[]{:S(2)}) collective-permute-start(bf16[128,640]{1,0:T(8,128)(2,1)S(1)} %get-tuple-element.19), channel_id=1, source_target_pairs={{0,4},{4,0},{8,12},{12,8},{1,5},{5,1},{9,13},{13,9},{2,6},{6,2},{1... | collective-permute-start | bytes 491528 | tf_op jit(solution)/shard_map/ppermute | solution.py:426
  36.1 4.9 %collective-permute-done.12.refs_4_ = bf16[128,640]{1,0:T(8,128)(2,1)S(1)} collective-permute-done((bf16[128,640]{1,0:T(8,128)(2,1)S(1)}, bf16[128,640]{1,0:T(8,128)(2,1)S(1)}, u32[]{:S(2)}, u32[]{:S(2)}) %collective-permute-start.12) | collective-permute-done | bytes 163872 | tf_op jit(solution)/shard_map/ppermute | solution.py:426
  41.0 0.1 select_convert_fusion
  41.0 1.1 %collective-permute-start.13 = (bf16[128,640]{1,0:T(8,128)(2,1)S(1)}, bf16[128,640]{1,0:T(8,128)(2,1)S(1)}, u32[]{:S(2)}, u32[]{:S(2)}) collective-permute-start(bf16[128,640]{1,0:T(8,128)(2,1)S(1)} %select_convert_fusion), channel_id=1, source_target_pairs={{0,8},{4,12},{8,0},{12,4},{1,9},{5,13},{9,1},{13,5},{2,10},{6,14},... | collective-permute-start | bytes 491528 | tf_op jit(solution)/shard_map/ppermute | solution.py:439
  42.2 0.1 pad_add_fusion.flag_ref
  42.2 8.8 %collective-permute-done.13.refs_2_.refs_5_ = bf16[128,640]{1,0:T(8,128)(2,1)S(1)} collective-permute-done((bf16[128,640]{1,0:T(8,128)(2,1)S(1)}, bf16[128,640]{1,0:T(8,128)(2,1)S(1)}, u32[]{:S(2)}, u32[]{:S(2)}) %collective-permute-start.13) | collective-permute-done | bytes 163872 | tf_op jit(solution)/shard_map/ppermute | solution.py:439
  51.0 1.7 %finish.1 = (f32[128,640]{1,0:T(8,128)}, f32[1,128]{1,0:T(1,128)S(1)}) custom-call(s32[3]{0:T(128)S(1)} %pad_add_fusion.flag_ref, s32[4,128]{1,0:T(4,128)S(1)} %bitcast.20, s32[4,128]{1,0:T(4,128)S(1)} %bitcast.21, f32[4,128]{1,0:T(4,128)S(1)} %bitcast.13, f32[1,640]{1,0:T(1,128)S(1)} %broadcast_in_dim.3.partner_ref, ...), custom_call_target="tpu_custom_call" | custom-call | flops 2200000000 | bytes 200000 | tf_op jit(solution)/shard_map/finish/pallas_call | solution.py:33
  52.7 1.5 %collective-permute-start.15 = (f32[1,128]{1,0:T(1,128)S(1)}, f32[1,128]{1,0:T(1,128)S(1)}, u32[]{:S(2)}, u32[]{:S(2)}) collective-permute-start(f32[1,128]{1,0:T(1,128)S(1)} %get-tuple-element.21), channel_id=1, source_target_pairs={{0,2},{1,3},{2,0},{3,1},{4,6},{5,7},{6,4},{7,5},{8,10},{9,11},{10,... | collective-permute-start | bytes 1544 | tf_op jit(solution)/shard_map/ppermute | solution.py:477
  54.2 0.3 collective-permute-start.16
  54.6 1.7 %collective-permute-done.15 = f32[1,128]{1,0:T(1,128)S(1)} collective-permute-done((f32[1,128]{1,0:T(1,128)S(1)}, f32[1,128]{1,0:T(1,128)S(1)}, u32[]{:S(2)}, u32[]{:S(2)}) %collective-permute-start.15) | collective-permute-done | bytes 544 | tf_op jit(solution)/shard_map/ppermute | solution.py:477
  56.3 0.9 %collective-permute-done.16 = f32[1,128]{1,0:T(1,128)S(1)} collective-permute-done((f32[1,128]{1,0:T(1,128)S(1)}, f32[1,128]{1,0:T(1,128)S(1)}, u32[]{:S(2)}, u32[]{:S(2)}) %collective-permute-start.16) | collective-permute-done | bytes 544 | tf_op jit(solution)/shard_map/ppermute | solution.py:477
  57.2 0.6 %bitcast_divide_fusion = f32[128]{0:T(128)} fusion(f32[512]{0:T(512)S(1)} %copy-done, s32[]{:T(128)S(6)} %select_n.19, f32[1,128]{1,0:T(1,128)S(1)} %collective-permute-done.15, f32[1,128]{1,0:T(1,128)S(1)} %collective-permute-done.16, f32[1,128]{1,0:T(1,128)S(1)} %get-tuple-element.21, f32[1,128]{1,0:T(1,128)S(1)} %collective-permute-done.14), kind=kLoop, calls=%fused_computation.4 | loop fusion | flops 768 | bytes 3076 | tf_op jit(solution)/shard_map/div | solution.py:482
  (15 shorter events, 0.0 us)
Async XLA Ops:
  2.2 9.5 %collective-permute-start = (bf16[3,96,128]{2,1,0:T(8,128)(2,1)S(1)}, bf16[3,96,128]{2,1,0:T(8,128)(2,1)S(1)}, u32[]{:S(2)}, u32[]{:S(2)}) collective-permute-start(bf16[3,96,128]{2,1,0:T(8,128)(2,1)S(1)} %get-tuple-element.12), channel_id=1, source_target_pairs={{0,4},{4,0},{8,12},{12,8},{1,5},{5,1},{9,13},{13,9},{2,6},{6,2},{1... | collective-permute-start | bytes 221192 | tf_op jit(solution)/shard_map/ppermute | solution.py:400
  5.3 6.4 %collective-permute-start.1 = (bf16[3,96,128]{2,1,0:T(8,128)(2,1)S(1)}, bf16[3,96,128]{2,1,0:T(8,128)(2,1)S(1)}, u32[]{:S(2)}, u32[]{:S(2)}) collective-permute-start(bf16[3,96,128]{2,1,0:T(8,128)(2,1)S(1)} %get-tuple-element.13), channel_id=1, source_target_pairs={{4,8},{8,4},{5,9},{9,5},{6,10},{10,6},{7,11},{11,7},{20,24},{24,20... | collective-permute-start | bytes 221192 | tf_op jit(solution)/shard_map/ppermute | solution.py:400
  6.0 5.7 %copy-start.1 = (bf16[3,768,128]{2,1,0:T(8,128)(2,1)S(1)}, bf16[3,768,128]{2,1,0:T(8,128)(2,1)}, u32[]{:S(2)}) copy-start(bf16[3,768,128]{2,1,0:T(8,128)(2,1)} %refs_4_.5) | copy-start | bytes 1769476
  6.0 5.7 %copy-start.2 = (f32[9,768,16]{1,2,0:T(8,128)S(1)}, f32[9,768,16]{1,2,0:T(8,128)}, u32[]{:S(2)}) copy-start(f32[9,768,16]{1,2,0:T(8,128)} %param.11) | copy-start | bytes 1327108
  6.0 5.7 %copy-start.3 = (s32[768,16]{0,1:T(8,128)S(1)}, s32[768,16]{0,1:T(8,128)}, u32[]{:S(2)}) copy-start(s32[768,16]{0,1:T(8,128)} %param.12) | copy-start | bytes 147460
  6.0 5.7 %copy-start.4 = (s32[768]{0:T(1024)S(1)}, s32[768]{0:T(1024)}, u32[]{:S(2)}) copy-start(s32[768]{0:T(1024)} %refs_2_.5) | copy-start | bytes 9220
  10.1 6.4 %collective-permute-start.2 = (bf16[128,768]{1,0:T(8,128)(2,1)S(1)}, bf16[128,768]{1,0:T(8,128)(2,1)S(1)}, u32[]{:S(2)}, u32[]{:S(2)}) collective-permute-start(bf16[128,768]{1,0:T(8,128)(2,1)S(1)} %images.3.refs_5_.refs_0_), channel_id=1, source_target_pairs={{2,0},{0,2},{3,1},{1,3},{6,4},{4,6},{7,5},{5,7},{10,8},{8,10},{11,... | collective-permute-start | bytes 589832 | tf_op jit(solution)/shard_map/ppermute | solution.py:404
  11.7 9.6 %collective-permute-start.4 = (bf16[128,768]{1,0:T(8,128)(2,1)S(1)}, bf16[128,768]{1,0:T(8,128)(2,1)S(1)}, u32[]{:S(2)}, u32[]{:S(2)}) collective-permute-start(bf16[128,768]{1,0:T(8,128)(2,1)S(1)} %images.3.refs_5_.refs_0_), channel_id=1, source_target_pairs={{0,1},{1,0},{2,3},{3,2},{4,5},{5,4},{6,7},{7,6},{8,9},{9,8},{10,11... | collective-permute-start | bytes 589832 | tf_op jit(solution)/shard_map/ppermute | solution.py:407
  14.8 7.4 %collective-permute-start.7 = (bf16[128,768]{1,0:T(8,128)(2,1)S(1)}, bf16[128,768]{1,0:T(8,128)(2,1)S(1)}, u32[]{:S(2)}, u32[]{:S(2)}) collective-permute-start(bf16[128,768]{1,0:T(8,128)(2,1)S(1)} %images.4.refs_7_.refs_1_), channel_id=1, source_target_pairs={{2,0},{0,2},{3,1},{1,3},{6,4},{4,6},{7,5},{5,7},{10,8},{8,10},{11,... | collective-permute-start | bytes 589832 | tf_op jit(solution)/shard_map/ppermute | solution.py:404
  15.4 6.8 %collective-permute-start.5 = (bf16[128,768]{1,0:T(8,128)(2,1)S(1)}, bf16[128,768]{1,0:T(8,128)(2,1)S(1)}, u32[]{:S(2)}, u32[]{:S(2)}) collective-permute-start(bf16[128,768]{1,0:T(8,128)(2,1)S(1)} %images.4.refs_7_.refs_1_), channel_id=1, source_target_pairs={{0,1},{1,0},{2,3},{3,2},{4,5},{5,4},{6,7},{7,6},{8,9},{9,8},{10,11... | collective-permute-start | bytes 589832 | tf_op jit(solution)/shard_map/ppermute | solution.py:407
  19.6 2.6 %collective-permute-start.6 = (bf16[128,768]{1,0:T(8,128)(2,1)S(1)}, bf16[128,768]{1,0:T(8,128)(2,1)S(1)}, u32[]{:S(2)}, u32[]{:S(2)}) collective-permute-start(bf16[128,768]{1,0:T(8,128)(2,1)S(1)} %images.5.refs_2_), channel_id=1, source_target_pairs={{0,1},{1,0},{2,3},{3,2},{4,5},{5,4},{6,7},{7,6},{8,9},{9,8},{10,11... | collective-permute-start | bytes 589832 | tf_op jit(solution)/shard_map/ppermute | solution.py:407
  19.7 7.3 %collective-permute-start.3 = (bf16[128,768]{1,0:T(8,128)(2,1)S(1)}, bf16[128,768]{1,0:T(8,128)(2,1)S(1)}, u32[]{:S(2)}, u32[]{:S(2)}) collective-permute-start(bf16[128,768]{1,0:T(8,128)(2,1)S(1)} %images.5.refs_2_), channel_id=1, source_target_pairs={{2,0},{0,2},{3,1},{1,3},{6,4},{4,6},{7,5},{5,7},{10,8},{8,10},{11,... | collective-permute-start | bytes 589832 | tf_op jit(solution)/shard_map/ppermute | solution.py:404
  21.2 9.9 %collective-permute-start.9 = (bf16[128,768]{1,0:T(8,128)(2,1)S(1)}, bf16[128,768]{1,0:T(8,128)(2,1)S(1)}, u32[]{:S(2)}, u32[]{:S(2)}) collective-permute-start(bf16[128,768]{1,0:T(8,128)(2,1)S(1)} %collective-permute-done.2.refs_8_.refs_6_.refs_0_), channel_id=1, source_target_pairs={{0,1},{1,0},{2,3},{3,2},{4,5},{5,4},{6,7},{7,6},{8,9},{9,8},{10,11... | collective-permute-start | bytes 589832 | tf_op jit(solution)/shard_map/ppermute | solution.py:407
  22.1 9.0 %collective-permute-start.10 = (bf16[128,768]{1,0:T(8,128)(2,1)S(1)}, bf16[128,768]{1,0:T(8,128)(2,1)S(1)}, u32[]{:S(2)}, u32[]{:S(2)}) collective-permute-start(bf16[128,768]{1,0:T(8,128)(2,1)S(1)} %collective-permute-done.7.refs_7_.refs_1_), channel_id=1, source_target_pairs={{0,1},{1,0},{2,3},{3,2},{4,5},{5,4},{6,7},{7,6},{8,9},{9,8},{10,11... | collective-permute-start | bytes 589832 | tf_op jit(solution)/shard_map/ppermute | solution.py:407
  25.6 16.6 %copy-start.7 = (f32[640]{0:T(1024)S(1)}, f32[640]{0:T(1024)}, u32[]{:S(2)}) copy-start(f32[640]{0:T(1024)} %param.15) | copy-start | bytes 7684
  25.6 25.4 %copy-start = (f32[512]{0:T(512)S(1)}, f32[512]{0:T(512)}, u32[]{:S(2)}) copy-start(f32[512]{0:T(512)} %param.14) | copy-start | bytes 6148
  25.6 25.4 %copy-start.5 = (s32[512]{0:T(512)S(1)}, s32[512]{0:T(512)}, u32[]{:S(2)}) copy-start(s32[512]{0:T(512)} %param.16) | copy-start | bytes 6148
  25.6 25.4 %copy-start.6 = (s32[512]{0:T(512)S(1)}, s32[512]{0:T(512)}, u32[]{:S(2)}) copy-start(s32[512]{0:T(512)} %param.17) | copy-start | bytes 6148
  27.0 4.1 %collective-permute-start.11 = (bf16[128,768]{1,0:T(8,128)(2,1)S(1)}, bf16[128,768]{1,0:T(8,128)(2,1)S(1)}, u32[]{:S(2)}, u32[]{:S(2)}) collective-permute-start(bf16[128,768]{1,0:T(8,128)(2,1)S(1)} %collective-permute-done.3.refs_2_), channel_id=1, source_target_pairs={{0,1},{1,0},{2,3},{3,2},{4,5},{5,4},{6,7},{7,6},{8,9},{9,8},{10,11... | collective-permute-start | bytes 589832 | tf_op jit(solution)/shard_map/ppermute | solution.py:407
  27.0 9.0 %collective-permute-start.8 = (bf16[128,640]{1,0:T(8,128)(2,1)S(1)}, bf16[128,640]{1,0:T(8,128)(2,1)S(1)}, u32[]{:S(2)}, u32[]{:S(2)}) collective-permute-start(bf16[128,640]{1,0:T(8,128)(2,1)S(1)} %get-tuple-element.16), channel_id=1, source_target_pairs={{0,4},{4,0},{8,12},{12,8},{1,5},{5,1},{9,13},{13,9},{2,6},{6,2},{1... | collective-permute-start | bytes 491528 | tf_op jit(solution)/shard_map/ppermute | solution.py:426
  34.6 6.4 %collective-permute-start.12 = (bf16[128,640]{1,0:T(8,128)(2,1)S(1)}, bf16[128,640]{1,0:T(8,128)(2,1)S(1)}, u32[]{:S(2)}, u32[]{:S(2)}) collective-permute-start(bf16[128,640]{1,0:T(8,128)(2,1)S(1)} %get-tuple-element.19), channel_id=1, source_target_pairs={{0,4},{4,0},{8,12},{12,8},{1,5},{5,1},{9,13},{13,9},{2,6},{6,2},{1... | collective-permute-start | bytes 491528 | tf_op jit(solution)/shard_map/ppermute | solution.py:426
  41.0 10.0 %collective-permute-start.13 = (bf16[128,640]{1,0:T(8,128)(2,1)S(1)}, bf16[128,640]{1,0:T(8,128)(2,1)S(1)}, u32[]{:S(2)}, u32[]{:S(2)}) collective-permute-start(bf16[128,640]{1,0:T(8,128)(2,1)S(1)} %select_convert_fusion), channel_id=1, source_target_pairs={{0,8},{4,12},{8,0},{12,4},{1,9},{5,13},{9,1},{13,5},{2,10},{6,14},... | collective-permute-start | bytes 491528 | tf_op jit(solution)/shard_map/ppermute | solution.py:439
  52.7 1.9 %collective-permute-start.14 = (f32[1,128]{1,0:T(1,128)S(1)}, f32[1,128]{1,0:T(1,128)S(1)}, u32[]{:S(2)}, u32[]{:S(2)}) collective-permute-start(f32[1,128]{1,0:T(1,128)S(1)} %get-tuple-element.21), channel_id=1, source_target_pairs={{0,1},{1,0},{2,3},{3,2},{4,5},{5,4},{6,7},{7,6},{8,9},{9,8},{10,11... | collective-permute-start | bytes 1544 | tf_op jit(solution)/shard_map/ppermute | solution.py:477
  52.7 3.5 %collective-permute-start.15 = (f32[1,128]{1,0:T(1,128)S(1)}, f32[1,128]{1,0:T(1,128)S(1)}, u32[]{:S(2)}, u32[]{:S(2)}) collective-permute-start(f32[1,128]{1,0:T(1,128)S(1)} %get-tuple-element.21), channel_id=1, source_target_pairs={{0,2},{1,3},{2,0},{3,1},{4,6},{5,7},{6,4},{7,5},{8,10},{9,11},{10,... | collective-permute-start | bytes 1544 | tf_op jit(solution)/shard_map/ppermute | solution.py:477
  54.2 3.0 %collective-permute-start.16 = (f32[1,128]{1,0:T(1,128)S(1)}, f32[1,128]{1,0:T(1,128)S(1)}, u32[]{:S(2)}, u32[]{:S(2)}) collective-permute-start(f32[1,128]{1,0:T(1,128)S(1)} %get-tuple-element.21), channel_id=1, source_target_pairs={{0,3},{1,2},{2,1},{3,0},{4,7},{5,6},{6,5},{7,4},{8,11},{9,10},{10,... | collective-permute-start | bytes 1544 | tf_op jit(solution)/shard_map/ppermute | solution.py:477

commit v11 on v9

--- a/solution.py
+++ b/solution.py
@@ -196,13 +196,14 @@
     return call(kernel, "images", in_specs, out_specs, out_shape, operands, 0.8 + 1.2 * len(blocks), scratch)
 
 
-def products_of(chunks, place, partners, mine, theirs, after=(), busy_us=2.0):
+def products_of(chunks, place, partners, mine, theirs, after=(), busy_us=2.0, parts=1):
     rows, cols = mine[0].shape[0], partners.shape[2]
     count = len(chunks)
     depth = partners.shape[1]
 
     def kernel(place_ref, partners_hbm, *refs):
-        keep_ref, send_ref, left_ref, partners_ref, sems = refs[-5:]
+        keep_ref, *send_refs = refs[-4 - parts : -3]
+        left_ref, partners_ref, sems = refs[-3:]
         copies = [
             pltpu.make_async_copy(partners_hbm.at[r], partners_ref.at[r], sems.at[r]) for r in range(3)
         ]
@@ -226,14 +227,16 @@
             )
             total = part if total is None else total + part
         keep_ref[...] = total[:rows]
-        send_ref[...] = total[rows:].astype(jnp.bfloat16)
+        for part, send_ref in enumerate(send_refs):
+            at = rows + part * (rows // parts)
+            send_ref[...] = total[at : at + rows // parts].astype(jnp.bfloat16)
 
     return call(
         kernel,
         "products",
         [SMEM, HBM] + [VMEM] * (2 * count) + [ANY] * len(after),
-        [VMEM, VMEM],
-        [pltpu.VMEM((rows, cols), jnp.float32), pltpu.VMEM((rows, cols), jnp.bfloat16)],
+        [VMEM] * (1 + parts),
+        [pltpu.VMEM((rows, cols), jnp.float32)] + [pltpu.VMEM((rows // parts, cols), jnp.bfloat16)] * parts,
         (place, partners, *mine, *theirs, *after),
         busy_us,
         [
@@ -284,26 +287,31 @@
 
 
 def finish(flag, early, late, starts, lengths, freqs, partner_freq, norm_scale):
-    rows, cols = early[0].shape
-    n_early = len(early)
-    operands = [flag, starts, lengths, freqs, partner_freq, *early, *late]
+    rows, cols = early[0][0].shape
+    terms = early + late
+    operands = [flag, starts, lengths, freqs, partner_freq, *[piece for term in terms for piece in term]]
     step = 16
 
     def kernel(flag_ref, starts_ref, lengths_ref, freqs_ref, partner_ref, *refs):
         out_ref, sum_ref, start_ref, end_ref, freq_ref, folded_ref = refs[-6:]
-        def sums(some):
-            total = some[0][...]
-            for ref in some[1:]:
-                total = total + ref[...].astype(jnp.float32)
-            return total
+        pieces = iter(refs[:-6])
+        grouped = [[next(pieces) for _ in term] for term in terms]
+
+        def add_up(some):
+            out_ref[...] = some[0][0][...]
+            for term in some[1:]:
+                span = rows // len(term)
+                for i, ref in enumerate(term):
+                    at = slice(i * span, (i + 1) * span)
+                    out_ref[at, :] = out_ref[at, :] + ref[...].astype(jnp.float32)
 
         @pl.when(flag_ref[0] == 1)
         def _():
-            out_ref[...] = sums(refs[:n_early])
+            add_up(grouped[: len(early)])
 
         @pl.when(flag_ref[0] == 0)
         def _():
-            out_ref[...] = sums(refs[n_early:-6])
+            add_up(grouped[len(early) :])
 
         def turned(row):
             return jnp.broadcast_to(row, (LANES, rows)).T
@@ -400,25 +408,32 @@
     if rows_dev == modes and groups == 2:
         place = jnp.stack([half, (atom_index & 1).astype(jnp.int32)])
 
-        def next_door(some_mine, some_theirs, after=()):
-            keep, send = products_of(
-                chunks, place, partners, some_mine, some_theirs, after, EARLY_US if after else LATE_US
+        def next_door(some_mine, some_theirs, after=(), parts=1):
+            keep, *sends = products_of(
+                chunks, place, partners, some_mine, some_theirs, after, EARLY_US if after else LATE_US, parts
             )
-            return keep, lax.ppermute(send, "atoms", pairs)
+            return keep, [lax.ppermute(send, "atoms", pairs) for send in sends]
 
         far = far_all[1]
         early = next_door(mine, theirs, far[:2])
         third, kept = lax.optimization_barrier((far[2], early[0]))
         early = (kept, early[1])
         far = [far[0], far[1], third]
-        late = next_door(far, [from_sibling(cells) for cells in far])
-        sent = jnp.where(
-            group_index == goal,
-            late[0] + late[1].astype(jnp.float32),
-            early[0] + early[1].astype(jnp.float32),
-        ).astype(jnp.bfloat16)
-        swapped = lax.ppermute(sent, "atoms", [(z, z ^ 2) for z in range(atom_count)])
-        early, late = [*early, swapped], [*late, swapped]
+        parts = 2
+        span = modes // parts
+        late = next_door(far, [from_sibling(cells) for cells in far], parts=parts)
+        swapped = []
+        for part, got in enumerate(late[1]):
+            at = slice(part * span, (part + 1) * span)
+            if part:
+                got, _ = lax.optimization_barrier((got, sent))
+            sent = jnp.where(
+                group_index == goal,
+                late[0][at] + got.astype(jnp.float32),
+                early[0][at] + early[1][0][at].astype(jnp.float32),
+            ).astype(jnp.bfloat16)
+            swapped.append(lax.ppermute(sent, "atoms", [(z, z ^ 2) for z in range(atom_count)]))
+        early, late = [[early[0]], early[1], swapped], [[late[0]], late[1], swapped]
     else:
 
         def settled(some_mine, some_theirs, shift):
@@ -434,6 +449,7 @@
             else:
                 here = (group_index ^ shift) == goal
                 late = [jnp.where(here, new, old) for new, old in zip(terms, late)]
+        early, late = [[term] for term in early], [[term] for term in late]
 
     my_freq = lax.dynamic_slice_in_dim(panel_freq, atom_index * rows_dev, rows_dev, 0)
     flag = jnp.stack(
@@ -453,14 +469,12 @@
         partner_freq[None, :],
         1.0 / math.sqrt(3 * atom_rows * atom_count),
     )
-    holders = groups * 2
-    sums = [numerator] + [
-        lax.ppermute(numerator, ("modes", "sub"), [(i, i ^ code) for i in range(holders)])
-        for code in range(1, holders)
-    ]
-    while len(sums) > 1:
-        sums = [sums[i] + sums[i + 1] for i in range(0, len(sums), 2)]
-    diffusivity = math.pi / 3.0 * sums[0][0] / (my_freq * my_freq)
+    numerator = numerator + lax.ppermute(numerator, "sub", [(0, 1), (1, 0)])
+    step = 1
+    while step < groups:
+        numerator = numerator + lax.ppermute(numerator, "modes", [(m, m ^ step) for m in range(groups)])
+        step *= 2
+    diffusivity = math.pi / 3.0 * numerator[0] / (my_freq * my_freq)
     return (elements, diffusivity)
 
 

time: 56.1 us -> 54.5 us (0.971)
  waiting for transfers between devices: 18.3 us -> 14.4 us
  starting transfers between devices: 17.1 us -> 19.5 us
    ppermute x1 -> x2, waiting for transfers between devices: 8.95 us -> 6.14 us  [body(): lax.ppermute(sent, 'atoms', [(z, z ^ 2) for z in range(atom_count)])]
    ppermute x1 -> x2, starting transfers between devices: 0.96 us -> 3.06 us  [body(): lax.ppermute(sent, 'atoms', [(z, z ^ 2) for z in range(atom_count)])]
    ppermute x5, waiting for transfers between devices: 7.51 us -> 6.41 us  [the longest x3 3.24 us: next_door(): return (keep, [lax.ppermute(send, 'atoms', pairs) for send in sends])]
  transfers between devices with their start and end apart: 17 -> 18, of which waited for: 6 -> 6; matrix products, arithmetic and copies ran while one was open for 0% -> 0% of each run, Pallas kernels for 23% -> 24%
where the time goes in v11:
time: 54.5 us; the launch traced here: 54.3 us
  starting transfers between devices  19.5 us (36%)
  Pallas kernels  18.7 us (34%)
  waiting for transfers between devices  14.4 us (26%)
  other arithmetic  0.89 us (2%)
  between operations  0.8 us (1%)
    pallas_call x6, Pallas kernels, call(): pl.pallas_call(kernel, in_specs=in_specs, out_specs=out_specs, out_shape=...  18.7 us
    ppermute x3, starting transfers between devices, next_door(): return (keep, [lax.ppermute(send, 'atoms', pairs) for send in sends])  6.49 us
    ppermute x2, waiting for transfers between devices, body(): lax.ppermute(sent, 'atoms', [(z, z ^ 2) for z in range(atom_count)])  6.14 us
    ppermute x3, starting transfers between devices, from_group(): return lax.ppermute(cells, 'modes', [(m ^ shift, m) for m in range(groups)])  5.1 us
    ppermute x3, waiting for transfers between devices, next_door(): return (keep, [lax.ppermute(send, 'atoms', pairs) for send in sends])  3.24 us
    ppermute x2, starting transfers between devices, body(): lax.ppermute(sent, 'atoms', [(z, z ^ 2) for z in range(atom_count)])  3.06 us
    ppermute x1, waiting for transfers between devices, body(): lax.ppermute(numerator, 'modes', [(m, m ^ step) for m in range(groups)])  2.05 us
    ppermute x3, waiting for transfers between devices, from_group(): return lax.ppermute(cells, 'modes', [(m ^ shift, m) for m in range(groups)])  1.83 us
  transfers between devices with their start and end apart: 18, of which 6 were waited for; matrix products, arithmetic and copies ran while one was open for 0% of the time, Pallas kernels for 24%

profile of v11, /device:TPU:0, one launch (start us, length us, event | category | flops | bytes accessed | tf_op | source)
XLA Modules:
  0.0 54.3 jit_solution(7389609320225642821)
XLA Ops:
  0.6 0.1 pad_add_fusion.1.refs_0_
  0.7 4.1 %images.3 = (bf16[128,768]{1,0:T(8,128)(2,1)S(1)}, bf16[3,96,128]{2,1,0:T(8,128)(2,1)S(1)}, bf16[3,96,128]{2,1,0:T(8,128)(2,1)S(1)}) custom-call(s32[2]{0:T(128)S(1)} %pad_add_fusion.1.refs_0_, s32[16,768]{1,0:T(8,128)} %bitcast.17, s32[768]{0:T(1024)} %refs_2_.5, f32[9,16,768]{2,1,0:T(8,128)} %bitcast.14, bf16[3,768,128]{2,1,0:T(8,128)(2,1)} %refs_4_.5), custom_call_target="tpu_custom_call" | custom-call | flops 3520000000 | bytes 320000 | tf_op jit(solution)/shard_map/images/pallas_call | solution.py:33
  4.8 3.0 %collective-permute-start.2 = (bf16[128,768]{1,0:T(8,128)(2,1)S(1)}, bf16[128,768]{1,0:T(8,128)(2,1)S(1)}, u32[]{:S(2)}, u32[]{:S(2)}) collective-permute-start(bf16[128,768]{1,0:T(8,128)(2,1)S(1)} %get-tuple-element.17.refs_5_.refs_0_), channel_id=1, source_target_pairs={{2,0},{0,2},{3,1},{1,3},{6,4},{4,6},{7,5},{5,7},{10,8},{8,10},{11,... | collective-permute-start | bytes 589832 | tf_op jit(solution)/shard_map/ppermute | solution.py:393
  7.8 1.6 %collective-permute-start = (bf16[3,96,128]{2,1,0:T(8,128)(2,1)S(1)}, bf16[3,96,128]{2,1,0:T(8,128)(2,1)S(1)}, u32[]{:S(2)}, u32[]{:S(2)}) collective-permute-start(bf16[3,96,128]{2,1,0:T(8,128)(2,1)S(1)} %get-tuple-element.15), channel_id=1, source_target_pairs={{0,4},{4,0},{8,12},{12,8},{1,5},{5,1},{9,13},{13,9},{2,6},{6,2},{1... | collective-permute-start | bytes 221192 | tf_op jit(solution)/shard_map/ppermute | solution.py:390
  9.4 0.7 %collective-permute-start.1 = (bf16[3,96,128]{2,1,0:T(8,128)(2,1)S(1)}, bf16[3,96,128]{2,1,0:T(8,128)(2,1)S(1)}, u32[]{:S(2)}, u32[]{:S(2)}) collective-permute-start(bf16[3,96,128]{2,1,0:T(8,128)(2,1)S(1)} %get-tuple-element.16), channel_id=1, source_target_pairs={{4,8},{8,4},{5,9},{9,5},{6,10},{10,6},{7,11},{11,7},{20,24},{24,20... | collective-permute-start | bytes 221192 | tf_op jit(solution)/shard_map/ppermute | solution.py:390
  10.1 3.1 %images.4.refs_7_.refs_1_ = bf16[128,768]{1,0:T(8,128)(2,1)S(1)} custom-call(s32[2]{0:T(128)S(1)} %pad_add_fusion.1.refs_0_, s32[16,768]{1,0:T(8,128)S(1)} %bitcast.18, s32[768]{0:T(1024)S(1)} %copy-done.4, f32[9,16,768]{2,1,0:T(8,128)S(1)} %bitcast.15, bf16[3,768,128]{2,1,0:T(8,128)(2,1)S(1)} %copy-done.1, ...), custom_call_target="tpu_custom_call" | custom-call | flops 3520000000 | bytes 320000 | tf_op jit(solution)/shard_map/images/pallas_call | solution.py:33
  13.2 0.6 %collective-permute-start.7 = (bf16[128,768]{1,0:T(8,128)(2,1)S(1)}, bf16[128,768]{1,0:T(8,128)(2,1)S(1)}, u32[]{:S(2)}, u32[]{:S(2)}) collective-permute-start(bf16[128,768]{1,0:T(8,128)(2,1)S(1)} %images.4.refs_7_.refs_1_), channel_id=1, source_target_pairs={{2,0},{0,2},{3,1},{1,3},{6,4},{4,6},{7,5},{5,7},{10,8},{8,10},{11,... | collective-permute-start | bytes 589832 | tf_op jit(solution)/shard_map/ppermute | solution.py:393
  13.8 0.0 collective-permute-start.5
  13.8 0.0 collective-permute-done.refs_5_
  13.8 0.5 collective-permute-start.4
  14.3 0.0 collective-permute-done.1.refs_6_
  14.3 0.0 collective-permute-done.2.refs_8_.refs_6_.refs_0_
  14.3 3.0 %images.5.refs_2_ = bf16[128,768]{1,0:T(8,128)(2,1)S(1)} custom-call(s32[2]{0:T(128)S(1)} %pad_add_fusion.1.refs_0_, s32[16,768]{1,0:T(8,128)S(1)} %bitcast.19, s32[768]{0:T(1024)S(1)} %copy-done.4, f32[9,16,768]{2,1,0:T(8,128)S(1)} %bitcast.16, bf16[3,768,128]{2,1,0:T(8,128)(2,1)S(1)} %copy-done.1, bf16[3,96,128]{2,1,0:T(8,128)(2,1)S(1)} %collective-permute-done.refs_5_, ...), custom_call_target="tpu_custom_call" | custom-call | flops 3520000000 | bytes 320000 | tf_op jit(solution)/shard_map/images/pallas_call | solution.py:33
  17.4 0.1 collective-permute-start.6
  17.5 0.1 pad_add_fusion.2.place_ref
  17.5 1.5 %collective-permute-start.3 = (bf16[128,768]{1,0:T(8,128)(2,1)S(1)}, bf16[128,768]{1,0:T(8,128)(2,1)S(1)}, u32[]{:S(2)}, u32[]{:S(2)}) collective-permute-start(bf16[128,768]{1,0:T(8,128)(2,1)S(1)} %images.5.refs_2_), channel_id=1, source_target_pairs={{2,0},{0,2},{3,1},{1,3},{6,4},{4,6},{7,5},{5,7},{10,8},{8,10},{11,... | collective-permute-start | bytes 589832 | tf_op jit(solution)/shard_map/ppermute | solution.py:393
  19.0 0.3 collective-permute-done.7.refs_7_.refs_1_
  19.3 0.0 collective-permute-start.9
  19.3 0.0 collective-permute-done.5.refs_4_
  19.3 0.5 collective-permute-start.10
  19.8 0.0 collective-permute-done.4.refs_3_
  19.8 0.0 collective-permute-done.6.refs_5_
  19.8 3.4 %products.2 = (f32[128,640]{1,0:T(8,128)S(1)}, bf16[128,640]{1,0:T(8,128)(2,1)S(1)}) custom-call(s32[2]{0:T(128)S(1)} %pad_add_fusion.2.place_ref, bf16[3,768,640]{2,1,0:T(8,128)(2,1)} %partners_hbm.3, bf16[128,768]{1,0:T(8,128)(2,1)S(1)} %get-tuple-element.17.refs_5_.refs_0_, bf16[128,768]{1,0:T(8,128)(2,1)S(1)} %images.4.refs_7_.refs_1_, ...), custom_call_target="tpu_custom_call" | custom-call | flops 6600000000 | bytes 600000 | tf_op jit(solution)/shard_map/products/pallas_call | solution.py:33
  23.3 0.0 copy-start.7
  23.3 0.0 copy-start
  23.3 0.0 copy-start.5
  23.3 0.0 copy-start.6
  23.3 1.5 %collective-permute-done.3.refs_2_ = bf16[128,768]{1,0:T(8,128)(2,1)S(1)} collective-permute-done((bf16[128,768]{1,0:T(8,128)(2,1)S(1)}, bf16[128,768]{1,0:T(8,128)(2,1)S(1)}, u32[]{:S(2)}, u32[]{:S(2)}) %collective-permute-start.3) | collective-permute-done | bytes 196640 | tf_op jit(solution)/shard_map/ppermute | solution.py:393
  24.8 0.0 collective-permute-start.11
  24.8 4.4 %collective-permute-start.8 = (bf16[128,640]{1,0:T(8,128)(2,1)S(1)}, bf16[128,640]{1,0:T(8,128)(2,1)S(1)}, u32[]{:S(2)}, u32[]{:S(2)}) collective-permute-start(bf16[128,640]{1,0:T(8,128)(2,1)S(1)} %get-tuple-element.20), channel_id=1, source_target_pairs={{0,4},{4,0},{8,12},{12,8},{1,5},{5,1},{9,13},{13,9},{2,6},{6,2},{1... | collective-permute-start | bytes 491528 | tf_op jit(solution)/shard_map/ppermute | solution.py:415
  29.2 0.0 collective-permute-done.10.refs_4_
  29.2 0.0 collective-permute-done.9.refs_3_
  29.2 0.0 collective-permute-done.11.refs_5_
  29.2 3.4 %products.3 = (f32[128,640]{1,0:T(8,128)S(1)}, bf16[64,640]{1,0:T(8,128)(2,1)S(1)}, bf16[64,640]{1,0:T(8,128)(2,1)S(1)}) custom-call(s32[2]{0:T(128)S(1)} %pad_add_fusion.2.place_ref, bf16[3,768,640]{2,1,0:T(8,128)(2,1)} %partners_hbm.3, bf16[128,768]{1,0:T(8,128)(2,1)S(1)} %collective-permute-done.2.refs_8_.refs_6_.refs_0_, ...), custom_call_target="tpu_custom_call" | custom-call | flops 110000000 | bytes 10000 | tf_op jit(solution)/shard_map/products/pallas_call | solution.py:33
  32.6 1.5 %collective-permute-start.12 = (bf16[64,640]{1,0:T(8,128)(2,1)S(1)}, bf16[64,640]{1,0:T(8,128)(2,1)S(1)}, u32[]{:S(2)}, u32[]{:S(2)}) collective-permute-start(bf16[64,640]{1,0:T(8,128)(2,1)S(1)} %get-tuple-element.23), channel_id=1, source_target_pairs={{0,4},{4,0},{8,12},{12,8},{1,5},{5,1},{9,13},{13,9},{2,6},{6,2},{1... | collective-permute-start | bytes 245768 | tf_op jit(solution)/shard_map/ppermute | solution.py:415
  34.1 0.6 %collective-permute-start.14 = (bf16[64,640]{1,0:T(8,128)(2,1)S(1)}, bf16[64,640]{1,0:T(8,128)(2,1)S(1)}, u32[]{:S(2)}, u32[]{:S(2)}) collective-permute-start(bf16[64,640]{1,0:T(8,128)(2,1)S(1)} %get-tuple-element.24), channel_id=1, source_target_pairs={{0,4},{4,0},{8,12},{12,8},{1,5},{5,1},{9,13},{13,9},{2,6},{6,2},{1... | collective-permute-start | bytes 245768 | tf_op jit(solution)/shard_map/ppermute | solution.py:415
  34.7 0.0 collective-permute-done.8.refs_1_
  34.7 3.2 %collective-permute-done.12.refs_5_ = bf16[64,640]{1,0:T(8,128)(2,1)S(1)} collective-permute-done((bf16[64,640]{1,0:T(8,128)(2,1)S(1)}, bf16[64,640]{1,0:T(8,128)(2,1)S(1)}, u32[]{:S(2)}, u32[]{:S(2)}) %collective-permute-start.12) | collective-permute-done | bytes 81952 | tf_op jit(solution)/shard_map/ppermute | solution.py:415
  38.0 1.1 %collective-permute-start.13 = (bf16[64,640]{1,0:T(8,128)(2,1)S(1)}, bf16[64,640]{1,0:T(8,128)(2,1)S(1)}, u32[]{:S(2)}, u32[]{:S(2)}) collective-permute-start(bf16[64,640]{1,0:T(8,128)(2,1)S(1)} %select_convert_fusion.1), channel_id=1, source_target_pairs={{0,8},{4,12},{8,0},{12,4},{1,9},{5,13},{9,1},{13,5},{2,10},{6,14},... | collective-permute-start | bytes 245768 | tf_op jit(solution)/shard_map/ppermute | solution.py:435
  39.1 0.0 collective-permute-done.14.refs_6_
  39.1 2.0 %collective-permute-start.15 = (bf16[64,640]{1,0:T(8,128)(2,1)S(1)}, bf16[64,640]{1,0:T(8,128)(2,1)S(1)}, u32[]{:S(2)}, u32[]{:S(2)}) collective-permute-start(bf16[64,640]{1,0:T(8,128)(2,1)S(1)} %select_convert_fusion), channel_id=1, source_target_pairs={{0,8},{4,12},{8,0},{12,4},{1,9},{5,13},{9,1},{13,5},{2,10},{6,14},... | collective-permute-start | bytes 245768 | tf_op jit(solution)/shard_map/ppermute | solution.py:435
  41.1 0.1 pad_add_fusion.flag_ref
  41.2 6.1 %collective-permute-done.15.refs_3_.refs_8_ = bf16[64,640]{1,0:T(8,128)(2,1)S(1)} collective-permute-done((bf16[64,640]{1,0:T(8,128)(2,1)S(1)}, bf16[64,640]{1,0:T(8,128)(2,1)S(1)}, u32[]{:S(2)}, u32[]{:S(2)}) %collective-permute-start.15) | collective-permute-done | bytes 81952 | tf_op jit(solution)/shard_map/ppermute | solution.py:435
  47.3 1.7 %finish.1 = (f32[128,640]{1,0:T(8,128)}, f32[1,128]{1,0:T(1,128)S(1)}) custom-call(s32[3]{0:T(128)S(1)} %pad_add_fusion.flag_ref, s32[4,128]{1,0:T(4,128)S(1)} %bitcast.20, s32[4,128]{1,0:T(4,128)S(1)} %bitcast.21, f32[4,128]{1,0:T(4,128)S(1)} %bitcast.13, f32[1,640]{1,0:T(1,128)S(1)} %broadcast_in_dim.3.partner_ref, ...), custom_call_target="tpu_custom_call" | custom-call | flops 2200000000 | bytes 200000 | tf_op jit(solution)/shard_map/finish/pallas_call | solution.py:33
  49.1 1.1 %collective-permute-done.16 = f32[1,128]{1,0:T(1,128)S(1)} collective-permute-done((f32[1,128]{1,0:T(1,128)S(1)}, f32[1,128]{1,0:T(1,128)S(1)}, u32[]{:S(2)}, u32[]{:S(2)}) %collective-permute-start.16) | collective-permute-done | bytes 544 | tf_op jit(solution)/shard_map/ppermute | solution.py:472
  50.2 1.5 %collective-permute-start.17 = (f32[1,128]{1,0:T(1,128)S(1)}, f32[1,128]{1,0:T(1,128)S(1)}, u32[]{:S(2)}, u32[]{:S(2)}) collective-permute-start(f32[1,128]{1,0:T(1,128)S(1)} %add.30), channel_id=1, source_target_pairs={{0,2},{2,0},{1,3},{3,1},{4,6},{6,4},{5,7},{7,5},{8,10},{10,8},{9,1... | collective-permute-start | bytes 1544 | tf_op jit(solution)/shard_map/ppermute | solution.py:475
  51.7 2.1 %collective-permute-done.17 = f32[1,128]{1,0:T(1,128)S(1)} collective-permute-done((f32[1,128]{1,0:T(1,128)S(1)}, f32[1,128]{1,0:T(1,128)S(1)}, u32[]{:S(2)}, u32[]{:S(2)}) %collective-permute-start.17) | collective-permute-done | bytes 544 | tf_op jit(solution)/shard_map/ppermute | solution.py:475
  53.7 0.6 %bitcast_divide_fusion = f32[128]{0:T(128)} fusion(f32[512]{0:T(512)S(1)} %copy-done, s32[]{:T(128)S(6)} %select_n.24, f32[1,128]{1,0:T(1,128)S(1)} %add.30, f32[1,128]{1,0:T(1,128)S(1)} %collective-permute-done.17), kind=kLoop, calls=%fused_computation.5 | loop fusion | flops 512 | bytes 2052 | tf_op jit(solution)/shard_map/div | solution.py:477
  (18 shorter events, 0.1 us)
Async XLA Ops:
  0.7 9.4 %copy-start.1 = (bf16[3,768,128]{2,1,0:T(8,128)(2,1)S(1)}, bf16[3,768,128]{2,1,0:T(8,128)(2,1)}, u32[]{:S(2)}) copy-start(bf16[3,768,128]{2,1,0:T(8,128)(2,1)} %refs_4_.5) | copy-start | bytes 1769476
  0.7 9.4 %copy-start.2 = (f32[9,768,16]{1,2,0:T(8,128)S(1)}, f32[9,768,16]{1,2,0:T(8,128)}, u32[]{:S(2)}) copy-start(f32[9,768,16]{1,2,0:T(8,128)} %param.11) | copy-start | bytes 1327108
  0.7 9.4 %copy-start.3 = (s32[768,16]{0,1:T(8,128)S(1)}, s32[768,16]{0,1:T(8,128)}, u32[]{:S(2)}) copy-start(s32[768,16]{0,1:T(8,128)} %param.12) | copy-start | bytes 147460
  0.7 9.4 %copy-start.4 = (s32[768]{0:T(1024)S(1)}, s32[768]{0:T(1024)}, u32[]{:S(2)}) copy-start(s32[768]{0:T(1024)} %refs_2_.5) | copy-start | bytes 9220
  4.8 9.5 %collective-permute-start.2 = (bf16[128,768]{1,0:T(8,128)(2,1)S(1)}, bf16[128,768]{1,0:T(8,128)(2,1)S(1)}, u32[]{:S(2)}, u32[]{:S(2)}) collective-permute-start(bf16[128,768]{1,0:T(8,128)(2,1)S(1)} %get-tuple-element.17.refs_5_.refs_0_), channel_id=1, source_target_pairs={{2,0},{0,2},{3,1},{1,3},{6,4},{4,6},{7,5},{5,7},{10,8},{8,10},{11,... | collective-permute-start | bytes 589832 | tf_op jit(solution)/shard_map/ppermute | solution.py:393
  7.8 6.0 %collective-permute-start = (bf16[3,96,128]{2,1,0:T(8,128)(2,1)S(1)}, bf16[3,96,128]{2,1,0:T(8,128)(2,1)S(1)}, u32[]{:S(2)}, u32[]{:S(2)}) collective-permute-start(bf16[3,96,128]{2,1,0:T(8,128)(2,1)S(1)} %get-tuple-element.15), channel_id=1, source_target_pairs={{0,4},{4,0},{8,12},{12,8},{1,5},{5,1},{9,13},{13,9},{2,6},{6,2},{1... | collective-permute-start | bytes 221192 | tf_op jit(solution)/shard_map/ppermute | solution.py:390
  9.4 4.9 %collective-permute-start.1 = (bf16[3,96,128]{2,1,0:T(8,128)(2,1)S(1)}, bf16[3,96,128]{2,1,0:T(8,128)(2,1)S(1)}, u32[]{:S(2)}, u32[]{:S(2)}) collective-permute-start(bf16[3,96,128]{2,1,0:T(8,128)(2,1)S(1)} %get-tuple-element.16), channel_id=1, source_target_pairs={{4,8},{8,4},{5,9},{9,5},{6,10},{10,6},{7,11},{11,7},{20,24},{24,20... | collective-permute-start | bytes 221192 | tf_op jit(solution)/shard_map/ppermute | solution.py:390
  13.2 6.2 %collective-permute-start.7 = (bf16[128,768]{1,0:T(8,128)(2,1)S(1)}, bf16[128,768]{1,0:T(8,128)(2,1)S(1)}, u32[]{:S(2)}, u32[]{:S(2)}) collective-permute-start(bf16[128,768]{1,0:T(8,128)(2,1)S(1)} %images.4.refs_7_.refs_1_), channel_id=1, source_target_pairs={{2,0},{0,2},{3,1},{1,3},{6,4},{4,6},{7,5},{5,7},{10,8},{8,10},{11,... | collective-permute-start | bytes 589832 | tf_op jit(solution)/shard_map/ppermute | solution.py:393
  13.8 5.5 %collective-permute-start.5 = (bf16[128,768]{1,0:T(8,128)(2,1)S(1)}, bf16[128,768]{1,0:T(8,128)(2,1)S(1)}, u32[]{:S(2)}, u32[]{:S(2)}) collective-permute-start(bf16[128,768]{1,0:T(8,128)(2,1)S(1)} %images.4.refs_7_.refs_1_), channel_id=1, source_target_pairs={{0,1},{1,0},{2,3},{3,2},{4,5},{5,4},{6,7},{7,6},{8,9},{9,8},{10,11... | collective-permute-start | bytes 589832 | tf_op jit(solution)/shard_map/ppermute | solution.py:396
  13.8 6.1 %collective-permute-start.4 = (bf16[128,768]{1,0:T(8,128)(2,1)S(1)}, bf16[128,768]{1,0:T(8,128)(2,1)S(1)}, u32[]{:S(2)}, u32[]{:S(2)}) collective-permute-start(bf16[128,768]{1,0:T(8,128)(2,1)S(1)} %get-tuple-element.17.refs_5_.refs_0_), channel_id=1, source_target_pairs={{0,1},{1,0},{2,3},{3,2},{4,5},{5,4},{6,7},{7,6},{8,9},{9,8},{10,11... | collective-permute-start | bytes 589832 | tf_op jit(solution)/shard_map/ppermute | solution.py:396
  17.4 2.5 %collective-permute-start.6 = (bf16[128,768]{1,0:T(8,128)(2,1)S(1)}, bf16[128,768]{1,0:T(8,128)(2,1)S(1)}, u32[]{:S(2)}, u32[]{:S(2)}) collective-permute-start(bf16[128,768]{1,0:T(8,128)(2,1)S(1)} %images.5.refs_2_), channel_id=1, source_target_pairs={{0,1},{1,0},{2,3},{3,2},{4,5},{5,4},{6,7},{7,6},{8,9},{9,8},{10,11... | collective-permute-start | bytes 589832 | tf_op jit(solution)/shard_map/ppermute | solution.py:396
  17.5 7.3 %collective-permute-start.3 = (bf16[128,768]{1,0:T(8,128)(2,1)S(1)}, bf16[128,768]{1,0:T(8,128)(2,1)S(1)}, u32[]{:S(2)}, u32[]{:S(2)}) collective-permute-start(bf16[128,768]{1,0:T(8,128)(2,1)S(1)} %images.5.refs_2_), channel_id=1, source_target_pairs={{2,0},{0,2},{3,1},{1,3},{6,4},{4,6},{7,5},{5,7},{10,8},{8,10},{11,... | collective-permute-start | bytes 589832 | tf_op jit(solution)/shard_map/ppermute | solution.py:393
  19.3 9.9 %collective-permute-start.9 = (bf16[128,768]{1,0:T(8,128)(2,1)S(1)}, bf16[128,768]{1,0:T(8,128)(2,1)S(1)}, u32[]{:S(2)}, u32[]{:S(2)}) collective-permute-start(bf16[128,768]{1,0:T(8,128)(2,1)S(1)} %collective-permute-done.2.refs_8_.refs_6_.refs_0_), channel_id=1, source_target_pairs={{0,1},{1,0},{2,3},{3,2},{4,5},{5,4},{6,7},{7,6},{8,9},{9,8},{10,11... | collective-permute-start | bytes 589832 | tf_op jit(solution)/shard_map/ppermute | solution.py:396
  19.3 9.9 %collective-permute-start.10 = (bf16[128,768]{1,0:T(8,128)(2,1)S(1)}, bf16[128,768]{1,0:T(8,128)(2,1)S(1)}, u32[]{:S(2)}, u32[]{:S(2)}) collective-permute-start(bf16[128,768]{1,0:T(8,128)(2,1)S(1)} %collective-permute-done.7.refs_7_.refs_1_), channel_id=1, source_target_pairs={{0,1},{1,0},{2,3},{3,2},{4,5},{5,4},{6,7},{7,6},{8,9},{9,8},{10,11... | collective-permute-start | bytes 589832 | tf_op jit(solution)/shard_map/ppermute | solution.py:396
  23.3 10.9 %copy-start.7 = (f32[640]{0:T(1024)S(1)}, f32[640]{0:T(1024)}, u32[]{:S(2)}) copy-start(f32[640]{0:T(1024)} %param.15) | copy-start | bytes 7684
  23.3 24.1 %copy-start = (f32[512]{0:T(512)S(1)}, f32[512]{0:T(512)}, u32[]{:S(2)}) copy-start(f32[512]{0:T(512)} %param.14) | copy-start | bytes 6148
  23.3 24.1 %copy-start.5 = (s32[512]{0:T(512)S(1)}, s32[512]{0:T(512)}, u32[]{:S(2)}) copy-start(s32[512]{0:T(512)} %param.16) | copy-start | bytes 6148
  23.3 24.0 %copy-start.6 = (s32[512]{0:T(512)S(1)}, s32[512]{0:T(512)}, u32[]{:S(2)}) copy-start(s32[512]{0:T(512)} %param.17) | copy-start | bytes 6148
  24.8 4.4 %collective-permute-start.11 = (bf16[128,768]{1,0:T(8,128)(2,1)S(1)}, bf16[128,768]{1,0:T(8,128)(2,1)S(1)}, u32[]{:S(2)}, u32[]{:S(2)}) collective-permute-start(bf16[128,768]{1,0:T(8,128)(2,1)S(1)} %collective-permute-done.3.refs_2_), channel_id=1, source_target_pairs={{0,1},{1,0},{2,3},{3,2},{4,5},{5,4},{6,7},{7,6},{8,9},{9,8},{10,11... | collective-permute-start | bytes 589832 | tf_op jit(solution)/shard_map/ppermute | solution.py:396
  24.8 9.9 %collective-permute-start.8 = (bf16[128,640]{1,0:T(8,128)(2,1)S(1)}, bf16[128,640]{1,0:T(8,128)(2,1)S(1)}, u32[]{:S(2)}, u32[]{:S(2)}) collective-permute-start(bf16[128,640]{1,0:T(8,128)(2,1)S(1)} %get-tuple-element.20), channel_id=1, source_target_pairs={{0,4},{4,0},{8,12},{12,8},{1,5},{5,1},{9,13},{13,9},{2,6},{6,2},{1... | collective-permute-start | bytes 491528 | tf_op jit(solution)/shard_map/ppermute | solution.py:415
  32.6 5.3 %collective-permute-start.12 = (bf16[64,640]{1,0:T(8,128)(2,1)S(1)}, bf16[64,640]{1,0:T(8,128)(2,1)S(1)}, u32[]{:S(2)}, u32[]{:S(2)}) collective-permute-start(bf16[64,640]{1,0:T(8,128)(2,1)S(1)} %get-tuple-element.23), channel_id=1, source_target_pairs={{0,4},{4,0},{8,12},{12,8},{1,5},{5,1},{9,13},{13,9},{2,6},{6,2},{1... | collective-permute-start | bytes 245768 | tf_op jit(solution)/shard_map/ppermute | solution.py:415
  34.1 4.9 %collective-permute-start.14 = (bf16[64,640]{1,0:T(8,128)(2,1)S(1)}, bf16[64,640]{1,0:T(8,128)(2,1)S(1)}, u32[]{:S(2)}, u32[]{:S(2)}) collective-permute-start(bf16[64,640]{1,0:T(8,128)(2,1)S(1)} %get-tuple-element.24), channel_id=1, source_target_pairs={{0,4},{4,0},{8,12},{12,8},{1,5},{5,1},{9,13},{13,9},{2,6},{6,2},{1... | collective-permute-start | bytes 245768 | tf_op jit(solution)/shard_map/ppermute | solution.py:415
  38.0 9.3 %collective-permute-start.13 = (bf16[64,640]{1,0:T(8,128)(2,1)S(1)}, bf16[64,640]{1,0:T(8,128)(2,1)S(1)}, u32[]{:S(2)}, u32[]{:S(2)}) collective-permute-start(bf16[64,640]{1,0:T(8,128)(2,1)S(1)} %select_convert_fusion.1), channel_id=1, source_target_pairs={{0,8},{4,12},{8,0},{12,4},{1,9},{5,13},{9,1},{13,5},{2,10},{6,14},... | collective-permute-start | bytes 245768 | tf_op jit(solution)/shard_map/ppermute | solution.py:435
  39.1 8.2 %collective-permute-start.15 = (bf16[64,640]{1,0:T(8,128)(2,1)S(1)}, bf16[64,640]{1,0:T(8,128)(2,1)S(1)}, u32[]{:S(2)}, u32[]{:S(2)}) collective-permute-start(bf16[64,640]{1,0:T(8,128)(2,1)S(1)} %select_convert_fusion), channel_id=1, source_target_pairs={{0,8},{4,12},{8,0},{12,4},{1,9},{5,13},{9,1},{13,5},{2,10},{6,14},... | collective-permute-start | bytes 245768 | tf_op jit(solution)/shard_map/ppermute | solution.py:435
  49.1 1.1 %collective-permute-start.16 = (f32[1,128]{1,0:T(1,128)S(1)}, f32[1,128]{1,0:T(1,128)S(1)}, u32[]{:S(2)}, u32[]{:S(2)}) collective-permute-start(f32[1,128]{1,0:T(1,128)S(1)} %get-tuple-element.27), channel_id=1, source_target_pairs={{0,1},{1,0},{2,3},{3,2},{4,5},{5,4},{6,7},{7,6},{8,9},{9,8},{10,11... | collective-permute-start | bytes 1544 | tf_op jit(solution)/shard_map/ppermute | solution.py:472
  50.2 3.5 %collective-permute-start.17 = (f32[1,128]{1,0:T(1,128)S(1)}, f32[1,128]{1,0:T(1,128)S(1)}, u32[]{:S(2)}, u32[]{:S(2)}) collective-permute-start(f32[1,128]{1,0:T(1,128)S(1)} %add.30), channel_id=1, source_target_pairs={{0,2},{2,0},{1,3},{3,1},{4,6},{6,4},{5,7},{7,5},{8,10},{10,8},{9,1... | collective-permute-start | bytes 1544 | tf_op jit(solution)/shard_map/ppermute | solution.py:475

commit v12 on v11

--- a/solution.py
+++ b/solution.py
@@ -386,7 +386,7 @@
     shared = (spot, mode_panel, nbr, coef, bond_count)
     near, edge_one, edge_two = images_of(chunks[0], *shared, edges=True)
     pairs = [(z, z ^ 1) for z in range(atom_count)]
-    others = [(z, ((z + 1) ^ 1) - 1) for z in range(1, atom_count - 1)]
+    others = [(z, (z + 1 if z & 1 else z - 1) % atom_count) for z in range(atom_count)]
     halos = (lax.ppermute(edge_one, "atoms", pairs), lax.ppermute(edge_two, "atoms", others))
 
     def from_group(cells, shift):

time: 54.5 us -> 53.1 us (0.974)
  starting transfers between devices: 19.5 us -> 17.5 us
  waiting for transfers between devices: 14.4 us -> 15 us
    ppermute x3, starting transfers between devices: 6.49 us -> 2.76 us  [next_door(): return (keep, [lax.ppermute(send, 'atoms', pairs) for send in sends])]
    ppermute x1, starting transfers between devices: 0.65 us -> 2.48 us  [body(): lax.ppermute(edge_two, 'atoms', others)]
    ppermute x6, waiting for transfers between devices: 0.02 us -> 0.78 us  [from_sibling(): return lax.ppermute(cells, 'sub', [(0, 1), (1, 0)])]
where the time goes in v12:
time: 53.1 us; the launch traced here: 52.9 us
  Pallas kernels  18.7 us (35%)
  starting transfers between devices  17.5 us (33%)
  waiting for transfers between devices  15 us (28%)
  other arithmetic  0.9 us (2%)
  between operations  0.77 us (1%)
    pallas_call x6, Pallas kernels, call(): pl.pallas_call(kernel, in_specs=in_specs, out_specs=out_specs, out_shape=...  18.7 us
    ppermute x2, waiting for transfers between devices, body(): lax.ppermute(sent, 'atoms', [(z, z ^ 2) for z in range(atom_count)])  5.92 us
    ppermute x3, starting transfers between devices, from_group(): return lax.ppermute(cells, 'modes', [(m ^ shift, m) for m in range(groups)])  5.1 us
    ppermute x3, waiting for transfers between devices, next_door(): return (keep, [lax.ppermute(send, 'atoms', pairs) for send in sends])  3.26 us
    ppermute x2, starting transfers between devices, body(): lax.ppermute(sent, 'atoms', [(z, z ^ 2) for z in range(atom_count)])  3.06 us
    ppermute x3, starting transfers between devices, next_door(): return (keep, [lax.ppermute(send, 'atoms', pairs) for send in sends])  2.76 us
    ppermute x1, starting transfers between devices, body(): lax.ppermute(edge_two, 'atoms', others)  2.48 us
    ppermute x1, waiting for transfers between devices, body(): lax.ppermute(numerator, 'modes', [(m, m ^ step) for m in range(groups)])  2.06 us
  transfers between devices with their start and end apart: 18, of which 6 were waited for; matrix products, arithmetic and copies ran while one was open for 0% of the time, Pallas kernels for 24%

profile of v12, /device:TPU:0, one launch (start us, length us, event | category | flops | bytes accessed | tf_op | source)
XLA Modules:
  0.0 52.9 jit_solution(11761481749779046036)
XLA Ops:
  0.6 0.1 pad_add_fusion.1.refs_0_
  0.7 4.1 %images.3 = (bf16[128,768]{1,0:T(8,128)(2,1)S(1)}, bf16[3,96,128]{2,1,0:T(8,128)(2,1)S(1)}, bf16[3,96,128]{2,1,0:T(8,128)(2,1)S(1)}) custom-call(s32[2]{0:T(128)S(1)} %pad_add_fusion.1.refs_0_, s32[16,768]{1,0:T(8,128)} %bitcast.17, s32[768]{0:T(1024)} %refs_2_.5, f32[9,16,768]{2,1,0:T(8,128)} %bitcast.14, bf16[3,768,128]{2,1,0:T(8,128)(2,1)} %refs_4_.5), custom_call_target="tpu_custom_call" | custom-call | flops 3520000000 | bytes 320000 | tf_op jit(solution)/shard_map/images/pallas_call | solution.py:33
  4.8 3.0 %collective-permute-start.2 = (bf16[128,768]{1,0:T(8,128)(2,1)S(1)}, bf16[128,768]{1,0:T(8,128)(2,1)S(1)}, u32[]{:S(2)}, u32[]{:S(2)}) collective-permute-start(bf16[128,768]{1,0:T(8,128)(2,1)S(1)} %get-tuple-element.17.refs_5_.refs_0_), channel_id=1, source_target_pairs={{2,0},{0,2},{3,1},{1,3},{6,4},{4,6},{7,5},{5,7},{10,8},{8,10},{11,... | collective-permute-start | bytes 589832 | tf_op jit(solution)/shard_map/ppermute | solution.py:393
  7.8 1.6 %collective-permute-start = (bf16[3,96,128]{2,1,0:T(8,128)(2,1)S(1)}, bf16[3,96,128]{2,1,0:T(8,128)(2,1)S(1)}, u32[]{:S(2)}, u32[]{:S(2)}) collective-permute-start(bf16[3,96,128]{2,1,0:T(8,128)(2,1)S(1)} %get-tuple-element.15), channel_id=1, source_target_pairs={{0,4},{4,0},{8,12},{12,8},{1,5},{5,1},{9,13},{13,9},{2,6},{6,2},{1... | collective-permute-start | bytes 221192 | tf_op jit(solution)/shard_map/ppermute | solution.py:390
  9.4 2.5 %collective-permute-start.1 = (bf16[3,96,128]{2,1,0:T(8,128)(2,1)S(1)}, bf16[3,96,128]{2,1,0:T(8,128)(2,1)S(1)}, u32[]{:S(2)}, u32[]{:S(2)}) collective-permute-start(bf16[3,96,128]{2,1,0:T(8,128)(2,1)S(1)} %get-tuple-element.16), channel_id=1, source_target_pairs={{0,12},{4,8},{8,4},{12,0},{1,13},{5,9},{9,5},{13,1},{2,14},{6,10},... | collective-permute-start | bytes 221192 | tf_op jit(solution)/shard_map/ppermute | solution.py:390
  11.9 3.1 %images.4.refs_7_.refs_1_ = bf16[128,768]{1,0:T(8,128)(2,1)S(1)} custom-call(s32[2]{0:T(128)S(1)} %pad_add_fusion.1.refs_0_, s32[16,768]{1,0:T(8,128)S(1)} %bitcast.18, s32[768]{0:T(1024)S(1)} %copy-done.4, f32[9,16,768]{2,1,0:T(8,128)S(1)} %bitcast.15, bf16[3,768,128]{2,1,0:T(8,128)(2,1)S(1)} %copy-done.1, ...), custom_call_target="tpu_custom_call" | custom-call | flops 3520000000 | bytes 320000 | tf_op jit(solution)/shard_map/images/pallas_call | solution.py:33
  15.0 0.6 %collective-permute-start.7 = (bf16[128,768]{1,0:T(8,128)(2,1)S(1)}, bf16[128,768]{1,0:T(8,128)(2,1)S(1)}, u32[]{:S(2)}, u32[]{:S(2)}) collective-permute-start(bf16[128,768]{1,0:T(8,128)(2,1)S(1)} %images.4.refs_7_.refs_1_), channel_id=1, source_target_pairs={{2,0},{0,2},{3,1},{1,3},{6,4},{4,6},{7,5},{5,7},{10,8},{8,10},{11,... | collective-permute-start | bytes 589832 | tf_op jit(solution)/shard_map/ppermute | solution.py:393
  15.6 0.0 collective-permute-start.5
  15.6 0.0 collective-permute-done.refs_5_
  15.6 0.5 collective-permute-start.4
  16.1 0.0 collective-permute-done.1.refs_6_
  16.1 0.0 collective-permute-done.2.refs_8_.refs_6_.refs_0_
  16.1 3.1 %images.5.refs_2_ = bf16[128,768]{1,0:T(8,128)(2,1)S(1)} custom-call(s32[2]{0:T(128)S(1)} %pad_add_fusion.1.refs_0_, s32[16,768]{1,0:T(8,128)S(1)} %bitcast.19, s32[768]{0:T(1024)S(1)} %copy-done.4, f32[9,16,768]{2,1,0:T(8,128)S(1)} %bitcast.16, bf16[3,768,128]{2,1,0:T(8,128)(2,1)S(1)} %copy-done.1, bf16[3,96,128]{2,1,0:T(8,128)(2,1)S(1)} %collective-permute-done.refs_5_, ...), custom_call_target="tpu_custom_call" | custom-call | flops 3520000000 | bytes 320000 | tf_op jit(solution)/shard_map/images/pallas_call | solution.py:33
  19.2 0.1 collective-permute-start.6
  19.2 0.1 pad_add_fusion.2.place_ref
  19.3 1.5 %collective-permute-start.3 = (bf16[128,768]{1,0:T(8,128)(2,1)S(1)}, bf16[128,768]{1,0:T(8,128)(2,1)S(1)}, u32[]{:S(2)}, u32[]{:S(2)}) collective-permute-start(bf16[128,768]{1,0:T(8,128)(2,1)S(1)} %images.5.refs_2_), channel_id=1, source_target_pairs={{2,0},{0,2},{3,1},{1,3},{6,4},{4,6},{7,5},{5,7},{10,8},{8,10},{11,... | collective-permute-start | bytes 589832 | tf_op jit(solution)/shard_map/ppermute | solution.py:393
  20.8 0.0 collective-permute-done.7.refs_7_.refs_1_
  20.8 0.2 collective-permute-start.9
  21.0 0.3 collective-permute-start.10
  21.4 0.0 collective-permute-done.4.refs_3_
  21.4 0.0 collective-permute-done.6.refs_5_
  21.4 3.4 %products.2 = (f32[128,640]{1,0:T(8,128)S(1)}, bf16[128,640]{1,0:T(8,128)(2,1)S(1)}) custom-call(s32[2]{0:T(128)S(1)} %pad_add_fusion.2.place_ref, bf16[3,768,640]{2,1,0:T(8,128)(2,1)} %partners_hbm.3, bf16[128,768]{1,0:T(8,128)(2,1)S(1)} %get-tuple-element.17.refs_5_.refs_0_, bf16[128,768]{1,0:T(8,128)(2,1)S(1)} %images.4.refs_7_.refs_1_, ...), custom_call_target="tpu_custom_call" | custom-call | flops 6600000000 | bytes 600000 | tf_op jit(solution)/shard_map/products/pallas_call | solution.py:33
  24.8 0.0 copy-start.7
  24.8 0.0 copy-start
  24.8 0.0 copy-start.5
  24.8 0.0 copy-start.6
  24.8 1.8 %collective-permute-done.3.refs_2_ = bf16[128,768]{1,0:T(8,128)(2,1)S(1)} collective-permute-done((bf16[128,768]{1,0:T(8,128)(2,1)S(1)}, bf16[128,768]{1,0:T(8,128)(2,1)S(1)}, u32[]{:S(2)}, u32[]{:S(2)}) %collective-permute-start.3) | collective-permute-done | bytes 196640 | tf_op jit(solution)/shard_map/ppermute | solution.py:393
  26.6 0.0 collective-permute-start.11
  26.6 0.7 %collective-permute-start.8 = (bf16[128,640]{1,0:T(8,128)(2,1)S(1)}, bf16[128,640]{1,0:T(8,128)(2,1)S(1)}, u32[]{:S(2)}, u32[]{:S(2)}) collective-permute-start(bf16[128,640]{1,0:T(8,128)(2,1)S(1)} %get-tuple-element.20), channel_id=1, source_target_pairs={{0,4},{4,0},{8,12},{12,8},{1,5},{5,1},{9,13},{13,9},{2,6},{6,2},{1... | collective-permute-start | bytes 491528 | tf_op jit(solution)/shard_map/ppermute | solution.py:415
  27.3 0.0 collective-permute-done.10.refs_4_
  27.3 0.0 collective-permute-done.9.refs_3_
  27.3 0.8 %collective-permute-done.11.refs_5_ = bf16[128,768]{1,0:T(8,128)(2,1)S(1)} collective-permute-done((bf16[128,768]{1,0:T(8,128)(2,1)S(1)}, bf16[128,768]{1,0:T(8,128)(2,1)S(1)}, u32[]{:S(2)}, u32[]{:S(2)}) %collective-permute-start.11) | collective-permute-done | bytes 196640 | tf_op jit(solution)/shard_map/ppermute | solution.py:396
  28.1 3.4 %products.3 = (f32[128,640]{1,0:T(8,128)S(1)}, bf16[64,640]{1,0:T(8,128)(2,1)S(1)}, bf16[64,640]{1,0:T(8,128)(2,1)S(1)}) custom-call(s32[2]{0:T(128)S(1)} %pad_add_fusion.2.place_ref, bf16[3,768,640]{2,1,0:T(8,128)(2,1)} %partners_hbm.3, bf16[128,768]{1,0:T(8,128)(2,1)S(1)} %collective-permute-done.2.refs_8_.refs_6_.refs_0_, ...), custom_call_target="tpu_custom_call" | custom-call | flops 110000000 | bytes 10000 | tf_op jit(solution)/shard_map/products/pallas_call | solution.py:33
  31.5 0.7 %collective-permute-start.12 = (bf16[64,640]{1,0:T(8,128)(2,1)S(1)}, bf16[64,640]{1,0:T(8,128)(2,1)S(1)}, u32[]{:S(2)}, u32[]{:S(2)}) collective-permute-start(bf16[64,640]{1,0:T(8,128)(2,1)S(1)} %get-tuple-element.23), channel_id=1, source_target_pairs={{0,4},{4,0},{8,12},{12,8},{1,5},{5,1},{9,13},{13,9},{2,6},{6,2},{1... | collective-permute-start | bytes 245768 | tf_op jit(solution)/shard_map/ppermute | solution.py:415
  32.2 1.4 %collective-permute-start.14 = (bf16[64,640]{1,0:T(8,128)(2,1)S(1)}, bf16[64,640]{1,0:T(8,128)(2,1)S(1)}, u32[]{:S(2)}, u32[]{:S(2)}) collective-permute-start(bf16[64,640]{1,0:T(8,128)(2,1)S(1)} %get-tuple-element.24), channel_id=1, source_target_pairs={{0,4},{4,0},{8,12},{12,8},{1,5},{5,1},{9,13},{13,9},{2,6},{6,2},{1... | collective-permute-start | bytes 245768 | tf_op jit(solution)/shard_map/ppermute | solution.py:415
  33.6 3.3 %collective-permute-done.12.refs_5_ = bf16[64,640]{1,0:T(8,128)(2,1)S(1)} collective-permute-done((bf16[64,640]{1,0:T(8,128)(2,1)S(1)}, bf16[64,640]{1,0:T(8,128)(2,1)S(1)}, u32[]{:S(2)}, u32[]{:S(2)}) %collective-permute-start.12) | collective-permute-done | bytes 81952 | tf_op jit(solution)/shard_map/ppermute | solution.py:415
  36.9 1.1 %collective-permute-start.13 = (bf16[64,640]{1,0:T(8,128)(2,1)S(1)}, bf16[64,640]{1,0:T(8,128)(2,1)S(1)}, u32[]{:S(2)}, u32[]{:S(2)}) collective-permute-start(bf16[64,640]{1,0:T(8,128)(2,1)S(1)} %select_convert_fusion.1), channel_id=1, source_target_pairs={{0,8},{4,12},{8,0},{12,4},{1,9},{5,13},{9,1},{13,5},{2,10},{6,14},... | collective-permute-start | bytes 245768 | tf_op jit(solution)/shard_map/ppermute | solution.py:435
  38.0 0.0 collective-permute-done.14.refs_6_
  38.0 1.9 %collective-permute-start.15 = (bf16[64,640]{1,0:T(8,128)(2,1)S(1)}, bf16[64,640]{1,0:T(8,128)(2,1)S(1)}, u32[]{:S(2)}, u32[]{:S(2)}) collective-permute-start(bf16[64,640]{1,0:T(8,128)(2,1)S(1)} %select_convert_fusion), channel_id=1, source_target_pairs={{0,8},{4,12},{8,0},{12,4},{1,9},{5,13},{9,1},{13,5},{2,10},{6,14},... | collective-permute-start | bytes 245768 | tf_op jit(solution)/shard_map/ppermute | solution.py:435
  40.0 0.1 pad_add_fusion.flag_ref
  40.0 5.9 %collective-permute-done.15.refs_3_.refs_8_ = bf16[64,640]{1,0:T(8,128)(2,1)S(1)} collective-permute-done((bf16[64,640]{1,0:T(8,128)(2,1)S(1)}, bf16[64,640]{1,0:T(8,128)(2,1)S(1)}, u32[]{:S(2)}, u32[]{:S(2)}) %collective-permute-start.15) | collective-permute-done | bytes 81952 | tf_op jit(solution)/shard_map/ppermute | solution.py:435
  45.9 0.0 collective-permute-done.13.refs_2_.refs_7_
  46.0 1.7 %finish.1 = (f32[128,640]{1,0:T(8,128)}, f32[1,128]{1,0:T(1,128)S(1)}) custom-call(s32[3]{0:T(128)S(1)} %pad_add_fusion.flag_ref, s32[4,128]{1,0:T(4,128)S(1)} %bitcast.20, s32[4,128]{1,0:T(4,128)S(1)} %bitcast.21, f32[4,128]{1,0:T(4,128)S(1)} %bitcast.13, f32[1,640]{1,0:T(1,128)S(1)} %broadcast_in_dim.3.partner_ref, ...), custom_call_target="tpu_custom_call" | custom-call | flops 2200000000 | bytes 200000 | tf_op jit(solution)/shard_map/finish/pallas_call | solution.py:33
  47.7 0.0 collective-permute-start.16
  47.7 1.1 %collective-permute-done.16 = f32[1,128]{1,0:T(1,128)S(1)} collective-permute-done((f32[1,128]{1,0:T(1,128)S(1)}, f32[1,128]{1,0:T(1,128)S(1)}, u32[]{:S(2)}, u32[]{:S(2)}) %collective-permute-start.16) | collective-permute-done | bytes 544 | tf_op jit(solution)/shard_map/ppermute | solution.py:472
  48.8 1.5 %collective-permute-start.17 = (f32[1,128]{1,0:T(1,128)S(1)}, f32[1,128]{1,0:T(1,128)S(1)}, u32[]{:S(2)}, u32[]{:S(2)}) collective-permute-start(f32[1,128]{1,0:T(1,128)S(1)} %add.30), channel_id=1, source_target_pairs={{0,2},{2,0},{1,3},{3,1},{4,6},{6,4},{5,7},{7,5},{8,10},{10,8},{9,1... | collective-permute-start | bytes 1544 | tf_op jit(solution)/shard_map/ppermute | solution.py:475
  50.3 2.1 %collective-permute-done.17 = f32[1,128]{1,0:T(1,128)S(1)} collective-permute-done((f32[1,128]{1,0:T(1,128)S(1)}, f32[1,128]{1,0:T(1,128)S(1)}, u32[]{:S(2)}, u32[]{:S(2)}) %collective-permute-start.17) | collective-permute-done | bytes 544 | tf_op jit(solution)/shard_map/ppermute | solution.py:475
  52.4 0.6 %bitcast_divide_fusion = f32[128]{0:T(128)} fusion(f32[512]{0:T(512)S(1)} %copy-done, s32[]{:T(128)S(6)} %select_n.24, f32[1,128]{1,0:T(1,128)S(1)} %add.30, f32[1,128]{1,0:T(1,128)S(1)} %collective-permute-done.17), kind=kLoop, calls=%fused_computation.5 | loop fusion | flops 512 | bytes 2052 | tf_op jit(solution)/shard_map/div | solution.py:477
  (18 shorter events, 0.1 us)
Async XLA Ops:
  0.7 11.2 %copy-start.1 = (bf16[3,768,128]{2,1,0:T(8,128)(2,1)S(1)}, bf16[3,768,128]{2,1,0:T(8,128)(2,1)}, u32[]{:S(2)}) copy-start(bf16[3,768,128]{2,1,0:T(8,128)(2,1)} %refs_4_.5) | copy-start | bytes 1769476
  0.7 11.2 %copy-start.2 = (f32[9,768,16]{1,2,0:T(8,128)S(1)}, f32[9,768,16]{1,2,0:T(8,128)}, u32[]{:S(2)}) copy-start(f32[9,768,16]{1,2,0:T(8,128)} %param.11) | copy-start | bytes 1327108
  0.7 11.2 %copy-start.3 = (s32[768,16]{0,1:T(8,128)S(1)}, s32[768,16]{0,1:T(8,128)}, u32[]{:S(2)}) copy-start(s32[768,16]{0,1:T(8,128)} %param.12) | copy-start | bytes 147460
  0.7 11.2 %copy-start.4 = (s32[768]{0:T(1024)S(1)}, s32[768]{0:T(1024)}, u32[]{:S(2)}) copy-start(s32[768]{0:T(1024)} %refs_2_.5) | copy-start | bytes 9220
  4.8 11.3 %collective-permute-start.2 = (bf16[128,768]{1,0:T(8,128)(2,1)S(1)}, bf16[128,768]{1,0:T(8,128)(2,1)S(1)}, u32[]{:S(2)}, u32[]{:S(2)}) collective-permute-start(bf16[128,768]{1,0:T(8,128)(2,1)S(1)} %get-tuple-element.17.refs_5_.refs_0_), channel_id=1, source_target_pairs={{2,0},{0,2},{3,1},{1,3},{6,4},{4,6},{7,5},{5,7},{10,8},{8,10},{11,... | collective-permute-start | bytes 589832 | tf_op jit(solution)/shard_map/ppermute | solution.py:393
  7.8 7.7 %collective-permute-start = (bf16[3,96,128]{2,1,0:T(8,128)(2,1)S(1)}, bf16[3,96,128]{2,1,0:T(8,128)(2,1)S(1)}, u32[]{:S(2)}, u32[]{:S(2)}) collective-permute-start(bf16[3,96,128]{2,1,0:T(8,128)(2,1)S(1)} %get-tuple-element.15), channel_id=1, source_target_pairs={{0,4},{4,0},{8,12},{12,8},{1,5},{5,1},{9,13},{13,9},{2,6},{6,2},{1... | collective-permute-start | bytes 221192 | tf_op jit(solution)/shard_map/ppermute | solution.py:390
  9.4 6.7 %collective-permute-start.1 = (bf16[3,96,128]{2,1,0:T(8,128)(2,1)S(1)}, bf16[3,96,128]{2,1,0:T(8,128)(2,1)S(1)}, u32[]{:S(2)}, u32[]{:S(2)}) collective-permute-start(bf16[3,96,128]{2,1,0:T(8,128)(2,1)S(1)} %get-tuple-element.16), channel_id=1, source_target_pairs={{0,12},{4,8},{8,4},{12,0},{1,13},{5,9},{9,5},{13,1},{2,14},{6,10},... | collective-permute-start | bytes 221192 | tf_op jit(solution)/shard_map/ppermute | solution.py:390
  15.0 5.9 %collective-permute-start.7 = (bf16[128,768]{1,0:T(8,128)(2,1)S(1)}, bf16[128,768]{1,0:T(8,128)(2,1)S(1)}, u32[]{:S(2)}, u32[]{:S(2)}) collective-permute-start(bf16[128,768]{1,0:T(8,128)(2,1)S(1)} %images.4.refs_7_.refs_1_), channel_id=1, source_target_pairs={{2,0},{0,2},{3,1},{1,3},{6,4},{4,6},{7,5},{5,7},{10,8},{8,10},{11,... | collective-permute-start | bytes 589832 | tf_op jit(solution)/shard_map/ppermute | solution.py:393
  15.6 5.5 %collective-permute-start.5 = (bf16[128,768]{1,0:T(8,128)(2,1)S(1)}, bf16[128,768]{1,0:T(8,128)(2,1)S(1)}, u32[]{:S(2)}, u32[]{:S(2)}) collective-permute-start(bf16[128,768]{1,0:T(8,128)(2,1)S(1)} %images.4.refs_7_.refs_1_), channel_id=1, source_target_pairs={{0,1},{1,0},{2,3},{3,2},{4,5},{5,4},{6,7},{7,6},{8,9},{9,8},{10,11... | collective-permute-start | bytes 589832 | tf_op jit(solution)/shard_map/ppermute | solution.py:396
  15.6 5.8 %collective-permute-start.4 = (bf16[128,768]{1,0:T(8,128)(2,1)S(1)}, bf16[128,768]{1,0:T(8,128)(2,1)S(1)}, u32[]{:S(2)}, u32[]{:S(2)}) collective-permute-start(bf16[128,768]{1,0:T(8,128)(2,1)S(1)} %get-tuple-element.17.refs_5_.refs_0_), channel_id=1, source_target_pairs={{0,1},{1,0},{2,3},{3,2},{4,5},{5,4},{6,7},{7,6},{8,9},{9,8},{10,11... | collective-permute-start | bytes 589832 | tf_op jit(solution)/shard_map/ppermute | solution.py:396
  19.2 2.2 %collective-permute-start.6 = (bf16[128,768]{1,0:T(8,128)(2,1)S(1)}, bf16[128,768]{1,0:T(8,128)(2,1)S(1)}, u32[]{:S(2)}, u32[]{:S(2)}) collective-permute-start(bf16[128,768]{1,0:T(8,128)(2,1)S(1)} %images.5.refs_2_), channel_id=1, source_target_pairs={{0,1},{1,0},{2,3},{3,2},{4,5},{5,4},{6,7},{7,6},{8,9},{9,8},{10,11... | collective-permute-start | bytes 589832 | tf_op jit(solution)/shard_map/ppermute | solution.py:396
  19.3 7.3 %collective-permute-start.3 = (bf16[128,768]{1,0:T(8,128)(2,1)S(1)}, bf16[128,768]{1,0:T(8,128)(2,1)S(1)}, u32[]{:S(2)}, u32[]{:S(2)}) collective-permute-start(bf16[128,768]{1,0:T(8,128)(2,1)S(1)} %images.5.refs_2_), channel_id=1, source_target_pairs={{2,0},{0,2},{3,1},{1,3},{6,4},{4,6},{7,5},{5,7},{10,8},{8,10},{11,... | collective-permute-start | bytes 589832 | tf_op jit(solution)/shard_map/ppermute | solution.py:393
  20.8 6.5 %collective-permute-start.9 = (bf16[128,768]{1,0:T(8,128)(2,1)S(1)}, bf16[128,768]{1,0:T(8,128)(2,1)S(1)}, u32[]{:S(2)}, u32[]{:S(2)}) collective-permute-start(bf16[128,768]{1,0:T(8,128)(2,1)S(1)} %collective-permute-done.2.refs_8_.refs_6_.refs_0_), channel_id=1, source_target_pairs={{0,1},{1,0},{2,3},{3,2},{4,5},{5,4},{6,7},{7,6},{8,9},{9,8},{10,11... | collective-permute-start | bytes 589832 | tf_op jit(solution)/shard_map/ppermute | solution.py:396
  21.0 6.3 %collective-permute-start.10 = (bf16[128,768]{1,0:T(8,128)(2,1)S(1)}, bf16[128,768]{1,0:T(8,128)(2,1)S(1)}, u32[]{:S(2)}, u32[]{:S(2)}) collective-permute-start(bf16[128,768]{1,0:T(8,128)(2,1)S(1)} %collective-permute-done.7.refs_7_.refs_1_), channel_id=1, source_target_pairs={{0,1},{1,0},{2,3},{3,2},{4,5},{5,4},{6,7},{7,6},{8,9},{9,8},{10,11... | collective-permute-start | bytes 589832 | tf_op jit(solution)/shard_map/ppermute | solution.py:396
  24.8 7.4 %copy-start.7 = (f32[640]{0:T(1024)S(1)}, f32[640]{0:T(1024)}, u32[]{:S(2)}) copy-start(f32[640]{0:T(1024)} %param.15) | copy-start | bytes 7684
  24.8 21.2 %copy-start = (f32[512]{0:T(512)S(1)}, f32[512]{0:T(512)}, u32[]{:S(2)}) copy-start(f32[512]{0:T(512)} %param.14) | copy-start | bytes 6148
  24.8 21.2 %copy-start.5 = (s32[512]{0:T(512)S(1)}, s32[512]{0:T(512)}, u32[]{:S(2)}) copy-start(s32[512]{0:T(512)} %param.16) | copy-start | bytes 6148
  24.8 21.2 %copy-start.6 = (s32[512]{0:T(512)S(1)}, s32[512]{0:T(512)}, u32[]{:S(2)}) copy-start(s32[512]{0:T(512)} %param.17) | copy-start | bytes 6148
  26.6 1.4 %collective-permute-start.11 = (bf16[128,768]{1,0:T(8,128)(2,1)S(1)}, bf16[128,768]{1,0:T(8,128)(2,1)S(1)}, u32[]{:S(2)}, u32[]{:S(2)}) collective-permute-start(bf16[128,768]{1,0:T(8,128)(2,1)S(1)} %collective-permute-done.3.refs_2_), channel_id=1, source_target_pairs={{0,1},{1,0},{2,3},{3,2},{4,5},{5,4},{6,7},{7,6},{8,9},{9,8},{10,11... | collective-permute-start | bytes 589832 | tf_op jit(solution)/shard_map/ppermute | solution.py:396
  26.6 6.9 %collective-permute-start.8 = (bf16[128,640]{1,0:T(8,128)(2,1)S(1)}, bf16[128,640]{1,0:T(8,128)(2,1)S(1)}, u32[]{:S(2)}, u32[]{:S(2)}) collective-permute-start(bf16[128,640]{1,0:T(8,128)(2,1)S(1)} %get-tuple-element.20), channel_id=1, source_target_pairs={{0,4},{4,0},{8,12},{12,8},{1,5},{5,1},{9,13},{13,9},{2,6},{6,2},{1... | collective-permute-start | bytes 491528 | tf_op jit(solution)/shard_map/ppermute | solution.py:415
  31.5 5.4 %collective-permute-start.12 = (bf16[64,640]{1,0:T(8,128)(2,1)S(1)}, bf16[64,640]{1,0:T(8,128)(2,1)S(1)}, u32[]{:S(2)}, u32[]{:S(2)}) collective-permute-start(bf16[64,640]{1,0:T(8,128)(2,1)S(1)} %get-tuple-element.23), channel_id=1, source_target_pairs={{0,4},{4,0},{8,12},{12,8},{1,5},{5,1},{9,13},{13,9},{2,6},{6,2},{1... | collective-permute-start | bytes 245768 | tf_op jit(solution)/shard_map/ppermute | solution.py:415
  32.2 5.8 %collective-permute-start.14 = (bf16[64,640]{1,0:T(8,128)(2,1)S(1)}, bf16[64,640]{1,0:T(8,128)(2,1)S(1)}, u32[]{:S(2)}, u32[]{:S(2)}) collective-permute-start(bf16[64,640]{1,0:T(8,128)(2,1)S(1)} %get-tuple-element.24), channel_id=1, source_target_pairs={{0,4},{4,0},{8,12},{12,8},{1,5},{5,1},{9,13},{13,9},{2,6},{6,2},{1... | collective-permute-start | bytes 245768 | tf_op jit(solution)/shard_map/ppermute | solution.py:415
  36.9 9.1 %collective-permute-start.13 = (bf16[64,640]{1,0:T(8,128)(2,1)S(1)}, bf16[64,640]{1,0:T(8,128)(2,1)S(1)}, u32[]{:S(2)}, u32[]{:S(2)}) collective-permute-start(bf16[64,640]{1,0:T(8,128)(2,1)S(1)} %select_convert_fusion.1), channel_id=1, source_target_pairs={{0,8},{4,12},{8,0},{12,4},{1,9},{5,13},{9,1},{13,5},{2,10},{6,14},... | collective-permute-start | bytes 245768 | tf_op jit(solution)/shard_map/ppermute | solution.py:435
  38.0 7.9 %collective-permute-start.15 = (bf16[64,640]{1,0:T(8,128)(2,1)S(1)}, bf16[64,640]{1,0:T(8,128)(2,1)S(1)}, u32[]{:S(2)}, u32[]{:S(2)}) collective-permute-start(bf16[64,640]{1,0:T(8,128)(2,1)S(1)} %select_convert_fusion), channel_id=1, source_target_pairs={{0,8},{4,12},{8,0},{12,4},{1,9},{5,13},{9,1},{13,5},{2,10},{6,14},... | collective-permute-start | bytes 245768 | tf_op jit(solution)/shard_map/ppermute | solution.py:435
  47.7 1.1 %collective-permute-start.16 = (f32[1,128]{1,0:T(1,128)S(1)}, f32[1,128]{1,0:T(1,128)S(1)}, u32[]{:S(2)}, u32[]{:S(2)}) collective-permute-start(f32[1,128]{1,0:T(1,128)S(1)} %get-tuple-element.27), channel_id=1, source_target_pairs={{0,1},{1,0},{2,3},{3,2},{4,5},{5,4},{6,7},{7,6},{8,9},{9,8},{10,11... | collective-permute-start | bytes 1544 | tf_op jit(solution)/shard_map/ppermute | solution.py:472
  48.8 3.5 %collective-permute-start.17 = (f32[1,128]{1,0:T(1,128)S(1)}, f32[1,128]{1,0:T(1,128)S(1)}, u32[]{:S(2)}, u32[]{:S(2)}) collective-permute-start(f32[1,128]{1,0:T(1,128)S(1)} %add.30), channel_id=1, source_target_pairs={{0,2},{2,0},{1,3},{3,1},{4,6},{6,4},{5,7},{7,5},{8,10},{10,8},{9,1... | collective-permute-start | bytes 1544 | tf_op jit(solution)/shard_map/ppermute | solution.py:475

commit v13 on v12

--- a/solution.py
+++ b/solution.py
@@ -196,13 +196,14 @@
     return call(kernel, "images", in_specs, out_specs, out_shape, operands, 0.8 + 1.2 * len(blocks), scratch)
 
 
-def products_of(chunks, place, partners, mine, theirs, after=(), busy_us=2.0, parts=1):
+def products_of(chunks, place, partners, mine, theirs, after=(), busy_us=2.0, cuts=()):
     rows, cols = mine[0].shape[0], partners.shape[2]
     count = len(chunks)
+    spans = list(zip([0, *cuts], [*cuts, rows]))
     depth = partners.shape[1]
 
     def kernel(place_ref, partners_hbm, *refs):
-        keep_ref, *send_refs = refs[-4 - parts : -3]
+        keep_ref, *send_refs = refs[-4 - len(spans) : -3]
         left_ref, partners_ref, sems = refs[-3:]
         copies = [
             pltpu.make_async_copy(partners_hbm.at[r], partners_ref.at[r], sems.at[r]) for r in range(3)
@@ -227,16 +228,16 @@
             )
             total = part if total is None else total + part
         keep_ref[...] = total[:rows]
-        for part, send_ref in enumerate(send_refs):
-            at = rows + part * (rows // parts)
-            send_ref[...] = total[at : at + rows // parts].astype(jnp.bfloat16)
+        for (begin, end), send_ref in zip(spans, send_refs):
+            send_ref[...] = total[rows + begin : rows + end].astype(jnp.bfloat16)
 
     return call(
         kernel,
         "products",
         [SMEM, HBM] + [VMEM] * (2 * count) + [ANY] * len(after),
-        [VMEM] * (1 + parts),
-        [pltpu.VMEM((rows, cols), jnp.float32)] + [pltpu.VMEM((rows // parts, cols), jnp.bfloat16)] * parts,
+        [VMEM] * (1 + len(spans)),
+        [pltpu.VMEM((rows, cols), jnp.float32)]
+        + [pltpu.VMEM((end - begin, cols), jnp.bfloat16) for begin, end in spans],
         (place, partners, *mine, *theirs, *after),
         busy_us,
         [
@@ -300,10 +301,11 @@
         def add_up(some):
             out_ref[...] = some[0][0][...]
             for term in some[1:]:
-                span = rows // len(term)
-                for i, ref in enumerate(term):
-                    at = slice(i * span, (i + 1) * span)
+                begin = 0
+                for ref in term:
+                    at = slice(begin, begin + ref.shape[0])
                     out_ref[at, :] = out_ref[at, :] + ref[...].astype(jnp.float32)
+                    begin += ref.shape[0]
 
         @pl.when(flag_ref[0] == 1)
         def _():
@@ -408,9 +410,9 @@
     if rows_dev == modes and groups == 2:
         place = jnp.stack([half, (atom_index & 1).astype(jnp.int32)])
 
-        def next_door(some_mine, some_theirs, after=(), parts=1):
+        def next_door(some_mine, some_theirs, after=(), cuts=()):
             keep, *sends = products_of(
-                chunks, place, partners, some_mine, some_theirs, after, EARLY_US if after else LATE_US, parts
+                chunks, place, partners, some_mine, some_theirs, after, EARLY_US if after else LATE_US, cuts
             )
             return keep, [lax.ppermute(send, "atoms", pairs) for send in sends]
 
@@ -419,13 +421,12 @@
         third, kept = lax.optimization_barrier((far[2], early[0]))
         early = (kept, early[1])
         far = [far[0], far[1], third]
-        parts = 2
-        span = modes // parts
-        late = next_door(far, [from_sibling(cells) for cells in far], parts=parts)
+        late = next_door(far, [from_sibling(cells) for cells in far], cuts=(modes // 4,))
         swapped = []
-        for part, got in enumerate(late[1]):
-            at = slice(part * span, (part + 1) * span)
-            if part:
+        for got in late[1]:
+            begin = sum(piece.shape[0] for piece in swapped)
+            at = slice(begin, begin + got.shape[0])
+            if swapped:
                 got, _ = lax.optimization_barrier((got, sent))
             sent = jnp.where(
                 group_index == goal,

time: 53.1 us -> 54.9 us (1.034)
  waiting for transfers between devices: 15 us -> 16.8 us
    ppermute x3, waiting for transfers between devices: 3.26 us -> 4.19 us  [next_door(): return (keep, [lax.ppermute(send, 'atoms', pairs) for send in sends])]
    ppermute x2, waiting for transfers between devices: 5.92 us -> 6.82 us  [body(): lax.ppermute(sent, 'atoms', [(z, z ^ 2) for z in range(atom_count)])]
  transfers between devices with their start and end apart: 18 -> 18, of which waited for: 6 -> 7; matrix products, arithmetic and copies ran while one was open for 0% -> 0% of each run, Pallas kernels for 24% -> 24%
where the time goes in v13:
time: 54.9 us; the launch traced here: 54.7 us
  Pallas kernels  18.7 us (34%)
  starting transfers between devices  17.5 us (32%)
  waiting for transfers between devices  16.8 us (31%)
  other arithmetic  0.89 us (2%)
  between operations  0.76 us (1%)
    pallas_call x6, Pallas kernels, call(): pl.pallas_call(kernel, in_specs=in_specs, out_specs=out_specs, out_shape=...  18.7 us
    ppermute x2, waiting for transfers between devices, body(): lax.ppermute(sent, 'atoms', [(z, z ^ 2) for z in range(atom_count)])  6.82 us
    ppermute x3, starting transfers between devices, from_group(): return lax.ppermute(cells, 'modes', [(m ^ shift, m) for m in range(groups)])  5.1 us
    ppermute x3, waiting for transfers between devices, next_door(): return (keep, [lax.ppermute(send, 'atoms', pairs) for send in sends])  4.19 us
    ppermute x2, starting transfers between devices, body(): lax.ppermute(sent, 'atoms', [(z, z ^ 2) for z in range(atom_count)])  2.99 us
    ppermute x3, starting transfers between devices, next_door(): return (keep, [lax.ppermute(send, 'atoms', pairs) for send in sends])  2.76 us
    ppermute x1, starting transfers between devices, body(): lax.ppermute(edge_two, 'atoms', others)  2.48 us
    ppermute x1, waiting for transfers between devices, body(): lax.ppermute(numerator, 'modes', [(m, m ^ step) for m in range(groups)])  2.05 us
  transfers between devices with their start and end apart: 18, of which 7 were waited for; matrix products, arithmetic and copies ran while one was open for 0% of the time, Pallas kernels for 24%

profile of v13, /device:TPU:0, one launch (start us, length us, event | category | flops | bytes accessed | tf_op | source)
XLA Modules:
  0.0 54.7 jit_solution(4001383426001513758)
XLA Ops:
  0.6 0.1 pad_add_fusion.1.refs_0_
  0.7 4.1 %images.3 = (bf16[128,768]{1,0:T(8,128)(2,1)S(1)}, bf16[3,96,128]{2,1,0:T(8,128)(2,1)S(1)}, bf16[3,96,128]{2,1,0:T(8,128)(2,1)S(1)}) custom-call(s32[2]{0:T(128)S(1)} %pad_add_fusion.1.refs_0_, s32[16,768]{1,0:T(8,128)} %bitcast.17, s32[768]{0:T(1024)} %refs_2_.5, f32[9,16,768]{2,1,0:T(8,128)} %bitcast.14, bf16[3,768,128]{2,1,0:T(8,128)(2,1)} %refs_4_.5), custom_call_target="tpu_custom_call" | custom-call | flops 3520000000 | bytes 320000 | tf_op jit(solution)/shard_map/images/pallas_call | solution.py:33
  4.8 3.0 %collective-permute-start.2 = (bf16[128,768]{1,0:T(8,128)(2,1)S(1)}, bf16[128,768]{1,0:T(8,128)(2,1)S(1)}, u32[]{:S(2)}, u32[]{:S(2)}) collective-permute-start(bf16[128,768]{1,0:T(8,128)(2,1)S(1)} %get-tuple-element.17.refs_5_.refs_0_), channel_id=1, source_target_pairs={{2,0},{0,2},{3,1},{1,3},{6,4},{4,6},{7,5},{5,7},{10,8},{8,10},{11,... | collective-permute-start | bytes 589832 | tf_op jit(solution)/shard_map/ppermute | solution.py:395
  7.8 1.6 %collective-permute-start = (bf16[3,96,128]{2,1,0:T(8,128)(2,1)S(1)}, bf16[3,96,128]{2,1,0:T(8,128)(2,1)S(1)}, u32[]{:S(2)}, u32[]{:S(2)}) collective-permute-start(bf16[3,96,128]{2,1,0:T(8,128)(2,1)S(1)} %get-tuple-element.15), channel_id=1, source_target_pairs={{0,4},{4,0},{8,12},{12,8},{1,5},{5,1},{9,13},{13,9},{2,6},{6,2},{1... | collective-permute-start | bytes 221192 | tf_op jit(solution)/shard_map/ppermute | solution.py:392
  9.4 2.5 %collective-permute-start.1 = (bf16[3,96,128]{2,1,0:T(8,128)(2,1)S(1)}, bf16[3,96,128]{2,1,0:T(8,128)(2,1)S(1)}, u32[]{:S(2)}, u32[]{:S(2)}) collective-permute-start(bf16[3,96,128]{2,1,0:T(8,128)(2,1)S(1)} %get-tuple-element.16), channel_id=1, source_target_pairs={{0,12},{4,8},{8,4},{12,0},{1,13},{5,9},{9,5},{13,1},{2,14},{6,10},... | collective-permute-start | bytes 221192 | tf_op jit(solution)/shard_map/ppermute | solution.py:392
  11.9 3.1 %images.4.refs_7_.refs_1_ = bf16[128,768]{1,0:T(8,128)(2,1)S(1)} custom-call(s32[2]{0:T(128)S(1)} %pad_add_fusion.1.refs_0_, s32[16,768]{1,0:T(8,128)S(1)} %bitcast.18, s32[768]{0:T(1024)S(1)} %copy-done.4, f32[9,16,768]{2,1,0:T(8,128)S(1)} %bitcast.15, bf16[3,768,128]{2,1,0:T(8,128)(2,1)S(1)} %copy-done.1, ...), custom_call_target="tpu_custom_call" | custom-call | flops 3520000000 | bytes 320000 | tf_op jit(solution)/shard_map/images/pallas_call | solution.py:33
  15.0 0.6 %collective-permute-start.7 = (bf16[128,768]{1,0:T(8,128)(2,1)S(1)}, bf16[128,768]{1,0:T(8,128)(2,1)S(1)}, u32[]{:S(2)}, u32[]{:S(2)}) collective-permute-start(bf16[128,768]{1,0:T(8,128)(2,1)S(1)} %images.4.refs_7_.refs_1_), channel_id=1, source_target_pairs={{2,0},{0,2},{3,1},{1,3},{6,4},{4,6},{7,5},{5,7},{10,8},{8,10},{11,... | collective-permute-start | bytes 589832 | tf_op jit(solution)/shard_map/ppermute | solution.py:395
  15.6 0.0 collective-permute-start.5
  15.6 0.0 collective-permute-done.refs_5_
  15.6 0.5 collective-permute-start.4
  16.1 0.0 collective-permute-done.1.refs_6_
  16.1 0.0 collective-permute-done.2.refs_8_.refs_6_.refs_0_
  16.1 3.1 %images.5.refs_2_ = bf16[128,768]{1,0:T(8,128)(2,1)S(1)} custom-call(s32[2]{0:T(128)S(1)} %pad_add_fusion.1.refs_0_, s32[16,768]{1,0:T(8,128)S(1)} %bitcast.19, s32[768]{0:T(1024)S(1)} %copy-done.4, f32[9,16,768]{2,1,0:T(8,128)S(1)} %bitcast.16, bf16[3,768,128]{2,1,0:T(8,128)(2,1)S(1)} %copy-done.1, bf16[3,96,128]{2,1,0:T(8,128)(2,1)S(1)} %collective-permute-done.refs_5_, ...), custom_call_target="tpu_custom_call" | custom-call | flops 3520000000 | bytes 320000 | tf_op jit(solution)/shard_map/images/pallas_call | solution.py:33
  19.2 0.1 collective-permute-start.6
  19.2 0.1 pad_add_fusion.2.place_ref
  19.3 1.5 %collective-permute-start.3 = (bf16[128,768]{1,0:T(8,128)(2,1)S(1)}, bf16[128,768]{1,0:T(8,128)(2,1)S(1)}, u32[]{:S(2)}, u32[]{:S(2)}) collective-permute-start(bf16[128,768]{1,0:T(8,128)(2,1)S(1)} %images.5.refs_2_), channel_id=1, source_target_pairs={{2,0},{0,2},{3,1},{1,3},{6,4},{4,6},{7,5},{5,7},{10,8},{8,10},{11,... | collective-permute-start | bytes 589832 | tf_op jit(solution)/shard_map/ppermute | solution.py:395
  20.8 0.0 collective-permute-done.7.refs_7_.refs_1_
  20.8 0.2 collective-permute-start.9
  21.0 0.0 collective-permute-done.5.refs_4_
  21.0 0.3 collective-permute-start.10
  21.4 0.0 collective-permute-done.4.refs_3_
  21.4 0.0 collective-permute-done.6.refs_5_
  21.4 3.4 %products.2 = (f32[128,640]{1,0:T(8,128)S(1)}, bf16[128,640]{1,0:T(8,128)(2,1)S(1)}) custom-call(s32[2]{0:T(128)S(1)} %pad_add_fusion.2.place_ref, bf16[3,768,640]{2,1,0:T(8,128)(2,1)} %partners_hbm.3, bf16[128,768]{1,0:T(8,128)(2,1)S(1)} %get-tuple-element.17.refs_5_.refs_0_, bf16[128,768]{1,0:T(8,128)(2,1)S(1)} %images.4.refs_7_.refs_1_, ...), custom_call_target="tpu_custom_call" | custom-call | flops 6600000000 | bytes 600000 | tf_op jit(solution)/shard_map/products/pallas_call | solution.py:33
  24.8 0.0 copy-start.7
  24.8 0.0 copy-start
  24.8 0.0 copy-start.5
  24.8 0.0 copy-start.6
  24.8 1.8 %collective-permute-done.3.refs_2_ = bf16[128,768]{1,0:T(8,128)(2,1)S(1)} collective-permute-done((bf16[128,768]{1,0:T(8,128)(2,1)S(1)}, bf16[128,768]{1,0:T(8,128)(2,1)S(1)}, u32[]{:S(2)}, u32[]{:S(2)}) %collective-permute-start.3) | collective-permute-done | bytes 196640 | tf_op jit(solution)/shard_map/ppermute | solution.py:395
  26.6 0.0 collective-permute-start.11
  26.6 0.7 %collective-permute-start.8 = (bf16[128,640]{1,0:T(8,128)(2,1)S(1)}, bf16[128,640]{1,0:T(8,128)(2,1)S(1)}, u32[]{:S(2)}, u32[]{:S(2)}) collective-permute-start(bf16[128,640]{1,0:T(8,128)(2,1)S(1)} %get-tuple-element.20), channel_id=1, source_target_pairs={{0,4},{4,0},{8,12},{12,8},{1,5},{5,1},{9,13},{13,9},{2,6},{6,2},{1... | collective-permute-start | bytes 491528 | tf_op jit(solution)/shard_map/ppermute | solution.py:417
  27.3 0.0 collective-permute-done.10.refs_4_
  27.3 0.0 collective-permute-done.9.refs_3_
  27.3 0.8 %collective-permute-done.11.refs_5_ = bf16[128,768]{1,0:T(8,128)(2,1)S(1)} collective-permute-done((bf16[128,768]{1,0:T(8,128)(2,1)S(1)}, bf16[128,768]{1,0:T(8,128)(2,1)S(1)}, u32[]{:S(2)}, u32[]{:S(2)}) %collective-permute-start.11) | collective-permute-done | bytes 196640 | tf_op jit(solution)/shard_map/ppermute | solution.py:398
  28.1 3.4 %products.3 = (f32[128,640]{1,0:T(8,128)S(1)}, bf16[32,640]{1,0:T(8,128)(2,1)S(1)}, bf16[96,640]{1,0:T(8,128)(2,1)S(1)}) custom-call(s32[2]{0:T(128)S(1)} %pad_add_fusion.2.place_ref, bf16[3,768,640]{2,1,0:T(8,128)(2,1)} %partners_hbm.3, bf16[128,768]{1,0:T(8,128)(2,1)S(1)} %collective-permute-done.2.refs_8_.refs_6_.refs_0_, ...), custom_call_target="tpu_custom_call" | custom-call | flops 110000000 | bytes 10000 | tf_op jit(solution)/shard_map/products/pallas_call | solution.py:33
  31.5 0.7 %collective-permute-start.12 = (bf16[32,640]{1,0:T(8,128)(2,1)S(1)}, bf16[32,640]{1,0:T(8,128)(2,1)S(1)}, u32[]{:S(2)}, u32[]{:S(2)}) collective-permute-start(bf16[32,640]{1,0:T(8,128)(2,1)S(1)} %get-tuple-element.23), channel_id=1, source_target_pairs={{0,4},{4,0},{8,12},{12,8},{1,5},{5,1},{9,13},{13,9},{2,6},{6,2},{1... | collective-permute-start | bytes 122888 | tf_op jit(solution)/shard_map/ppermute | solution.py:417
  32.2 1.4 %collective-permute-start.14 = (bf16[96,640]{1,0:T(8,128)(2,1)S(1)}, bf16[96,640]{1,0:T(8,128)(2,1)S(1)}, u32[]{:S(2)}, u32[]{:S(2)}) collective-permute-start(bf16[96,640]{1,0:T(8,128)(2,1)S(1)} %get-tuple-element.24), channel_id=1, source_target_pairs={{0,4},{4,0},{8,12},{12,8},{1,5},{5,1},{9,13},{13,9},{2,6},{6,2},{1... | collective-permute-start | bytes 368648 | tf_op jit(solution)/shard_map/ppermute | solution.py:417
  33.6 2.4 %collective-permute-done.12.refs_5_ = bf16[32,640]{1,0:T(8,128)(2,1)S(1)} collective-permute-done((bf16[32,640]{1,0:T(8,128)(2,1)S(1)}, bf16[32,640]{1,0:T(8,128)(2,1)S(1)}, u32[]{:S(2)}, u32[]{:S(2)}) %collective-permute-start.12) | collective-permute-done | bytes 40992 | tf_op jit(solution)/shard_map/ppermute | solution.py:417
  36.0 1.8 %collective-permute-done.14.refs_6_ = bf16[96,640]{1,0:T(8,128)(2,1)S(1)} collective-permute-done((bf16[96,640]{1,0:T(8,128)(2,1)S(1)}, bf16[96,640]{1,0:T(8,128)(2,1)S(1)}, u32[]{:S(2)}, u32[]{:S(2)}) %collective-permute-start.14) | collective-permute-done | bytes 122912 | tf_op jit(solution)/shard_map/ppermute | solution.py:417
  37.8 1.6 %collective-permute-start.15 = (bf16[96,640]{1,0:T(8,128)(2,1)S(1)}, bf16[96,640]{1,0:T(8,128)(2,1)S(1)}, u32[]{:S(2)}, u32[]{:S(2)}) collective-permute-start(bf16[96,640]{1,0:T(8,128)(2,1)S(1)} %select_convert_fusion), channel_id=1, source_target_pairs={{0,8},{4,12},{8,0},{12,4},{1,9},{5,13},{9,1},{13,5},{2,10},{6,14},... | collective-permute-start | bytes 368648 | tf_op jit(solution)/shard_map/ppermute | solution.py:436
  39.4 1.4 %collective-permute-start.13 = (bf16[32,640]{1,0:T(8,128)(2,1)S(1)}, bf16[32,640]{1,0:T(8,128)(2,1)S(1)}, u32[]{:S(2)}, u32[]{:S(2)}) collective-permute-start(bf16[32,640]{1,0:T(8,128)(2,1)S(1)} %select_convert_fusion.1), channel_id=1, source_target_pairs={{0,8},{4,12},{8,0},{12,4},{1,9},{5,13},{9,1},{13,5},{2,10},{6,14},... | collective-permute-start | bytes 122888 | tf_op jit(solution)/shard_map/ppermute | solution.py:436
  40.8 0.1 pad_add_fusion.flag_ref
  40.9 6.8 %collective-permute-done.13.refs_2_.refs_7_ = bf16[32,640]{1,0:T(8,128)(2,1)S(1)} collective-permute-done((bf16[32,640]{1,0:T(8,128)(2,1)S(1)}, bf16[32,640]{1,0:T(8,128)(2,1)S(1)}, u32[]{:S(2)}, u32[]{:S(2)}) %collective-permute-start.13) | collective-permute-done | bytes 40992 | tf_op jit(solution)/shard_map/ppermute | solution.py:436
  47.7 0.0 collective-permute-done.15.refs_3_.refs_8_
  47.7 1.7 %finish.1 = (f32[128,640]{1,0:T(8,128)}, f32[1,128]{1,0:T(1,128)S(1)}) custom-call(s32[3]{0:T(128)S(1)} %pad_add_fusion.flag_ref, s32[4,128]{1,0:T(4,128)S(1)} %bitcast.20, s32[4,128]{1,0:T(4,128)S(1)} %bitcast.21, f32[4,128]{1,0:T(4,128)S(1)} %bitcast.13, f32[1,640]{1,0:T(1,128)S(1)} %broadcast_in_dim.3.partner_ref, ...), custom_call_target="tpu_custom_call" | custom-call | flops 2200000000 | bytes 200000 | tf_op jit(solution)/shard_map/finish/pallas_call | solution.py:33
  49.4 1.1 %collective-permute-done.16 = f32[1,128]{1,0:T(1,128)S(1)} collective-permute-done((f32[1,128]{1,0:T(1,128)S(1)}, f32[1,128]{1,0:T(1,128)S(1)}, u32[]{:S(2)}, u32[]{:S(2)}) %collective-permute-start.16) | collective-permute-done | bytes 544 | tf_op jit(solution)/shard_map/ppermute | solution.py:473
  50.6 1.5 %collective-permute-start.17 = (f32[1,128]{1,0:T(1,128)S(1)}, f32[1,128]{1,0:T(1,128)S(1)}, u32[]{:S(2)}, u32[]{:S(2)}) collective-permute-start(f32[1,128]{1,0:T(1,128)S(1)} %add.30), channel_id=1, source_target_pairs={{0,2},{2,0},{1,3},{3,1},{4,6},{6,4},{5,7},{7,5},{8,10},{10,8},{9,1... | collective-permute-start | bytes 1544 | tf_op jit(solution)/shard_map/ppermute | solution.py:476
  52.1 2.1 %collective-permute-done.17 = f32[1,128]{1,0:T(1,128)S(1)} collective-permute-done((f32[1,128]{1,0:T(1,128)S(1)}, f32[1,128]{1,0:T(1,128)S(1)}, u32[]{:S(2)}, u32[]{:S(2)}) %collective-permute-start.17) | collective-permute-done | bytes 544 | tf_op jit(solution)/shard_map/ppermute | solution.py:476
  54.1 0.6 %bitcast_divide_fusion = f32[128]{0:T(128)} fusion(f32[512]{0:T(512)S(1)} %copy-done, s32[]{:T(128)S(6)} %select_n.29, f32[1,128]{1,0:T(1,128)S(1)} %add.30, f32[1,128]{1,0:T(1,128)S(1)} %collective-permute-done.17), kind=kLoop, calls=%fused_computation.5 | loop fusion | flops 512 | bytes 2052 | tf_op jit(solution)/shard_map/div | solution.py:478
  (18 shorter events, 0.1 us)
Async XLA Ops:
  0.7 11.2 %copy-start.1 = (bf16[3,768,128]{2,1,0:T(8,128)(2,1)S(1)}, bf16[3,768,128]{2,1,0:T(8,128)(2,1)}, u32[]{:S(2)}) copy-start(bf16[3,768,128]{2,1,0:T(8,128)(2,1)} %refs_4_.5) | copy-start | bytes 1769476
  0.7 11.2 %copy-start.2 = (f32[9,768,16]{1,2,0:T(8,128)S(1)}, f32[9,768,16]{1,2,0:T(8,128)}, u32[]{:S(2)}) copy-start(f32[9,768,16]{1,2,0:T(8,128)} %param.11) | copy-start | bytes 1327108
  0.7 11.2 %copy-start.3 = (s32[768,16]{0,1:T(8,128)S(1)}, s32[768,16]{0,1:T(8,128)}, u32[]{:S(2)}) copy-start(s32[768,16]{0,1:T(8,128)} %param.12) | copy-start | bytes 147460
  0.7 11.2 %copy-start.4 = (s32[768]{0:T(1024)S(1)}, s32[768]{0:T(1024)}, u32[]{:S(2)}) copy-start(s32[768]{0:T(1024)} %refs_2_.5) | copy-start | bytes 9220
  4.8 11.3 %collective-permute-start.2 = (bf16[128,768]{1,0:T(8,128)(2,1)S(1)}, bf16[128,768]{1,0:T(8,128)(2,1)S(1)}, u32[]{:S(2)}, u32[]{:S(2)}) collective-permute-start(bf16[128,768]{1,0:T(8,128)(2,1)S(1)} %get-tuple-element.17.refs_5_.refs_0_), channel_id=1, source_target_pairs={{2,0},{0,2},{3,1},{1,3},{6,4},{4,6},{7,5},{5,7},{10,8},{8,10},{11,... | collective-permute-start | bytes 589832 | tf_op jit(solution)/shard_map/ppermute | solution.py:395
  7.8 7.7 %collective-permute-start = (bf16[3,96,128]{2,1,0:T(8,128)(2,1)S(1)}, bf16[3,96,128]{2,1,0:T(8,128)(2,1)S(1)}, u32[]{:S(2)}, u32[]{:S(2)}) collective-permute-start(bf16[3,96,128]{2,1,0:T(8,128)(2,1)S(1)} %get-tuple-element.15), channel_id=1, source_target_pairs={{0,4},{4,0},{8,12},{12,8},{1,5},{5,1},{9,13},{13,9},{2,6},{6,2},{1... | collective-permute-start | bytes 221192 | tf_op jit(solution)/shard_map/ppermute | solution.py:392
  9.4 6.7 %collective-permute-start.1 = (bf16[3,96,128]{2,1,0:T(8,128)(2,1)S(1)}, bf16[3,96,128]{2,1,0:T(8,128)(2,1)S(1)}, u32[]{:S(2)}, u32[]{:S(2)}) collective-permute-start(bf16[3,96,128]{2,1,0:T(8,128)(2,1)S(1)} %get-tuple-element.16), channel_id=1, source_target_pairs={{0,12},{4,8},{8,4},{12,0},{1,13},{5,9},{9,5},{13,1},{2,14},{6,10},... | collective-permute-start | bytes 221192 | tf_op jit(solution)/shard_map/ppermute | solution.py:392
  15.0 5.9 %collective-permute-start.7 = (bf16[128,768]{1,0:T(8,128)(2,1)S(1)}, bf16[128,768]{1,0:T(8,128)(2,1)S(1)}, u32[]{:S(2)}, u32[]{:S(2)}) collective-permute-start(bf16[128,768]{1,0:T(8,128)(2,1)S(1)} %images.4.refs_7_.refs_1_), channel_id=1, source_target_pairs={{2,0},{0,2},{3,1},{1,3},{6,4},{4,6},{7,5},{5,7},{10,8},{8,10},{11,... | collective-permute-start | bytes 589832 | tf_op jit(solution)/shard_map/ppermute | solution.py:395
  15.6 5.5 %collective-permute-start.5 = (bf16[128,768]{1,0:T(8,128)(2,1)S(1)}, bf16[128,768]{1,0:T(8,128)(2,1)S(1)}, u32[]{:S(2)}, u32[]{:S(2)}) collective-permute-start(bf16[128,768]{1,0:T(8,128)(2,1)S(1)} %images.4.refs_7_.refs_1_), channel_id=1, source_target_pairs={{0,1},{1,0},{2,3},{3,2},{4,5},{5,4},{6,7},{7,6},{8,9},{9,8},{10,11... | collective-permute-start | bytes 589832 | tf_op jit(solution)/shard_map/ppermute | solution.py:398
  15.6 5.8 %collective-permute-start.4 = (bf16[128,768]{1,0:T(8,128)(2,1)S(1)}, bf16[128,768]{1,0:T(8,128)(2,1)S(1)}, u32[]{:S(2)}, u32[]{:S(2)}) collective-permute-start(bf16[128,768]{1,0:T(8,128)(2,1)S(1)} %get-tuple-element.17.refs_5_.refs_0_), channel_id=1, source_target_pairs={{0,1},{1,0},{2,3},{3,2},{4,5},{5,4},{6,7},{7,6},{8,9},{9,8},{10,11... | collective-permute-start | bytes 589832 | tf_op jit(solution)/shard_map/ppermute | solution.py:398
  19.2 2.2 %collective-permute-start.6 = (bf16[128,768]{1,0:T(8,128)(2,1)S(1)}, bf16[128,768]{1,0:T(8,128)(2,1)S(1)}, u32[]{:S(2)}, u32[]{:S(2)}) collective-permute-start(bf16[128,768]{1,0:T(8,128)(2,1)S(1)} %images.5.refs_2_), channel_id=1, source_target_pairs={{0,1},{1,0},{2,3},{3,2},{4,5},{5,4},{6,7},{7,6},{8,9},{9,8},{10,11... | collective-permute-start | bytes 589832 | tf_op jit(solution)/shard_map/ppermute | solution.py:398
  19.3 7.3 %collective-permute-start.3 = (bf16[128,768]{1,0:T(8,128)(2,1)S(1)}, bf16[128,768]{1,0:T(8,128)(2,1)S(1)}, u32[]{:S(2)}, u32[]{:S(2)}) collective-permute-start(bf16[128,768]{1,0:T(8,128)(2,1)S(1)} %images.5.refs_2_), channel_id=1, source_target_pairs={{2,0},{0,2},{3,1},{1,3},{6,4},{4,6},{7,5},{5,7},{10,8},{8,10},{11,... | collective-permute-start | bytes 589832 | tf_op jit(solution)/shard_map/ppermute | solution.py:395
  20.8 6.5 %collective-permute-start.9 = (bf16[128,768]{1,0:T(8,128)(2,1)S(1)}, bf16[128,768]{1,0:T(8,128)(2,1)S(1)}, u32[]{:S(2)}, u32[]{:S(2)}) collective-permute-start(bf16[128,768]{1,0:T(8,128)(2,1)S(1)} %collective-permute-done.2.refs_8_.refs_6_.refs_0_), channel_id=1, source_target_pairs={{0,1},{1,0},{2,3},{3,2},{4,5},{5,4},{6,7},{7,6},{8,9},{9,8},{10,11... | collective-permute-start | bytes 589832 | tf_op jit(solution)/shard_map/ppermute | solution.py:398
  21.0 6.3 %collective-permute-start.10 = (bf16[128,768]{1,0:T(8,128)(2,1)S(1)}, bf16[128,768]{1,0:T(8,128)(2,1)S(1)}, u32[]{:S(2)}, u32[]{:S(2)}) collective-permute-start(bf16[128,768]{1,0:T(8,128)(2,1)S(1)} %collective-permute-done.7.refs_7_.refs_1_), channel_id=1, source_target_pairs={{0,1},{1,0},{2,3},{3,2},{4,5},{5,4},{6,7},{7,6},{8,9},{9,8},{10,11... | collective-permute-start | bytes 589832 | tf_op jit(solution)/shard_map/ppermute | solution.py:398
  24.8 16.1 %copy-start.7 = (f32[640]{0:T(1024)S(1)}, f32[640]{0:T(1024)}, u32[]{:S(2)}) copy-start(f32[640]{0:T(1024)} %param.15) | copy-start | bytes 7684
  24.8 22.9 %copy-start = (f32[512]{0:T(512)S(1)}, f32[512]{0:T(512)}, u32[]{:S(2)}) copy-start(f32[512]{0:T(512)} %param.14) | copy-start | bytes 6148
  24.8 22.9 %copy-start.5 = (s32[512]{0:T(512)S(1)}, s32[512]{0:T(512)}, u32[]{:S(2)}) copy-start(s32[512]{0:T(512)} %param.16) | copy-start | bytes 6148
  24.8 22.9 %copy-start.6 = (s32[512]{0:T(512)S(1)}, s32[512]{0:T(512)}, u32[]{:S(2)}) copy-start(s32[512]{0:T(512)} %param.17) | copy-start | bytes 6148
  26.6 1.4 %collective-permute-start.11 = (bf16[128,768]{1,0:T(8,128)(2,1)S(1)}, bf16[128,768]{1,0:T(8,128)(2,1)S(1)}, u32[]{:S(2)}, u32[]{:S(2)}) collective-permute-start(bf16[128,768]{1,0:T(8,128)(2,1)S(1)} %collective-permute-done.3.refs_2_), channel_id=1, source_target_pairs={{0,1},{1,0},{2,3},{3,2},{4,5},{5,4},{6,7},{7,6},{8,9},{9,8},{10,11... | collective-permute-start | bytes 589832 | tf_op jit(solution)/shard_map/ppermute | solution.py:398
  26.6 6.9 %collective-permute-start.8 = (bf16[128,640]{1,0:T(8,128)(2,1)S(1)}, bf16[128,640]{1,0:T(8,128)(2,1)S(1)}, u32[]{:S(2)}, u32[]{:S(2)}) collective-permute-start(bf16[128,640]{1,0:T(8,128)(2,1)S(1)} %get-tuple-element.20), channel_id=1, source_target_pairs={{0,4},{4,0},{8,12},{12,8},{1,5},{5,1},{9,13},{13,9},{2,6},{6,2},{1... | collective-permute-start | bytes 491528 | tf_op jit(solution)/shard_map/ppermute | solution.py:417
  31.5 4.5 %collective-permute-start.12 = (bf16[32,640]{1,0:T(8,128)(2,1)S(1)}, bf16[32,640]{1,0:T(8,128)(2,1)S(1)}, u32[]{:S(2)}, u32[]{:S(2)}) collective-permute-start(bf16[32,640]{1,0:T(8,128)(2,1)S(1)} %get-tuple-element.23), channel_id=1, source_target_pairs={{0,4},{4,0},{8,12},{12,8},{1,5},{5,1},{9,13},{13,9},{2,6},{6,2},{1... | collective-permute-start | bytes 122888 | tf_op jit(solution)/shard_map/ppermute | solution.py:417
  32.2 5.6 %collective-permute-start.14 = (bf16[96,640]{1,0:T(8,128)(2,1)S(1)}, bf16[96,640]{1,0:T(8,128)(2,1)S(1)}, u32[]{:S(2)}, u32[]{:S(2)}) collective-permute-start(bf16[96,640]{1,0:T(8,128)(2,1)S(1)} %get-tuple-element.24), channel_id=1, source_target_pairs={{0,4},{4,0},{8,12},{12,8},{1,5},{5,1},{9,13},{13,9},{2,6},{6,2},{1... | collective-permute-start | bytes 368648 | tf_op jit(solution)/shard_map/ppermute | solution.py:417
  37.8 9.9 %collective-permute-start.15 = (bf16[96,640]{1,0:T(8,128)(2,1)S(1)}, bf16[96,640]{1,0:T(8,128)(2,1)S(1)}, u32[]{:S(2)}, u32[]{:S(2)}) collective-permute-start(bf16[96,640]{1,0:T(8,128)(2,1)S(1)} %select_convert_fusion), channel_id=1, source_target_pairs={{0,8},{4,12},{8,0},{12,4},{1,9},{5,13},{9,1},{13,5},{2,10},{6,14},... | collective-permute-start | bytes 368648 | tf_op jit(solution)/shard_map/ppermute | solution.py:436
  39.4 8.3 %collective-permute-start.13 = (bf16[32,640]{1,0:T(8,128)(2,1)S(1)}, bf16[32,640]{1,0:T(8,128)(2,1)S(1)}, u32[]{:S(2)}, u32[]{:S(2)}) collective-permute-start(bf16[32,640]{1,0:T(8,128)(2,1)S(1)} %select_convert_fusion.1), channel_id=1, source_target_pairs={{0,8},{4,12},{8,0},{12,4},{1,9},{5,13},{9,1},{13,5},{2,10},{6,14},... | collective-permute-start | bytes 122888 | tf_op jit(solution)/shard_map/ppermute | solution.py:436
  49.4 1.1 %collective-permute-start.16 = (f32[1,128]{1,0:T(1,128)S(1)}, f32[1,128]{1,0:T(1,128)S(1)}, u32[]{:S(2)}, u32[]{:S(2)}) collective-permute-start(f32[1,128]{1,0:T(1,128)S(1)} %get-tuple-element.27), channel_id=1, source_target_pairs={{0,1},{1,0},{2,3},{3,2},{4,5},{5,4},{6,7},{7,6},{8,9},{9,8},{10,11... | collective-permute-start | bytes 1544 | tf_op jit(solution)/shard_map/ppermute | solution.py:473
  50.6 3.5 %collective-permute-start.17 = (f32[1,128]{1,0:T(1,128)S(1)}, f32[1,128]{1,0:T(1,128)S(1)}, u32[]{:S(2)}, u32[]{:S(2)}) collective-permute-start(f32[1,128]{1,0:T(1,128)S(1)} %add.30), channel_id=1, source_target_pairs={{0,2},{2,0},{1,3},{3,1},{4,6},{6,4},{5,7},{7,5},{8,10},{10,8},{9,1... | collective-permute-start | bytes 1544 | tf_op jit(solution)/shard_map/ppermute | solution.py:476

commit v14 on v12

--- a/solution.py
+++ b/solution.py
@@ -386,7 +386,7 @@
     shared = (spot, mode_panel, nbr, coef, bond_count)
     near, edge_one, edge_two = images_of(chunks[0], *shared, edges=True)
     pairs = [(z, z ^ 1) for z in range(atom_count)]
-    others = [(z, (z + 1 if z & 1 else z - 1) % atom_count) for z in range(atom_count)]
+    others = [(z, min(max(z + 1 if z & 1 else z - 1, 0), atom_count - 1)) for z in range(atom_count)]
     halos = (lax.ppermute(edge_one, "atoms", pairs), lax.ppermute(edge_two, "atoms", others))
 
     def from_group(cells, shift):

time: 53.1 us -> 54.5 us (1.026)
  starting transfers between devices: 17.5 us -> 19.5 us
  waiting for transfers between devices: 15 us -> 14.4 us
    ppermute x3, starting transfers between devices: 2.76 us -> 6.49 us  [next_door(): return (keep, [lax.ppermute(send, 'atoms', pairs) for send in sends])]
    ppermute x1, starting transfers between devices: 2.48 us -> 0.65 us  [body(): lax.ppermute(edge_two, 'atoms', others)]
    ppermute x6, waiting for transfers between devices: 0.78 us -> 0.02 us  [from_sibling(): return lax.ppermute(cells, 'sub', [(0, 1), (1, 0)])]
where the time goes in v14:
time: 54.5 us; the launch traced here: 54.3 us
  starting transfers between devices  19.5 us (36%)
  Pallas kernels  18.7 us (34%)
  waiting for transfers between devices  14.4 us (26%)
  other arithmetic  0.89 us (2%)
  between operations  0.8 us (1%)
    pallas_call x6, Pallas kernels, call(): pl.pallas_call(kernel, in_specs=in_specs, out_specs=out_specs, out_shape=...  18.7 us
    ppermute x3, starting transfers between devices, next_door(): return (keep, [lax.ppermute(send, 'atoms', pairs) for send in sends])  6.49 us
    ppermute x2, waiting for transfers between devices, body(): lax.ppermute(sent, 'atoms', [(z, z ^ 2) for z in range(atom_count)])  6.14 us
    ppermute x3, starting transfers between devices, from_group(): return lax.ppermute(cells, 'modes', [(m ^ shift, m) for m in range(groups)])  5.1 us
    ppermute x3, waiting for transfers between devices, next_door(): return (keep, [lax.ppermute(send, 'atoms', pairs) for send in sends])  3.24 us
    ppermute x2, starting transfers between devices, body(): lax.ppermute(sent, 'atoms', [(z, z ^ 2) for z in range(atom_count)])  3.06 us
    ppermute x1, waiting for transfers between devices, body(): lax.ppermute(numerator, 'modes', [(m, m ^ step) for m in range(groups)])  2.05 us
    ppermute x3, waiting for transfers between devices, from_group(): return lax.ppermute(cells, 'modes', [(m ^ shift, m) for m in range(groups)])  1.83 us
  transfers between devices with their start and end apart: 18, of which 6 were waited for; matrix products, arithmetic and copies ran while one was open for 0% of the time, Pallas kernels for 24%

profile of v14, /device:TPU:0, one launch (start us, length us, event | category | flops | bytes accessed | tf_op | source)
XLA Modules:
  0.0 54.3 jit_solution(3793016147323264955)
XLA Ops:
  0.6 0.1 pad_add_fusion.1.refs_0_
  0.7 4.1 %images.3 = (bf16[128,768]{1,0:T(8,128)(2,1)S(1)}, bf16[3,96,128]{2,1,0:T(8,128)(2,1)S(1)}, bf16[3,96,128]{2,1,0:T(8,128)(2,1)S(1)}) custom-call(s32[2]{0:T(128)S(1)} %pad_add_fusion.1.refs_0_, s32[16,768]{1,0:T(8,128)} %bitcast.17, s32[768]{0:T(1024)} %refs_2_.5, f32[9,16,768]{2,1,0:T(8,128)} %bitcast.14, bf16[3,768,128]{2,1,0:T(8,128)(2,1)} %refs_4_.5), custom_call_target="tpu_custom_call" | custom-call | flops 3520000000 | bytes 320000 | tf_op jit(solution)/shard_map/images/pallas_call | solution.py:33
  4.8 3.0 %collective-permute-start.2 = (bf16[128,768]{1,0:T(8,128)(2,1)S(1)}, bf16[128,768]{1,0:T(8,128)(2,1)S(1)}, u32[]{:S(2)}, u32[]{:S(2)}) collective-permute-start(bf16[128,768]{1,0:T(8,128)(2,1)S(1)} %get-tuple-element.17.refs_5_.refs_0_), channel_id=1, source_target_pairs={{2,0},{0,2},{3,1},{1,3},{6,4},{4,6},{7,5},{5,7},{10,8},{8,10},{11,... | collective-permute-start | bytes 589832 | tf_op jit(solution)/shard_map/ppermute | solution.py:393
  7.8 1.6 %collective-permute-start = (bf16[3,96,128]{2,1,0:T(8,128)(2,1)S(1)}, bf16[3,96,128]{2,1,0:T(8,128)(2,1)S(1)}, u32[]{:S(2)}, u32[]{:S(2)}) collective-permute-start(bf16[3,96,128]{2,1,0:T(8,128)(2,1)S(1)} %get-tuple-element.15), channel_id=1, source_target_pairs={{0,4},{4,0},{8,12},{12,8},{1,5},{5,1},{9,13},{13,9},{2,6},{6,2},{1... | collective-permute-start | bytes 221192 | tf_op jit(solution)/shard_map/ppermute | solution.py:390
  9.4 0.7 %collective-permute-start.1 = (bf16[3,96,128]{2,1,0:T(8,128)(2,1)S(1)}, bf16[3,96,128]{2,1,0:T(8,128)(2,1)S(1)}, u32[]{:S(2)}, u32[]{:S(2)}) collective-permute-start(bf16[3,96,128]{2,1,0:T(8,128)(2,1)S(1)} %get-tuple-element.16), channel_id=1, source_target_pairs={{0,0},{4,8},{8,4},{12,12},{1,1},{5,9},{9,5},{13,13},{2,2},{6,10},{... | collective-permute-start | bytes 221192 | tf_op jit(solution)/shard_map/ppermute | solution.py:390
  10.1 3.1 %images.4.refs_7_.refs_1_ = bf16[128,768]{1,0:T(8,128)(2,1)S(1)} custom-call(s32[2]{0:T(128)S(1)} %pad_add_fusion.1.refs_0_, s32[16,768]{1,0:T(8,128)S(1)} %bitcast.18, s32[768]{0:T(1024)S(1)} %copy-done.4, f32[9,16,768]{2,1,0:T(8,128)S(1)} %bitcast.15, bf16[3,768,128]{2,1,0:T(8,128)(2,1)S(1)} %copy-done.1, ...), custom_call_target="tpu_custom_call" | custom-call | flops 3520000000 | bytes 320000 | tf_op jit(solution)/shard_map/images/pallas_call | solution.py:33
  13.2 0.6 %collective-permute-start.7 = (bf16[128,768]{1,0:T(8,128)(2,1)S(1)}, bf16[128,768]{1,0:T(8,128)(2,1)S(1)}, u32[]{:S(2)}, u32[]{:S(2)}) collective-permute-start(bf16[128,768]{1,0:T(8,128)(2,1)S(1)} %images.4.refs_7_.refs_1_), channel_id=1, source_target_pairs={{2,0},{0,2},{3,1},{1,3},{6,4},{4,6},{7,5},{5,7},{10,8},{8,10},{11,... | collective-permute-start | bytes 589832 | tf_op jit(solution)/shard_map/ppermute | solution.py:393
  13.8 0.0 collective-permute-start.5
  13.8 0.0 collective-permute-done.refs_5_
  13.8 0.5 collective-permute-start.4
  14.3 0.0 collective-permute-done.1.refs_6_
  14.3 0.0 collective-permute-done.2.refs_8_.refs_6_.refs_0_
  14.3 3.0 %images.5.refs_2_ = bf16[128,768]{1,0:T(8,128)(2,1)S(1)} custom-call(s32[2]{0:T(128)S(1)} %pad_add_fusion.1.refs_0_, s32[16,768]{1,0:T(8,128)S(1)} %bitcast.19, s32[768]{0:T(1024)S(1)} %copy-done.4, f32[9,16,768]{2,1,0:T(8,128)S(1)} %bitcast.16, bf16[3,768,128]{2,1,0:T(8,128)(2,1)S(1)} %copy-done.1, bf16[3,96,128]{2,1,0:T(8,128)(2,1)S(1)} %collective-permute-done.refs_5_, ...), custom_call_target="tpu_custom_call" | custom-call | flops 3520000000 | bytes 320000 | tf_op jit(solution)/shard_map/images/pallas_call | solution.py:33
  17.4 0.1 collective-permute-start.6
  17.5 0.1 pad_add_fusion.2.place_ref
  17.5 1.5 %collective-permute-start.3 = (bf16[128,768]{1,0:T(8,128)(2,1)S(1)}, bf16[128,768]{1,0:T(8,128)(2,1)S(1)}, u32[]{:S(2)}, u32[]{:S(2)}) collective-permute-start(bf16[128,768]{1,0:T(8,128)(2,1)S(1)} %images.5.refs_2_), channel_id=1, source_target_pairs={{2,0},{0,2},{3,1},{1,3},{6,4},{4,6},{7,5},{5,7},{10,8},{8,10},{11,... | collective-permute-start | bytes 589832 | tf_op jit(solution)/shard_map/ppermute | solution.py:393
  19.0 0.3 collective-permute-done.7.refs_7_.refs_1_
  19.3 0.0 collective-permute-start.9
  19.3 0.0 collective-permute-done.5.refs_4_
  19.3 0.5 collective-permute-start.10
  19.8 0.0 collective-permute-done.4.refs_3_
  19.8 0.0 collective-permute-done.6.refs_5_
  19.8 3.4 %products.2 = (f32[128,640]{1,0:T(8,128)S(1)}, bf16[128,640]{1,0:T(8,128)(2,1)S(1)}) custom-call(s32[2]{0:T(128)S(1)} %pad_add_fusion.2.place_ref, bf16[3,768,640]{2,1,0:T(8,128)(2,1)} %partners_hbm.3, bf16[128,768]{1,0:T(8,128)(2,1)S(1)} %get-tuple-element.17.refs_5_.refs_0_, bf16[128,768]{1,0:T(8,128)(2,1)S(1)} %images.4.refs_7_.refs_1_, ...), custom_call_target="tpu_custom_call" | custom-call | flops 6600000000 | bytes 600000 | tf_op jit(solution)/shard_map/products/pallas_call | solution.py:33
  23.3 0.0 copy-start.7
  23.3 0.0 copy-start
  23.3 0.0 copy-start.5
  23.3 0.0 copy-start.6
  23.3 1.5 %collective-permute-done.3.refs_2_ = bf16[128,768]{1,0:T(8,128)(2,1)S(1)} collective-permute-done((bf16[128,768]{1,0:T(8,128)(2,1)S(1)}, bf16[128,768]{1,0:T(8,128)(2,1)S(1)}, u32[]{:S(2)}, u32[]{:S(2)}) %collective-permute-start.3) | collective-permute-done | bytes 196640 | tf_op jit(solution)/shard_map/ppermute | solution.py:393
  24.8 0.0 collective-permute-start.11
  24.8 4.4 %collective-permute-start.8 = (bf16[128,640]{1,0:T(8,128)(2,1)S(1)}, bf16[128,640]{1,0:T(8,128)(2,1)S(1)}, u32[]{:S(2)}, u32[]{:S(2)}) collective-permute-start(bf16[128,640]{1,0:T(8,128)(2,1)S(1)} %get-tuple-element.20), channel_id=1, source_target_pairs={{0,4},{4,0},{8,12},{12,8},{1,5},{5,1},{9,13},{13,9},{2,6},{6,2},{1... | collective-permute-start | bytes 491528 | tf_op jit(solution)/shard_map/ppermute | solution.py:415
  29.2 0.0 collective-permute-done.10.refs_4_
  29.2 0.0 collective-permute-done.9.refs_3_
  29.2 0.0 collective-permute-done.11.refs_5_
  29.2 3.4 %products.3 = (f32[128,640]{1,0:T(8,128)S(1)}, bf16[64,640]{1,0:T(8,128)(2,1)S(1)}, bf16[64,640]{1,0:T(8,128)(2,1)S(1)}) custom-call(s32[2]{0:T(128)S(1)} %pad_add_fusion.2.place_ref, bf16[3,768,640]{2,1,0:T(8,128)(2,1)} %partners_hbm.3, bf16[128,768]{1,0:T(8,128)(2,1)S(1)} %collective-permute-done.2.refs_8_.refs_6_.refs_0_, ...), custom_call_target="tpu_custom_call" | custom-call | flops 110000000 | bytes 10000 | tf_op jit(solution)/shard_map/products/pallas_call | solution.py:33
  32.6 1.5 %collective-permute-start.12 = (bf16[64,640]{1,0:T(8,128)(2,1)S(1)}, bf16[64,640]{1,0:T(8,128)(2,1)S(1)}, u32[]{:S(2)}, u32[]{:S(2)}) collective-permute-start(bf16[64,640]{1,0:T(8,128)(2,1)S(1)} %get-tuple-element.23), channel_id=1, source_target_pairs={{0,4},{4,0},{8,12},{12,8},{1,5},{5,1},{9,13},{13,9},{2,6},{6,2},{1... | collective-permute-start | bytes 245768 | tf_op jit(solution)/shard_map/ppermute | solution.py:415
  34.1 0.6 %collective-permute-start.14 = (bf16[64,640]{1,0:T(8,128)(2,1)S(1)}, bf16[64,640]{1,0:T(8,128)(2,1)S(1)}, u32[]{:S(2)}, u32[]{:S(2)}) collective-permute-start(bf16[64,640]{1,0:T(8,128)(2,1)S(1)} %get-tuple-element.24), channel_id=1, source_target_pairs={{0,4},{4,0},{8,12},{12,8},{1,5},{5,1},{9,13},{13,9},{2,6},{6,2},{1... | collective-permute-start | bytes 245768 | tf_op jit(solution)/shard_map/ppermute | solution.py:415
  34.7 0.0 collective-permute-done.8.refs_1_
  34.7 3.2 %collective-permute-done.12.refs_5_ = bf16[64,640]{1,0:T(8,128)(2,1)S(1)} collective-permute-done((bf16[64,640]{1,0:T(8,128)(2,1)S(1)}, bf16[64,640]{1,0:T(8,128)(2,1)S(1)}, u32[]{:S(2)}, u32[]{:S(2)}) %collective-permute-start.12) | collective-permute-done | bytes 81952 | tf_op jit(solution)/shard_map/ppermute | solution.py:415
  38.0 1.1 %collective-permute-start.13 = (bf16[64,640]{1,0:T(8,128)(2,1)S(1)}, bf16[64,640]{1,0:T(8,128)(2,1)S(1)}, u32[]{:S(2)}, u32[]{:S(2)}) collective-permute-start(bf16[64,640]{1,0:T(8,128)(2,1)S(1)} %select_convert_fusion.1), channel_id=1, source_target_pairs={{0,8},{4,12},{8,0},{12,4},{1,9},{5,13},{9,1},{13,5},{2,10},{6,14},... | collective-permute-start | bytes 245768 | tf_op jit(solution)/shard_map/ppermute | solution.py:435
  39.1 0.0 collective-permute-done.14.refs_6_
  39.1 2.0 %collective-permute-start.15 = (bf16[64,640]{1,0:T(8,128)(2,1)S(1)}, bf16[64,640]{1,0:T(8,128)(2,1)S(1)}, u32[]{:S(2)}, u32[]{:S(2)}) collective-permute-start(bf16[64,640]{1,0:T(8,128)(2,1)S(1)} %select_convert_fusion), channel_id=1, source_target_pairs={{0,8},{4,12},{8,0},{12,4},{1,9},{5,13},{9,1},{13,5},{2,10},{6,14},... | collective-permute-start | bytes 245768 | tf_op jit(solution)/shard_map/ppermute | solution.py:435
  41.1 0.1 pad_add_fusion.flag_ref
  41.2 6.1 %collective-permute-done.15.refs_3_.refs_8_ = bf16[64,640]{1,0:T(8,128)(2,1)S(1)} collective-permute-done((bf16[64,640]{1,0:T(8,128)(2,1)S(1)}, bf16[64,640]{1,0:T(8,128)(2,1)S(1)}, u32[]{:S(2)}, u32[]{:S(2)}) %collective-permute-start.15) | collective-permute-done | bytes 81952 | tf_op jit(solution)/shard_map/ppermute | solution.py:435
  47.3 1.7 %finish.1 = (f32[128,640]{1,0:T(8,128)}, f32[1,128]{1,0:T(1,128)S(1)}) custom-call(s32[3]{0:T(128)S(1)} %pad_add_fusion.flag_ref, s32[4,128]{1,0:T(4,128)S(1)} %bitcast.20, s32[4,128]{1,0:T(4,128)S(1)} %bitcast.21, f32[4,128]{1,0:T(4,128)S(1)} %bitcast.13, f32[1,640]{1,0:T(1,128)S(1)} %broadcast_in_dim.3.partner_ref, ...), custom_call_target="tpu_custom_call" | custom-call | flops 2200000000 | bytes 200000 | tf_op jit(solution)/shard_map/finish/pallas_call | solution.py:33
  49.1 1.1 %collective-permute-done.16 = f32[1,128]{1,0:T(1,128)S(1)} collective-permute-done((f32[1,128]{1,0:T(1,128)S(1)}, f32[1,128]{1,0:T(1,128)S(1)}, u32[]{:S(2)}, u32[]{:S(2)}) %collective-permute-start.16) | collective-permute-done | bytes 544 | tf_op jit(solution)/shard_map/ppermute | solution.py:472
  50.2 1.5 %collective-permute-start.17 = (f32[1,128]{1,0:T(1,128)S(1)}, f32[1,128]{1,0:T(1,128)S(1)}, u32[]{:S(2)}, u32[]{:S(2)}) collective-permute-start(f32[1,128]{1,0:T(1,128)S(1)} %add.30), channel_id=1, source_target_pairs={{0,2},{2,0},{1,3},{3,1},{4,6},{6,4},{5,7},{7,5},{8,10},{10,8},{9,1... | collective-permute-start | bytes 1544 | tf_op jit(solution)/shard_map/ppermute | solution.py:475
  51.7 2.1 %collective-permute-done.17 = f32[1,128]{1,0:T(1,128)S(1)} collective-permute-done((f32[1,128]{1,0:T(1,128)S(1)}, f32[1,128]{1,0:T(1,128)S(1)}, u32[]{:S(2)}, u32[]{:S(2)}) %collective-permute-start.17) | collective-permute-done | bytes 544 | tf_op jit(solution)/shard_map/ppermute | solution.py:475
  53.7 0.6 %bitcast_divide_fusion = f32[128]{0:T(128)} fusion(f32[512]{0:T(512)S(1)} %copy-done, s32[]{:T(128)S(6)} %select_n.24, f32[1,128]{1,0:T(1,128)S(1)} %add.30, f32[1,128]{1,0:T(1,128)S(1)} %collective-permute-done.17), kind=kLoop, calls=%fused_computation.5 | loop fusion | flops 512 | bytes 2052 | tf_op jit(solution)/shard_map/div | solution.py:477
  (18 shorter events, 0.1 us)
Async XLA Ops:
  0.7 9.4 %copy-start.1 = (bf16[3,768,128]{2,1,0:T(8,128)(2,1)S(1)}, bf16[3,768,128]{2,1,0:T(8,128)(2,1)}, u32[]{:S(2)}) copy-start(bf16[3,768,128]{2,1,0:T(8,128)(2,1)} %refs_4_.5) | copy-start | bytes 1769476
  0.7 9.4 %copy-start.2 = (f32[9,768,16]{1,2,0:T(8,128)S(1)}, f32[9,768,16]{1,2,0:T(8,128)}, u32[]{:S(2)}) copy-start(f32[9,768,16]{1,2,0:T(8,128)} %param.11) | copy-start | bytes 1327108
  0.7 9.4 %copy-start.3 = (s32[768,16]{0,1:T(8,128)S(1)}, s32[768,16]{0,1:T(8,128)}, u32[]{:S(2)}) copy-start(s32[768,16]{0,1:T(8,128)} %param.12) | copy-start | bytes 147460
  0.7 9.4 %copy-start.4 = (s32[768]{0:T(1024)S(1)}, s32[768]{0:T(1024)}, u32[]{:S(2)}) copy-start(s32[768]{0:T(1024)} %refs_2_.5) | copy-start | bytes 9220
  4.8 9.5 %collective-permute-start.2 = (bf16[128,768]{1,0:T(8,128)(2,1)S(1)}, bf16[128,768]{1,0:T(8,128)(2,1)S(1)}, u32[]{:S(2)}, u32[]{:S(2)}) collective-permute-start(bf16[128,768]{1,0:T(8,128)(2,1)S(1)} %get-tuple-element.17.refs_5_.refs_0_), channel_id=1, source_target_pairs={{2,0},{0,2},{3,1},{1,3},{6,4},{4,6},{7,5},{5,7},{10,8},{8,10},{11,... | collective-permute-start | bytes 589832 | tf_op jit(solution)/shard_map/ppermute | solution.py:393
  7.8 6.0 %collective-permute-start = (bf16[3,96,128]{2,1,0:T(8,128)(2,1)S(1)}, bf16[3,96,128]{2,1,0:T(8,128)(2,1)S(1)}, u32[]{:S(2)}, u32[]{:S(2)}) collective-permute-start(bf16[3,96,128]{2,1,0:T(8,128)(2,1)S(1)} %get-tuple-element.15), channel_id=1, source_target_pairs={{0,4},{4,0},{8,12},{12,8},{1,5},{5,1},{9,13},{13,9},{2,6},{6,2},{1... | collective-permute-start | bytes 221192 | tf_op jit(solution)/shard_map/ppermute | solution.py:390
  9.4 4.9 %collective-permute-start.1 = (bf16[3,96,128]{2,1,0:T(8,128)(2,1)S(1)}, bf16[3,96,128]{2,1,0:T(8,128)(2,1)S(1)}, u32[]{:S(2)}, u32[]{:S(2)}) collective-permute-start(bf16[3,96,128]{2,1,0:T(8,128)(2,1)S(1)} %get-tuple-element.16), channel_id=1, source_target_pairs={{0,0},{4,8},{8,4},{12,12},{1,1},{5,9},{9,5},{13,13},{2,2},{6,10},{... | collective-permute-start | bytes 221192 | tf_op jit(solution)/shard_map/ppermute | solution.py:390
  13.2 6.2 %collective-permute-start.7 = (bf16[128,768]{1,0:T(8,128)(2,1)S(1)}, bf16[128,768]{1,0:T(8,128)(2,1)S(1)}, u32[]{:S(2)}, u32[]{:S(2)}) collective-permute-start(bf16[128,768]{1,0:T(8,128)(2,1)S(1)} %images.4.refs_7_.refs_1_), channel_id=1, source_target_pairs={{2,0},{0,2},{3,1},{1,3},{6,4},{4,6},{7,5},{5,7},{10,8},{8,10},{11,... | collective-permute-start | bytes 589832 | tf_op jit(solution)/shard_map/ppermute | solution.py:393
  13.8 5.5 %collective-permute-start.5 = (bf16[128,768]{1,0:T(8,128)(2,1)S(1)}, bf16[128,768]{1,0:T(8,128)(2,1)S(1)}, u32[]{:S(2)}, u32[]{:S(2)}) collective-permute-start(bf16[128,768]{1,0:T(8,128)(2,1)S(1)} %images.4.refs_7_.refs_1_), channel_id=1, source_target_pairs={{0,1},{1,0},{2,3},{3,2},{4,5},{5,4},{6,7},{7,6},{8,9},{9,8},{10,11... | collective-permute-start | bytes 589832 | tf_op jit(solution)/shard_map/ppermute | solution.py:396
  13.8 6.1 %collective-permute-start.4 = (bf16[128,768]{1,0:T(8,128)(2,1)S(1)}, bf16[128,768]{1,0:T(8,128)(2,1)S(1)}, u32[]{:S(2)}, u32[]{:S(2)}) collective-permute-start(bf16[128,768]{1,0:T(8,128)(2,1)S(1)} %get-tuple-element.17.refs_5_.refs_0_), channel_id=1, source_target_pairs={{0,1},{1,0},{2,3},{3,2},{4,5},{5,4},{6,7},{7,6},{8,9},{9,8},{10,11... | collective-permute-start | bytes 589832 | tf_op jit(solution)/shard_map/ppermute | solution.py:396
  17.4 2.5 %collective-permute-start.6 = (bf16[128,768]{1,0:T(8,128)(2,1)S(1)}, bf16[128,768]{1,0:T(8,128)(2,1)S(1)}, u32[]{:S(2)}, u32[]{:S(2)}) collective-permute-start(bf16[128,768]{1,0:T(8,128)(2,1)S(1)} %images.5.refs_2_), channel_id=1, source_target_pairs={{0,1},{1,0},{2,3},{3,2},{4,5},{5,4},{6,7},{7,6},{8,9},{9,8},{10,11... | collective-permute-start | bytes 589832 | tf_op jit(solution)/shard_map/ppermute | solution.py:396
  17.5 7.3 %collective-permute-start.3 = (bf16[128,768]{1,0:T(8,128)(2,1)S(1)}, bf16[128,768]{1,0:T(8,128)(2,1)S(1)}, u32[]{:S(2)}, u32[]{:S(2)}) collective-permute-start(bf16[128,768]{1,0:T(8,128)(2,1)S(1)} %images.5.refs_2_), channel_id=1, source_target_pairs={{2,0},{0,2},{3,1},{1,3},{6,4},{4,6},{7,5},{5,7},{10,8},{8,10},{11,... | collective-permute-start | bytes 589832 | tf_op jit(solution)/shard_map/ppermute | solution.py:393
  19.3 9.9 %collective-permute-start.9 = (bf16[128,768]{1,0:T(8,128)(2,1)S(1)}, bf16[128,768]{1,0:T(8,128)(2,1)S(1)}, u32[]{:S(2)}, u32[]{:S(2)}) collective-permute-start(bf16[128,768]{1,0:T(8,128)(2,1)S(1)} %collective-permute-done.2.refs_8_.refs_6_.refs_0_), channel_id=1, source_target_pairs={{0,1},{1,0},{2,3},{3,2},{4,5},{5,4},{6,7},{7,6},{8,9},{9,8},{10,11... | collective-permute-start | bytes 589832 | tf_op jit(solution)/shard_map/ppermute | solution.py:396
  19.3 9.9 %collective-permute-start.10 = (bf16[128,768]{1,0:T(8,128)(2,1)S(1)}, bf16[128,768]{1,0:T(8,128)(2,1)S(1)}, u32[]{:S(2)}, u32[]{:S(2)}) collective-permute-start(bf16[128,768]{1,0:T(8,128)(2,1)S(1)} %collective-permute-done.7.refs_7_.refs_1_), channel_id=1, source_target_pairs={{0,1},{1,0},{2,3},{3,2},{4,5},{5,4},{6,7},{7,6},{8,9},{9,8},{10,11... | collective-permute-start | bytes 589832 | tf_op jit(solution)/shard_map/ppermute | solution.py:396
  23.3 10.9 %copy-start.7 = (f32[640]{0:T(1024)S(1)}, f32[640]{0:T(1024)}, u32[]{:S(2)}) copy-start(f32[640]{0:T(1024)} %param.15) | copy-start | bytes 7684
  23.3 24.1 %copy-start = (f32[512]{0:T(512)S(1)}, f32[512]{0:T(512)}, u32[]{:S(2)}) copy-start(f32[512]{0:T(512)} %param.14) | copy-start | bytes 6148
  23.3 24.1 %copy-start.5 = (s32[512]{0:T(512)S(1)}, s32[512]{0:T(512)}, u32[]{:S(2)}) copy-start(s32[512]{0:T(512)} %param.16) | copy-start | bytes 6148
  23.3 24.0 %copy-start.6 = (s32[512]{0:T(512)S(1)}, s32[512]{0:T(512)}, u32[]{:S(2)}) copy-start(s32[512]{0:T(512)} %param.17) | copy-start | bytes 6148
  24.8 4.4 %collective-permute-start.11 = (bf16[128,768]{1,0:T(8,128)(2,1)S(1)}, bf16[128,768]{1,0:T(8,128)(2,1)S(1)}, u32[]{:S(2)}, u32[]{:S(2)}) collective-permute-start(bf16[128,768]{1,0:T(8,128)(2,1)S(1)} %collective-permute-done.3.refs_2_), channel_id=1, source_target_pairs={{0,1},{1,0},{2,3},{3,2},{4,5},{5,4},{6,7},{7,6},{8,9},{9,8},{10,11... | collective-permute-start | bytes 589832 | tf_op jit(solution)/shard_map/ppermute | solution.py:396
  24.8 9.9 %collective-permute-start.8 = (bf16[128,640]{1,0:T(8,128)(2,1)S(1)}, bf16[128,640]{1,0:T(8,128)(2,1)S(1)}, u32[]{:S(2)}, u32[]{:S(2)}) collective-permute-start(bf16[128,640]{1,0:T(8,128)(2,1)S(1)} %get-tuple-element.20), channel_id=1, source_target_pairs={{0,4},{4,0},{8,12},{12,8},{1,5},{5,1},{9,13},{13,9},{2,6},{6,2},{1... | collective-permute-start | bytes 491528 | tf_op jit(solution)/shard_map/ppermute | solution.py:415
  32.6 5.3 %collective-permute-start.12 = (bf16[64,640]{1,0:T(8,128)(2,1)S(1)}, bf16[64,640]{1,0:T(8,128)(2,1)S(1)}, u32[]{:S(2)}, u32[]{:S(2)}) collective-permute-start(bf16[64,640]{1,0:T(8,128)(2,1)S(1)} %get-tuple-element.23), channel_id=1, source_target_pairs={{0,4},{4,0},{8,12},{12,8},{1,5},{5,1},{9,13},{13,9},{2,6},{6,2},{1... | collective-permute-start | bytes 245768 | tf_op jit(solution)/shard_map/ppermute | solution.py:415
  34.1 4.9 %collective-permute-start.14 = (bf16[64,640]{1,0:T(8,128)(2,1)S(1)}, bf16[64,640]{1,0:T(8,128)(2,1)S(1)}, u32[]{:S(2)}, u32[]{:S(2)}) collective-permute-start(bf16[64,640]{1,0:T(8,128)(2,1)S(1)} %get-tuple-element.24), channel_id=1, source_target_pairs={{0,4},{4,0},{8,12},{12,8},{1,5},{5,1},{9,13},{13,9},{2,6},{6,2},{1... | collective-permute-start | bytes 245768 | tf_op jit(solution)/shard_map/ppermute | solution.py:415
  38.0 9.3 %collective-permute-start.13 = (bf16[64,640]{1,0:T(8,128)(2,1)S(1)}, bf16[64,640]{1,0:T(8,128)(2,1)S(1)}, u32[]{:S(2)}, u32[]{:S(2)}) collective-permute-start(bf16[64,640]{1,0:T(8,128)(2,1)S(1)} %select_convert_fusion.1), channel_id=1, source_target_pairs={{0,8},{4,12},{8,0},{12,4},{1,9},{5,13},{9,1},{13,5},{2,10},{6,14},... | collective-permute-start | bytes 245768 | tf_op jit(solution)/shard_map/ppermute | solution.py:435
  39.1 8.2 %collective-permute-start.15 = (bf16[64,640]{1,0:T(8,128)(2,1)S(1)}, bf16[64,640]{1,0:T(8,128)(2,1)S(1)}, u32[]{:S(2)}, u32[]{:S(2)}) collective-permute-start(bf16[64,640]{1,0:T(8,128)(2,1)S(1)} %select_convert_fusion), channel_id=1, source_target_pairs={{0,8},{4,12},{8,0},{12,4},{1,9},{5,13},{9,1},{13,5},{2,10},{6,14},... | collective-permute-start | bytes 245768 | tf_op jit(solution)/shard_map/ppermute | solution.py:435
  49.1 1.1 %collective-permute-start.16 = (f32[1,128]{1,0:T(1,128)S(1)}, f32[1,128]{1,0:T(1,128)S(1)}, u32[]{:S(2)}, u32[]{:S(2)}) collective-permute-start(f32[1,128]{1,0:T(1,128)S(1)} %get-tuple-element.27), channel_id=1, source_target_pairs={{0,1},{1,0},{2,3},{3,2},{4,5},{5,4},{6,7},{7,6},{8,9},{9,8},{10,11... | collective-permute-start | bytes 1544 | tf_op jit(solution)/shard_map/ppermute | solution.py:472
  50.2 3.5 %collective-permute-start.17 = (f32[1,128]{1,0:T(1,128)S(1)}, f32[1,128]{1,0:T(1,128)S(1)}, u32[]{:S(2)}, u32[]{:S(2)}) collective-permute-start(f32[1,128]{1,0:T(1,128)S(1)} %add.30), channel_id=1, source_target_pairs={{0,2},{2,0},{1,3},{3,1},{4,6},{6,4},{5,7},{7,5},{8,10},{10,8},{9,1... | collective-permute-start | bytes 1544 | tf_op jit(solution)/shard_map/ppermute | solution.py:475

commit v15 on v12

--- a/solution.py
+++ b/solution.py
@@ -200,12 +200,14 @@
     rows, cols = mine[0].shape[0], partners.shape[2]
     count = len(chunks)
     depth = partners.shape[1]
+    pieces = [(r, pl.ds(h * (depth // 2), depth // 2)) for r in range(3) for h in range(2)]
 
     def kernel(place_ref, partners_hbm, *refs):
         keep_ref, *send_refs = refs[-4 - parts : -3]
         left_ref, partners_ref, sems = refs[-3:]
         copies = [
-            pltpu.make_async_copy(partners_hbm.at[r], partners_ref.at[r], sems.at[r]) for r in range(3)
+            pltpu.make_async_copy(partners_hbm.at[r, at], partners_ref.at[r, at], sems.at[i])
+            for i, (r, at) in enumerate(pieces)
         ]
         for copy in copies:
             copy.start()
@@ -220,10 +222,13 @@
                         at, to = r * width + spot * LANES, r * depth + block * LANES
                         left_ref[at_rows, to : to + length * LANES] = image_ref[:, at : at + length * LANES]
         total = None
-        for r, copy in enumerate(copies):
+        for (r, at), copy in zip(pieces, copies):
             copy.wait()
+            from_row = r * depth + at.start
             part = jnp.dot(
-                left_ref[:, r * depth : (r + 1) * depth], partners_ref[r], preferred_element_type=jnp.float32
+                left_ref[:, from_row : from_row + at.size],
+                partners_ref[r, at],
+                preferred_element_type=jnp.float32,
             )
             total = part if total is None else total + part
         keep_ref[...] = total[:rows]
@@ -242,7 +247,7 @@
         [
             pltpu.VMEM((2 * rows, 3 * depth), jnp.bfloat16),
             pltpu.VMEM((3, depth, cols), jnp.bfloat16),
-            pltpu.SemaphoreType.DMA((3,)),
+            pltpu.SemaphoreType.DMA((len(pieces),)),
         ],
     )
 

time: 53.1 us -> 53.5 us (level)
  Pallas kernels: 18.7 us -> 19.4 us
    pallas_call x6, Pallas kernels: 18.7 us -> 19.4 us  [call(): pl.pallas_call(kernel, in_specs=in_specs, out_specs=out_specs, out_shape=...]
  transfers between devices with their start and end apart: 18 -> 18, of which waited for: 6 -> 6; matrix products, arithmetic and copies ran while one was open for 0% -> 0% of each run, Pallas kernels for 24% -> 25%
where the time goes in v15:
time: 53.5 us; the launch traced here: 53.3 us
  Pallas kernels  19.4 us (36%)
  starting transfers between devices  17.5 us (33%)
  waiting for transfers between devices  14.6 us (27%)
  other arithmetic  0.9 us (2%)
  between operations  0.77 us (1%)
    pallas_call x6, Pallas kernels, call(): pl.pallas_call(kernel, in_specs=in_specs, out_specs=out_specs, out_shape=...  19.4 us
    ppermute x2, waiting for transfers between devices, body(): lax.ppermute(sent, 'atoms', [(z, z ^ 2) for z in range(atom_count)])  5.92 us
    ppermute x3, starting transfers between devices, from_group(): return lax.ppermute(cells, 'modes', [(m ^ shift, m) for m in range(groups)])  5.1 us
    ppermute x3, waiting for transfers between devices, next_door(): return (keep, [lax.ppermute(send, 'atoms', pairs) for send in sends])  3.26 us
    ppermute x2, starting transfers between devices, body(): lax.ppermute(sent, 'atoms', [(z, z ^ 2) for z in range(atom_count)])  3.06 us
    ppermute x3, starting transfers between devices, next_door(): return (keep, [lax.ppermute(send, 'atoms', pairs) for send in sends])  2.76 us
    ppermute x1, starting transfers between devices, body(): lax.ppermute(edge_two, 'atoms', others)  2.48 us
    ppermute x1, waiting for transfers between devices, body(): lax.ppermute(numerator, 'modes', [(m, m ^ step) for m in range(groups)])  2.06 us
  transfers between devices with their start and end apart: 18, of which 6 were waited for; matrix products, arithmetic and copies ran while one was open for 0% of the time, Pallas kernels for 25%

profile of v15, /device:TPU:0, one launch (start us, length us, event | category | flops | bytes accessed | tf_op | source)
XLA Modules:
  0.0 53.3 jit_solution(12908372726867710698)
XLA Ops:
  0.6 0.1 pad_add_fusion.1.refs_0_
  0.7 4.1 %images.3 = (bf16[128,768]{1,0:T(8,128)(2,1)S(1)}, bf16[3,96,128]{2,1,0:T(8,128)(2,1)S(1)}, bf16[3,96,128]{2,1,0:T(8,128)(2,1)S(1)}) custom-call(s32[2]{0:T(128)S(1)} %pad_add_fusion.1.refs_0_, s32[16,768]{1,0:T(8,128)} %bitcast.17, s32[768]{0:T(1024)} %refs_2_.5, f32[9,16,768]{2,1,0:T(8,128)} %bitcast.14, bf16[3,768,128]{2,1,0:T(8,128)(2,1)} %refs_4_.5), custom_call_target="tpu_custom_call" | custom-call | flops 3520000000 | bytes 320000 | tf_op jit(solution)/shard_map/images/pallas_call | solution.py:33
  4.8 3.0 %collective-permute-start.2 = (bf16[128,768]{1,0:T(8,128)(2,1)S(1)}, bf16[128,768]{1,0:T(8,128)(2,1)S(1)}, u32[]{:S(2)}, u32[]{:S(2)}) collective-permute-start(bf16[128,768]{1,0:T(8,128)(2,1)S(1)} %get-tuple-element.17.refs_5_.refs_0_), channel_id=1, source_target_pairs={{2,0},{0,2},{3,1},{1,3},{6,4},{4,6},{7,5},{5,7},{10,8},{8,10},{11,... | collective-permute-start | bytes 589832 | tf_op jit(solution)/shard_map/ppermute | solution.py:398
  7.8 1.6 %collective-permute-start = (bf16[3,96,128]{2,1,0:T(8,128)(2,1)S(1)}, bf16[3,96,128]{2,1,0:T(8,128)(2,1)S(1)}, u32[]{:S(2)}, u32[]{:S(2)}) collective-permute-start(bf16[3,96,128]{2,1,0:T(8,128)(2,1)S(1)} %get-tuple-element.15), channel_id=1, source_target_pairs={{0,4},{4,0},{8,12},{12,8},{1,5},{5,1},{9,13},{13,9},{2,6},{6,2},{1... | collective-permute-start | bytes 221192 | tf_op jit(solution)/shard_map/ppermute | solution.py:395
  9.4 2.5 %collective-permute-start.1 = (bf16[3,96,128]{2,1,0:T(8,128)(2,1)S(1)}, bf16[3,96,128]{2,1,0:T(8,128)(2,1)S(1)}, u32[]{:S(2)}, u32[]{:S(2)}) collective-permute-start(bf16[3,96,128]{2,1,0:T(8,128)(2,1)S(1)} %get-tuple-element.16), channel_id=1, source_target_pairs={{0,12},{4,8},{8,4},{12,0},{1,13},{5,9},{9,5},{13,1},{2,14},{6,10},... | collective-permute-start | bytes 221192 | tf_op jit(solution)/shard_map/ppermute | solution.py:395
  11.9 3.1 %images.4.refs_7_.refs_1_ = bf16[128,768]{1,0:T(8,128)(2,1)S(1)} custom-call(s32[2]{0:T(128)S(1)} %pad_add_fusion.1.refs_0_, s32[16,768]{1,0:T(8,128)S(1)} %bitcast.18, s32[768]{0:T(1024)S(1)} %copy-done.4, f32[9,16,768]{2,1,0:T(8,128)S(1)} %bitcast.15, bf16[3,768,128]{2,1,0:T(8,128)(2,1)S(1)} %copy-done.1, ...), custom_call_target="tpu_custom_call" | custom-call | flops 3520000000 | bytes 320000 | tf_op jit(solution)/shard_map/images/pallas_call | solution.py:33
  15.0 0.6 %collective-permute-start.7 = (bf16[128,768]{1,0:T(8,128)(2,1)S(1)}, bf16[128,768]{1,0:T(8,128)(2,1)S(1)}, u32[]{:S(2)}, u32[]{:S(2)}) collective-permute-start(bf16[128,768]{1,0:T(8,128)(2,1)S(1)} %images.4.refs_7_.refs_1_), channel_id=1, source_target_pairs={{2,0},{0,2},{3,1},{1,3},{6,4},{4,6},{7,5},{5,7},{10,8},{8,10},{11,... | collective-permute-start | bytes 589832 | tf_op jit(solution)/shard_map/ppermute | solution.py:398
  15.6 0.0 collective-permute-start.5
  15.6 0.0 collective-permute-done.refs_5_
  15.6 0.5 collective-permute-start.4
  16.1 0.0 collective-permute-done.1.refs_6_
  16.1 0.0 collective-permute-done.2.refs_8_.refs_6_.refs_0_
  16.1 3.1 %images.5.refs_2_ = bf16[128,768]{1,0:T(8,128)(2,1)S(1)} custom-call(s32[2]{0:T(128)S(1)} %pad_add_fusion.1.refs_0_, s32[16,768]{1,0:T(8,128)S(1)} %bitcast.19, s32[768]{0:T(1024)S(1)} %copy-done.4, f32[9,16,768]{2,1,0:T(8,128)S(1)} %bitcast.16, bf16[3,768,128]{2,1,0:T(8,128)(2,1)S(1)} %copy-done.1, bf16[3,96,128]{2,1,0:T(8,128)(2,1)S(1)} %collective-permute-done.refs_5_, ...), custom_call_target="tpu_custom_call" | custom-call | flops 3520000000 | bytes 320000 | tf_op jit(solution)/shard_map/images/pallas_call | solution.py:33
  19.2 0.1 collective-permute-start.6
  19.2 0.1 pad_add_fusion.2.place_ref
  19.3 1.5 %collective-permute-start.3 = (bf16[128,768]{1,0:T(8,128)(2,1)S(1)}, bf16[128,768]{1,0:T(8,128)(2,1)S(1)}, u32[]{:S(2)}, u32[]{:S(2)}) collective-permute-start(bf16[128,768]{1,0:T(8,128)(2,1)S(1)} %images.5.refs_2_), channel_id=1, source_target_pairs={{2,0},{0,2},{3,1},{1,3},{6,4},{4,6},{7,5},{5,7},{10,8},{8,10},{11,... | collective-permute-start | bytes 589832 | tf_op jit(solution)/shard_map/ppermute | solution.py:398
  20.8 0.0 collective-permute-done.7.refs_7_.refs_1_
  20.8 0.2 collective-permute-start.9
  21.0 0.0 collective-permute-done.5.refs_4_
  21.0 0.3 collective-permute-start.10
  21.4 0.0 collective-permute-done.4.refs_3_
  21.4 0.0 collective-permute-done.6.refs_5_
  21.4 3.7 %products.2 = (f32[128,640]{1,0:T(8,128)S(1)}, bf16[128,640]{1,0:T(8,128)(2,1)S(1)}) custom-call(s32[2]{0:T(128)S(1)} %pad_add_fusion.2.place_ref, bf16[3,768,640]{2,1,0:T(8,128)(2,1)} %partners_hbm.3, bf16[128,768]{1,0:T(8,128)(2,1)S(1)} %get-tuple-element.17.refs_5_.refs_0_, bf16[128,768]{1,0:T(8,128)(2,1)S(1)} %images.4.refs_7_.refs_1_, ...), custom_call_target="tpu_custom_call" | custom-call | flops 6600000000 | bytes 600000 | tf_op jit(solution)/shard_map/products/pallas_call | solution.py:33
  25.1 0.0 copy-start.7
  25.1 0.0 copy-start
  25.1 0.0 copy-start.5
  25.1 0.0 copy-start.6
  25.2 1.5 %collective-permute-done.3.refs_2_ = bf16[128,768]{1,0:T(8,128)(2,1)S(1)} collective-permute-done((bf16[128,768]{1,0:T(8,128)(2,1)S(1)}, bf16[128,768]{1,0:T(8,128)(2,1)S(1)}, u32[]{:S(2)}, u32[]{:S(2)}) %collective-permute-start.3) | collective-permute-done | bytes 196640 | tf_op jit(solution)/shard_map/ppermute | solution.py:398
  26.6 0.0 collective-permute-start.11
  26.6 0.7 %collective-permute-start.8 = (bf16[128,640]{1,0:T(8,128)(2,1)S(1)}, bf16[128,640]{1,0:T(8,128)(2,1)S(1)}, u32[]{:S(2)}, u32[]{:S(2)}) collective-permute-start(bf16[128,640]{1,0:T(8,128)(2,1)S(1)} %get-tuple-element.20), channel_id=1, source_target_pairs={{0,4},{4,0},{8,12},{12,8},{1,5},{5,1},{9,13},{13,9},{2,6},{6,2},{1... | collective-permute-start | bytes 491528 | tf_op jit(solution)/shard_map/ppermute | solution.py:420
  27.3 0.0 collective-permute-done.10.refs_4_
  27.3 0.0 collective-permute-done.9.refs_3_
  27.3 0.8 %collective-permute-done.11.refs_5_ = bf16[128,768]{1,0:T(8,128)(2,1)S(1)} collective-permute-done((bf16[128,768]{1,0:T(8,128)(2,1)S(1)}, bf16[128,768]{1,0:T(8,128)(2,1)S(1)}, u32[]{:S(2)}, u32[]{:S(2)}) %collective-permute-start.11) | collective-permute-done | bytes 196640 | tf_op jit(solution)/shard_map/ppermute | solution.py:401
  28.1 3.7 %products.3 = (f32[128,640]{1,0:T(8,128)S(1)}, bf16[64,640]{1,0:T(8,128)(2,1)S(1)}, bf16[64,640]{1,0:T(8,128)(2,1)S(1)}) custom-call(s32[2]{0:T(128)S(1)} %pad_add_fusion.2.place_ref, bf16[3,768,640]{2,1,0:T(8,128)(2,1)} %partners_hbm.3, bf16[128,768]{1,0:T(8,128)(2,1)S(1)} %collective-permute-done.2.refs_8_.refs_6_.refs_0_, ...), custom_call_target="tpu_custom_call" | custom-call | flops 110000000 | bytes 10000 | tf_op jit(solution)/shard_map/products/pallas_call | solution.py:33
  31.8 0.7 %collective-permute-start.12 = (bf16[64,640]{1,0:T(8,128)(2,1)S(1)}, bf16[64,640]{1,0:T(8,128)(2,1)S(1)}, u32[]{:S(2)}, u32[]{:S(2)}) collective-permute-start(bf16[64,640]{1,0:T(8,128)(2,1)S(1)} %get-tuple-element.23), channel_id=1, source_target_pairs={{0,4},{4,0},{8,12},{12,8},{1,5},{5,1},{9,13},{13,9},{2,6},{6,2},{1... | collective-permute-start | bytes 245768 | tf_op jit(solution)/shard_map/ppermute | solution.py:420
  32.5 1.4 %collective-permute-start.14 = (bf16[64,640]{1,0:T(8,128)(2,1)S(1)}, bf16[64,640]{1,0:T(8,128)(2,1)S(1)}, u32[]{:S(2)}, u32[]{:S(2)}) collective-permute-start(bf16[64,640]{1,0:T(8,128)(2,1)S(1)} %get-tuple-element.24), channel_id=1, source_target_pairs={{0,4},{4,0},{8,12},{12,8},{1,5},{5,1},{9,13},{13,9},{2,6},{6,2},{1... | collective-permute-start | bytes 245768 | tf_op jit(solution)/shard_map/ppermute | solution.py:420
  33.9 0.0 collective-permute-done.8.refs_1_
  33.9 3.3 %collective-permute-done.12.refs_5_ = bf16[64,640]{1,0:T(8,128)(2,1)S(1)} collective-permute-done((bf16[64,640]{1,0:T(8,128)(2,1)S(1)}, bf16[64,640]{1,0:T(8,128)(2,1)S(1)}, u32[]{:S(2)}, u32[]{:S(2)}) %collective-permute-start.12) | collective-permute-done | bytes 81952 | tf_op jit(solution)/shard_map/ppermute | solution.py:420
  37.2 1.1 %collective-permute-start.13 = (bf16[64,640]{1,0:T(8,128)(2,1)S(1)}, bf16[64,640]{1,0:T(8,128)(2,1)S(1)}, u32[]{:S(2)}, u32[]{:S(2)}) collective-permute-start(bf16[64,640]{1,0:T(8,128)(2,1)S(1)} %select_convert_fusion.1), channel_id=1, source_target_pairs={{0,8},{4,12},{8,0},{12,4},{1,9},{5,13},{9,1},{13,5},{2,10},{6,14},... | collective-permute-start | bytes 245768 | tf_op jit(solution)/shard_map/ppermute | solution.py:440
  38.3 0.0 collective-permute-done.14.refs_6_
  38.4 1.9 %collective-permute-start.15 = (bf16[64,640]{1,0:T(8,128)(2,1)S(1)}, bf16[64,640]{1,0:T(8,128)(2,1)S(1)}, u32[]{:S(2)}, u32[]{:S(2)}) collective-permute-start(bf16[64,640]{1,0:T(8,128)(2,1)S(1)} %select_convert_fusion), channel_id=1, source_target_pairs={{0,8},{4,12},{8,0},{12,4},{1,9},{5,13},{9,1},{13,5},{2,10},{6,14},... | collective-permute-start | bytes 245768 | tf_op jit(solution)/shard_map/ppermute | solution.py:440
  40.3 0.1 pad_add_fusion.flag_ref
  40.4 5.9 %collective-permute-done.15.refs_3_.refs_8_ = bf16[64,640]{1,0:T(8,128)(2,1)S(1)} collective-permute-done((bf16[64,640]{1,0:T(8,128)(2,1)S(1)}, bf16[64,640]{1,0:T(8,128)(2,1)S(1)}, u32[]{:S(2)}, u32[]{:S(2)}) %collective-permute-start.15) | collective-permute-done | bytes 81952 | tf_op jit(solution)/shard_map/ppermute | solution.py:440
  46.3 1.7 %finish.1 = (f32[128,640]{1,0:T(8,128)}, f32[1,128]{1,0:T(1,128)S(1)}) custom-call(s32[3]{0:T(128)S(1)} %pad_add_fusion.flag_ref, s32[4,128]{1,0:T(4,128)S(1)} %bitcast.20, s32[4,128]{1,0:T(4,128)S(1)} %bitcast.21, f32[4,128]{1,0:T(4,128)S(1)} %bitcast.13, f32[1,640]{1,0:T(1,128)S(1)} %broadcast_in_dim.3.partner_ref, ...), custom_call_target="tpu_custom_call" | custom-call | flops 2200000000 | bytes 200000 | tf_op jit(solution)/shard_map/finish/pallas_call | solution.py:33
  48.0 1.1 %collective-permute-done.16 = f32[1,128]{1,0:T(1,128)S(1)} collective-permute-done((f32[1,128]{1,0:T(1,128)S(1)}, f32[1,128]{1,0:T(1,128)S(1)}, u32[]{:S(2)}, u32[]{:S(2)}) %collective-permute-start.16) | collective-permute-done | bytes 544 | tf_op jit(solution)/shard_map/ppermute | solution.py:477
  49.1 1.5 %collective-permute-start.17 = (f32[1,128]{1,0:T(1,128)S(1)}, f32[1,128]{1,0:T(1,128)S(1)}, u32[]{:S(2)}, u32[]{:S(2)}) collective-permute-start(f32[1,128]{1,0:T(1,128)S(1)} %add.30), channel_id=1, source_target_pairs={{0,2},{2,0},{1,3},{3,1},{4,6},{6,4},{5,7},{7,5},{8,10},{10,8},{9,1... | collective-permute-start | bytes 1544 | tf_op jit(solution)/shard_map/ppermute | solution.py:480
  50.6 2.1 %collective-permute-done.17 = f32[1,128]{1,0:T(1,128)S(1)} collective-permute-done((f32[1,128]{1,0:T(1,128)S(1)}, f32[1,128]{1,0:T(1,128)S(1)}, u32[]{:S(2)}, u32[]{:S(2)}) %collective-permute-start.17) | collective-permute-done | bytes 544 | tf_op jit(solution)/shard_map/ppermute | solution.py:480
  52.7 0.6 %bitcast_divide_fusion = f32[128]{0:T(128)} fusion(f32[512]{0:T(512)S(1)} %copy-done, s32[]{:T(128)S(6)} %select_n.24, f32[1,128]{1,0:T(1,128)S(1)} %add.30, f32[1,128]{1,0:T(1,128)S(1)} %collective-permute-done.17), kind=kLoop, calls=%fused_computation.5 | loop fusion | flops 512 | bytes 2052 | tf_op jit(solution)/shard_map/div | solution.py:482
  (18 shorter events, 0.1 us)
Async XLA Ops:
  0.7 11.2 %copy-start.1 = (bf16[3,768,128]{2,1,0:T(8,128)(2,1)S(1)}, bf16[3,768,128]{2,1,0:T(8,128)(2,1)}, u32[]{:S(2)}) copy-start(bf16[3,768,128]{2,1,0:T(8,128)(2,1)} %refs_4_.5) | copy-start | bytes 1769476
  0.7 11.2 %copy-start.2 = (f32[9,768,16]{1,2,0:T(8,128)S(1)}, f32[9,768,16]{1,2,0:T(8,128)}, u32[]{:S(2)}) copy-start(f32[9,768,16]{1,2,0:T(8,128)} %param.11) | copy-start | bytes 1327108
  0.7 11.2 %copy-start.3 = (s32[768,16]{0,1:T(8,128)S(1)}, s32[768,16]{0,1:T(8,128)}, u32[]{:S(2)}) copy-start(s32[768,16]{0,1:T(8,128)} %param.12) | copy-start | bytes 147460
  0.7 11.2 %copy-start.4 = (s32[768]{0:T(1024)S(1)}, s32[768]{0:T(1024)}, u32[]{:S(2)}) copy-start(s32[768]{0:T(1024)} %refs_2_.5) | copy-start | bytes 9220
  4.8 11.3 %collective-permute-start.2 = (bf16[128,768]{1,0:T(8,128)(2,1)S(1)}, bf16[128,768]{1,0:T(8,128)(2,1)S(1)}, u32[]{:S(2)}, u32[]{:S(2)}) collective-permute-start(bf16[128,768]{1,0:T(8,128)(2,1)S(1)} %get-tuple-element.17.refs_5_.refs_0_), channel_id=1, source_target_pairs={{2,0},{0,2},{3,1},{1,3},{6,4},{4,6},{7,5},{5,7},{10,8},{8,10},{11,... | collective-permute-start | bytes 589832 | tf_op jit(solution)/shard_map/ppermute | solution.py:398
  7.8 7.7 %collective-permute-start = (bf16[3,96,128]{2,1,0:T(8,128)(2,1)S(1)}, bf16[3,96,128]{2,1,0:T(8,128)(2,1)S(1)}, u32[]{:S(2)}, u32[]{:S(2)}) collective-permute-start(bf16[3,96,128]{2,1,0:T(8,128)(2,1)S(1)} %get-tuple-element.15), channel_id=1, source_target_pairs={{0,4},{4,0},{8,12},{12,8},{1,5},{5,1},{9,13},{13,9},{2,6},{6,2},{1... | collective-permute-start | bytes 221192 | tf_op jit(solution)/shard_map/ppermute | solution.py:395
  9.4 6.7 %collective-permute-start.1 = (bf16[3,96,128]{2,1,0:T(8,128)(2,1)S(1)}, bf16[3,96,128]{2,1,0:T(8,128)(2,1)S(1)}, u32[]{:S(2)}, u32[]{:S(2)}) collective-permute-start(bf16[3,96,128]{2,1,0:T(8,128)(2,1)S(1)} %get-tuple-element.16), channel_id=1, source_target_pairs={{0,12},{4,8},{8,4},{12,0},{1,13},{5,9},{9,5},{13,1},{2,14},{6,10},... | collective-permute-start | bytes 221192 | tf_op jit(solution)/shard_map/ppermute | solution.py:395
  15.0 5.9 %collective-permute-start.7 = (bf16[128,768]{1,0:T(8,128)(2,1)S(1)}, bf16[128,768]{1,0:T(8,128)(2,1)S(1)}, u32[]{:S(2)}, u32[]{:S(2)}) collective-permute-start(bf16[128,768]{1,0:T(8,128)(2,1)S(1)} %images.4.refs_7_.refs_1_), channel_id=1, source_target_pairs={{2,0},{0,2},{3,1},{1,3},{6,4},{4,6},{7,5},{5,7},{10,8},{8,10},{11,... | collective-permute-start | bytes 589832 | tf_op jit(solution)/shard_map/ppermute | solution.py:398
  15.6 5.5 %collective-permute-start.5 = (bf16[128,768]{1,0:T(8,128)(2,1)S(1)}, bf16[128,768]{1,0:T(8,128)(2,1)S(1)}, u32[]{:S(2)}, u32[]{:S(2)}) collective-permute-start(bf16[128,768]{1,0:T(8,128)(2,1)S(1)} %images.4.refs_7_.refs_1_), channel_id=1, source_target_pairs={{0,1},{1,0},{2,3},{3,2},{4,5},{5,4},{6,7},{7,6},{8,9},{9,8},{10,11... | collective-permute-start | bytes 589832 | tf_op jit(solution)/shard_map/ppermute | solution.py:401
  15.6 5.8 %collective-permute-start.4 = (bf16[128,768]{1,0:T(8,128)(2,1)S(1)}, bf16[128,768]{1,0:T(8,128)(2,1)S(1)}, u32[]{:S(2)}, u32[]{:S(2)}) collective-permute-start(bf16[128,768]{1,0:T(8,128)(2,1)S(1)} %get-tuple-element.17.refs_5_.refs_0_), channel_id=1, source_target_pairs={{0,1},{1,0},{2,3},{3,2},{4,5},{5,4},{6,7},{7,6},{8,9},{9,8},{10,11... | collective-permute-start | bytes 589832 | tf_op jit(solution)/shard_map/ppermute | solution.py:401
  19.2 2.2 %collective-permute-start.6 = (bf16[128,768]{1,0:T(8,128)(2,1)S(1)}, bf16[128,768]{1,0:T(8,128)(2,1)S(1)}, u32[]{:S(2)}, u32[]{:S(2)}) collective-permute-start(bf16[128,768]{1,0:T(8,128)(2,1)S(1)} %images.5.refs_2_), channel_id=1, source_target_pairs={{0,1},{1,0},{2,3},{3,2},{4,5},{5,4},{6,7},{7,6},{8,9},{9,8},{10,11... | collective-permute-start | bytes 589832 | tf_op jit(solution)/shard_map/ppermute | solution.py:401
  19.3 7.3 %collective-permute-start.3 = (bf16[128,768]{1,0:T(8,128)(2,1)S(1)}, bf16[128,768]{1,0:T(8,128)(2,1)S(1)}, u32[]{:S(2)}, u32[]{:S(2)}) collective-permute-start(bf16[128,768]{1,0:T(8,128)(2,1)S(1)} %images.5.refs_2_), channel_id=1, source_target_pairs={{2,0},{0,2},{3,1},{1,3},{6,4},{4,6},{7,5},{5,7},{10,8},{8,10},{11,... | collective-permute-start | bytes 589832 | tf_op jit(solution)/shard_map/ppermute | solution.py:398
  20.8 6.5 %collective-permute-start.9 = (bf16[128,768]{1,0:T(8,128)(2,1)S(1)}, bf16[128,768]{1,0:T(8,128)(2,1)S(1)}, u32[]{:S(2)}, u32[]{:S(2)}) collective-permute-start(bf16[128,768]{1,0:T(8,128)(2,1)S(1)} %collective-permute-done.2.refs_8_.refs_6_.refs_0_), channel_id=1, source_target_pairs={{0,1},{1,0},{2,3},{3,2},{4,5},{5,4},{6,7},{7,6},{8,9},{9,8},{10,11... | collective-permute-start | bytes 589832 | tf_op jit(solution)/shard_map/ppermute | solution.py:401
  21.0 6.3 %collective-permute-start.10 = (bf16[128,768]{1,0:T(8,128)(2,1)S(1)}, bf16[128,768]{1,0:T(8,128)(2,1)S(1)}, u32[]{:S(2)}, u32[]{:S(2)}) collective-permute-start(bf16[128,768]{1,0:T(8,128)(2,1)S(1)} %collective-permute-done.7.refs_7_.refs_1_), channel_id=1, source_target_pairs={{0,1},{1,0},{2,3},{3,2},{4,5},{5,4},{6,7},{7,6},{8,9},{9,8},{10,11... | collective-permute-start | bytes 589832 | tf_op jit(solution)/shard_map/ppermute | solution.py:401
  25.1 7.4 %copy-start.7 = (f32[640]{0:T(1024)S(1)}, f32[640]{0:T(1024)}, u32[]{:S(2)}) copy-start(f32[640]{0:T(1024)} %param.15) | copy-start | bytes 7684
  25.1 21.2 %copy-start = (f32[512]{0:T(512)S(1)}, f32[512]{0:T(512)}, u32[]{:S(2)}) copy-start(f32[512]{0:T(512)} %param.14) | copy-start | bytes 6148
  25.1 21.2 %copy-start.5 = (s32[512]{0:T(512)S(1)}, s32[512]{0:T(512)}, u32[]{:S(2)}) copy-start(s32[512]{0:T(512)} %param.16) | copy-start | bytes 6148
  25.1 21.2 %copy-start.6 = (s32[512]{0:T(512)S(1)}, s32[512]{0:T(512)}, u32[]{:S(2)}) copy-start(s32[512]{0:T(512)} %param.17) | copy-start | bytes 6148
  26.6 1.4 %collective-permute-start.11 = (bf16[128,768]{1,0:T(8,128)(2,1)S(1)}, bf16[128,768]{1,0:T(8,128)(2,1)S(1)}, u32[]{:S(2)}, u32[]{:S(2)}) collective-permute-start(bf16[128,768]{1,0:T(8,128)(2,1)S(1)} %collective-permute-done.3.refs_2_), channel_id=1, source_target_pairs={{0,1},{1,0},{2,3},{3,2},{4,5},{5,4},{6,7},{7,6},{8,9},{9,8},{10,11... | collective-permute-start | bytes 589832 | tf_op jit(solution)/shard_map/ppermute | solution.py:401
  26.6 7.3 %collective-permute-start.8 = (bf16[128,640]{1,0:T(8,128)(2,1)S(1)}, bf16[128,640]{1,0:T(8,128)(2,1)S(1)}, u32[]{:S(2)}, u32[]{:S(2)}) collective-permute-start(bf16[128,640]{1,0:T(8,128)(2,1)S(1)} %get-tuple-element.20), channel_id=1, source_target_pairs={{0,4},{4,0},{8,12},{12,8},{1,5},{5,1},{9,13},{13,9},{2,6},{6,2},{1... | collective-permute-start | bytes 491528 | tf_op jit(solution)/shard_map/ppermute | solution.py:420
  31.8 5.4 %collective-permute-start.12 = (bf16[64,640]{1,0:T(8,128)(2,1)S(1)}, bf16[64,640]{1,0:T(8,128)(2,1)S(1)}, u32[]{:S(2)}, u32[]{:S(2)}) collective-permute-start(bf16[64,640]{1,0:T(8,128)(2,1)S(1)} %get-tuple-element.23), channel_id=1, source_target_pairs={{0,4},{4,0},{8,12},{12,8},{1,5},{5,1},{9,13},{13,9},{2,6},{6,2},{1... | collective-permute-start | bytes 245768 | tf_op jit(solution)/shard_map/ppermute | solution.py:420
  32.5 5.8 %collective-permute-start.14 = (bf16[64,640]{1,0:T(8,128)(2,1)S(1)}, bf16[64,640]{1,0:T(8,128)(2,1)S(1)}, u32[]{:S(2)}, u32[]{:S(2)}) collective-permute-start(bf16[64,640]{1,0:T(8,128)(2,1)S(1)} %get-tuple-element.24), channel_id=1, source_target_pairs={{0,4},{4,0},{8,12},{12,8},{1,5},{5,1},{9,13},{13,9},{2,6},{6,2},{1... | collective-permute-start | bytes 245768 | tf_op jit(solution)/shard_map/ppermute | solution.py:420
  37.2 9.1 %collective-permute-start.13 = (bf16[64,640]{1,0:T(8,128)(2,1)S(1)}, bf16[64,640]{1,0:T(8,128)(2,1)S(1)}, u32[]{:S(2)}, u32[]{:S(2)}) collective-permute-start(bf16[64,640]{1,0:T(8,128)(2,1)S(1)} %select_convert_fusion.1), channel_id=1, source_target_pairs={{0,8},{4,12},{8,0},{12,4},{1,9},{5,13},{9,1},{13,5},{2,10},{6,14},... | collective-permute-start | bytes 245768 | tf_op jit(solution)/shard_map/ppermute | solution.py:440
  38.4 7.9 %collective-permute-start.15 = (bf16[64,640]{1,0:T(8,128)(2,1)S(1)}, bf16[64,640]{1,0:T(8,128)(2,1)S(1)}, u32[]{:S(2)}, u32[]{:S(2)}) collective-permute-start(bf16[64,640]{1,0:T(8,128)(2,1)S(1)} %select_convert_fusion), channel_id=1, source_target_pairs={{0,8},{4,12},{8,0},{12,4},{1,9},{5,13},{9,1},{13,5},{2,10},{6,14},... | collective-permute-start | bytes 245768 | tf_op jit(solution)/shard_map/ppermute | solution.py:440
  48.0 1.1 %collective-permute-start.16 = (f32[1,128]{1,0:T(1,128)S(1)}, f32[1,128]{1,0:T(1,128)S(1)}, u32[]{:S(2)}, u32[]{:S(2)}) collective-permute-start(f32[1,128]{1,0:T(1,128)S(1)} %get-tuple-element.27), channel_id=1, source_target_pairs={{0,1},{1,0},{2,3},{3,2},{4,5},{5,4},{6,7},{7,6},{8,9},{9,8},{10,11... | collective-permute-start | bytes 1544 | tf_op jit(solution)/shard_map/ppermute | solution.py:477
  49.1 3.5 %collective-permute-start.17 = (f32[1,128]{1,0:T(1,128)S(1)}, f32[1,128]{1,0:T(1,128)S(1)}, u32[]{:S(2)}, u32[]{:S(2)}) collective-permute-start(f32[1,128]{1,0:T(1,128)S(1)} %add.30), channel_id=1, source_target_pairs={{0,2},{2,0},{1,3},{3,1},{4,6},{6,4},{5,7},{7,5},{8,10},{10,8},{9,1... | collective-permute-start | bytes 1544 | tf_op jit(solution)/shard_map/ppermute | solution.py:480

commit v16 on v12

--- a/solution.py
+++ b/solution.py
@@ -401,7 +401,8 @@
     mine = [near, middle_images, images_of(chunks[2], *shared, halos=halos, before=before)[0]]
     for shift, far in far_all.items():
         far += [from_group(cells, shift) for cells in mine[1:]]
-    theirs = [from_sibling(cells) for cells in mine]
+    late_near, late_middle, late_edge = lax.optimization_barrier(tuple(mine))
+    theirs = [from_sibling(cells) for cells in (late_near, late_middle, late_edge)]
     half = half_index.astype(jnp.int32)
     goal = atom_index * groups // atom_count
 

time: 53.1 us -> 53.2 us (level)
  no operation moved by 1% of the time
where the time goes in v16:
time: 53.2 us; the launch traced here: 53 us
  Pallas kernels  18.7 us (35%)
  starting transfers between devices  17.6 us (33%)
  waiting for transfers between devices  14.9 us (28%)
  other arithmetic  0.89 us (2%)
  between operations  0.77 us (1%)
    pallas_call x6, Pallas kernels, call(): pl.pallas_call(kernel, in_specs=in_specs, out_specs=out_specs, out_shape=...  18.7 us
    ppermute x2, waiting for transfers between devices, body(): lax.ppermute(sent, 'atoms', [(z, z ^ 2) for z in range(atom_count)])  5.92 us
    ppermute x3, starting transfers between devices, from_group(): return lax.ppermute(cells, 'modes', [(m ^ shift, m) for m in range(groups)])  5.09 us
    ppermute x3, waiting for transfers between devices, next_door(): return (keep, [lax.ppermute(send, 'atoms', pairs) for send in sends])  3.26 us
    ppermute x2, starting transfers between devices, body(): lax.ppermute(sent, 'atoms', [(z, z ^ 2) for z in range(atom_count)])  3.06 us
    ppermute x3, starting transfers between devices, next_door(): return (keep, [lax.ppermute(send, 'atoms', pairs) for send in sends])  2.76 us
    ppermute x1, starting transfers between devices, body(): lax.ppermute(edge_two, 'atoms', others)  2.48 us
    ppermute x1, waiting for transfers between devices, body(): lax.ppermute(numerator, 'modes', [(m, m ^ step) for m in range(groups)])  2.06 us
  transfers between devices with their start and end apart: 18, of which 6 were waited for; matrix products, arithmetic and copies ran while one was open for 0% of the time, Pallas kernels for 24%

profile of v16, /device:TPU:0, one launch (start us, length us, event | category | flops | bytes accessed | tf_op | source)
XLA Modules:
  0.0 53.0 jit_solution(15558724481172508369)
XLA Ops:
  0.6 0.1 pad_add_fusion.1.refs_0_
  0.7 4.1 %images.3 = (bf16[128,768]{1,0:T(8,128)(2,1)S(1)}, bf16[3,96,128]{2,1,0:T(8,128)(2,1)S(1)}, bf16[3,96,128]{2,1,0:T(8,128)(2,1)S(1)}) custom-call(s32[2]{0:T(128)S(1)} %pad_add_fusion.1.refs_0_, s32[16,768]{1,0:T(8,128)} %bitcast.17, s32[768]{0:T(1024)} %refs_2_.5, f32[9,16,768]{2,1,0:T(8,128)} %bitcast.14, bf16[3,768,128]{2,1,0:T(8,128)(2,1)} %refs_4_.5), custom_call_target="tpu_custom_call" | custom-call | flops 3520000000 | bytes 320000 | tf_op jit(solution)/shard_map/images/pallas_call | solution.py:33
  4.8 3.0 %collective-permute-start.2 = (bf16[128,768]{1,0:T(8,128)(2,1)S(1)}, bf16[128,768]{1,0:T(8,128)(2,1)S(1)}, u32[]{:S(2)}, u32[]{:S(2)}) collective-permute-start(bf16[128,768]{1,0:T(8,128)(2,1)S(1)} %get-tuple-element.21.refs_5_.refs_0_), channel_id=1, source_target_pairs={{2,0},{0,2},{3,1},{1,3},{6,4},{4,6},{7,5},{5,7},{10,8},{8,10},{11,... | collective-permute-start | bytes 589832 | tf_op jit(solution)/shard_map/ppermute | solution.py:393
  7.8 1.6 %collective-permute-start = (bf16[3,96,128]{2,1,0:T(8,128)(2,1)S(1)}, bf16[3,96,128]{2,1,0:T(8,128)(2,1)S(1)}, u32[]{:S(2)}, u32[]{:S(2)}) collective-permute-start(bf16[3,96,128]{2,1,0:T(8,128)(2,1)S(1)} %get-tuple-element.18), channel_id=1, source_target_pairs={{0,4},{4,0},{8,12},{12,8},{1,5},{5,1},{9,13},{13,9},{2,6},{6,2},{1... | collective-permute-start | bytes 221192 | tf_op jit(solution)/shard_map/ppermute | solution.py:390
  9.4 2.5 %collective-permute-start.1 = (bf16[3,96,128]{2,1,0:T(8,128)(2,1)S(1)}, bf16[3,96,128]{2,1,0:T(8,128)(2,1)S(1)}, u32[]{:S(2)}, u32[]{:S(2)}) collective-permute-start(bf16[3,96,128]{2,1,0:T(8,128)(2,1)S(1)} %get-tuple-element.19), channel_id=1, source_target_pairs={{0,12},{4,8},{8,4},{12,0},{1,13},{5,9},{9,5},{13,1},{2,14},{6,10},... | collective-permute-start | bytes 221192 | tf_op jit(solution)/shard_map/ppermute | solution.py:390
  11.9 3.1 %images.4.refs_7_.refs_1_ = bf16[128,768]{1,0:T(8,128)(2,1)S(1)} custom-call(s32[2]{0:T(128)S(1)} %pad_add_fusion.1.refs_0_, s32[16,768]{1,0:T(8,128)S(1)} %bitcast.18, s32[768]{0:T(1024)S(1)} %copy-done.4, f32[9,16,768]{2,1,0:T(8,128)S(1)} %bitcast.15, bf16[3,768,128]{2,1,0:T(8,128)(2,1)S(1)} %copy-done.1, ...), custom_call_target="tpu_custom_call" | custom-call | flops 3520000000 | bytes 320000 | tf_op jit(solution)/shard_map/images/pallas_call | solution.py:33
  15.0 0.6 %collective-permute-start.7 = (bf16[128,768]{1,0:T(8,128)(2,1)S(1)}, bf16[128,768]{1,0:T(8,128)(2,1)S(1)}, u32[]{:S(2)}, u32[]{:S(2)}) collective-permute-start(bf16[128,768]{1,0:T(8,128)(2,1)S(1)} %images.4.refs_7_.refs_1_), channel_id=1, source_target_pairs={{2,0},{0,2},{3,1},{1,3},{6,4},{4,6},{7,5},{5,7},{10,8},{8,10},{11,... | collective-permute-start | bytes 589832 | tf_op jit(solution)/shard_map/ppermute | solution.py:393
  15.6 0.0 collective-permute-done.refs_5_
  15.6 0.0 collective-permute-done.1.refs_6_
  15.6 0.0 collective-permute-done.2.refs_8_.refs_6_.refs_0_
  15.6 3.1 %images.5.refs_2_ = bf16[128,768]{1,0:T(8,128)(2,1)S(1)} custom-call(s32[2]{0:T(128)S(1)} %pad_add_fusion.1.refs_0_, s32[16,768]{1,0:T(8,128)S(1)} %bitcast.19, s32[768]{0:T(1024)S(1)} %copy-done.4, f32[9,16,768]{2,1,0:T(8,128)S(1)} %bitcast.16, bf16[3,768,128]{2,1,0:T(8,128)(2,1)S(1)} %copy-done.1, bf16[3,96,128]{2,1,0:T(8,128)(2,1)S(1)} %collective-permute-done.refs_5_, ...), custom_call_target="tpu_custom_call" | custom-call | flops 3520000000 | bytes 320000 | tf_op jit(solution)/shard_map/images/pallas_call | solution.py:33
  18.6 0.1 collective-permute-start.4
  18.7 0.5 collective-permute-start.5
  19.2 0.1 collective-permute-start.6
  19.3 0.1 pad_add_fusion.2.place_ref
  19.4 1.5 %collective-permute-start.3 = (bf16[128,768]{1,0:T(8,128)(2,1)S(1)}, bf16[128,768]{1,0:T(8,128)(2,1)S(1)}, u32[]{:S(2)}, u32[]{:S(2)}) collective-permute-start(bf16[128,768]{1,0:T(8,128)(2,1)S(1)} %images.5.refs_2_), channel_id=1, source_target_pairs={{2,0},{0,2},{3,1},{1,3},{6,4},{4,6},{7,5},{5,7},{10,8},{8,10},{11,... | collective-permute-start | bytes 589832 | tf_op jit(solution)/shard_map/ppermute | solution.py:393
  20.9 0.0 collective-permute-done.7.refs_7_.refs_1_
  20.9 0.2 collective-permute-start.9
  21.0 0.0 collective-permute-done.4.refs_3_
  21.0 0.3 collective-permute-start.10
  21.4 0.0 collective-permute-done.5.refs_4_
  21.4 3.4 %products.2 = (f32[128,640]{1,0:T(8,128)S(1)}, bf16[128,640]{1,0:T(8,128)(2,1)S(1)}) custom-call(s32[2]{0:T(128)S(1)} %pad_add_fusion.2.place_ref, bf16[3,768,640]{2,1,0:T(8,128)(2,1)} %partners_hbm.3, bf16[128,768]{1,0:T(8,128)(2,1)S(1)} %get-tuple-element.21.refs_5_.refs_0_, bf16[128,768]{1,0:T(8,128)(2,1)S(1)} %images.4.refs_7_.refs_1_, ...), custom_call_target="tpu_custom_call" | custom-call | flops 6600000000 | bytes 600000 | tf_op jit(solution)/shard_map/products/pallas_call | solution.py:33
  24.8 0.0 copy-start.7
  24.8 0.0 copy-start
  24.8 0.0 copy-start.5
  24.8 0.0 copy-start.6
  24.8 1.8 %collective-permute-done.3.refs_2_ = bf16[128,768]{1,0:T(8,128)(2,1)S(1)} collective-permute-done((bf16[128,768]{1,0:T(8,128)(2,1)S(1)}, bf16[128,768]{1,0:T(8,128)(2,1)S(1)}, u32[]{:S(2)}, u32[]{:S(2)}) %collective-permute-start.3) | collective-permute-done | bytes 196640 | tf_op jit(solution)/shard_map/ppermute | solution.py:393
  26.6 0.0 collective-permute-start.11
  26.6 0.7 %collective-permute-start.8 = (bf16[128,640]{1,0:T(8,128)(2,1)S(1)}, bf16[128,640]{1,0:T(8,128)(2,1)S(1)}, u32[]{:S(2)}, u32[]{:S(2)}) collective-permute-start(bf16[128,640]{1,0:T(8,128)(2,1)S(1)} %get-tuple-element.26), channel_id=1, source_target_pairs={{0,4},{4,0},{8,12},{12,8},{1,5},{5,1},{9,13},{13,9},{2,6},{6,2},{1... | collective-permute-start | bytes 491528 | tf_op jit(solution)/shard_map/ppermute | solution.py:416
  27.3 0.0 collective-permute-done.10.refs_4_
  27.3 0.0 collective-permute-done.9.refs_3_
  27.3 0.8 %collective-permute-done.11.refs_5_ = bf16[128,768]{1,0:T(8,128)(2,1)S(1)} collective-permute-done((bf16[128,768]{1,0:T(8,128)(2,1)S(1)}, bf16[128,768]{1,0:T(8,128)(2,1)S(1)}, u32[]{:S(2)}, u32[]{:S(2)}) %collective-permute-start.11) | collective-permute-done | bytes 196640 | tf_op jit(solution)/shard_map/ppermute | solution.py:396
  28.1 3.4 %products.3 = (f32[128,640]{1,0:T(8,128)S(1)}, bf16[64,640]{1,0:T(8,128)(2,1)S(1)}, bf16[64,640]{1,0:T(8,128)(2,1)S(1)}) custom-call(s32[2]{0:T(128)S(1)} %pad_add_fusion.2.place_ref, bf16[3,768,640]{2,1,0:T(8,128)(2,1)} %partners_hbm.3, bf16[128,768]{1,0:T(8,128)(2,1)S(1)} %collective-permute-done.2.refs_8_.refs_6_.refs_0_, ...), custom_call_target="tpu_custom_call" | custom-call | flops 110000000 | bytes 10000 | tf_op jit(solution)/shard_map/products/pallas_call | solution.py:33
  31.5 0.7 %collective-permute-start.12 = (bf16[64,640]{1,0:T(8,128)(2,1)S(1)}, bf16[64,640]{1,0:T(8,128)(2,1)S(1)}, u32[]{:S(2)}, u32[]{:S(2)}) collective-permute-start(bf16[64,640]{1,0:T(8,128)(2,1)S(1)} %get-tuple-element.29), channel_id=1, source_target_pairs={{0,4},{4,0},{8,12},{12,8},{1,5},{5,1},{9,13},{13,9},{2,6},{6,2},{1... | collective-permute-start | bytes 245768 | tf_op jit(solution)/shard_map/ppermute | solution.py:416
  32.2 1.4 %collective-permute-start.14 = (bf16[64,640]{1,0:T(8,128)(2,1)S(1)}, bf16[64,640]{1,0:T(8,128)(2,1)S(1)}, u32[]{:S(2)}, u32[]{:S(2)}) collective-permute-start(bf16[64,640]{1,0:T(8,128)(2,1)S(1)} %get-tuple-element.30), channel_id=1, source_target_pairs={{0,4},{4,0},{8,12},{12,8},{1,5},{5,1},{9,13},{13,9},{2,6},{6,2},{1... | collective-permute-start | bytes 245768 | tf_op jit(solution)/shard_map/ppermute | solution.py:416
  33.6 3.3 %collective-permute-done.12.refs_5_ = bf16[64,640]{1,0:T(8,128)(2,1)S(1)} collective-permute-done((bf16[64,640]{1,0:T(8,128)(2,1)S(1)}, bf16[64,640]{1,0:T(8,128)(2,1)S(1)}, u32[]{:S(2)}, u32[]{:S(2)}) %collective-permute-start.12) | collective-permute-done | bytes 81952 | tf_op jit(solution)/shard_map/ppermute | solution.py:416
  36.9 1.6 %collective-permute-start.13 = (bf16[64,640]{1,0:T(8,128)(2,1)S(1)}, bf16[64,640]{1,0:T(8,128)(2,1)S(1)}, u32[]{:S(2)}, u32[]{:S(2)}) collective-permute-start(bf16[64,640]{1,0:T(8,128)(2,1)S(1)} %select_convert_fusion.1), channel_id=1, source_target_pairs={{0,8},{4,12},{8,0},{12,4},{1,9},{5,13},{9,1},{13,5},{2,10},{6,14},... | collective-permute-start | bytes 245768 | tf_op jit(solution)/shard_map/ppermute | solution.py:436
  38.5 0.0 collective-permute-done.14.refs_6_
  38.6 1.4 %collective-permute-start.15 = (bf16[64,640]{1,0:T(8,128)(2,1)S(1)}, bf16[64,640]{1,0:T(8,128)(2,1)S(1)}, u32[]{:S(2)}, u32[]{:S(2)}) collective-permute-start(bf16[64,640]{1,0:T(8,128)(2,1)S(1)} %select_convert_fusion), channel_id=1, source_target_pairs={{0,8},{4,12},{8,0},{12,4},{1,9},{5,13},{9,1},{13,5},{2,10},{6,14},... | collective-permute-start | bytes 245768 | tf_op jit(solution)/shard_map/ppermute | solution.py:436
  40.0 0.1 pad_add_fusion.flag_ref
  40.1 5.9 %collective-permute-done.15.refs_3_.refs_8_ = bf16[64,640]{1,0:T(8,128)(2,1)S(1)} collective-permute-done((bf16[64,640]{1,0:T(8,128)(2,1)S(1)}, bf16[64,640]{1,0:T(8,128)(2,1)S(1)}, u32[]{:S(2)}, u32[]{:S(2)}) %collective-permute-start.15) | collective-permute-done | bytes 81952 | tf_op jit(solution)/shard_map/ppermute | solution.py:436
  46.0 0.0 collective-permute-done.13.refs_2_.refs_7_
  46.0 1.7 %finish.1 = (f32[128,640]{1,0:T(8,128)}, f32[1,128]{1,0:T(1,128)S(1)}) custom-call(s32[3]{0:T(128)S(1)} %pad_add_fusion.flag_ref, s32[4,128]{1,0:T(4,128)S(1)} %bitcast.20, s32[4,128]{1,0:T(4,128)S(1)} %bitcast.21, f32[4,128]{1,0:T(4,128)S(1)} %bitcast.13, f32[1,640]{1,0:T(1,128)S(1)} %broadcast_in_dim.3.partner_ref, ...), custom_call_target="tpu_custom_call" | custom-call | flops 2200000000 | bytes 200000 | tf_op jit(solution)/shard_map/finish/pallas_call | solution.py:33
  47.7 0.0 collective-permute-start.16
  47.7 1.1 %collective-permute-done.16 = f32[1,128]{1,0:T(1,128)S(1)} collective-permute-done((f32[1,128]{1,0:T(1,128)S(1)}, f32[1,128]{1,0:T(1,128)S(1)}, u32[]{:S(2)}, u32[]{:S(2)}) %collective-permute-start.16) | collective-permute-done | bytes 544 | tf_op jit(solution)/shard_map/ppermute | solution.py:473
  48.8 1.5 %collective-permute-start.17 = (f32[1,128]{1,0:T(1,128)S(1)}, f32[1,128]{1,0:T(1,128)S(1)}, u32[]{:S(2)}, u32[]{:S(2)}) collective-permute-start(f32[1,128]{1,0:T(1,128)S(1)} %add.30), channel_id=1, source_target_pairs={{0,2},{2,0},{1,3},{3,1},{4,6},{6,4},{5,7},{7,5},{8,10},{10,8},{9,1... | collective-permute-start | bytes 1544 | tf_op jit(solution)/shard_map/ppermute | solution.py:476
  50.3 2.1 %collective-permute-done.17 = f32[1,128]{1,0:T(1,128)S(1)} collective-permute-done((f32[1,128]{1,0:T(1,128)S(1)}, f32[1,128]{1,0:T(1,128)S(1)}, u32[]{:S(2)}, u32[]{:S(2)}) %collective-permute-start.17) | collective-permute-done | bytes 544 | tf_op jit(solution)/shard_map/ppermute | solution.py:476
  52.4 0.6 %bitcast_divide_fusion = f32[128]{0:T(128)} fusion(f32[512]{0:T(512)S(1)} %copy-done, s32[]{:T(128)S(6)} %select_n.24, f32[1,128]{1,0:T(1,128)S(1)} %add.30, f32[1,128]{1,0:T(1,128)S(1)} %collective-permute-done.17), kind=kLoop, calls=%fused_computation.5 | loop fusion | flops 512 | bytes 2052 | tf_op jit(solution)/shard_map/div | solution.py:478
  (18 shorter events, 0.1 us)
Async XLA Ops:
  0.7 11.2 %copy-start.1 = (bf16[3,768,128]{2,1,0:T(8,128)(2,1)S(1)}, bf16[3,768,128]{2,1,0:T(8,128)(2,1)}, u32[]{:S(2)}) copy-start(bf16[3,768,128]{2,1,0:T(8,128)(2,1)} %refs_4_.5) | copy-start | bytes 1769476
  0.7 11.2 %copy-start.2 = (f32[9,768,16]{1,2,0:T(8,128)S(1)}, f32[9,768,16]{1,2,0:T(8,128)}, u32[]{:S(2)}) copy-start(f32[9,768,16]{1,2,0:T(8,128)} %param.11) | copy-start | bytes 1327108
  0.7 11.2 %copy-start.3 = (s32[768,16]{0,1:T(8,128)S(1)}, s32[768,16]{0,1:T(8,128)}, u32[]{:S(2)}) copy-start(s32[768,16]{0,1:T(8,128)} %param.12) | copy-start | bytes 147460
  0.7 11.2 %copy-start.4 = (s32[768]{0:T(1024)S(1)}, s32[768]{0:T(1024)}, u32[]{:S(2)}) copy-start(s32[768]{0:T(1024)} %refs_2_.5) | copy-start | bytes 9220
  4.8 10.7 %collective-permute-start.2 = (bf16[128,768]{1,0:T(8,128)(2,1)S(1)}, bf16[128,768]{1,0:T(8,128)(2,1)S(1)}, u32[]{:S(2)}, u32[]{:S(2)}) collective-permute-start(bf16[128,768]{1,0:T(8,128)(2,1)S(1)} %get-tuple-element.21.refs_5_.refs_0_), channel_id=1, source_target_pairs={{2,0},{0,2},{3,1},{1,3},{6,4},{4,6},{7,5},{5,7},{10,8},{8,10},{11,... | collective-permute-start | bytes 589832 | tf_op jit(solution)/shard_map/ppermute | solution.py:393
  7.8 7.7 %collective-permute-start = (bf16[3,96,128]{2,1,0:T(8,128)(2,1)S(1)}, bf16[3,96,128]{2,1,0:T(8,128)(2,1)S(1)}, u32[]{:S(2)}, u32[]{:S(2)}) collective-permute-start(bf16[3,96,128]{2,1,0:T(8,128)(2,1)S(1)} %get-tuple-element.18), channel_id=1, source_target_pairs={{0,4},{4,0},{8,12},{12,8},{1,5},{5,1},{9,13},{13,9},{2,6},{6,2},{1... | collective-permute-start | bytes 221192 | tf_op jit(solution)/shard_map/ppermute | solution.py:390
  9.4 6.2 %collective-permute-start.1 = (bf16[3,96,128]{2,1,0:T(8,128)(2,1)S(1)}, bf16[3,96,128]{2,1,0:T(8,128)(2,1)S(1)}, u32[]{:S(2)}, u32[]{:S(2)}) collective-permute-start(bf16[3,96,128]{2,1,0:T(8,128)(2,1)S(1)} %get-tuple-element.19), channel_id=1, source_target_pairs={{0,12},{4,8},{8,4},{12,0},{1,13},{5,9},{9,5},{13,1},{2,14},{6,10},... | collective-permute-start | bytes 221192 | tf_op jit(solution)/shard_map/ppermute | solution.py:390
  15.0 5.9 %collective-permute-start.7 = (bf16[128,768]{1,0:T(8,128)(2,1)S(1)}, bf16[128,768]{1,0:T(8,128)(2,1)S(1)}, u32[]{:S(2)}, u32[]{:S(2)}) collective-permute-start(bf16[128,768]{1,0:T(8,128)(2,1)S(1)} %images.4.refs_7_.refs_1_), channel_id=1, source_target_pairs={{2,0},{0,2},{3,1},{1,3},{6,4},{4,6},{7,5},{5,7},{10,8},{8,10},{11,... | collective-permute-start | bytes 589832 | tf_op jit(solution)/shard_map/ppermute | solution.py:393
  18.6 2.4 %collective-permute-start.4 = (bf16[128,768]{1,0:T(8,128)(2,1)S(1)}, bf16[128,768]{1,0:T(8,128)(2,1)S(1)}, u32[]{:S(2)}, u32[]{:S(2)}) collective-permute-start(bf16[128,768]{1,0:T(8,128)(2,1)S(1)} %get-tuple-element.21.refs_5_.refs_0_), channel_id=1, source_target_pairs={{0,1},{1,0},{2,3},{3,2},{4,5},{5,4},{6,7},{7,6},{8,9},{9,8},{10,11... | collective-permute-start | bytes 589832 | tf_op jit(solution)/shard_map/ppermute | solution.py:396
  18.7 2.7 %collective-permute-start.5 = (bf16[128,768]{1,0:T(8,128)(2,1)S(1)}, bf16[128,768]{1,0:T(8,128)(2,1)S(1)}, u32[]{:S(2)}, u32[]{:S(2)}) collective-permute-start(bf16[128,768]{1,0:T(8,128)(2,1)S(1)} %images.4.refs_7_.refs_1_), channel_id=1, source_target_pairs={{0,1},{1,0},{2,3},{3,2},{4,5},{5,4},{6,7},{7,6},{8,9},{9,8},{10,11... | collective-permute-start | bytes 589832 | tf_op jit(solution)/shard_map/ppermute | solution.py:396
  19.2 2.2 %collective-permute-start.6 = (bf16[128,768]{1,0:T(8,128)(2,1)S(1)}, bf16[128,768]{1,0:T(8,128)(2,1)S(1)}, u32[]{:S(2)}, u32[]{:S(2)}) collective-permute-start(bf16[128,768]{1,0:T(8,128)(2,1)S(1)} %images.5.refs_2_), channel_id=1, source_target_pairs={{0,1},{1,0},{2,3},{3,2},{4,5},{5,4},{6,7},{7,6},{8,9},{9,8},{10,11... | collective-permute-start | bytes 589832 | tf_op jit(solution)/shard_map/ppermute | solution.py:396
  19.4 7.3 %collective-permute-start.3 = (bf16[128,768]{1,0:T(8,128)(2,1)S(1)}, bf16[128,768]{1,0:T(8,128)(2,1)S(1)}, u32[]{:S(2)}, u32[]{:S(2)}) collective-permute-start(bf16[128,768]{1,0:T(8,128)(2,1)S(1)} %images.5.refs_2_), channel_id=1, source_target_pairs={{2,0},{0,2},{3,1},{1,3},{6,4},{4,6},{7,5},{5,7},{10,8},{8,10},{11,... | collective-permute-start | bytes 589832 | tf_op jit(solution)/shard_map/ppermute | solution.py:393
  20.9 6.4 %collective-permute-start.9 = (bf16[128,768]{1,0:T(8,128)(2,1)S(1)}, bf16[128,768]{1,0:T(8,128)(2,1)S(1)}, u32[]{:S(2)}, u32[]{:S(2)}) collective-permute-start(bf16[128,768]{1,0:T(8,128)(2,1)S(1)} %collective-permute-done.2.refs_8_.refs_6_.refs_0_), channel_id=1, source_target_pairs={{0,1},{1,0},{2,3},{3,2},{4,5},{5,4},{6,7},{7,6},{8,9},{9,8},{10,11... | collective-permute-start | bytes 589832 | tf_op jit(solution)/shard_map/ppermute | solution.py:396
  21.0 6.3 %collective-permute-start.10 = (bf16[128,768]{1,0:T(8,128)(2,1)S(1)}, bf16[128,768]{1,0:T(8,128)(2,1)S(1)}, u32[]{:S(2)}, u32[]{:S(2)}) collective-permute-start(bf16[128,768]{1,0:T(8,128)(2,1)S(1)} %collective-permute-done.7.refs_7_.refs_1_), channel_id=1, source_target_pairs={{0,1},{1,0},{2,3},{3,2},{4,5},{5,4},{6,7},{7,6},{8,9},{9,8},{10,11... | collective-permute-start | bytes 589832 | tf_op jit(solution)/shard_map/ppermute | solution.py:396
  24.8 7.4 %copy-start.7 = (f32[640]{0:T(1024)S(1)}, f32[640]{0:T(1024)}, u32[]{:S(2)}) copy-start(f32[640]{0:T(1024)} %param.15) | copy-start | bytes 7684
  24.8 21.2 %copy-start = (f32[512]{0:T(512)S(1)}, f32[512]{0:T(512)}, u32[]{:S(2)}) copy-start(f32[512]{0:T(512)} %param.14) | copy-start | bytes 6148
  24.8 21.2 %copy-start.5 = (s32[512]{0:T(512)S(1)}, s32[512]{0:T(512)}, u32[]{:S(2)}) copy-start(s32[512]{0:T(512)} %param.16) | copy-start | bytes 6148
  24.8 21.1 %copy-start.6 = (s32[512]{0:T(512)S(1)}, s32[512]{0:T(512)}, u32[]{:S(2)}) copy-start(s32[512]{0:T(512)} %param.17) | copy-start | bytes 6148
  26.6 1.4 %collective-permute-start.11 = (bf16[128,768]{1,0:T(8,128)(2,1)S(1)}, bf16[128,768]{1,0:T(8,128)(2,1)S(1)}, u32[]{:S(2)}, u32[]{:S(2)}) collective-permute-start(bf16[128,768]{1,0:T(8,128)(2,1)S(1)} %collective-permute-done.3.refs_2_), channel_id=1, source_target_pairs={{0,1},{1,0},{2,3},{3,2},{4,5},{5,4},{6,7},{7,6},{8,9},{9,8},{10,11... | collective-permute-start | bytes 589832 | tf_op jit(solution)/shard_map/ppermute | solution.py:396
  26.6 6.9 %collective-permute-start.8 = (bf16[128,640]{1,0:T(8,128)(2,1)S(1)}, bf16[128,640]{1,0:T(8,128)(2,1)S(1)}, u32[]{:S(2)}, u32[]{:S(2)}) collective-permute-start(bf16[128,640]{1,0:T(8,128)(2,1)S(1)} %get-tuple-element.26), channel_id=1, source_target_pairs={{0,4},{4,0},{8,12},{12,8},{1,5},{5,1},{9,13},{13,9},{2,6},{6,2},{1... | collective-permute-start | bytes 491528 | tf_op jit(solution)/shard_map/ppermute | solution.py:416
  31.5 5.4 %collective-permute-start.12 = (bf16[64,640]{1,0:T(8,128)(2,1)S(1)}, bf16[64,640]{1,0:T(8,128)(2,1)S(1)}, u32[]{:S(2)}, u32[]{:S(2)}) collective-permute-start(bf16[64,640]{1,0:T(8,128)(2,1)S(1)} %get-tuple-element.29), channel_id=1, source_target_pairs={{0,4},{4,0},{8,12},{12,8},{1,5},{5,1},{9,13},{13,9},{2,6},{6,2},{1... | collective-permute-start | bytes 245768 | tf_op jit(solution)/shard_map/ppermute | solution.py:416
  32.2 6.3 %collective-permute-start.14 = (bf16[64,640]{1,0:T(8,128)(2,1)S(1)}, bf16[64,640]{1,0:T(8,128)(2,1)S(1)}, u32[]{:S(2)}, u32[]{:S(2)}) collective-permute-start(bf16[64,640]{1,0:T(8,128)(2,1)S(1)} %get-tuple-element.30), channel_id=1, source_target_pairs={{0,4},{4,0},{8,12},{12,8},{1,5},{5,1},{9,13},{13,9},{2,6},{6,2},{1... | collective-permute-start | bytes 245768 | tf_op jit(solution)/shard_map/ppermute | solution.py:416
  36.9 9.1 %collective-permute-start.13 = (bf16[64,640]{1,0:T(8,128)(2,1)S(1)}, bf16[64,640]{1,0:T(8,128)(2,1)S(1)}, u32[]{:S(2)}, u32[]{:S(2)}) collective-permute-start(bf16[64,640]{1,0:T(8,128)(2,1)S(1)} %select_convert_fusion.1), channel_id=1, source_target_pairs={{0,8},{4,12},{8,0},{12,4},{1,9},{5,13},{9,1},{13,5},{2,10},{6,14},... | collective-permute-start | bytes 245768 | tf_op jit(solution)/shard_map/ppermute | solution.py:436
  38.6 7.4 %collective-permute-start.15 = (bf16[64,640]{1,0:T(8,128)(2,1)S(1)}, bf16[64,640]{1,0:T(8,128)(2,1)S(1)}, u32[]{:S(2)}, u32[]{:S(2)}) collective-permute-start(bf16[64,640]{1,0:T(8,128)(2,1)S(1)} %select_convert_fusion), channel_id=1, source_target_pairs={{0,8},{4,12},{8,0},{12,4},{1,9},{5,13},{9,1},{13,5},{2,10},{6,14},... | collective-permute-start | bytes 245768 | tf_op jit(solution)/shard_map/ppermute | solution.py:436
  47.7 1.1 %collective-permute-start.16 = (f32[1,128]{1,0:T(1,128)S(1)}, f32[1,128]{1,0:T(1,128)S(1)}, u32[]{:S(2)}, u32[]{:S(2)}) collective-permute-start(f32[1,128]{1,0:T(1,128)S(1)} %get-tuple-element.33), channel_id=1, source_target_pairs={{0,1},{1,0},{2,3},{3,2},{4,5},{5,4},{6,7},{7,6},{8,9},{9,8},{10,11... | collective-permute-start | bytes 1544 | tf_op jit(solution)/shard_map/ppermute | solution.py:473
  48.8 3.5 %collective-permute-start.17 = (f32[1,128]{1,0:T(1,128)S(1)}, f32[1,128]{1,0:T(1,128)S(1)}, u32[]{:S(2)}, u32[]{:S(2)}) collective-permute-start(f32[1,128]{1,0:T(1,128)S(1)} %add.30), channel_id=1, source_target_pairs={{0,2},{2,0},{1,3},{3,1},{4,6},{6,4},{5,7},{7,5},{8,10},{10,8},{9,1... | collective-permute-start | bytes 1544 | tf_op jit(solution)/shard_map/ppermute | solution.py:476
